TPU v7x, 32 devices: a whole 2x2x4 slice. The times are simulated.
32 devices in a mesh: seq: 8 (over z, x), fsdp: 4 (over y, core).
Axes of the slice: x: 2, y: 2, z: 4, core: 2. Of those that a mesh axis runs over, the one named last changes fastest.
Arguments:
- hidden: bfloat16 [4, 1024, 2048], P('fsdp', 'seq'), may hold values from -6 to 6
- lengths: int32 [4], P('fsdp'), may hold values from 512 to 1024, as said below
- adapter_ids: int32 [4], P('fsdp'), may hold values from 0 to 7
- norm_gain: bfloat16 [2048], replicated, may hold values from 0.5 to 1.5
- in_proj_x: bfloat16 [2048, 4096], P(('seq', 'fsdp')), may hold values from -0.125 to 0.125
- in_proj_z: bfloat16 [2048, 4096], P(('seq', 'fsdp')), may hold values from -0.125 to 0.125
- conv_weight: bfloat16 [4, 4096], P(None, 'seq'), may hold values from -3 to 3
- conv_bias: bfloat16 [4096], P('seq'), may hold values from -3 to 3
- state_proj: bfloat16 [4096, 160], P('seq'), may hold values from -0.09375 to 0.09375
- step_proj: bfloat16 [128, 4096], P(None, 'seq'), may hold values from -0.5 to 0.5
- step_bias: bfloat16 [4096], P('seq'), may hold values from -6.5 to -2.5
- decay_log: bfloat16 [16, 4096], P(None, 'seq'), may hold values from 0 to 2.796875
- skip_gain: bfloat16 [4096], P('seq'), may hold values from 0.5 to 1.5
- out_proj: bfloat16 [4096, 2048], P(('seq', 'fsdp')), may hold values from -0.375 to 0.375
- in_down: bfloat16 [8, 2048, 16], replicated, may hold values from -0.125 to 0.125
- in_up: bfloat16 [8, 16, 8192], replicated, may hold values from -0.75 to 0.75
- state_down: bfloat16 [8, 4096, 16], P(None, 'seq'), may hold values from -0.09375 to 0.09375
- state_up: bfloat16 [8, 16, 160], replicated, may hold values from -0.75 to 0.75
- step_down: bfloat16 [8, 128, 16], replicated, may hold values from -0.5 to 0.5
- step_up: bfloat16 [8, 16, 4096], P(None, None, 'seq'), may hold values from -0.75 to 0.75
- out_down: bfloat16 [8, 4096, 16], replicated, may hold values from -0.09375 to 0.09375
- out_up: bfloat16 [8, 16, 2048], replicated, may hold values from -1.5 to 1.5
- cotangent: bfloat16 [4, 1024, 2048], P('fsdp', 'seq'), may hold values from -6 to 6
Outputs:
- block_out: bfloat16 [4, 1024, 2048], P('fsdp', 'seq')
- input_grad: float32 [4, 1024, 2048], P('fsdp', 'seq')
- in_down_grad: float32 [8, 2048, 16], replicated
- in_up_grad: float32 [8, 16, 8192], replicated
- state_down_grad: float32 [8, 4096, 16], P(None, 'seq')
- state_up_grad: float32 [8, 16, 160], replicated
- step_down_grad: float32 [8, 128, 16], replicated
- step_up_grad: float32 [8, 16, 4096], P(None, None, 'seq')
- out_down_grad: float32 [8, 4096, 16], replicated
- out_up_grad: float32 [8, 16, 2048], replicated
Inputs may be any that keep to these rules, and one draw needn't show every extreme that they name: Positions from lengths[b] on are padding; one sequence has all 1024 positions valid and one has 512.
All inputs are finite; a program needn't handle non-finite values.
Results may differ from a plain program's by a relative error of at most 0.015.
The roundings to bfloat16 on the way count: a program that leaves them out, or rounds other values in their place, can miss the bound.
Values may be sent and summed in bfloat16 or wider, within the bound.
No kernel may reach another device: no remote copies, remote signals or barrier semaphores. Data moves between devices by JAX's collectives and lax.ppermute only.
A program may use at most 256 MiB of HBM per device.

v0:
```python
import jax
import jax.numpy as jnp
from jax import lax
from jax.sharding import PartitionSpec as P

EPS = 1e-05
PRECISE = lax.Precision.HIGHEST


def product(left, right, precision=None):
    return jnp.dot(left, right, precision=precision, preferred_element_type=jnp.float32)


def product_t(left, right, precision=None):
    return lax.dot_general(
        left,
        right,
        (((1,), (1,)), ((), ())),
        precision=precision,
        preferred_element_type=jnp.float32,
    )


def product_tn(left, right, precision=None):
    return lax.dot_general(
        left,
        right,
        (((0,), (0,)), ((), ())),
        precision=precision,
        preferred_element_type=jnp.float32,
    )


def silu_grad(values):
    sigma = jax.nn.sigmoid(values)
    return sigma * (1.0 + values * (1.0 - sigma))


def select_one(picker, table):
    return jnp.einsum("a,abc->bc", picker, table, preferred_element_type=jnp.float32).astype(
        jnp.bfloat16
    )


def segments(values, length):
    return values.reshape((values.shape[0] // length, length) + values.shape[1:])


def combine_pairs(first, second):
    return (second[0] * first[0], second[0] * first[1] + second[1])


def scan_forward(delta, inputs, b_rows, c_rows, decay, skip):
    length = 16
    seg_delta = segments(delta, length)
    seg_input = segments(inputs, length)
    seg_b = segments(b_rows, length)
    seg_c = segments(c_rows, length)
    running = jnp.cumsum(seg_delta, axis=1)
    remaining = running[:, -1:, :] - running
    driven = seg_delta * seg_input
    ending = jnp.sum(
        jnp.exp(remaining[:, :, None, :] * decay) * driven[:, :, None, :] * seg_b[:, :, :, None],
        axis=1,
    )
    factor = jnp.exp(running[:, -1, None, :] * decay)
    joined = lax.associative_scan(combine_pairs, (factor, ending))[1]
    starts = jnp.concatenate([jnp.zeros_like(joined[:1]), joined[:-1]], axis=0)
    history = [starts]
    outputs = []
    for turn in range(length):
        carry = (
            jnp.exp(seg_delta[:, turn, None, :] * decay) * history[-1]
            + driven[:, turn, None, :] * seg_b[:, turn, :, None]
        )
        history.append(carry)
        outputs.append(jnp.sum(carry * seg_c[:, turn, :, None], axis=1))
    scanned = jnp.stack(outputs, axis=1).reshape(delta.shape) + skip * inputs
    return (scanned, history)


def scan_backward(delta, inputs, b_rows, c_rows, decay, skip, history, back_scan):
    length = 16
    seg_delta = segments(delta, length)
    seg_input = segments(inputs, length)
    seg_b = segments(b_rows, length)
    seg_c = segments(c_rows, length)
    seg_back = segments(back_scan, length)
    running = jnp.cumsum(seg_delta, axis=1)
    entering = jnp.sum(
        jnp.exp(running[:, :, None, :] * decay) * seg_c[:, :, :, None] * seg_back[:, :, None, :],
        axis=1,
    )
    factor = jnp.exp(running[:, -1, None, :] * decay)
    reversed_sums = lax.associative_scan(combine_pairs, (factor[::-1], entering[::-1]))[1][::-1]
    incoming = jnp.concatenate([reversed_sums[1:], jnp.zeros_like(reversed_sums[:1])], axis=0)
    grad_delta = [None] * length
    grad_input = [None] * length
    grad_b = [None] * length
    grad_c = [None] * length
    adjoint = incoming
    following = None
    for turn in range(length - 1, -1, -1):
        rate = jnp.exp(seg_delta[:, turn, None, :] * decay)
        carried = adjoint if turn == length - 1 else following * adjoint
        adjoint = seg_c[:, turn, :, None] * seg_back[:, turn, None, :] + carried
        following = rate
        grad_delta[turn] = jnp.sum(
            adjoint
            * (
                decay * rate * history[turn] + seg_b[:, turn, :, None] * seg_input[:, turn, None, :]
            ),
            axis=1,
        )
        grad_input[turn] = (
            jnp.sum(adjoint * seg_b[:, turn, :, None], axis=1) * seg_delta[:, turn]
            + skip * seg_back[:, turn]
        )
        grad_b[turn] = jnp.sum(
            adjoint * (seg_delta[:, turn] * seg_input[:, turn])[:, None, :], axis=2
        )
        grad_c[turn] = jnp.sum(seg_back[:, turn, None, :] * history[turn + 1], axis=2)
    return (
        jnp.stack(grad_delta, axis=1).reshape(delta.shape),
        jnp.stack(grad_input, axis=1).reshape(delta.shape),
        jnp.stack(grad_b, axis=1).reshape(b_rows.shape),
        jnp.stack(grad_c, axis=1).reshape(c_rows.shape),
    )


def body(
    hidden,
    lengths,
    adapter_ids,
    norm_gain,
    in_proj_x,
    in_proj_z,
    conv_weight,
    conv_bias,
    state_proj,
    step_proj,
    step_bias,
    decay_log,
    skip_gain,
    out_proj,
    in_down,
    in_up,
    state_down,
    state_up,
    step_down,
    step_up,
    out_down,
    out_up,
    cotangent,
):
    tokens = hidden.shape[1]
    inner = out_down.shape[1]
    ranks = step_proj.shape[0]
    states = decay_log.shape[0]
    adapter_count = in_down.shape[0]
    onehot = (lax.broadcasted_iota(jnp.int32, (adapter_count,), 0) == adapter_ids[0]).astype(
        jnp.float32
    )
    picker = onehot.astype(jnp.bfloat16)

    def spread_one(gradient):
        return onehot[:, None, None] * gradient[None]

    hidden_f = hidden[0].astype(jnp.float32)
    gain_f = norm_gain.astype(jnp.float32)
    inverse = lax.rsqrt(jnp.mean(hidden_f * hidden_f, axis=-1, keepdims=True) + EPS)
    normed = (hidden_f * inverse * gain_f).astype(jnp.bfloat16)
    in_down_sel = select_one(picker, in_down)
    in_up_sel = select_one(picker, in_up)
    low_in = product(normed, in_down_sel).astype(jnp.bfloat16)
    adapter_x = product(low_in, in_up_sel[:, :inner])
    adapter_z = product(low_in, in_up_sel[:, inner:])
    whole_x, whole_z, whole_out = (
        lax.all_gather(in_proj_x, ("seq", "fsdp"), axis=0, tiled=True),
        lax.all_gather(in_proj_z, ("seq", "fsdp"), axis=0, tiled=True),
        lax.all_gather(out_proj, ("seq", "fsdp"), axis=0, tiled=True),
    )
    proj_x = adapter_x + product(normed, whole_x)
    proj_z = adapter_z + product(normed, whole_z)
    x_chan, gate_chan = (
        lax.all_to_all(proj_x.astype(jnp.bfloat16), "seq", split_axis=1, concat_axis=0, tiled=True),
        lax.all_to_all(proj_z.astype(jnp.bfloat16), "seq", split_axis=1, concat_axis=0, tiled=True),
    )
    seq_len = x_chan.shape[0]
    kernel = conv_weight.astype(jnp.float32)
    taps = kernel.shape[0]
    x_float = x_chan.astype(jnp.float32)
    padded = jnp.concatenate(
        [jnp.zeros((taps - 1, x_float.shape[1]), jnp.float32), x_float], axis=0
    )
    conv_pre = conv_bias.astype(jnp.float32) + kernel[0] * padded[0:seq_len]
    for tap in range(1, taps):
        conv_pre = conv_pre + kernel[tap] * padded[tap : tap + seq_len]
    conv_out = jax.nn.silu(conv_pre).astype(jnp.bfloat16)
    state_down_sel = select_one(picker, state_down)
    state_up_sel = select_one(picker, state_up)
    step_down_sel = select_one(picker, step_down)
    step_up_sel = select_one(picker, step_up)
    proj_sum, low_sum = lax.psum(
        (product(conv_out, state_proj), product(conv_out, state_down_sel)), "seq"
    )
    low_state = low_sum.astype(jnp.bfloat16)
    mixed = proj_sum + product(low_state, state_up_sel)
    step_low = mixed[:, :ranks].astype(jnp.bfloat16)
    b_rows = mixed[:, ranks : ranks + states]
    c_rows = mixed[:, ranks + states :]
    step_mid = product(step_low, step_down_sel).astype(jnp.bfloat16)
    step_pre = (
        product(step_low, step_proj)
        + product(step_mid, step_up_sel)
        + step_bias.astype(jnp.float32)
    )
    delta = jax.nn.softplus(step_pre)
    decay = -jnp.exp(decay_log.astype(jnp.float32))
    inputs_f = conv_out.astype(jnp.float32)
    skip = skip_gain.astype(jnp.float32)
    scanned, history = scan_forward(delta, inputs_f, b_rows, c_rows, decay, skip)
    gate_f = gate_chan.astype(jnp.float32)
    gate_act = jax.nn.silu(gate_f)
    gated = (scanned * gate_act).astype(jnp.bfloat16)
    gated_tok = lax.all_to_all(gated, "seq", split_axis=0, concat_axis=1, tiled=True)
    out_down_sel = select_one(picker, out_down)
    out_up_sel = select_one(picker, out_up)
    low_out = product(gated_tok, out_down_sel).astype(jnp.bfloat16)
    base_out = product(low_out, out_up_sel)
    branch = base_out + product(gated_tok, whole_out)
    positions = lax.axis_index("seq") * tokens + lax.broadcasted_iota(jnp.int32, (tokens,), 0)
    valid = (positions < lengths[0]).astype(jnp.float32)[:, None]
    block_out = (hidden_f + valid * branch).astype(jnp.bfloat16)
    cot_f = cotangent[0].astype(jnp.float32)
    back_out = (valid * cot_f).astype(jnp.bfloat16)
    back_low_out = product_t(back_out, out_up_sel).astype(jnp.bfloat16)
    base_back = product_t(back_low_out, out_down_sel)
    gated_back = base_back + product_t(back_out, whole_out)
    grad_out_down = product_tn(gated_tok, back_low_out)
    grad_out_up = product_tn(low_out, back_out)
    back_chan = lax.all_to_all(
        gated_back.astype(jnp.bfloat16), "seq", split_axis=1, concat_axis=0, tiled=True
    ).astype(jnp.float32)
    back_scan = back_chan * gate_act
    back_gate = back_chan * scanned * silu_grad(gate_f)
    back_delta, back_conv, back_b, back_c = scan_backward(
        delta, inputs_f, b_rows, c_rows, decay, skip, history, back_scan
    )
    back_pre = (back_delta * jax.nn.sigmoid(step_pre)).astype(jnp.bfloat16)
    back_mid = product_t(back_pre, step_up_sel)
    back_step_low = product_t(back_pre, step_proj) + product_t(
        back_mid, step_down_sel.astype(jnp.float32), precision=PRECISE
    )
    grad_step_up = product_tn(step_mid, back_pre)
    grad_step_down = product_tn(step_low.astype(jnp.float32), back_mid, precision=PRECISE)
    back_mixed = lax.psum(
        jnp.concatenate([back_step_low, back_b, back_c], axis=1).astype(jnp.bfloat16), "seq"
    )
    back_low_state = product_t(back_mixed, state_up_sel).astype(jnp.bfloat16)
    grad_state_up = product_tn(low_state, back_mixed)
    grad_state_down = product_tn(conv_out, back_low_state)
    back_conv = (
        back_conv + product_t(back_mixed, state_proj) + product_t(back_low_state, state_down_sel)
    )
    back_conv_pre = back_conv * silu_grad(conv_pre)
    padded_back = jnp.concatenate(
        [back_conv_pre, jnp.zeros((taps - 1, back_conv_pre.shape[1]), jnp.float32)], axis=0
    )
    back_x = kernel[0] * padded_back[taps - 1 : taps - 1 + seq_len]
    for tap in range(1, taps):
        back_x = back_x + kernel[tap] * padded_back[taps - 1 - tap : taps - 1 - tap + seq_len]
    back_x_tok, back_z_tok = (
        lax.all_to_all(back_x.astype(jnp.bfloat16), "seq", split_axis=0, concat_axis=1, tiled=True),
        lax.all_to_all(
            back_gate.astype(jnp.bfloat16), "seq", split_axis=0, concat_axis=1, tiled=True
        ),
    )
    back_low_in = (
        product_t(back_x_tok, in_up_sel[:, :inner]) + product_t(back_z_tok, in_up_sel[:, inner:])
    ).astype(jnp.bfloat16)
    base_in = product_t(back_low_in, in_down_sel)
    back_normed = base_in + product_t(back_x_tok, whole_x) + product_t(back_z_tok, whole_z)
    grad_in_down = product_tn(normed, back_low_in)
    grad_in_up = jnp.concatenate(
        [product_tn(low_in, back_x_tok), product_tn(low_in, back_z_tok)], axis=1
    )
    gained = back_normed * gain_f
    input_grad = (
        cot_f
        + inverse * gained
        - hidden_f
        * inverse
        * inverse
        * inverse
        * jnp.mean(hidden_f * gained, axis=-1, keepdims=True)
    )
    in_down_grad, in_up_grad, step_down_grad, out_down_grad, out_up_grad = lax.psum(
        (
            spread_one(grad_in_down),
            spread_one(grad_in_up),
            spread_one(grad_step_down),
            spread_one(grad_out_down),
            spread_one(grad_out_up),
        ),
        ("seq", "fsdp"),
    )
    state_down_grad, state_up_grad, step_up_grad = (
        lax.psum(spread_one(grad_state_down).astype(jnp.bfloat16), "fsdp").astype(jnp.float32),
        lax.psum(spread_one(grad_state_up).astype(jnp.bfloat16), "fsdp").astype(jnp.float32),
        lax.psum(spread_one(grad_step_up).astype(jnp.bfloat16), "fsdp").astype(jnp.float32),
    )
    return (
        block_out[None],
        input_grad[None],
        in_down_grad,
        in_up_grad,
        state_down_grad,
        state_up_grad,
        step_down_grad,
        step_up_grad,
        out_down_grad,
        out_up_grad,
    )


def solution(mesh):
    in_specs = (
        P("fsdp", "seq", None),
        P("fsdp"),
        P("fsdp"),
        P(),
        P(("seq", "fsdp"), None),
        P(("seq", "fsdp"), None),
        P(None, "seq"),
        P("seq"),
        P("seq", None),
        P(None, "seq"),
        P("seq"),
        P(None, "seq"),
        P("seq"),
        P(("seq", "fsdp"), None),
        P(),
        P(),
        P(None, "seq", None),
        P(),
        P(),
        P(None, None, "seq"),
        P(),
        P(),
        P("fsdp", "seq", None),
    )
    out_specs = (
        P("fsdp", "seq", None),
        P("fsdp", "seq", None),
        P(),
        P(),
        P(None, "seq", None),
        P(),
        P(),
        P(None, None, "seq"),
        P(),
        P(),
    )
    return jax.shard_map(body, mesh=mesh, in_specs=in_specs, out_specs=out_specs, check_vma=False)
```

profile of v0, /device:TPU:0, one launch (start us, length us, event | category | flops | bytes accessed | tf_op | source)
XLA Modules:
  0.0 1330.3 jit_solution(1219553158264687934)
XLA Ops:
  16.0 11.0 fusion.42
  27.0 13.4 %copy.101 = bf16[1,4096,16]{1,2,0:T(8,128)(2,1)S(1)} copy(bf16[1,4096,16]{0,1,2:T(8,128)(2,1)} %fusion.42) | data formatting | bytes 262144 | tf_op jit(solution)/shard_map/a,abc->bc/dot_general | solution.py:40
  41.2 87.6 %all-gather.4.cloned.1.call-done = bf16[2048,4096]{1,0:T(8,128)(2,1)} async-done(((bf16[64,4096]{1,0:T(8,128)(2,1)}), bf16[2048,4096]{1,0:T(8,128)(2,1)}) %all-gather.4.cloned.1.call-update) | async-done | bytes 16777232 | tf_op jit(solution)/shard_map/all_gather | solution.py:179
  128.8 8.2 fusion.106
  138.5 3.8 all-to-all-start
  143.8 113.3 %all-gather.8.cloned.1.call-done = bf16[4096,2048]{1,0:T(8,128)(2,1)} async-done(((bf16[128,2048]{1,0:T(8,128)(2,1)}), bf16[4096,2048]{1,0:T(8,128)(2,1)}) %all-gather.8.cloned.1.call-update) | async-done | bytes 16777232 | tf_op jit(solution)/shard_map/all_gather | solution.py:181
  257.1 12.7 fusion.99
  278.7 107.4 %all-gather.6.cloned.1.call-done = bf16[2048,4096]{1,0:T(8,128)(2,1)} async-done(((bf16[64,4096]{1,0:T(8,128)(2,1)}), bf16[2048,4096]{1,0:T(8,128)(2,1)}) %all-gather.6.cloned.1.call-update) | async-done | bytes 16777232 | tf_op jit(solution)/shard_map/all_gather | solution.py:180
  386.1 8.2 fusion.104
  396.0 3.6 all-to-all-start.1
  408.9 48.1 %psum.78 = bf16[1024,16]{0,1:T(8,128)(2,1)S(1)} all-reduce(f32[1024,16]{0,1:T(8,128)S(1)} %fusion.63), channel_id=1, replica_groups=mesh['seq'=8,'fsdp'=4] {'seq'}, use_global_device_ids=true, to_apply=%region_2.3 | all-reduce | flops 16384 | bytes 98304 | tf_op jit(solution)/shard_map/psum | solution.py:204
  476.0 12.4 all-reduce.35.cloned.1.call-done
  500.8 5.4 slice.796
  506.2 4.1 slice.797
  510.3 5.5 slice.801
  516.1 4.9 slice_reduce_fusion
  521.2 4.1 copy.78
  525.6 4.9 slice_reduce_fusion.1
  531.6 11.5 fusion.109
  545.6 19.5 %multiply_reduce_fusion = (f32[64,16,512]{2,1,0:T(8,128)}, f32[64,16,512]{2,1,0:T(8,128)}) fusion(f32[64,16,512]{2,1,0:T(8,128)} %copy-done.10, f32[64,16,16]{2,1,0:T(8,128)S(1)} %copy.79, f32[64,16,512]{2,1,0:T(8,128)} %copy.78, f32[16,512]{1,0:T(8,128)S(1)} %exponential_negate_fusion, f32[64,16,16]{2,1,0:T(8,128)S(1)} %copy-done.106, ...), kind=kLoop, calls=%fused_computation | loop fusion | flops 66060288 | bytes 12746752 | tf_op jit(solution)/shard_map/reduce_sum | solution.py:90
  565.1 4.3 fusion.111
  646.6 5.4 slice.921
  721.6 10.0 slice_multiply_fusion.12
  731.7 6.2 slice_multiply_fusion.2
  740.6 6.2 pad.87
  749.2 6.2 pad.86
  758.4 6.8 pad.129
  765.2 6.8 pad.186
  779.9 6.2 pad.99
  788.5 6.2 pad.98
  797.4 6.7 pad.131
  804.1 6.7 pad.187
  810.8 4.1 slice_add_fusion.4
  815.0 4.1 slice.968
  825.5 8.6 multiply_reduce_fusion.39
  840.0 5.1 multiply_reduce_fusion.43
  845.2 6.5 multiply_reduce_fusion.45
  851.8 5.3 multiply_reduce_fusion.47
  857.1 4.8 multiply_reduce_fusion.65
  866.4 4.7 multiply_reduce_fusion.41
  877.4 7.4 multiply_reduce_fusion.34
  884.9 4.7 multiply_reduce_fusion.37
  890.5 4.4 multiply_reduce_fusion.52
  895.2 5.2 stack.291
  918.5 7.9 stack.273
  926.4 4.5 fusion.10
  933.2 3.9 all-to-all-start.2
  960.8 4.9 multiply_reduce_fusion.59
  983.3 7.1 multiply_add_fusion.37
  990.4 5.0 multiply_add_fusion.38
  995.5 4.4 multiply_add_fusion.39
  1002.0 7.8 stack.274
  1010.6 45.1 %all-reduce.37.cloned.1.call-done = bf16[1024,160]{0,1:T(8,128)(2,1)} async-done(((bf16[1024,160]{0,1:T(8,128)(2,1)}), bf16[1024,160]{0,1:T(8,128)(2,1)}) %all-reduce.37.cloned.1.call-update) | async-done | bytes 327696 | tf_op jit(solution)/shard_map/psum | solution.py:257
  1059.7 3.8 all-to-all-start.5
  1063.7 3.8 fusion.13
  1069.9 11.3 psum.83
  1081.8 8.0 all-reduce.41.cloned.1.call-done
  1093.7 5.5 all-to-all-start.4
  1102.9 21.3 %all-to-all-done.4 = bf16[8,128,512]{1,2,0:T(8,128)(2,1)} async-done(((bf16[8,128,512]{1,2,0:T(8,128)(2,1)}), bf16[8,128,512]{1,2,0:T(8,128)(2,1)}, u32[]{:S(2)}, u32[]{:S(2)}) %all-to-all-start.4) | async-done | bytes 1048608 | tf_op jit(solution)/shard_map/all_to_all | solution.py:274
  1131.6 9.3 fusion.130
  1142.1 12.8 fusion.133
  1154.9 13.2 fusion.132
  1171.3 141.2 %all-reduce.39.cloned.1.call-done = (f32[8,2048,16]{1,2,0:T(8,128)}, f32[8,16,8192]{2,1,0:T(8,128)}, f32[8,128,16]{1,2,0:T(8,128)}, f32[8,4096,16]{1,2,0:T(8,128)}, f32[8,16,2048]{2,1,0:T(8,128)}) async-done(((f32[8,2048,16]{1,2,0:T(8,128)}, f32[8,16,8192]{2,1,0:T(8,128)}, f32[8,128,16]{1,2,0:T(8,128)}, f32[8,4096,16]{1,2,0:T(8,128)}, f32[8,16,2048]{2,1,0:T(8,128)}), (f32[8,2048,16]{1,2,0:T(8,128)}, ...) | async-done | bytes 8454160 | tf_op jit(solution)/shard_map/psum | solution.py:298
  1314.7 4.8 copy.357
  (937 shorter events, 353.0 us)
Async XLA Ops:
  7.2 121.6 %all-gather.4.cloned.1.call-start = ((), (), s32[]{:S(2)}) async-start(), calls=%async_computation.6 | async-start | bytes 17301504 | tf_op jit(solution)/shard_map/all_gather | solution.py:179
  7.9 249.1 %all-gather.8.cloned.1.call-start = ((), (), s32[]{:S(2)}) async-start(), calls=%async_computation.9 | async-start | bytes 17301504 | tf_op jit(solution)/shard_map/all_gather | solution.py:181
  8.7 377.4 %all-gather.6.cloned.1.call-start = ((), (), s32[]{:S(2)}) async-start(), calls=%async_computation.8 | async-start | bytes 17301504 | tf_op jit(solution)/shard_map/all_gather | solution.py:180
  10.1 376.0 %copy-start.76 = (f32[2048]{0:T(1024)}, f32[2048]{0:T(1024)S(1)}, u32[]{:S(2)}) copy-start(f32[2048]{0:T(1024)S(1)} %convert_element_type.204) | copy-start | bytes 24580
  12.6 28.3 %copy-start.22 = (bf16[1,2048,16]{2,1,0:T(8,128)(2,1)}, bf16[1,2048,16]{2,1,0:T(8,128)(2,1)S(1)}, u32[]{:S(2)}) copy-start(bf16[1,2048,16]{2,1,0:T(8,128)(2,1)S(1)} %copy.89) | copy-start | bytes 196612
  15.4 379.0 %copy-start.47 = (bf16[1,16,8192]{2,1,0:T(8,128)(2,1)}, bf16[1,16,8192]{2,1,0:T(8,128)(2,1)S(1)}, u32[]{:S(2)}) copy-start(bf16[1,16,8192]{2,1,0:T(8,128)(2,1)S(1)} %copy.314) | copy-start | bytes 786436
  27.0 13.4 %copy-start.7 = (bf16[1,128,2048]{2,1,0:T(8,128)(2,1)S(1)}, bf16[1,128,2048]{2,1,0:T(8,128)(2,1)}, u32[]{:S(2)}) copy-start(bf16[1,128,2048]{2,1,0:T(8,128)(2,1)} %param.23) | copy-start | bytes 1572868
  27.0 13.6 %copy-start.283 = (bf16[16,512]{1,0:T(8,128)(2,1)S(1)}, bf16[16,512]{1,0:T(8,128)(2,1)}, u32[]{:S(2)}) copy-start(bf16[16,512]{1,0:T(8,128)(2,1)} %param.34) | copy-start | bytes 49156
  27.0 13.6 %copy-start.246 = (bf16[8,16,160]{2,1,0:T(8,128)(2,1)S(1)}, bf16[8,16,160]{2,1,0:T(8,128)(2,1)}, u32[]{:S(2)}) copy-start(bf16[8,16,160]{2,1,0:T(8,128)(2,1)} %param.40) | copy-start | bytes 122884
  40.4 229.4 %copy-start.67 = (bf16[1,4096,16]{1,2,0:T(8,128)(2,1)}, bf16[1,4096,16]{1,2,0:T(8,128)(2,1)S(1)}, u32[]{:S(2)}) copy-start(bf16[1,4096,16]{1,2,0:T(8,128)(2,1)S(1)} %copy.101) | copy-start | bytes 393220
  40.6 345.5 %copy-start.261 = (f32[128]{0:T(128)}, f32[128]{0:T(128)S(1)}, u32[]{:S(2)}) copy-start(f32[128]{0:T(128)S(1)} %add_rsqrt_fusion) | copy-start | bytes 1540
  40.8 447.6 %copy-start.244 = (bf16[1,16,160]{2,0,1:T(2,128)(2,1)}, bf16[1,16,160]{2,0,1:T(2,128)(2,1)S(1)}, u32[]{:S(2)}) copy-start(bf16[1,16,160]{2,0,1:T(2,128)(2,1)S(1)} %fusion.64) | copy-start | bytes 15364
  41.2 353.2 %copy-start.228 = (bf16[128,16]{0,1:T(8,128)(2,1)}, bf16[128,16]{0,1:T(8,128)(2,1)S(1)}, u32[]{:S(2)}) copy-start(bf16[128,16]{0,1:T(8,128)(2,1)S(1)} %convolution_convert_fusion.3) | copy-start | bytes 12292
  138.5 134.4 %all-to-all-start = ((bf16[128,8,512]{2,0,1:T(8,128)(2,1)}), bf16[128,8,512]{2,0,1:T(8,128)(2,1)S(1)}, u32[]{:S(2)}, u32[]{:S(2)}) async-start(bf16[128,8,512]{2,0,1:T(8,128)(2,1)} %bitcast.503), calls=%async_computation | async-start | bytes 2097152 | tf_op jit(solution)/shard_map/all_to_all | solution.py:186
  142.3 127.5 %copy-start.288 = (f32[128]{0:T(128)}, f32[128]{0:T(128)S(1)}, u32[]{:S(2)}) copy-start(f32[128]{0:T(128)S(1)} %compare_convert_fusion.1) | copy-start | bytes 1540
  143.8 126.0 %copy-start.273 = (bf16[128,16]{0,1:T(8,128)(2,1)}, bf16[128,16]{0,1:T(8,128)(2,1)S(1)}, u32[]{:S(2)}) copy-start(bf16[128,16]{0,1:T(8,128)(2,1)S(1)} %convolution_convert_fusion.4) | copy-start | bytes 12292
  273.9 122.0 %all-to-all-start.3 = ((bf16[128,8,512]{2,0,1:T(8,128)(2,1)}), bf16[128,8,512]{2,0,1:T(8,128)(2,1)S(1)}, u32[]{:S(2)}, u32[]{:S(2)}) async-start(bf16[128,8,512]{2,0,1:T(8,128)(2,1)} %bitcast.447), calls=%async_computation.3 | async-start | bytes 2097152 | tf_op jit(solution)/shard_map/all_to_all | solution.py:242
  396.0 11.0 copy-start.14
  396.0 63.8 %all-to-all-start.1 = ((bf16[128,8,512]{2,0,1:T(8,128)(2,1)}), bf16[128,8,512]{2,0,1:T(8,128)(2,1)S(1)}, u32[]{:S(2)}, u32[]{:S(2)}) async-start(bf16[128,8,512]{2,0,1:T(8,128)(2,1)} %bitcast.502), calls=%async_computation.1 | async-start | bytes 2097152 | tf_op jit(solution)/shard_map/all_to_all | solution.py:187
  399.5 88.9 %all-reduce.35.cloned.1.call-start = ((), (), s32[]{:S(2)}) async-start(), calls=%async_computation.7 | async-start | bytes 1310720 | tf_op jit(solution)/shard_map/psum | solution.py:204
  400.5 89.7 %copy-start.188 = (bf16[1,128,16]{2,1,0:T(8,128)(2,1)}, bf16[1,128,16]{2,1,0:T(8,128)(2,1)S(1)}, u32[]{:S(2)}) copy-start(bf16[1,128,16]{2,1,0:T(8,128)(2,1)S(1)} %copy.97) | copy-start | bytes 12292
  457.1 31.3 %copy-start.192 = (bf16[1024,16]{0,1:T(8,128)(2,1)}, bf16[1024,16]{0,1:T(8,128)(2,1)S(1)}, u32[]{:S(2)}) copy-start(bf16[1024,16]{0,1:T(8,128)(2,1)S(1)} %psum.78) | copy-start | bytes 98308
  472.4 17.4 %copy-start.171 = (bf16[128,512]{1,0:T(8,128)(2,1)S(1)}, bf16[128,512]{1,0:T(8,128)(2,1)}, u32[]{:S(2)}) copy-start(bf16[128,512]{1,0:T(8,128)(2,1)} %param.32) | copy-start | bytes 393220
  531.6 11.5 copy-start.20
  719.6 12.0 copy-start.3
  822.5 54.8 %copy-start.49 = (f32[64,512]{1,0:T(8,128)}, f32[64,512]{1,0:T(8,128)S(1)}, u32[]{:S(2)}) copy-start(f32[64,512]{1,0:T(8,128)S(1)} %get-tuple-element.352) | copy-start | bytes 393220
  822.5 62.3 %copy-start.42 = (f32[64,512]{1,0:T(8,128)}, f32[64,512]{1,0:T(8,128)S(1)}, u32[]{:S(2)}) copy-start(f32[64,512]{1,0:T(8,128)S(1)} %get-tuple-element.351) | copy-start | bytes 393220
  823.6 38.9 %copy-start.51 = (f32[64,512]{1,0:T(8,128)}, f32[64,512]{1,0:T(8,128)S(1)}, u32[]{:S(2)}) copy-start(f32[64,512]{1,0:T(8,128)S(1)} %get-tuple-element.284) | copy-start | bytes 393220
  823.7 61.2 %copy-start.44 = (f32[64,512]{1,0:T(8,128)}, f32[64,512]{1,0:T(8,128)S(1)}, u32[]{:S(2)}) copy-start(f32[64,512]{1,0:T(8,128)S(1)} %get-tuple-element.350) | copy-start | bytes 393220
  824.5 65.9 %copy-start.56 = (f32[64,512]{1,0:T(8,128)}, f32[64,512]{1,0:T(8,128)S(1)}, u32[]{:S(2)}) copy-start(f32[64,512]{1,0:T(8,128)S(1)} %get-tuple-element.362) | copy-start | bytes 393220
  834.1 50.8 %copy-start.12 = (f32[64,16,512]{2,0,1:T(8,128)}, f32[64,16,512]{2,0,1:T(8,128)S(1)}, u32[]{:S(2)}) copy-start(f32[64,16,512]{2,0,1:T(8,128)S(1)} %get-tuple-element.133) | copy-start | bytes 6291460
  845.1 21.3 %copy-start.4 = (f32[64,16,512]{2,0,1:T(8,128)}, f32[64,16,512]{2,0,1:T(8,128)S(1)}, u32[]{:S(2)}) copy-start(f32[64,16,512]{2,0,1:T(8,128)S(1)} %get-tuple-element.135) | copy-start | bytes 6291460
  905.8 10.5 copy-start.179
  906.7 10.4 copy-start.84
  906.7 11.1 copy-start.83
  930.9 10.7 copy-start.280
  930.9 11.3 copy-start.279
  930.9 14.5 %copy-start.278 = (bf16[64,16]{0,1:T(8,128)(2,1)S(1)}, bf16[64,16]{0,1:T(8,128)(2,1)}, u32[]{:S(2)}) copy-start(bf16[64,16]{0,1:T(8,128)(2,1)} %get-tuple-element.48) | copy-start | bytes 6148
  930.9 15.0 %copy-start.277 = (bf16[64,16]{0,1:T(8,128)(2,1)S(1)}, bf16[64,16]{0,1:T(8,128)(2,1)}, u32[]{:S(2)}) copy-start(bf16[64,16]{0,1:T(8,128)(2,1)} %get-tuple-element.26) | copy-start | bytes 6148
  930.9 26.8 %copy-start.282 = (bf16[64,16]{0,1:T(8,128)(2,1)S(1)}, bf16[64,16]{0,1:T(8,128)(2,1)}, u32[]{:S(2)}) copy-start(bf16[64,16]{0,1:T(8,128)(2,1)} %get-tuple-element.47) | copy-start | bytes 6148
  930.9 27.4 %copy-start.271 = (bf16[64,16]{0,1:T(8,128)(2,1)S(1)}, bf16[64,16]{0,1:T(8,128)(2,1)}, u32[]{:S(2)}) copy-start(bf16[64,16]{0,1:T(8,128)(2,1)} %get-tuple-element.64) | copy-start | bytes 6148
  930.9 28.0 %copy-start.281 = (bf16[64,16]{0,1:T(8,128)(2,1)S(1)}, bf16[64,16]{0,1:T(8,128)(2,1)}, u32[]{:S(2)}) copy-start(bf16[64,16]{0,1:T(8,128)(2,1)} %get-tuple-element.87) | copy-start | bytes 6148
  930.9 28.6 %copy-start.276 = (bf16[64,16]{0,1:T(8,128)(2,1)S(1)}, bf16[64,16]{0,1:T(8,128)(2,1)}, u32[]{:S(2)}) copy-start(bf16[64,16]{0,1:T(8,128)(2,1)} %get-tuple-element.65) | copy-start | bytes 6148
  930.9 29.2 %copy-start.275 = (bf16[64,16]{0,1:T(8,128)(2,1)S(1)}, bf16[64,16]{0,1:T(8,128)(2,1)}, u32[]{:S(2)}) copy-start(bf16[64,16]{0,1:T(8,128)(2,1)} %get-tuple-element.88) | copy-start | bytes 6148
  930.9 29.8 %copy-start.254 = (f32[64,16]{0,1:T(8,128)S(1)}, f32[64,16]{0,1:T(8,128)}, u32[]{:S(2)}) copy-start(f32[64,16]{0,1:T(8,128)} %get-tuple-element.98) | copy-start | bytes 12292
  933.2 126.5 %all-to-all-start.2 = ((bf16[8,128,512]{1,2,0:T(8,128)(2,1)}), bf16[8,128,512]{1,2,0:T(8,128)(2,1)S(1)}, u32[]{:S(2)}, u32[]{:S(2)}) async-start(bf16[8,128,512]{1,2,0:T(8,128)(2,1)} %copy.76), calls=%async_computation.2 | async-start | bytes 2097152 | tf_op jit(solution)/shard_map/all_to_all | solution.py:226
  937.1 118.5 %all-reduce.37.cloned.1.call-start = ((), (), s32[]{:S(2)}) async-start(), calls=%async_computation.10 | async-start | bytes 655360 | tf_op jit(solution)/shard_map/psum | solution.py:257
  954.2 12.7 copy-start.285
  957.7 10.3 copy-start.113
  957.7 10.3 copy-start.114
  983.2 106.6 %all-reduce.41.cloned.1.call-start = ((), (), s32[]{:S(2)}) async-start(), calls=%async_computation.12 | async-start | bytes 524288 | tf_op jit(solution)/shard_map/psum | solution.py:309
  1002.0 53.7 %copy-start.245 = (bf16[1,16,160]{2,0,1:T(2,128)(2,1)S(1)}, bf16[1,16,160]{2,0,1:T(2,128)(2,1)}, u32[]{:S(2)}) copy-start(bf16[1,16,160]{2,0,1:T(2,128)(2,1)} %copy-done.244) | copy-start | bytes 15364
  1002.0 55.9 %copy-start.79 = (bf16[512,160]{0,1:T(8,128)(2,1)S(1)}, bf16[512,160]{0,1:T(8,128)(2,1)}, u32[]{:S(2)}) copy-start(bf16[512,160]{0,1:T(8,128)(2,1)} %param.31) | copy-start | bytes 491524
  1059.7 34.0 %all-to-all-start.5 = ((bf16[8,128,512]{1,2,0:T(8,128)(2,1)}), bf16[8,128,512]{1,2,0:T(8,128)(2,1)S(1)}, u32[]{:S(2)}, u32[]{:S(2)}) async-start(bf16[8,128,512]{1,2,0:T(8,128)(2,1)} %copy.87), calls=%async_computation.5 | async-start | bytes 2097152 | tf_op jit(solution)/shard_map/all_to_all | solution.py:275
  1068.5 24.6 %copy-start.68 = (bf16[1,4096,16]{1,2,0:T(8,128)(2,1)S(1)}, bf16[1,4096,16]{1,2,0:T(8,128)(2,1)}, u32[]{:S(2)}) copy-start(bf16[1,4096,16]{1,2,0:T(8,128)(2,1)} %copy-done.67) | copy-start | bytes 393220
  1068.6 24.7 %copy-start.274 = (bf16[128,16]{0,1:T(8,128)(2,1)S(1)}, bf16[128,16]{0,1:T(8,128)(2,1)}, u32[]{:S(2)}) copy-start(bf16[128,16]{0,1:T(8,128)(2,1)} %copy-done.273) | copy-start | bytes 12292
  1093.7 30.6 %all-to-all-start.4 = ((bf16[8,128,512]{1,2,0:T(8,128)(2,1)}), bf16[8,128,512]{1,2,0:T(8,128)(2,1)}, u32[]{:S(2)}, u32[]{:S(2)}) async-start(bf16[8,128,512]{1,2,0:T(8,128)(2,1)} %copy.86), calls=%async_computation.4 | async-start | bytes 2097152 | tf_op jit(solution)/shard_map/all_to_all | solution.py:274
  1099.2 213.2 %all-reduce.39.cloned.1.call-start = ((), (), s32[]{:S(2)}) async-start(), calls=%async_computation.11 | async-start | bytes 16908288 | tf_op jit(solution)/shard_map/psum | solution.py:298
  1100.2 24.1 %copy-start.48 = (bf16[1,16,8192]{2,1,0:T(8,128)(2,1)S(1)}, bf16[1,16,8192]{2,1,0:T(8,128)(2,1)}, u32[]{:S(2)}) copy-start(bf16[1,16,8192]{2,1,0:T(8,128)(2,1)} %copy-done.47) | copy-start | bytes 786436
  1102.9 24.6 %copy-start.8 = (bf16[1,128,2048]{2,1,0:T(8,128)(2,1)S(1)}, bf16[1,128,2048]{2,1,0:T(8,128)(2,1)}, u32[]{:S(2)}) copy-start(bf16[1,128,2048]{2,1,0:T(8,128)(2,1)} %param.23) | copy-start | bytes 1572868
  1102.9 24.6 %copy-start.77 = (f32[2048]{0:T(1024)S(1)}, f32[2048]{0:T(1024)}, u32[]{:S(2)}) copy-start(f32[2048]{0:T(1024)} %copy-done.76) | copy-start | bytes 24580
  1102.9 24.6 %copy-start.262 = (f32[128]{0:T(128)S(1)}, f32[128]{0:T(128)}, u32[]{:S(2)}) copy-start(f32[128]{0:T(128)} %copy-done.261) | copy-start | bytes 1540
  1154.9 13.2 copy-start.23
  1154.9 13.2 copy-start.27
  (242 other events, 1049.2 us)
Sparse Core Ops, SparseCore 0:
  10.9 117.8 all-gather.3
  131.6 125.3 all-gather.7
  259.9 126.1 all-gather.5
  405.5 82.8 all-reduce.34
  983.3 72.2 all-reduce.36
  1058.5 31.2 all-reduce.40
  1131.7 180.6 all-reduce.38
where the time goes:
time: 1350 us; the launch traced here: 1330 us
  waiting for transfers between devices  538 us (40%)
  local copies, waits for them, and re-layouts  368 us (27%)
  other arithmetic  209 us (15%)
  matrix products  111 us (8%)
  blocking collectives  59.4 us (4%)
  starting transfers between devices  24.7 us (2%)
  between operations  19.6 us (1%)
    psum x1, waiting for transfers between devices, body(): lax.psum((spread_one(grad_in_down), spread_one(grad_in_up), spread_one(gr...  141 us
    all_gather x1, waiting for transfers between devices, body(): lax.all_gather(out_proj, ('seq', 'fsdp'), axis=0, tiled=True)  113 us
    all_gather x1, waiting for transfers between devices, body(): lax.all_gather(in_proj_z, ('seq', 'fsdp'), axis=0, tiled=True)  107 us
    all_gather x1, waiting for transfers between devices, body(): lax.all_gather(in_proj_x, ('seq', 'fsdp'), axis=0, tiled=True)  87.6 us
    slice x31, local copies, waits for them, and re-layouts, scan_forward(): joined = lax.associative_scan(combine_pairs, (factor, ending))[1]  76.3 us
    unnamed x666, local copies, waits for them, and re-layouts  75.5 us
    slice x36, local copies, waits for them, and re-layouts, scan_backward(): lax.associative_scan(combine_pairs, (factor[::-1], entering[::-1]))[1][::-1]  69.5 us
    dot_general x14, matrix products, product_t(): lax.dot_general(left, right, (((1,), (1,)), ((), ())), precision=precisio...  54.5 us
  transfers between devices with their start and end apart: 13, of which 8 were waited for; matrix products, arithmetic and copies ran while one was open for 17% of the time, Pallas kernels for 0%

commit v1 on v0

v1 whole, which is shorter than its diff:
```python
import functools
import jax
import jax.numpy as jnp
from jax import lax
from jax.experimental import pallas as pl
from jax.experimental.pallas import tpu as pltpu
from jax.sharding import PartitionSpec as P

F32 = jnp.float32
BF16 = jnp.bfloat16
LOG2E = 1.4426950408889634


def silu_grad(values):
    sigma = jax.nn.sigmoid(values)
    return sigma * (1.0 + values * (1.0 - sigma))


def softplus(v):
    return jnp.maximum(v, 0.0) + jnp.log1p(jnp.exp(-jnp.abs(v)))


def nt(left, right):
    return lax.dot_general(left, right, (((1,), (1,)), ((), ())), preferred_element_type=F32)


def nn(left, right):
    return jnp.dot(left, right, preferred_element_type=F32)


def spread_matrix(states, sub):
    row = lax.broadcasted_iota(jnp.int32, (states, sub * states), 0)
    col = lax.broadcasted_iota(jnp.int32, (states, sub * states), 1)
    return (lax.rem(col, states) == row).astype(BF16)


def own_step_mask(rows, states, sub):
    row = lax.broadcasted_iota(jnp.int32, (rows, sub * states), 0)
    col = lax.broadcasted_iota(jnp.int32, (rows, sub * states), 1)
    return (lax.rem(row, sub) == lax.div(col, states)).astype(F32)


def scan_forward_kernel(
    low_ref, wstep_ref, bias_ref, bt_ref, c_ref, u_ref, z_ref, decay_ref, skip_ref,
    gated_ref, scanned_ref, states_ref,
    carry, delta_s, du_s, cm_s, *, sub,
):
    rows = u_ref.shape[0]
    states = decay_ref.shape[0]

    @pl.when(pl.program_id(0) == 0)
    def _():
        carry[...] = jnp.zeros_like(carry)

    pre = nn(low_ref[...], wstep_ref[...]) + bias_ref[...]
    delta = softplus(pre)
    u = u_ref[...].astype(F32)
    delta_s[...] = delta
    du_s[...] = delta * u
    cm_s[...] = (nn(c_ref[...], spread_matrix(states, sub)) * own_step_mask(rows, states, sub)).astype(BF16)
    rate = decay_ref[...] * LOG2E

    def group(k, s):
        base = pl.multiple_of(k * sub, sub)
        bt = bt_ref[k]
        for t in range(sub):
            dl = delta_s[pl.ds(base + t, 1), :]
            du = du_s[pl.ds(base + t, 1), :]
            s = jnp.exp2(dl * rate) * s + du * bt[:, t : t + 1]
            states_ref[pl.ds(pl.multiple_of((base + t) * states, states), states), :] = s.astype(BF16)
        scanned_ref[pl.ds(base, sub), :] = nn(
            cm_s[pl.ds(base, sub), :],
            states_ref[pl.ds(pl.multiple_of(base * states, sub * states), sub * states), :],
        )
        return s

    carry[...] = lax.fori_loop(0, rows // sub, group, carry[...])
    scanned = scanned_ref[...] + skip_ref[...] * u
    scanned_ref[...] = scanned
    gated_ref[...] = (scanned * jax.nn.silu(z_ref[...].astype(F32))).astype(BF16)


def scan_forward(low, wstep, bias, bt, c, u, z, decay, skip, block=128):
    length, chans = u.shape
    states = decay.shape[0]
    sub = bt.shape[2]
    block = min(block, length)
    seq = lambda cols: pl.BlockSpec((block, cols), lambda i: (i, 0))
    whole = lambda a: pl.BlockSpec(a.shape, lambda i: (0,) * a.ndim)
    return pl.pallas_call(
        functools.partial(scan_forward_kernel, sub=sub),
        grid=(length // block,),
        in_specs=[
            seq(low.shape[1]), whole(wstep), whole(bias),
            pl.BlockSpec((block // sub, states, sub), lambda i: (i, 0, 0)),
            seq(states), seq(chans), seq(chans), whole(decay), whole(skip),
        ],
        out_specs=[seq(chans), seq(chans), pl.BlockSpec((block * states, chans), lambda i: (i, 0))],
        out_shape=[
            jax.ShapeDtypeStruct((length, chans), BF16),
            jax.ShapeDtypeStruct((length, chans), F32),
            jax.ShapeDtypeStruct((length * states, chans), BF16),
        ],
        scratch_shapes=[
            pltpu.VMEM((states, chans), F32),
            pltpu.VMEM((block, chans), F32),
            pltpu.VMEM((block, chans), F32),
            pltpu.VMEM((block, sub * states), BF16),
        ],
        compiler_params=pltpu.CompilerParams(vmem_limit_bytes=40 << 20),
        name="scan_forward",
    )(low, wstep, bias, bt, c, u, z, decay, skip)


def scan_backward_kernel(
    low_ref, wstep_ref, bias_ref, ct_ref, b_ref, u_ref, z_ref, scanned_ref, bg_ref, states_ref, before_ref,
    decay_ref, skip_ref,
    pre_ref, conv_ref, bz_ref, mixed_ref,
    carry, delta_s, du_s, bs_s, bm_s, g_s, q_s, w_s, bd_s, r1_s, r2_s, *, sub,
):
    rows = u_ref.shape[0]
    states = decay_ref.shape[0]
    step = pl.program_id(0)
    first = step == pl.num_programs(0) - 1

    @pl.when(step == 0)
    def _():
        carry[...] = jnp.zeros_like(carry)

    pre = nn(low_ref[...], wstep_ref[...]) + bias_ref[...]
    delta = softplus(pre)
    u = u_ref[...].astype(F32)
    z = z_ref[...].astype(F32)
    bg = bg_ref[...].astype(F32)
    sigma = jax.nn.sigmoid(z)
    bs_s[...] = bg * (z * sigma)
    bz_ref[...] = (bg * scanned_ref[...] * (sigma * (1.0 + z * (1.0 - sigma)))).astype(BF16)
    delta_s[...] = delta
    du_s[...] = delta * u
    mask = own_step_mask(rows, states, sub)
    bm_s[...] = (nn(b_ref[...], spread_matrix(states, sub)) * mask).astype(BF16)
    ones = own_step_mask(sub, states, sub).astype(BF16)
    decay = decay_ref[...]
    rate = decay * LOG2E
    groups = rows // sub

    def group(i, h):
        k = groups - 1 - i
        base = pl.multiple_of(k * sub, sub)
        ct = ct_ref[k]
        for t in range(sub - 1, -1, -1):
            dl = delta_s[pl.ds(base + t, 1), :]
            bs = bs_s[pl.ds(base + t, 1), :]
            g = bs * ct[:, t : t + 1] + h
            h = g * jnp.exp2(dl * rate)
            if t:
                sp = states_ref[pl.ds(pl.multiple_of((base + t - 1) * states, states), states), :].astype(F32)
            else:
                at = pl.multiple_of(jnp.maximum(base - 1, 0) * states, states)
                inside = states_ref[pl.ds(at, states), :].astype(F32)
                sp = jnp.where(k > 0, inside, jnp.where(first, 0.0, before_ref[...].astype(F32)))
            g_s[t * states : (t + 1) * states, :] = g.astype(BF16)
            q_s[t * states : (t + 1) * states, :] = (h * decay * sp).astype(BF16)
        bd_s[pl.ds(base, sub), :] = nn(ones, q_s[...])
        w_s[pl.ds(base, sub), :] = nn(bm_s[pl.ds(base, sub), :], g_s[...])
        r1_s[pl.ds(base, sub), :] = nt(du_s[pl.ds(base, sub), :].astype(BF16), g_s[...])
        r2_s[pl.ds(base, sub), :] = nt(
            bs_s[pl.ds(base, sub), :].astype(BF16),
            states_ref[pl.ds(pl.multiple_of(base * states, sub * states), sub * states), :],
        )
        return h

    carry[...] = lax.fori_loop(0, groups, group, carry[...])
    w = w_s[...]
    conv_ref[...] = w * delta + skip_ref[...] * bs_s[...]
    back_pre = ((bd_s[...] + w * u) * jax.nn.sigmoid(pre)).astype(BF16)
    pre_ref[...] = back_pre
    fold = spread_matrix(states, sub)
    back_low = nt(back_pre, wstep_ref[...])
    ranks = back_low.shape[1] - states
    back_b = nt((r1_s[...] * mask).astype(BF16), fold)
    back_c = nt((r2_s[...] * mask).astype(BF16), fold)
    mixed_ref[...] = jnp.concatenate([back_low, back_b, back_c], axis=1)


def scan_backward(low, wstep, bias, ct, b, u, z, scanned, bg, kept, decay, skip, block=128):
    length, chans = u.shape
    states = decay.shape[0]
    sub = ct.shape[2]
    block = min(block, length)
    last = length // block - 1
    seq = lambda cols: pl.BlockSpec((block, cols), lambda i: (last - i, 0))
    whole = lambda a: pl.BlockSpec(a.shape, lambda i: (0,) * a.ndim)
    cols = low.shape[1] + 2 * states
    return pl.pallas_call(
        functools.partial(scan_backward_kernel, sub=sub),
        grid=(last + 1,),
        in_specs=[
            seq(low.shape[1]), whole(wstep), whole(bias),
            pl.BlockSpec((block // sub, states, sub), lambda i: (last - i, 0, 0)),
            seq(states), seq(chans), seq(chans), seq(chans), seq(chans),
            pl.BlockSpec((block * states, chans), lambda i: (last - i, 0)),
            pl.BlockSpec((states, chans), lambda i: (jnp.maximum((last - i) * block - 1, 0), 0)),
            whole(decay), whole(skip),
        ],
        out_specs=[seq(chans), seq(chans), seq(chans), seq(cols)],
        out_shape=[
            jax.ShapeDtypeStruct((length, chans), BF16),
            jax.ShapeDtypeStruct((length, chans), F32),
            jax.ShapeDtypeStruct((length, chans), BF16),
            jax.ShapeDtypeStruct((length, cols), F32),
        ],
        scratch_shapes=[
            pltpu.VMEM((states, chans), F32),
            pltpu.VMEM((block, chans), F32),
            pltpu.VMEM((block, chans), F32),
            pltpu.VMEM((block, chans), F32),
            pltpu.VMEM((block, sub * states), BF16),
            pltpu.VMEM((sub * states, chans), BF16),
            pltpu.VMEM((sub * states, chans), BF16),
            pltpu.VMEM((block, chans), F32),
            pltpu.VMEM((block, chans), F32),
            pltpu.VMEM((block, sub * states), F32),
            pltpu.VMEM((block, sub * states), F32),
        ],
        compiler_params=pltpu.CompilerParams(vmem_limit_bytes=40 << 20),
        name="scan_backward",
    )(low, wstep, bias, ct, b, u, z, scanned, bg, kept, kept, decay, skip)


EPS = 1e-05


def ring_order(size):
    return list(range(0, size, 2)) + list(range(1, size, 2))[::-1]


def ring_place(size, offset, axis):
    order = ring_order(size)
    position = {place: i for i, place in enumerate(order)}
    table = [order[(position[i] + offset) % size] for i in range(size)]
    return jnp.asarray(table, jnp.int32)[lax.axis_index(axis)]


def ring_send(value, size, hop, axis):
    order = ring_order(size)
    pairs = [(order[i], order[(i + hop) % size]) for i in range(size)]
    return lax.ppermute(value, axis, pairs)


def ring_gather(own, size, axis):
    rows = own.shape[0]
    half = rows // 2
    pieces = [(0, 0, own)]
    ahead = back = own
    for step in range(1, size // 2):
        ahead, back = ring_send(ahead, size, 1, axis), ring_send(back, size, -1, axis)
        pieces += [(-step, 0, ahead), (step, 0, back)]
    far = size // 2
    pieces += [
        (-far, 0, ring_send(ahead[:half], size, 1, axis)),
        (far, half, ring_send(back[half:], size, -1, axis)),
    ]
    out = jnp.zeros((size * rows,) + own.shape[1:], own.dtype)
    for offset, start, piece in pieces:
        at = ring_place(size, offset, axis) * rows + start
        out = lax.dynamic_update_slice_in_dim(out, piece, at, 0)
    return out


def ring_scatter(partial, size, axis):
    rows = partial.shape[0] // size
    half = rows // 2

    def block(offset):
        at = ring_place(size, offset, axis) * rows
        return lax.dynamic_slice_in_dim(partial, at, rows, 0).astype(F32)

    far = size // 2
    ahead = ring_send(block(far)[:half].astype(BF16), size, 1, axis)
    back = ring_send(block(far)[half:].astype(BF16), size, -1, axis)
    for left in range(far - 1, 0, -1):
        mine, other = block(left), block(-left)
        if left == far - 1:
            mine = mine.at[:half].add(ahead.astype(F32))
            other = other.at[half:].add(back.astype(F32))
        else:
            mine, other = mine + ahead.astype(F32), other + back.astype(F32)
        ahead = ring_send(mine.astype(BF16), size, 1, axis)
        back = ring_send(other.astype(BF16), size, -1, axis)
    return block(0) + ahead.astype(F32) + back.astype(F32)


def swap(value, size, bit, axis):
    return lax.ppermute(value, axis, [(i, i ^ bit) for i in range(size)])


def bits_of(size):
    bit = size // 2
    while bit:
        yield bit
        bit //= 2


def swap_gather(own, size, axis):
    place = lax.axis_index(axis)
    held = [(place, own)]
    for bit in bits_of(size):
        held += [(at ^ bit, swap(block, size, bit, axis)) for at, block in held]
    return held


def small_gather(own, size, axis):
    place = lax.axis_index(axis)
    held = own[None]
    for bit in bits_of(size):
        got = swap(held, size, bit, axis)
        low = (place & bit) == 0
        held = jnp.where(low, jnp.stack([held, got]), jnp.stack([got, held]))
        held = held.reshape((-1,) + own.shape)
    count = len(list(bits_of(size)))
    dims = held.reshape((2,) * count + own.shape)
    order = tuple(range(count))[::-1] + tuple(range(count, dims.ndim))
    return dims.transpose(order).reshape((size * own.shape[0],) + own.shape[1:])


def small_scatter(partial, size, axis):
    got = lax.all_to_all(partial, axis, split_axis=0, concat_axis=0, tiled=True)
    return got.reshape((size, -1) + partial.shape[1:]).astype(F32).sum(0)


def shift_down(values, count):
    if not count:
        return values
    return jnp.concatenate([jnp.zeros((count, values.shape[1]), values.dtype), values[:-count]], 0)


def shift_up(values, count):
    if not count:
        return values
    return jnp.concatenate([values[count:], jnp.zeros((count, values.shape[1]), values.dtype)], 0)


def tn(left, right):
    return lax.dot_general(left, right, (((0,), (0,)), ((), ())), preferred_element_type=F32)


def body(
    hidden, lengths, adapter_ids, norm_gain, in_proj_x, in_proj_z, conv_weight, conv_bias, state_proj,
    step_proj, step_bias, decay_log, skip_gain, out_proj, in_down, in_up, state_down, state_up, step_down,
    step_up, out_down, out_up, cotangent,
):
    parts, groups = lax.axis_size("seq"), lax.axis_size("fsdp")
    part, group = lax.axis_index("seq"), lax.axis_index("fsdp")
    tokens, width = hidden.shape[1:]
    taps, chans = conv_weight.shape
    inner = out_down.shape[1]
    ranks = step_proj.shape[0]
    states = decay_log.shape[0]
    rank = in_down.shape[2]
    adapters = in_down.shape[0]
    ident = adapter_ids[0]
    sub = 16

    def pick(table):
        return lax.dynamic_index_in_dim(table, ident, 0, keepdims=False)

    hidden_f = hidden[0].astype(F32)
    gain_f = norm_gain.astype(F32)
    inverse = lax.rsqrt(jnp.mean(hidden_f * hidden_f, axis=-1, keepdims=True) + EPS)
    normed = (hidden_f * inverse * gain_f).astype(BF16)
    positions = part * tokens + lax.broadcasted_iota(jnp.int32, (tokens, 1), 0)
    valid = (positions < lengths[0]).astype(F32)
    cot_f = cotangent[0].astype(F32)
    back_out = (valid * cot_f).astype(BF16)

    def columns(weight):
        rows = weight.shape[0]
        mine = lax.all_to_all(weight, "seq", split_axis=1, concat_axis=0, tiled=True)
        out = jnp.zeros((parts, groups, rows, chans), weight.dtype)
        for at, block in swap_gather(mine.reshape(parts, 1, rows, chans), groups, "fsdp"):
            out = lax.dynamic_update_slice(out, block, (0, at, 0, 0))
        return out.reshape(parts * groups * rows, chans)

    def columns_later(weight):
        rows = weight.shape[0]
        mine = lax.all_to_all(weight, "seq", split_axis=1, concat_axis=0, tiled=True)
        out = lax.all_gather(mine, "fsdp").reshape(groups, parts, rows, chans)
        return out.transpose(1, 0, 2, 3).reshape(parts * groups * rows, chans)

    back_out_all = lax.all_gather(back_out, "seq", axis=0, tiled=True)
    whole_x = columns(in_proj_x)
    normed_all = ring_gather(normed, parts, "seq")
    whole_z = columns_later(in_proj_z)
    whole_out = lax.all_gather(out_proj, "fsdp", axis=0, tiled=True)

    in_down_sel = pick(in_down)
    up_x = lax.dynamic_slice(in_up, (ident, 0, part * chans), (1, rank, chans))[0]
    up_z = lax.dynamic_slice(in_up, (ident, 0, inner + part * chans), (1, rank, chans))[0]
    out_down_sel = lax.dynamic_slice(out_down, (ident, part * chans, 0), (1, chans, rank))[0]
    state_down_sel, state_up_sel = pick(state_down), pick(state_up)
    step_down_sel, step_up_sel = pick(step_down), pick(step_up)
    out_up_sel = pick(out_up)

    low_in = nn(normed_all, in_down_sel).astype(BF16)
    x = (nn(normed_all, whole_x) + nn(low_in, up_x)).astype(BF16)
    z = (nn(normed_all, whole_z) + nn(low_in, up_z)).astype(BF16)
    kernel = conv_weight.astype(F32)
    x_f = x.astype(F32)
    conv_pre = conv_bias.astype(F32)
    for tap in range(taps):
        conv_pre = conv_pre + kernel[tap] * shift_down(x_f, taps - 1 - tap)
    conv_out = jax.nn.silu(conv_pre).astype(BF16)
    state_all = jnp.concatenate([state_proj, state_down_sel], 1)
    sums = small_scatter(nn(conv_out, state_all).astype(BF16), parts, "seq")
    low_state_own = sums[:, ranks + 2 * states :].astype(BF16)
    mixed = sums[:, : ranks + 2 * states] + nn(low_state_own, state_up_sel)
    step_low_own = mixed[:, :ranks].astype(BF16)
    step_mid_own = nn(step_low_own, step_down_sel).astype(BF16)
    shared = jnp.concatenate([step_low_own, step_mid_own, mixed[:, ranks:].astype(BF16), low_state_own], 1)
    shared = small_gather(shared, parts, "seq")
    cuts = (ranks, ranks + rank, ranks + rank + states, ranks + rank + 2 * states)
    low, low_state = shared[:, : cuts[1]], shared[:, cuts[3] :]
    b_rows, c_rows = shared[:, cuts[1] : cuts[2]], shared[:, cuts[2] : cuts[3]]

    def by_group(rows):
        return rows.reshape(-1, sub, states).transpose(0, 2, 1).astype(F32)

    step_all = jnp.concatenate([step_proj, step_up_sel], 0)
    bias_f = step_bias.astype(F32)[None]
    skip_f = skip_gain.astype(F32)[None]
    decay = -jnp.exp(decay_log.astype(F32))
    gated, scanned, kept = scan_forward(
        low, step_all, bias_f, by_group(b_rows), c_rows, conv_out, z, decay, skip_f
    )
    branch = lax.psum_scatter(nn(gated, whole_out).astype(BF16), "seq", scatter_dimension=0, tiled=True).astype(F32)
    low_out_part = nn(gated, out_down_sel)

    back_low_out = nt(back_out_all, out_up_sel).astype(BF16)
    back_gated = (nt(back_out_all, whole_out) + nt(back_low_out, out_down_sel)).astype(BF16)
    back_pre, back_conv, back_z, mixed_part = scan_backward(
        low, step_all, bias_f, by_group(c_rows), b_rows, conv_out, z, scanned, back_gated, kept, decay, skip_f
    )
    sums = small_scatter(jnp.concatenate([mixed_part, low_out_part], 1).astype(BF16), parts, "seq")
    back_mid_own = sums[:, ranks : ranks + rank]
    back_step = sums[:, :ranks] + nt(back_mid_own, step_down_sel.astype(F32))
    low_out_own = sums[:, cuts[3] :].astype(BF16)
    shared = jnp.concatenate(
        [back_step.astype(BF16), sums[:, cuts[1] : cuts[3]].astype(BF16), back_mid_own.astype(BF16), low_out_own], 1
    )
    shared = small_gather(shared, parts, "seq")
    mixes = ranks + 2 * states
    back_mixed, back_mid, low_out = shared[:, :mixes], shared[:, mixes : mixes + rank], shared[:, mixes + rank :]
    block_out = (hidden_f + valid * (branch + nn(low_out_own, out_up_sel))).astype(BF16)

    back_low_state = nt(back_mixed, state_up_sel).astype(BF16)
    back_conv = back_conv + nt(back_mixed, state_proj) + nt(back_low_state, state_down_sel)
    back_conv_pre = back_conv * silu_grad(conv_pre)
    back_x = jnp.zeros_like(back_conv_pre)
    for tap in range(taps):
        back_x = back_x + kernel[tap] * shift_up(back_conv_pre, taps - 1 - tap)
    back_x = back_x.astype(BF16)
    low_parts = (nt(back_x, up_x) + nt(back_z, up_z)).astype(BF16)
    back_in = ring_scatter((nt(back_x, whole_x) + nt(back_z, whole_z)).astype(BF16), parts, "seq")
    back_low_in = lax.all_to_all(
        jnp.broadcast_to(low_parts.reshape(1, tokens, parts * rank), (parts, tokens, parts * rank)),
        "seq", split_axis=0, concat_axis=0, tiled=True,
    ).astype(F32).sum(0).reshape(parts * tokens, rank).astype(BF16)
    back_low_in_own = lax.dynamic_slice_in_dim(back_low_in, part * tokens, tokens, 0)
    back_normed = back_in + nt(back_low_in_own, in_down_sel)
    gained = back_normed * gain_f
    input_grad = (
        cot_f
        + inverse * gained
        - hidden_f * inverse * inverse * inverse * jnp.mean(hidden_f * gained, axis=-1, keepdims=True)
    )

    span = width // parts

    def own_columns(values):
        return lax.dynamic_slice_in_dim(values, part * span, span, 1)

    chosen = (lax.broadcasted_iota(jnp.int32, (rank, 128), 1) == ident).astype(F32)
    sliced = jnp.concatenate(
        [
            tn(low_in, back_x),
            tn(low_in, back_z),
            tn(back_low_out, gated),
            tn(low_out, own_columns(back_out_all)),
            tn(back_low_in, own_columns(normed_all)),
            tn(back_low_state, conv_out),
            tn(low[:, ranks:], back_pre),
            tn(back_mid, low[:, :ranks]),
            tn(low_state, back_mixed),
            chosen,
        ],
        1,
    ).astype(BF16)
    every = lax.all_gather(sliced, ("seq", "fsdp")).reshape((parts, groups) + sliced.shape).astype(F32)
    here = lax.dynamic_index_in_dim(every, part, 0, keepdims=False)
    picked = here[:, 0, -128 : -128 + adapters]

    def by_adapter(values):
        flat = (slice(None),) + (None,) * (values.ndim - 1)
        return sum(picked[g][flat] * values[g][None] for g in range(groups))

    ends = [0]
    for size in (chans, chans, chans, span, span, chans, chans, ranks, mixes):
        ends.append(ends[-1] + size)

    def joined(index):
        values = every[:, :, :, ends[index] : ends[index + 1]]
        return values.transpose(1, 2, 0, 3).reshape(groups, rank, -1)

    def local(index):
        return here[:, :, ends[index] : ends[index + 1]]

    in_up_grad = by_adapter(jnp.concatenate([joined(0), joined(1)], 2))
    out_down_grad = by_adapter(joined(2)).transpose(0, 2, 1)
    out_up_grad = by_adapter(joined(3))
    in_down_grad = by_adapter(joined(4)).transpose(0, 2, 1)
    state_down_grad = by_adapter(local(5)).transpose(0, 2, 1)
    step_up_grad = by_adapter(local(6))
    step_down_grad = by_adapter(local(7)).transpose(0, 2, 1)
    state_up_grad = by_adapter(local(8))
    return (
        block_out[None], input_grad[None], in_down_grad, in_up_grad, state_down_grad, state_up_grad,
        step_down_grad, step_up_grad, out_down_grad, out_up_grad,
    )


def solution(mesh):
    seq, rows = P("fsdp", "seq", None), P(("seq", "fsdp"), None)
    in_specs = (
        seq, P("fsdp"), P("fsdp"), P(), rows, rows, P(None, "seq"), P("seq"), P("seq", None), P(None, "seq"),
        P("seq"), P(None, "seq"), P("seq"), rows, P(), P(), P(None, "seq", None), P(), P(), P(None, None, "seq"),
        P(), P(), seq,
    )
    out_specs = (seq, seq, P(), P(), P(None, "seq", None), P(), P(), P(None, None, "seq"), P(), P())
    return jax.shard_map(body, mesh=mesh, in_specs=in_specs, out_specs=out_specs, check_vma=False)
```

time: 1350 us -> 468 us (0.35)
  waiting for transfers between devices: 538 us -> 145 us
  local copies, waits for them, and re-layouts: 368 us -> 70.8 us
  other arithmetic: 209 us -> 32.9 us
  Pallas kernels: 0 us -> 61.6 us
  matrix products: 111 us -> 68.7 us
  blocking collectives: 59.4 us -> 21.7 us
    all_gather x3 -> x4, waiting for transfers between devices: 308 us -> 0.01 us  [the longest x1 0.01 us: columns_later(): out = lax.all_gather(mine, 'fsdp').reshape(groups, parts, rows, chans)]
    psum x4 -> x0, waiting for transfers between devices: 207 us -> none  [the longest x1 141 us: body(): lax.psum((spread_one(grad_in_down), spread_one(grad_in_up), spread_one(gr...]
    slice x78 -> x19, local copies, waits for them, and re-layouts: 191 us -> 5.74 us  [the longest x2 2.79 us: joined(): values = every[:, :, :, ends[index]:ends[index + 1]]]
    ppermute x0 -> x25, waiting for transfers between devices: none -> 119 us  [the longest x16 71.6 us: ring_send(): return lax.ppermute(value, axis, pairs)]
    reduce_sum x17 -> x3, other arithmetic: 93 us -> 2.09 us  [the longest x2 1.1 us: small_scatter(): return got.reshape((size, -1) + partial.shape[1:]).astype(F32).sum(0)]
    pallas_call x0 -> x2, Pallas kernels: none -> 61.6 us  [the longest x1 38.3 us: scan_backward(): pl.pallas_call(functools.partial(scan_backward_kernel, sub=sub), grid=(la...]
    unnamed x666 -> x218, local copies, waits for them, and re-layouts: 75.5 us -> 14.4 us
    psum x2 -> x0, blocking collectives: 59.4 us -> none  [the longest x1 48.1 us: body(): lax.psum((product(conv_out, state_proj), product(conv_out, state_down_sel...]
  transfers between devices with their start and end apart: 13 -> 34, of which waited for: 8 -> 19; matrix products, arithmetic and copies ran while one was open for 17% -> 28% of each run, Pallas kernels for 0% -> 13%
where the time goes in v1:
time: 468 us; the launch traced here: 460 us
  waiting for transfers between devices  145 us (31%)
  local copies, waits for them, and re-layouts  70.8 us (15%)
  matrix products  68.7 us (15%)
  Pallas kernels  61.6 us (13%)
  starting transfers between devices  37.7 us (8%)
  other arithmetic  32.9 us (7%)
  between operations  21.8 us (5%)
  blocking collectives  21.7 us (5%)
    ppermute x16, waiting for transfers between devices, ring_send(): return lax.ppermute(value, axis, pairs)  71.6 us
    ppermute x9, waiting for transfers between devices, swap(): return lax.ppermute(value, axis, [(i, i ^ bit) for i in range(size)])  47.5 us
    pallas_call x1, Pallas kernels, scan_backward(): pl.pallas_call(functools.partial(scan_backward_kernel, sub=sub), grid=(la...  38.3 us
    dot_general x11, matrix products, nn(): return jnp.dot(left, right, preferred_element_type=F32)  29.3 us
    dot_general x12, matrix products, nt(): lax.dot_general(left, right, (((1,), (1,)), ((), ())), preferred_element_...  24.5 us
    pallas_call x1, Pallas kernels, scan_forward(): pl.pallas_call(functools.partial(scan_forward_kernel, sub=sub), grid=(len...  23.2 us
    all_to_all x2, waiting for transfers between devices, small_scatter(): got = lax.all_to_all(partial, axis, split_axis=0, concat_axis=0, tiled=True)  22.2 us
    all_to_all x1, blocking collectives, columns_later(): lax.all_to_all(weight, 'seq', split_axis=1, concat_axis=0, tiled=True)  21.7 us
  transfers between devices with their start and end apart: 34, of which 19 were waited for; matrix products, arithmetic and copies ran while one was open for 28% of the time, Pallas kernels for 13%

profile of v1, /device:TPU:0, one launch (start us, length us, event | category | flops | bytes accessed | tf_op | source)
XLA Modules:
  0.0 460.3 jit_solution(953310231600837245)
XLA Ops:
  8.5 21.7 %all_to_all.52 = bf16[64,8,512]{2,0,1:T(8,128)(2,1)} all-to-all(bf16[64,8,512]{2,0,1:T(8,128)(2,1)S(1)} %bitcast.362), channel_id=1, replica_groups=mesh['seq'=8,'fsdp'=4] {'seq'}, dimensions={1} | all-to-all | bytes 1048576 | tf_op jit(solution)/shard_map/all_to_all | solution.py:387
  31.2 2.5 broadcast_in_dim.40
  37.9 3.6 all-to-all-start
  54.1 2.0 collective-permute-start.2
  56.2 1.9 constant_dynamic-update-slice_fusion.11
  58.1 1.9 constant_dynamic-update-slice_fusion.10
  60.0 2.3 all-to-all-done
  64.1 3.7 collective-permute-done.2
  67.8 2.1 collective-permute-start.4
  69.8 1.9 constant_dynamic-update-slice_fusion.9
  71.7 1.9 constant_dynamic-update-slice_fusion.8
  73.6 9.5 %collective-permute-done.8 = bf16[8,1,64,512]{3,2,1,0:T(8,128)(2,1)S(1)} collective-permute-done((bf16[8,1,64,512]{3,2,1,0:T(8,128)(2,1)S(1)}, bf16[8,1,64,512]{3,2,1,0:T(8,128)(2,1)S(1)}, u32[]{:S(2)}, u32[]{:S(2)}) %collective-permute-start.8) | collective-permute-done | bytes 524320 | tf_op jit(solution)/shard_map/ppermute | solution.py:295
  83.3 1.7 collective-permute-start.6
  87.1 5.0 %collective-permute-done.6 = bf16[64,2048]{1,0:T(8,128)(2,1)S(1)} collective-permute-done((bf16[64,2048]{1,0:T(8,128)(2,1)S(1)}, bf16[64,2048]{1,0:T(8,128)(2,1)S(1)}, u32[]{:S(2)}, u32[]{:S(2)}) %collective-permute-start.6) | collective-permute-done | bytes 262176 | tf_op jit(solution)/shard_map/ppermute | solution.py:248
  94.2 3.6 convolution_convert_fusion.5
  98.4 5.3 %fusion.4 = f32[1024,512]{1,0:T(8,128)S(1)} fusion(f32[1024,512]{1,0:T(8,128)S(1)} %fusion.62, bf16[1024,2048]{1,0:T(8,128)(2,1)} %constant_dynamic-update-slice_fusion.4, bf16[2048,512]{1,0:T(8,128)(2,1)S(1)} %bitcast.354), kind=kOutput, calls=%fused_computation.20 | convolution fusion | flops 2149056512 | bytes 10485760 | tf_op jit(solution)/shard_map/dot_general | solution.py:28
  103.8 2.7 multiply_convert_fusion
  107.8 4.8 %all-to-all-start.1 = ((bf16[8,128,176]{1,2,0:T(8,128)(2,1)}), bf16[8,128,176]{1,2,0:T(8,128)(2,1)}, u32[]{:S(2)}, u32[]{:S(2)}) async-start(bf16[8,128,176]{1,2,0:T(8,128)(2,1)} %bitcast.321), calls=%async_computation.1 | async-start | bytes 720896 | tf_op jit(solution)/shard_map/all_to_all | solution.py:328
  115.5 8.9 %all-to-all-done.1 = bf16[8,128,176]{1,2,0:T(8,128)(2,1)} async-done(((bf16[8,128,176]{1,2,0:T(8,128)(2,1)}), bf16[8,128,176]{1,2,0:T(8,128)(2,1)}, u32[]{:S(2)}, u32[]{:S(2)}) %all-to-all-start.1) | async-done | bytes 360480 | tf_op jit(solution)/shard_map/all_to_all | solution.py:328
  127.9 1.8 fusion.58
  129.8 6.0 %collective-permute-done.11 = bf16[1,128,192]{1,2,0:T(8,128)(2,1)S(1)} collective-permute-done((bf16[1,128,192]{1,2,0:T(8,128)(2,1)S(1)}, bf16[1,128,192]{1,2,0:T(8,128)(2,1)S(1)}, u32[]{:S(2)}, u32[]{:S(2)}) %collective-permute-start.11) | collective-permute-done | bytes 49184 | tf_op jit(solution)/shard_map/ppermute | solution.py:295
  135.9 12.5 %collective-permute-done.12 = bf16[2,128,192]{1,2,0:T(8,128)(2,1)S(1)} collective-permute-done((bf16[2,128,192]{1,2,0:T(8,128)(2,1)S(1)}, bf16[2,128,192]{1,2,0:T(8,128)(2,1)S(1)}, u32[]{:S(2)}, u32[]{:S(2)}) %collective-permute-start.12) | collective-permute-done | bytes 98336 | tf_op jit(solution)/shard_map/ppermute | solution.py:295
  150.1 5.2 %collective-permute-done.13 = bf16[4,128,192]{1,2,0:T(8,128)(2,1)S(1)} collective-permute-done((bf16[4,128,192]{1,2,0:T(8,128)(2,1)S(1)}, bf16[4,128,192]{1,2,0:T(8,128)(2,1)S(1)}, u32[]{:S(2)}, u32[]{:S(2)}) %collective-permute-start.13) | collective-permute-done | bytes 196640 | tf_op jit(solution)/shard_map/ppermute | solution.py:295
  156.1 2.0 copy.123
  158.1 1.9 fusion.103
  160.9 1.9 copy.126
  163.2 5.0 %add_convert_fusion.3.z_ref = bf16[1024,512]{1,0:T(8,128)(2,1)S(1)} fusion(f32[1024,512]{1,0:T(8,128)S(1)} %copy-done.35, bf16[1024,2048]{1,0:T(8,128)(2,1)} %constant_dynamic-update-slice_fusion.4, bf16[2048,512]{1,0:T(8,128)(2,1)S(1)} %bitcast.357), kind=kOutput, calls=%fused_computation.12 | convolution fusion | flops 2148532224 | bytes 9437184 | tf_op jit(solution)/shard_map/dot_general | solution.py:28
  168.3 23.2 %scan_forward.1 = (bf16[1024,512]{1,0:T(8,128)(2,1)S(1)}, f32[1024,512]{1,0:T(8,128)S(1)}, bf16[16384,512]{1,0:T(8,128)(2,1)}) custom-call(bf16[1024,144]{1,0:T(8,128)(2,1)S(1)} %bitcast.335, bf16[144,512]{1,0:T(8,128)(2,1)S(1)} %pad_maximum_fusion.1.wstep_ref, f32[1,512]{1,0:T(1,128)S(1)} %bitcast.342, f32[64,16,16]{2,1,0:T(8,128)S(1)} %bitcast.341, ...), custom_call_target="tpu_custom_call" | custom-call | tf_op jit(solution)/shard_map/scan_forward/pallas_call | solution.py:90
  194.7 6.3 %convolution_convert_fusion = bf16[1024,2048]{1,0:T(8,128)(2,1)} fusion(bf16[1024,512]{1,0:T(8,128)(2,1)} %copy-done.5, bf16[512,2048]{1,0:T(8,128)(2,1)} %all-gather.7.cloned.1.call-done), kind=kOutput, calls=%fused_computation.2 | convolution fusion | flops 2149580800 | bytes 7340032 | tf_op jit(solution)/shard_map/dot_general | solution.py:28
  201.1 1.9 copy.127
  203.0 2.2 convolution_convert_fusion.3
  205.2 3.6 convolution_convert_fusion.4
  209.1 4.1 fusion.106
  214.7 38.3 %scan_backward.1 = (bf16[1024,512]{1,0:T(8,128)(2,1)S(1)}, f32[1024,512]{1,0:T(8,128)S(1)}, bf16[1024,512]{1,0:T(8,128)(2,1)S(1)}, f32[1024,176]{1,0:T(8,128)S(1)}) custom-call(bf16[1024,144]{1,0:T(8,128)(2,1)S(1)} %bitcast.336, bf16[144,512]{1,0:T(8,128)(2,1)S(1)} %pad_maximum_fusion.1.wstep_ref, f32[1,512]{1,0:T(1,128)S(1)} %bitcast.343, ...), custom_call_target="tpu_custom_call" | custom-call | tf_op jit(solution)/shard_map/scan_backward/pallas_call | solution.py:195
  258.6 3.9 all-to-all-start.3
  263.0 2.1 fusion.13
  265.1 2.2 fusion.15
  267.3 13.3 %all-to-all-done.3 = bf16[8,128,192]{1,2,0:T(8,128)(2,1)S(1)} async-done(((bf16[8,128,192]{1,2,0:T(8,128)(2,1)}), bf16[8,128,192]{1,2,0:T(8,128)(2,1)S(1)}, u32[]{:S(2)}, u32[]{:S(2)}) %all-to-all-start.3) | async-done | bytes 393248 | tf_op jit(solution)/shard_map/all_to_all | solution.py:328
  282.3 2.1 fusion.12
  284.4 5.3 %collective-permute-done.14 = bf16[1,128,192]{1,2,0:T(8,128)(2,1)S(1)} collective-permute-done((bf16[1,128,192]{1,2,0:T(8,128)(2,1)S(1)}, bf16[1,128,192]{1,2,0:T(8,128)(2,1)S(1)}, u32[]{:S(2)}, u32[]{:S(2)}) %collective-permute-start.14) | collective-permute-done | bytes 49184 | tf_op jit(solution)/shard_map/ppermute | solution.py:295
  289.8 4.6 collective-permute-done.15
  295.6 4.5 collective-permute-done.16
  303.5 2.8 multiply_multiply_fusion
  312.6 1.8 broadcast_in_dim.49
  315.9 4.0 all-to-all-start.4
  320.0 1.9 fusion.18
  322.0 1.8 fusion.17
  332.8 4.4 fusion.108
  337.3 2.4 add_convert_fusion
  342.0 7.8 %collective-permute-done.17 = bf16[64,2048]{1,0:T(8,128)(2,1)S(1)} collective-permute-done((bf16[64,2048]{1,0:T(8,128)(2,1)S(1)}, bf16[64,2048]{1,0:T(8,128)(2,1)S(1)}, u32[]{:S(2)}, u32[]{:S(2)}) %collective-permute-start.17) | collective-permute-done | bytes 262176 | tf_op jit(solution)/shard_map/ppermute | solution.py:248
  352.4 14.2 %collective-permute-done.18 = bf16[128,2048]{1,0:T(8,128)(2,1)S(1)} collective-permute-done((bf16[128,2048]{1,0:T(8,128)(2,1)S(1)}, bf16[128,2048]{1,0:T(8,128)(2,1)S(1)}, u32[]{:S(2)}, u32[]{:S(2)}) %collective-permute-start.18) | collective-permute-done | bytes 524320 | tf_op jit(solution)/shard_map/ppermute | solution.py:248
  367.1 12.3 %collective-permute-done.19 = bf16[128,2048]{1,0:T(8,128)(2,1)S(1)} collective-permute-done((bf16[128,2048]{1,0:T(8,128)(2,1)S(1)}, bf16[128,2048]{1,0:T(8,128)(2,1)S(1)}, u32[]{:S(2)}, u32[]{:S(2)}) %collective-permute-start.19) | collective-permute-done | bytes 524320 | tf_op jit(solution)/shard_map/ppermute | solution.py:248
  381.0 2.3 collective-permute-start.20
  383.2 18.4 %collective-permute-done.23 = bf16[128,2048]{1,0:T(8,128)(2,1)S(1)} collective-permute-done((bf16[128,2048]{1,0:T(8,128)(2,1)S(1)}, bf16[128,2048]{1,0:T(8,128)(2,1)S(1)}, u32[]{:S(2)}, u32[]{:S(2)}) %collective-permute-start.23) | collective-permute-done | bytes 524320 | tf_op jit(solution)/shard_map/ppermute | solution.py:248
  402.6 9.5 %collective-permute-done.24 = bf16[128,2048]{1,0:T(8,128)(2,1)} collective-permute-done((bf16[128,2048]{1,0:T(8,128)(2,1)}, bf16[128,2048]{1,0:T(8,128)(2,1)}, u32[]{:S(2)}, u32[]{:S(2)}) %collective-permute-start.24) | collective-permute-done | bytes 524320 | tf_op jit(solution)/shard_map/ppermute | solution.py:248
  412.1 1.9 fusion.27
  414.0 3.0 fusion.24
  417.0 2.3 fusion.3
  420.4 3.1 convert.87
  431.9 2.4 constant_dynamic-update-slice_fusion.14
  434.4 2.5 copy_bitcast_fusion
  439.3 1.8 slice_bitcast_fusion.3
  443.9 3.0 multiply_add_fusion
  450.2 1.9 multiply_add_fusion.1
  (384 shorter events, 92.1 us)
Async XLA Ops:
  7.2 90.7 %copy-start = (bf16[8,16,8192]{2,1,0:T(8,128)(2,1)S(1)}, bf16[8,16,8192]{2,1,0:T(8,128)(2,1)}, u32[]{:S(2)}) copy-start(bf16[8,16,8192]{2,1,0:T(8,128)(2,1)} %param.60) | copy-start | bytes 6291460
  7.2 23.8 %copy-start.87 = (bf16[2048]{0:T(1024)(128)(2,1)S(1)}, bf16[2048]{0:T(1024)(128)(2,1)}, u32[]{:S(2)}) copy-start(bf16[2048]{0:T(1024)(128)(2,1)} %param.48) | copy-start | bytes 12292
  7.2 23.8 %copy-start.23 = (bf16[1,128,2048]{2,1,0:T(8,128)(2,1)S(1)}, bf16[1,128,2048]{2,1,0:T(8,128)(2,1)}, u32[]{:S(2)}) copy-start(bf16[1,128,2048]{2,1,0:T(8,128)(2,1)} %param.45) | copy-start | bytes 1572868
  7.2 153.7 %all-gather.5.cloned.1.call-start = ((), (), s32[]{:S(2)}) async-start(), calls=%async_computation.6 | async-start | bytes 2621440 | tf_op jit(solution)/shard_map/all_gather | solution.py:388
  30.2 164.5 %all-gather.7.cloned.1.call-start = ((), (), s32[]{:S(2)}) async-start(), calls=%async_computation.7 | async-start | bytes 2621440 | tf_op jit(solution)/shard_map/all_gather | solution.py:395
  33.8 9.0 %copy-start.37 = (bf16[1,128,2048]{2,1,0:T(8,128)(2,1)S(1)}, bf16[1,128,2048]{2,1,0:T(8,128)(2,1)}, u32[]{:S(2)}) copy-start(bf16[1,128,2048]{2,1,0:T(8,128)(2,1)} %param.67) | copy-start | bytes 1572868
  34.9 8.8 %copy-start.101 = (s32[8]{0:T(128)S(1)}, s32[8]{0:T(128)}, u32[]{:S(2)}) copy-start(s32[8]{0:T(128)} %constant.178.clone) | copy-start | bytes 100
  34.9 10.1 %copy-start.100 = (s32[8]{0:T(128)S(1)}, s32[8]{0:T(128)}, u32[]{:S(2)}) copy-start(s32[8]{0:T(128)} %constant.179.clone) | copy-start | bytes 100
  34.9 11.3 %copy-start.99 = (s32[8]{0:T(128)S(1)}, s32[8]{0:T(128)}, u32[]{:S(2)}) copy-start(s32[8]{0:T(128)} %constant.180.clone) | copy-start | bytes 100
  34.9 12.6 %copy-start.98 = (s32[8]{0:T(128)S(1)}, s32[8]{0:T(128)}, u32[]{:S(2)}) copy-start(s32[8]{0:T(128)} %constant.181.clone) | copy-start | bytes 100
  34.9 13.8 %copy-start.97 = (s32[8]{0:T(128)S(1)}, s32[8]{0:T(128)}, u32[]{:S(2)}) copy-start(s32[8]{0:T(128)} %constant.182.clone) | copy-start | bytes 100
  35.0 15.1 %copy-start.96 = (s32[8]{0:T(128)S(1)}, s32[8]{0:T(128)}, u32[]{:S(2)}) copy-start(s32[8]{0:T(128)} %constant.183.clone) | copy-start | bytes 100
  35.0 16.3 %copy-start.95 = (s32[8]{0:T(128)S(1)}, s32[8]{0:T(128)}, u32[]{:S(2)}) copy-start(s32[8]{0:T(128)} %constant.184.clone) | copy-start | bytes 100
  35.0 18.2 %copy-start.92 = (bf16[512]{0:T(512)(128)(2,1)S(1)}, bf16[512]{0:T(512)(128)(2,1)}, u32[]{:S(2)}) copy-start(bf16[512]{0:T(512)(128)(2,1)} %param.52) | copy-start | bytes 3076
  35.0 19.0 %copy-start.84 = (bf16[4,512]{1,0:T(4,128)(2,1)S(1)}, bf16[4,512]{1,0:T(4,128)(2,1)}, u32[]{:S(2)}) copy-start(bf16[4,512]{1,0:T(4,128)(2,1)} %param.51) | copy-start | bytes 12292
  35.0 19.1 %collective-permute-start = (bf16[128,2048]{1,0:T(8,128)(2,1)}, bf16[128,2048]{1,0:T(8,128)(2,1)}, u32[]{:S(2)}, u32[]{:S(2)}) collective-permute-start(bf16[128,2048]{1,0:T(8,128)(2,1)} %get-tuple-element.51), channel_id=1, source_target_pairs={{0,8},{8,16},{16,24},{24,28},{28,20},{20,12},{12,4},{4,0},{1,9},{9... | collective-permute-start | bytes 1572872 | tf_op jit(solution)/shard_map/ppermute | solution.py:248
  36.2 20.0 %collective-permute-start.1 = (bf16[128,2048]{1,0:T(8,128)(2,1)}, bf16[128,2048]{1,0:T(8,128)(2,1)}, u32[]{:S(2)}, u32[]{:S(2)}) collective-permute-start(bf16[128,2048]{1,0:T(8,128)(2,1)} %get-tuple-element.51), channel_id=1, source_target_pairs={{0,4},{8,0},{16,8},{24,16},{28,24},{20,28},{12,20},{4,12},{1,5},{9... | collective-permute-start | bytes 1572872 | tf_op jit(solution)/shard_map/ppermute | solution.py:248
  37.9 24.3 %all-to-all-start = ((bf16[64,8,512]{2,0,1:T(8,128)(2,1)}), bf16[64,8,512]{2,0,1:T(8,128)(2,1)S(1)}, u32[]{:S(2)}, u32[]{:S(2)}) async-start(bf16[64,8,512]{2,0,1:T(8,128)(2,1)} %bitcast.320), calls=%async_computation | async-start | bytes 1048576 | tf_op jit(solution)/shard_map/all_to_all | solution.py:379
  41.5 163.7 %all-gather.9.cloned.1.call-start = ((), (), s32[]{:S(2)}) async-start(), calls=%async_computation.9 | async-start | bytes 4718592 | tf_op jit(solution)/shard_map/all_gather | solution.py:391
  54.0 52.5 %copy-start.47 = (bf16[512,16]{0,1:T(8,128)(2,1)}, bf16[512,16]{0,1:T(8,128)(2,1)S(1)}, u32[]{:S(2)}) copy-start(bf16[512,16]{0,1:T(8,128)(2,1)S(1)} %dynamic-slice_bitcast_fusion.2) | copy-start | bytes 49156
  54.0 49.7 %copy-start.75 = (f32[1,512]{1,0:T(1,128)}, f32[1,512]{1,0:T(1,128)S(1)}, u32[]{:S(2)}) copy-start(f32[1,512]{1,0:T(1,128)S(1)} %get-tuple-element.105) | copy-start | bytes 6148
  54.1 49.7 %copy-start.77 = (f32[1,512]{1,0:T(1,128)}, f32[1,512]{1,0:T(1,128)S(1)}, u32[]{:S(2)}) copy-start(f32[1,512]{1,0:T(1,128)S(1)} %get-tuple-element.106) | copy-start | bytes 6148
  54.1 49.7 %copy-start.79 = (f32[1,512]{1,0:T(1,128)}, f32[1,512]{1,0:T(1,128)S(1)}, u32[]{:S(2)}) copy-start(f32[1,512]{1,0:T(1,128)S(1)} %get-tuple-element.107) | copy-start | bytes 6148
  54.1 49.7 %copy-start.81 = (f32[1,512]{1,0:T(1,128)}, f32[1,512]{1,0:T(1,128)S(1)}, u32[]{:S(2)}) copy-start(f32[1,512]{1,0:T(1,128)S(1)} %get-tuple-element.108) | copy-start | bytes 6148
  54.1 13.7 %collective-permute-start.2 = (bf16[128,2048]{1,0:T(8,128)(2,1)}, bf16[128,2048]{1,0:T(8,128)(2,1)}, u32[]{:S(2)}, u32[]{:S(2)}) collective-permute-start(bf16[128,2048]{1,0:T(8,128)(2,1)} %collective-permute-done), channel_id=1, source_target_pairs={{0,8},{8,16},{16,24},{24,28},{28,20},{20,12},{12,4},{4,0},{1,9},{9... | collective-permute-start | bytes 1572872 | tf_op jit(solution)/shard_map/ppermute | solution.py:248
  56.1 13.7 %collective-permute-start.3 = (bf16[128,2048]{1,0:T(8,128)(2,1)}, bf16[128,2048]{1,0:T(8,128)(2,1)}, u32[]{:S(2)}, u32[]{:S(2)}) collective-permute-start(bf16[128,2048]{1,0:T(8,128)(2,1)} %collective-permute-done.1), channel_id=1, source_target_pairs={{0,4},{8,0},{16,8},{24,16},{28,24},{20,28},{12,20},{4,12},{1,5},{9... | collective-permute-start | bytes 1572872 | tf_op jit(solution)/shard_map/ppermute | solution.py:248
  62.3 20.9 %collective-permute-start.8 = (bf16[8,1,64,512]{3,2,1,0:T(8,128)(2,1)S(1)}, bf16[8,1,64,512]{3,2,1,0:T(8,128)(2,1)S(1)}, u32[]{:S(2)}, u32[]{:S(2)}) collective-permute-start(bf16[8,1,64,512]{3,2,1,0:T(8,128)(2,1)S(1)} %bitcast.360), channel_id=1, source_target_pairs={{0,2},{1,3},{2,0},{3,1},{4,6},{5,7},{6,4},{7,5},{8,10},{9,11},{10,... | collective-permute-start | bytes 1572872 | tf_op jit(solution)/shard_map/ppermute | solution.py:295
  63.8 19.4 %collective-permute-start.9 = (bf16[8,1,64,512]{3,2,1,0:T(8,128)(2,1)S(1)}, bf16[8,1,64,512]{3,2,1,0:T(8,128)(2,1)S(1)}, u32[]{:S(2)}, u32[]{:S(2)}) collective-permute-start(bf16[8,1,64,512]{3,2,1,0:T(8,128)(2,1)S(1)} %bitcast.361), channel_id=1, source_target_pairs={{0,1},{1,0},{2,3},{3,2},{4,5},{5,4},{6,7},{7,6},{8,9},{9,8},{10,11... | collective-permute-start | bytes 1572872 | tf_op jit(solution)/shard_map/ppermute | solution.py:295
  67.8 15.5 %collective-permute-start.4 = (bf16[128,2048]{1,0:T(8,128)(2,1)}, bf16[128,2048]{1,0:T(8,128)(2,1)S(1)}, u32[]{:S(2)}, u32[]{:S(2)}) collective-permute-start(bf16[128,2048]{1,0:T(8,128)(2,1)} %collective-permute-done.2), channel_id=1, source_target_pairs={{0,8},{8,16},{16,24},{24,28},{28,20},{20,12},{12,4},{4,0},{1,9},{9... | collective-permute-start | bytes 1572872 | tf_op jit(solution)/shard_map/ppermute | solution.py:248
  69.8 15.2 %collective-permute-start.5 = (bf16[128,2048]{1,0:T(8,128)(2,1)}, bf16[128,2048]{1,0:T(8,128)(2,1)S(1)}, u32[]{:S(2)}, u32[]{:S(2)}) collective-permute-start(bf16[128,2048]{1,0:T(8,128)(2,1)} %collective-permute-done.3), channel_id=1, source_target_pairs={{0,4},{8,0},{16,8},{24,16},{28,24},{20,28},{12,20},{4,12},{1,5},{9... | collective-permute-start | bytes 1572872 | tf_op jit(solution)/shard_map/ppermute | solution.py:248
  83.1 15.2 %collective-permute-start.10 = (bf16[8,1,64,512]{3,2,1,0:T(8,128)(2,1)S(1)}, bf16[8,1,64,512]{3,2,1,0:T(8,128)(2,1)S(1)}, u32[]{:S(2)}, u32[]{:S(2)}) collective-permute-start(bf16[8,1,64,512]{3,2,1,0:T(8,128)(2,1)S(1)} %collective-permute-done.8), channel_id=1, source_target_pairs={{0,1},{1,0},{2,3},{3,2},{4,5},{5,4},{6,7},{7,6},{8,9},{9,8},{10,11... | collective-permute-start | bytes 1572872 | tf_op jit(solution)/shard_map/ppermute | solution.py:295
  83.3 8.8 %collective-permute-start.6 = (bf16[64,2048]{1,0:T(8,128)(2,1)S(1)}, bf16[64,2048]{1,0:T(8,128)(2,1)S(1)}, u32[]{:S(2)}, u32[]{:S(2)}) collective-permute-start(bf16[64,2048]{1,0:T(8,128)(2,1)S(1)} %slice.411), channel_id=1, source_target_pairs={{0,8},{8,16},{16,24},{24,28},{28,20},{20,12},{12,4},{4,0},{1,9},{9... | collective-permute-start | bytes 786440 | tf_op jit(solution)/shard_map/ppermute | solution.py:248
  85.0 8.5 %collective-permute-start.7 = (bf16[64,2048]{1,0:T(8,128)(2,1)S(1)}, bf16[64,2048]{1,0:T(8,128)(2,1)S(1)}, u32[]{:S(2)}, u32[]{:S(2)}) collective-permute-start(bf16[64,2048]{1,0:T(8,128)(2,1)S(1)} %slice.412), channel_id=1, source_target_pairs={{0,4},{8,0},{16,8},{24,16},{28,24},{20,28},{12,20},{4,12},{1,5},{9... | collective-permute-start | bytes 786440 | tf_op jit(solution)/shard_map/ppermute | solution.py:248
  97.9 30.0 %copy-start.40 = (bf16[1024,16]{0,1:T(8,128)(2,1)}, bf16[1024,16]{0,1:T(8,128)(2,1)S(1)}, u32[]{:S(2)}) copy-start(bf16[1024,16]{0,1:T(8,128)(2,1)S(1)} %convolution_convert_fusion.5) | copy-start | bytes 98308
  106.5 7.0 %copy-start.94 = (bf16[512]{0:T(512)(128)(2,1)S(1)}, bf16[512]{0:T(512)(128)(2,1)}, u32[]{:S(2)}) copy-start(bf16[512]{0:T(512)(128)(2,1)} %param.57) | copy-start | bytes 3076
  106.5 8.3 %copy-start.60 = (bf16[128,512]{1,0:T(8,128)(2,1)S(1)}, bf16[128,512]{1,0:T(8,128)(2,1)}, u32[]{:S(2)}) copy-start(bf16[128,512]{1,0:T(8,128)(2,1)} %param.54) | copy-start | bytes 393220
  106.5 8.3 %copy-start.83 = (bf16[16,512]{1,0:T(8,128)(2,1)S(1)}, bf16[16,512]{1,0:T(8,128)(2,1)}, u32[]{:S(2)}) copy-start(bf16[16,512]{1,0:T(8,128)(2,1)} %param.56) | copy-start | bytes 49156
  107.8 16.6 %all-to-all-start.1 = ((bf16[8,128,176]{1,2,0:T(8,128)(2,1)}), bf16[8,128,176]{1,2,0:T(8,128)(2,1)}, u32[]{:S(2)}, u32[]{:S(2)}) async-start(bf16[8,128,176]{1,2,0:T(8,128)(2,1)} %bitcast.321), calls=%async_computation.1 | async-start | bytes 720896 | tf_op jit(solution)/shard_map/all_to_all | solution.py:328
  112.7 304.3 %reduce-scatter.2.cloned.1.call-start = ((), (), s32[]{:S(2)}) async-start(), calls=%async_computation.8 | async-start | bytes 4718592 | tf_op jit(solution)/shard_map/reduce_scatter | solution.py:436
  127.2 8.5 %collective-permute-start.11 = (bf16[1,128,192]{1,2,0:T(8,128)(2,1)S(1)}, bf16[1,128,192]{1,2,0:T(8,128)(2,1)S(1)}, u32[]{:S(2)}, u32[]{:S(2)}) collective-permute-start(bf16[1,128,192]{1,2,0:T(8,128)(2,1)S(1)} %get-tuple-element.104), channel_id=1, source_target_pairs={{0,16},{4,20},{8,24},{12,28},{16,0},{20,4},{24,8},{28,12},{1,17},{... | collective-permute-start | bytes 147464 | tf_op jit(solution)/shard_map/ppermute | solution.py:295
  135.8 12.6 %collective-permute-start.12 = (bf16[2,128,192]{1,2,0:T(8,128)(2,1)S(1)}, bf16[2,128,192]{1,2,0:T(8,128)(2,1)S(1)}, u32[]{:S(2)}, u32[]{:S(2)}) collective-permute-start(bf16[2,128,192]{1,2,0:T(8,128)(2,1)S(1)} %maximum_select_fusion.7), channel_id=1, source_target_pairs={{0,8},{4,12},{8,0},{12,4},{16,24},{20,28},{24,16},{28,20},{1,9},{5... | collective-permute-start | bytes 294920 | tf_op jit(solution)/shard_map/ppermute | solution.py:295
  148.4 6.9 %collective-permute-start.13 = (bf16[4,128,192]{1,2,0:T(8,128)(2,1)S(1)}, bf16[4,128,192]{1,2,0:T(8,128)(2,1)S(1)}, u32[]{:S(2)}, u32[]{:S(2)}) collective-permute-start(bf16[4,128,192]{1,2,0:T(8,128)(2,1)S(1)} %bitcast.398), channel_id=1, source_target_pairs={{0,4},{4,0},{8,12},{12,8},{16,20},{20,16},{24,28},{28,24},{1,5},{5... | collective-permute-start | bytes 589832 | tf_op jit(solution)/shard_map/ppermute | solution.py:295
  258.6 22.0 %all-to-all-start.3 = ((bf16[8,128,192]{1,2,0:T(8,128)(2,1)}), bf16[8,128,192]{1,2,0:T(8,128)(2,1)S(1)}, u32[]{:S(2)}, u32[]{:S(2)}) async-start(bf16[8,128,192]{1,2,0:T(8,128)(2,1)} %pad_maximum_fusion), calls=%async_computation.4 | async-start | bytes 786432 | tf_op jit(solution)/shard_map/all_to_all | solution.py:328
  282.2 7.5 %collective-permute-start.14 = (bf16[1,128,192]{1,2,0:T(8,128)(2,1)S(1)}, bf16[1,128,192]{1,2,0:T(8,128)(2,1)S(1)}, u32[]{:S(2)}, u32[]{:S(2)}) collective-permute-start(bf16[1,128,192]{1,2,0:T(8,128)(2,1)S(1)} %get-tuple-element.102), channel_id=1, source_target_pairs={{0,16},{4,20},{8,24},{12,28},{16,0},{20,4},{24,8},{28,12},{1,17},{... | collective-permute-start | bytes 147464 | tf_op jit(solution)/shard_map/ppermute | solution.py:295
  284.4 18.5 %copy-start.48 = (bf16[512,16]{0,1:T(8,128)(2,1)S(1)}, bf16[512,16]{0,1:T(8,128)(2,1)}, u32[]{:S(2)}) copy-start(bf16[512,16]{0,1:T(8,128)(2,1)} %copy-done.47) | copy-start | bytes 49156
  289.7 4.7 %collective-permute-start.15 = (bf16[2,128,192]{1,2,0:T(8,128)(2,1)S(1)}, bf16[2,128,192]{1,2,0:T(8,128)(2,1)S(1)}, u32[]{:S(2)}, u32[]{:S(2)}) collective-permute-start(bf16[2,128,192]{1,2,0:T(8,128)(2,1)S(1)} %maximum_select_fusion.9), channel_id=1, source_target_pairs={{0,8},{4,12},{8,0},{12,4},{16,24},{20,28},{24,16},{28,20},{1,9},{5... | collective-permute-start | bytes 294920 | tf_op jit(solution)/shard_map/ppermute | solution.py:295
  294.4 5.7 %collective-permute-start.16 = (bf16[4,128,192]{1,2,0:T(8,128)(2,1)S(1)}, bf16[4,128,192]{1,2,0:T(8,128)(2,1)S(1)}, u32[]{:S(2)}, u32[]{:S(2)}) collective-permute-start(bf16[4,128,192]{1,2,0:T(8,128)(2,1)S(1)} %bitcast.397), channel_id=1, source_target_pairs={{0,4},{4,0},{8,12},{12,8},{16,20},{20,16},{24,28},{28,24},{1,5},{5... | collective-permute-start | bytes 589832 | tf_op jit(solution)/shard_map/ppermute | solution.py:295
  315.9 12.3 %all-to-all-start.4 = ((bf16[8,128,128]{2,1,0:T(8,128)(2,1)}), bf16[8,128,128]{2,1,0:T(8,128)(2,1)}, u32[]{:S(2)}, u32[]{:S(2)}) async-start(bf16[8,128,128]{2,1,0:T(8,128)(2,1)} %broadcast_in_dim.50), calls=%async_computation.5 | async-start | bytes 524288 | tf_op jit(solution)/shard_map/all_to_all | solution.py:465
  320.0 99.3 %all-gather.11.cloned.1.call-start = ((), (), s32[]{:S(2)}) async-start(), calls=%async_computation.10 | async-start | bytes 3784704 | tf_op jit(solution)/shard_map/all_gather | solution.py:499
  320.0 7.0 %copy-start.45 = (bf16[1024,16]{0,1:T(8,128)(2,1)S(1)}, bf16[1024,16]{0,1:T(8,128)(2,1)}, u32[]{:S(2)}) copy-start(bf16[1024,16]{0,1:T(8,128)(2,1)} %copy-done.44) | copy-start | bytes 98308
  322.0 9.3 %copy-start.62 = (bf16[1,16,512]{2,1,0:T(8,128)(2,1)S(1)}, bf16[1,16,512]{2,1,0:T(8,128)(2,1)}, u32[]{:S(2)}) copy-start(bf16[1,16,512]{2,1,0:T(8,128)(2,1)} %fusion.13) | copy-start | bytes 49156
  339.6 62.0 %copy-start.28 = (bf16[1024,2048]{1,0:T(8,128)(2,1)}, bf16[1024,2048]{1,0:T(8,128)(2,1)S(1)}, u32[]{:S(2)}) copy-start(bf16[1024,2048]{1,0:T(8,128)(2,1)S(1)} %add_convert_fusion) | copy-start | bytes 12582916
  339.7 10.1 %collective-permute-start.17 = (bf16[64,2048]{1,0:T(8,128)(2,1)S(1)}, bf16[64,2048]{1,0:T(8,128)(2,1)S(1)}, u32[]{:S(2)}, u32[]{:S(2)}) collective-permute-start(bf16[64,2048]{1,0:T(8,128)(2,1)S(1)} %get-tuple-element.54), channel_id=1, source_target_pairs={{0,8},{8,16},{16,24},{24,28},{28,20},{20,12},{12,4},{4,0},{1,9},{9... | collective-permute-start | bytes 786440 | tf_op jit(solution)/shard_map/ppermute | solution.py:248
  340.7 11.0 %collective-permute-start.21 = (bf16[64,2048]{1,0:T(8,128)(2,1)S(1)}, bf16[64,2048]{1,0:T(8,128)(2,1)S(1)}, u32[]{:S(2)}, u32[]{:S(2)}) collective-permute-start(bf16[64,2048]{1,0:T(8,128)(2,1)S(1)} %get-tuple-element.55), channel_id=1, source_target_pairs={{0,4},{8,0},{16,8},{24,16},{28,24},{20,28},{12,20},{4,12},{1,5},{9... | collective-permute-start | bytes 786440 | tf_op jit(solution)/shard_map/ppermute | solution.py:248
  350.0 16.5 %collective-permute-start.18 = (bf16[128,2048]{1,0:T(8,128)(2,1)S(1)}, bf16[128,2048]{1,0:T(8,128)(2,1)S(1)}, u32[]{:S(2)}, u32[]{:S(2)}) collective-permute-start(bf16[128,2048]{1,0:T(8,128)(2,1)S(1)} %convert_element_type.253), channel_id=1, source_target_pairs={{0,8},{8,16},{16,24},{24,28},{28,20},{20,12},{12,4},{4,0},{1,9},{9... | collective-permute-start | bytes 1572872 | tf_op jit(solution)/shard_map/ppermute | solution.py:248
  351.9 15.1 %collective-permute-start.22 = (bf16[128,2048]{1,0:T(8,128)(2,1)S(1)}, bf16[128,2048]{1,0:T(8,128)(2,1)S(1)}, u32[]{:S(2)}, u32[]{:S(2)}) collective-permute-start(bf16[128,2048]{1,0:T(8,128)(2,1)S(1)} %convert_element_type.263), channel_id=1, source_target_pairs={{0,4},{8,0},{16,8},{24,16},{28,24},{20,28},{12,20},{4,12},{1,5},{9... | collective-permute-start | bytes 1572872 | tf_op jit(solution)/shard_map/ppermute | solution.py:248
  366.7 45.4 %copy-start.24 = (bf16[1,128,2048]{2,1,0:T(8,128)(2,1)S(1)}, bf16[1,128,2048]{2,1,0:T(8,128)(2,1)}, u32[]{:S(2)}) copy-start(bf16[1,128,2048]{2,1,0:T(8,128)(2,1)} %param.45) | copy-start | bytes 1572868
  366.7 45.4 %copy-start.50 = (f32[2048]{0:T(1024)S(1)}, f32[2048]{0:T(1024)}, u32[]{:S(2)}) copy-start(f32[2048]{0:T(1024)} %copy-done.49) | copy-start | bytes 24580
  366.7 12.6 %collective-permute-start.19 = (bf16[128,2048]{1,0:T(8,128)(2,1)S(1)}, bf16[128,2048]{1,0:T(8,128)(2,1)S(1)}, u32[]{:S(2)}, u32[]{:S(2)}) collective-permute-start(bf16[128,2048]{1,0:T(8,128)(2,1)S(1)} %add_convert_fusion.8), channel_id=1, source_target_pairs={{0,8},{8,16},{16,24},{24,28},{28,20},{20,12},{12,4},{4,0},{1,9},{9... | collective-permute-start | bytes 1572872 | tf_op jit(solution)/shard_map/ppermute | solution.py:248
  380.5 21.1 %collective-permute-start.23 = (bf16[128,2048]{1,0:T(8,128)(2,1)S(1)}, bf16[128,2048]{1,0:T(8,128)(2,1)S(1)}, u32[]{:S(2)}, u32[]{:S(2)}) collective-permute-start(bf16[128,2048]{1,0:T(8,128)(2,1)S(1)} %get-tuple-element.53), channel_id=1, source_target_pairs={{0,4},{8,0},{16,8},{24,16},{28,24},{20,28},{12,20},{4,12},{1,5},{9... | collective-permute-start | bytes 1572872 | tf_op jit(solution)/shard_map/ppermute | solution.py:248
  380.9 33.0 %copy-start.38 = (bf16[1,128,2048]{2,1,0:T(8,128)(2,1)S(1)}, bf16[1,128,2048]{2,1,0:T(8,128)(2,1)}, u32[]{:S(2)}) copy-start(bf16[1,128,2048]{2,1,0:T(8,128)(2,1)} %param.67) | copy-start | bytes 1572868
  380.9 33.0 %copy-start.89 = (f32[128]{0:T(128)S(1)}, f32[128]{0:T(128)}, u32[]{:S(2)}) copy-start(f32[128]{0:T(128)} %copy-done.88) | copy-start | bytes 1540
  381.0 21.6 %collective-permute-start.20 = (bf16[128,2048]{1,0:T(8,128)(2,1)}, bf16[128,2048]{1,0:T(8,128)(2,1)}, u32[]{:S(2)}, u32[]{:S(2)}) collective-permute-start(bf16[128,2048]{1,0:T(8,128)(2,1)} %get-tuple-element.52), channel_id=1, source_target_pairs={{0,8},{8,16},{16,24},{24,28},{28,20},{20,12},{12,4},{4,0},{1,9},{9... | collective-permute-start | bytes 1572872 | tf_op jit(solution)/shard_map/ppermute | solution.py:248
  402.6 9.5 %collective-permute-start.24 = (bf16[128,2048]{1,0:T(8,128)(2,1)}, bf16[128,2048]{1,0:T(8,128)(2,1)}, u32[]{:S(2)}, u32[]{:S(2)}) collective-permute-start(bf16[128,2048]{1,0:T(8,128)(2,1)} %add_convert_fusion.5), channel_id=1, source_target_pairs={{0,4},{8,0},{16,8},{24,16},{28,24},{20,28},{12,20},{4,12},{1,5},{9... | collective-permute-start | bytes 1572872 | tf_op jit(solution)/shard_map/ppermute | solution.py:248
  (72 other events, 218.6 us)
Sparse Core Ops, SparseCore 0:
  30.3 21.6 all-gather.4
  53.5 30.2 all-gather.6
  86.0 77.0 all-gather.8
  201.2 92.2 reduce-scatter.1
  332.9 66.9 all-gather.10

commit v2 on v1

v2 whole, which is shorter than its diff:
```python
import functools
import jax
import jax.numpy as jnp
from jax import lax
from jax.experimental import pallas as pl
from jax.experimental.pallas import tpu as pltpu
from jax.sharding import PartitionSpec as P

F32 = jnp.float32
BF16 = jnp.bfloat16
LOG2E = 1.4426950408889634


def silu_grad(values):
    sigma = jax.nn.sigmoid(values)
    return sigma * (1.0 + values * (1.0 - sigma))


def softplus(v):
    return jnp.maximum(v, 0.0) + jnp.log1p(jnp.exp(-jnp.abs(v)))


def nt(left, right):
    return lax.dot_general(left, right, (((1,), (1,)), ((), ())), preferred_element_type=F32)


def nn(left, right):
    return jnp.dot(left, right, preferred_element_type=F32)


def tn(left, right):
    return lax.dot_general(left, right, (((0,), (0,)), ((), ())), preferred_element_type=F32)


def spread_matrix(states, sub):
    row = lax.broadcasted_iota(jnp.int32, (states, sub * states), 0)
    col = lax.broadcasted_iota(jnp.int32, (states, sub * states), 1)
    return (lax.rem(col, states) == row).astype(BF16)


def own_step_mask(rows, width, sub):
    row = lax.broadcasted_iota(jnp.int32, (rows, sub * width), 0)
    col = lax.broadcasted_iota(jnp.int32, (rows, sub * width), 1)
    return (lax.rem(row, sub) == lax.div(col, width)).astype(F32)


def ring_place(position, size):
    position = lax.rem(position + size, size)
    return jnp.where(position < size // 2, 2 * position, 2 * (size - 1 - position) + 1)


def ring_position(place, size):
    return jnp.where(lax.rem(place, 2) == 0, lax.div(place, 2), size - 1 - lax.div(place, 2))


def ring_copies(out_ref, pieces, part, sems):
    size, rows = len(pieces) - 1, pieces[0].shape[0]
    far, half, here = size // 2, rows // 2, ring_position(part, size)
    copies = []
    for i, piece in enumerate(pieces):
        hop = (i + 1) // 2
        place = ring_place(here - hop if i % 2 else here + hop, size)
        at = place * rows
        if i == size:
            at = ring_place(here + far, size) * rows + half
        at = pl.multiple_of(at, half)
        copies.append(pltpu.make_async_copy(piece, out_ref.at[pl.ds(at, piece.shape[0]), :], sems.at[i]))
    return copies


def swap_order(size):
    order, bit = [0], size // 2
    while bit:
        order += [at ^ bit for at in order]
        bit //= 2
    return order


def place_of_block(block, part, size):
    apart, out, bit = jnp.bitwise_xor(block, part), 0, size // 2
    weight = 1
    while bit:
        out = out + weight * jnp.bitwise_and(lax.div(apart, bit), 1)
        weight, bit = weight * 2, bit // 2
    return out


def row_copies(out_ref, pieces, group, sems):
    copies = []
    for i, apart in enumerate(swap_order(out_ref.shape[1])):
        at = i if group is None else jnp.bitwise_xor(group, apart)
        piece = pieces.at[i] if group is None else pieces[i]
        copies.append(pltpu.make_async_copy(piece, out_ref.at[:, at], sems.at[i]))
    return copies


def run_all(copies):
    for copy in copies:
        copy.start()
    for copy in copies:
        copy.wait()


def flat(ref):
    return ref[...].reshape(-1, ref.shape[-1])


def conv_before(x, before, weight_ref, bias_ref):
    taps = weight_ref.shape[0]
    padded = jnp.concatenate([before, x], 0)
    out = bias_ref[...]
    for tap in range(taps):
        at = before.shape[0] - (taps - 1 - tap)
        out = out + weight_ref[tap : tap + 1, :] * padded[at : at + x.shape[0]]
    return out


def project_kernel(meta, *refs, parts, groups):
    pieces, refs = refs[: parts + 1], refs[parts + 1 :]
    columns, refs = refs[:groups], refs[groups:]
    (in_down_ref, up_ref, weight_ref, bias_ref, proj_ref, down_ref,
     low_in_ref, x_ref, conv_ref, sums_ref, before, rows_s, whole_s, piece_sems, column_sems) = refs
    step = pl.program_id(0)
    rows = x_ref.shape[0]

    @pl.when(step == 0)
    def _():
        run_all(ring_copies(rows_s, pieces, meta[1], piece_sems) + row_copies(whole_s, columns, meta[2], column_sems))
        before[...] = jnp.zeros_like(before)

    normed = rows_s[pl.ds(pl.multiple_of(step * rows, rows), rows), :]
    low_in = nt(normed, in_down_ref[0]).astype(BF16)
    low_in_ref[...] = low_in
    x = (nn(normed, flat(whole_s)) + nn(low_in, up_ref[0])).astype(BF16)
    x_ref[...] = x
    x_f = x.astype(F32)
    conv_out = jax.nn.silu(conv_before(x_f, before[...], weight_ref, bias_ref)).astype(BF16)
    before[...] = x_f[-8:]
    conv_ref[...] = conv_out
    cut = proj_ref.shape[0]
    sums_ref[:, :cut] = nt(conv_out, proj_ref[...]).astype(BF16)
    sums_ref[:, cut:] = nt(conv_out, down_ref[0]).astype(BF16)


def once(array):
    return pl.BlockSpec(array.shape, lambda i, *_: (0,) * array.ndim, pipeline_mode=pl.Buffered(1))


def chosen(table, which=0, width=None):
    if width is None:
        return pl.BlockSpec((1,) + table.shape[1:], lambda i, meta: (meta[0], 0, 0))
    return pl.BlockSpec((1, table.shape[1], width), lambda i, meta: (meta[0], 0, meta[1] + which))


LIMIT = 58 << 20
AT_ONCE = 4


def gate_kernel(meta, *refs, parts):
    pieces, refs = refs[: parts + 1], refs[parts + 1 :]
    columns, low_in_ref, up_ref, z_ref, rows_s, whole_s, piece_sems, column_sems = refs
    step = pl.program_id(0)

    @pl.when(step == 0)
    def _():
        run_all(ring_copies(rows_s, pieces, meta[1], piece_sems) + row_copies(whole_s, columns, None, column_sems))

    rows = z_ref.shape[0]
    normed = rows_s[pl.ds(pl.multiple_of(step * rows, rows), rows), :]
    z_ref[...] = (nn(normed, flat(whole_s)) + nn(low_in_ref[...], up_ref[0])).astype(BF16)


def gate(meta, pieces, columns, low_in, up, parts, groups):
    tokens, width = pieces[0].shape
    length, chans = tokens * parts, columns.shape[-1]
    block = AT_ONCE * tokens
    seq = lambda size: pl.BlockSpec((block, size), lambda i, meta: (i, 0))
    return pl.pallas_call(
        functools.partial(gate_kernel, parts=parts),
        grid_spec=pltpu.PrefetchScalarGridSpec(
            num_scalar_prefetch=1,
            grid=(length // block,),
            in_specs=[pl.BlockSpec(memory_space=pl.ANY)] * (len(pieces) + 1)
            + [seq(low_in.shape[1]), chosen(up, parts, chans)],
            out_specs=seq(chans),
            scratch_shapes=[
                pltpu.VMEM((length, width), BF16), pltpu.VMEM((parts, groups) + columns.shape[2:], BF16),
                pltpu.SemaphoreType.DMA((len(pieces),)), pltpu.SemaphoreType.DMA((groups,)),
            ],
        ),
        out_shape=jax.ShapeDtypeStruct((length, chans), BF16),
        compiler_params=pltpu.CompilerParams(vmem_limit_bytes=LIMIT),
        name="gate",
    )(meta, *pieces, columns, low_in, up)


def back_gate_kernel(meta, *refs, parts):
    pieces, refs = refs[: parts + 1], refs[parts + 1 :]
    out_proj_ref, out_down_ref, out_up_ref, back_low_ref, cols_ref, grad_ref, rows_s, sems = refs
    step = pl.program_id(0)

    @pl.when(step == 0)
    def _():
        run_all(ring_copies(rows_s, pieces, meta[1], sems))

    block, span = cols_ref.shape
    at = pl.ds(pl.multiple_of(step * block, block), block)
    share_of = max(span * parts // rows_s.shape[1], 1)
    cols_ref[...] = rows_s[at, pl.ds(pl.multiple_of(lax.div(meta[1], share_of) * span, span), span)]
    rows = rows_s[at, :]
    back_low = nt(rows, out_up_ref[0]).astype(BF16)
    back_low_ref[...] = back_low
    grad_ref[...] = (nt(rows, out_proj_ref[...]) + nn(back_low, out_down_ref[0])).astype(BF16)


def back_gate(meta, pieces, out_proj, out_down, out_up, parts):
    tokens, width = pieces[0].shape
    chans, rank, block, length = out_proj.shape[0], out_up.shape[1], AT_ONCE * tokens, tokens * parts
    span = max(width // parts, 128)
    seq = lambda size: pl.BlockSpec((block, size), lambda i, meta: (i, 0))
    return pl.pallas_call(
        functools.partial(back_gate_kernel, parts=parts),
        grid_spec=pltpu.PrefetchScalarGridSpec(
            num_scalar_prefetch=1,
            grid=(length // block,),
            in_specs=[pl.BlockSpec(memory_space=pl.ANY)] * len(pieces)
            + [once(out_proj), chosen(out_down, 0, chans), chosen(out_up)],
            out_specs=[seq(rank), seq(span), seq(chans)],
            scratch_shapes=[pltpu.VMEM((length, width), BF16), pltpu.SemaphoreType.DMA((len(pieces),))],
        ),
        out_shape=[jax.ShapeDtypeStruct((length, size), BF16) for size in (rank, span, chans)],
        compiler_params=pltpu.CompilerParams(vmem_limit_bytes=LIMIT),
        name="back_gate",
    )(meta, *pieces, out_proj, out_down, out_up)


def project(meta, pieces, columns, in_down, up, weight, bias, proj, down, parts, groups):
    tokens, width = pieces[0].shape
    length, chans, rank = tokens * parts, columns[0].shape[-1], in_down.shape[1]
    cols = proj.shape[0] + rank
    seq = lambda size: pl.BlockSpec((AT_ONCE * tokens, size), lambda i, meta: (i, 0))
    rows = columns[0].shape[1]
    whole_shape = (parts, groups, rows, chans)
    return pl.pallas_call(
        functools.partial(project_kernel, parts=parts, groups=groups),
        grid_spec=pltpu.PrefetchScalarGridSpec(
            num_scalar_prefetch=1,
            grid=(parts // AT_ONCE,),
            in_specs=[pl.BlockSpec(memory_space=pl.ANY)] * (len(pieces) + groups)
            + [chosen(in_down), chosen(up, 0, chans), once(weight), once(bias), once(proj), chosen(down)],
            out_specs=[seq(rank), seq(chans), seq(chans), seq(cols)],
            scratch_shapes=[
                pltpu.VMEM((8, chans), F32), pltpu.VMEM((length, width), BF16), pltpu.VMEM(whole_shape, BF16),
                pltpu.SemaphoreType.DMA((len(pieces),)), pltpu.SemaphoreType.DMA((groups,)),
            ],
        ),
        out_shape=[jax.ShapeDtypeStruct((length, size), BF16) for size in (rank, chans, chans, cols)],
        compiler_params=pltpu.CompilerParams(vmem_limit_bytes=LIMIT),
        name="project",
    )(meta, *pieces, *columns, in_down, up, weight, bias, proj, down)


def share_kernel(meta, got_ref, state_up_ref, step_down_ref, out_ref, *, ranks, states):
    sums = got_ref[0].astype(F32)
    for i in range(1, got_ref.shape[0]):
        sums = sums + got_ref[i].astype(F32)
    cut = ranks + 2 * states
    low_state = sums[:, cut:].astype(BF16)
    mixed = sums[:, :cut] + nn(low_state, state_up_ref[0])
    step_low = mixed[:, :ranks].astype(BF16)
    step_mid = nt(step_low, step_down_ref[0]).astype(BF16)
    out_ref[...] = jnp.concatenate([step_low, step_mid, mixed[:, ranks:].astype(BF16), low_state], 1)


def share(meta, got, state_up, step_down, ranks, states):
    tokens, rank = got.shape[1], step_down.shape[1]
    cols = ranks + 2 * rank + 2 * states
    return pl.pallas_call(
        functools.partial(share_kernel, ranks=ranks, states=states),
        grid_spec=pltpu.PrefetchScalarGridSpec(
            num_scalar_prefetch=1,
            grid=(1,),
            in_specs=[once(got), chosen(state_up), chosen(step_down)],
            out_specs=pl.BlockSpec((tokens, cols), lambda i, meta: (0, 0)),
        ),
        out_shape=jax.ShapeDtypeStruct((tokens, cols), BF16),
        name="share",
    )(meta, got, state_up, step_down)


def share_back_kernel(meta, got_ref, step_down_ref, out_ref, *, ranks, states):
    sums = got_ref[0].astype(F32)
    for i in range(1, got_ref.shape[0]):
        sums = sums + got_ref[i].astype(F32)
    rank = step_down_ref.shape[1]
    mid, end = ranks + rank, ranks + rank + 2 * states
    back_mid = sums[:, ranks:mid]
    down = step_down_ref[0].astype(F32)
    back_step = sums[:, :ranks] + jnp.dot(back_mid, down, precision=lax.Precision.HIGHEST, preferred_element_type=F32)
    out_ref[...] = jnp.concatenate([back_step, sums[:, mid:end], back_mid, sums[:, end:]], 1).astype(BF16)


def share_back(meta, got, step_down, ranks, states):
    tokens, cols = got.shape[1:]
    return pl.pallas_call(
        functools.partial(share_back_kernel, ranks=ranks, states=states),
        grid_spec=pltpu.PrefetchScalarGridSpec(
            num_scalar_prefetch=1,
            grid=(1,),
            in_specs=[once(got), chosen(step_down)],
            out_specs=pl.BlockSpec((tokens, cols), lambda i, meta: (0, 0)),
        ),
        out_shape=jax.ShapeDtypeStruct((tokens, cols), BF16),
        name="share_back",
    )(meta, got, step_down)


def columns_of_groups(values, ref, sub):
    turned = values.astype(F32).T
    for k in range(ref.shape[0]):
        ref[k] = turned[:, k * sub : (k + 1) * sub]


def scan_forward_kernel(
    meta, shared_ref, u_ref, z_ref, step_proj_ref, step_up_ref, bias_ref, rate_ref, skip_ref,
    gated_ref, scanned_ref, states_ref,
    carry, delta_s, du_s, cm_s, y_s, bt_s, held_a, held_b, *, sub, ranks,
):
    rows = u_ref.shape[0]
    states = rate_ref.shape[0]
    rank = step_up_ref.shape[1]

    @pl.when(pl.program_id(0) == 0)
    def _():
        carry[...] = jnp.zeros_like(carry)
        held_b[...] = jnp.zeros_like(held_b)
        cm_s[:sub, :] = jnp.zeros((sub, sub * states), BF16)

    shared = shared_ref[0]
    step_mid = shared[:, ranks : ranks + rank]
    pre = nn(shared[:, :ranks], step_proj_ref[...]) + nn(step_mid, step_up_ref[0]) + bias_ref[...]
    delta = softplus(pre)
    delta_s[...] = delta
    du_s[...] = delta * u_ref[...].astype(F32)
    b_rows = shared[:, ranks + rank : ranks + rank + states]
    c_rows = shared[:, ranks + rank + states : ranks + rank + 2 * states]
    columns_of_groups(b_rows, bt_s, sub)
    cm = nn(c_rows, spread_matrix(states, sub)) * own_step_mask(rows, states, sub)
    cm_s[sub:, :] = cm.astype(BF16)
    rate = rate_ref[...]

    def pair(k, s):
        for turn, (mine, other) in enumerate(((held_a, held_b), (held_b, held_a))):
            base = pl.multiple_of(k * (2 * sub) + turn * sub, sub)
            y_s[pl.ds(base, sub), :] = nn(cm_s[pl.ds(base, sub), :], other[...])
            bt = bt_s[k * 2 + turn]
            for t in range(sub):
                dl = delta_s[pl.ds(base + t, 1), :]
                du = du_s[pl.ds(base + t, 1), :]
                s = jnp.exp2(dl * rate) * s + du * bt[:, t : t + 1]
                low = s.astype(BF16)
                mine[t * states : (t + 1) * states, :] = low
                states_ref[pl.ds(pl.multiple_of((base + t) * states, states), states), :] = low
        return s

    carry[...] = lax.fori_loop(0, rows // (2 * sub), pair, carry[...])
    y_s[rows:, :] = nn(cm_s[rows:, :], held_b[...])
    scanned = y_s[sub:, :] + skip_ref[...] * u_ref[...].astype(F32)
    scanned_ref[...] = scanned
    gated_ref[...] = (scanned * jax.nn.silu(z_ref[...].astype(F32))).astype(BF16)


def scan_forward(meta, shared, u, z, step_proj, step_up, bias, rate, skip, parts, sub):
    length, chans = u.shape
    block = length // parts
    states, ranks = rate.shape[0], step_proj.shape[0]
    seq = lambda cols: pl.BlockSpec((block, cols), lambda i, meta: (i, 0))
    out = lambda cols, dtype=BF16, rows=length: jax.ShapeDtypeStruct((rows, cols), dtype)
    return pl.pallas_call(
        functools.partial(scan_forward_kernel, sub=sub, ranks=ranks),
        grid_spec=pltpu.PrefetchScalarGridSpec(
            num_scalar_prefetch=1,
            grid=(parts,),
            in_specs=[
                pl.BlockSpec((1,) + shared.shape[1:], lambda i, meta: (place_of_block(i, meta[1], parts), 0, 0)),
                seq(chans), seq(chans), once(step_proj), chosen(step_up), once(bias), once(rate), once(skip),
            ],
            out_specs=[seq(chans), seq(chans), pl.BlockSpec((block * states, chans), lambda i, meta: (i, 0))],
            scratch_shapes=[
                pltpu.VMEM((states, chans), F32),
                pltpu.VMEM((block, chans), F32),
                pltpu.VMEM((block, chans), F32),
                pltpu.VMEM((block + sub, sub * states), BF16),
                pltpu.VMEM((block + sub, chans), F32),
                pltpu.VMEM((block // sub, states, sub), F32),
                pltpu.VMEM((sub * states, chans), BF16),
                pltpu.VMEM((sub * states, chans), BF16),
            ],
        ),
        out_shape=[out(chans), out(chans, F32), out(chans, rows=length * states)],
        compiler_params=pltpu.CompilerParams(vmem_limit_bytes=LIMIT),
        name="scan_forward",
    )(meta, shared, u, z, step_proj, step_up, bias, rate, skip)


def scan_backward_kernel(meta, *refs, sub, ranks):
    (shared_ref, step_proj_ref, step_up_ref, bias_ref, u_ref, z_ref, scanned_ref, bg_ref, states_ref, before_ref,
     rate_ref, decay_ref, skip_ref, low_out_ref) = refs[:14]
    pre_ref, conv_ref, bz_ref, mixed_ref = refs[14:18]
    carry, delta_s, du_s, bs_s, pre_s, bm_s, w_s, bd_s, bb_s, bc_s, ct_s, g_a, g_b, q_a, q_b = refs[18:]
    rows, chans = u_ref.shape
    states, rank = rate_ref.shape[0], step_up_ref.shape[1]
    step = pl.program_id(0)
    first = step == pl.num_programs(0) - 1

    @pl.when(step == 0)
    def _():
        carry[...] = jnp.zeros_like(carry)
        for ref in (g_a, q_a):
            ref[...] = jnp.zeros_like(ref)
        bm_s[rows:, :] = jnp.zeros((sub, sub * states), BF16)
        du_s[rows:, :] = jnp.zeros((sub, chans), F32)

    shared = shared_ref[0]
    step_mid = shared[:, ranks : ranks + rank]
    pre = nn(shared[:, :ranks], step_proj_ref[...]) + nn(step_mid, step_up_ref[0]) + bias_ref[...]
    delta = softplus(pre)
    z = z_ref[...].astype(F32)
    bg = bg_ref[...].astype(F32)
    sigma = jax.nn.sigmoid(z)
    bs_s[...] = bg * (z * sigma)
    bz_ref[...] = (bg * scanned_ref[...] * (sigma * (1.0 + z * (1.0 - sigma)))).astype(BF16)
    pre_s[...] = pre
    delta_s[...] = delta
    du_s[:rows, :] = delta * u_ref[...].astype(F32)
    b_rows = shared[:, ranks + rank : ranks + rank + states]
    c_rows = shared[:, ranks + rank + states : ranks + rank + 2 * states]
    columns_of_groups(c_rows, ct_s, sub)
    bm = nn(b_rows, spread_matrix(states, sub)) * own_step_mask(rows, states, sub)
    bm_s[:rows, :] = bm.astype(BF16)
    ones = own_step_mask(sub, states, sub).astype(BF16)
    col = lax.broadcasted_iota(jnp.int32, (states, sub), 1)
    rate = rate_ref[...]
    decay = decay_ref[...]
    pairs = rows // (2 * sub)

    def diagonal(wide):
        out = wide[:states]
        for t in range(1, sub):
            out = jnp.where(col == t, wide[t * states : (t + 1) * states], out)
        return out

    def finish(at, k, g_ref, q_ref):
        w_s[at, :] = nn(bm_s[at, :], g_ref[...])
        bd_s[at, :] = nn(ones, q_ref[...])
        bb_s[k] = diagonal(nt(g_ref[...], du_s[at, :].astype(BF16)))

    def pair(i, h):
        for turn, (g_mine, q_mine, g_other, q_other) in enumerate(((g_b, q_b, g_a, q_a), (g_a, q_a, g_b, q_b))):
            k = (pairs - 1 - i) * 2 + 1 - turn
            base = pl.multiple_of(k * sub, sub)
            finish(pl.ds(pl.multiple_of(base + sub, sub), sub), k + 1, g_other, q_other)
            wide = pl.ds(pl.multiple_of(base * states, sub * states), sub * states)
            bc_s[k] = diagonal(nt(states_ref[wide, :], bs_s[pl.ds(base, sub), :].astype(BF16)))
            ct = ct_s[k]
            for t in range(sub - 1, -1, -1):
                dl = delta_s[pl.ds(base + t, 1), :]
                bs = bs_s[pl.ds(base + t, 1), :]
                g = bs * ct[:, t : t + 1] + h
                h = g * jnp.exp2(dl * rate)
                if t:
                    sp = states_ref[pl.ds(pl.multiple_of((base + t - 1) * states, states), states), :]
                else:
                    at = pl.multiple_of(jnp.maximum(base - 1, 0) * states, states)
                    inside = jnp.where(k > 0, 1.0, 0.0)
                    outside = jnp.where(first, 0.0, 1.0 - inside)
                    sp = states_ref[pl.ds(at, states), :] * inside.astype(BF16)
                    sp = sp + before_ref[...] * outside.astype(BF16)
                g_mine[t * states : (t + 1) * states, :] = g.astype(BF16)
                q_mine[t * states : (t + 1) * states, :] = h.astype(BF16) * (decay * sp)
        return h

    carry[...] = lax.fori_loop(0, pairs, pair, carry[...])
    finish(pl.ds(0, sub), 0, g_a, q_a)
    w = w_s[:rows, :]
    conv_ref[...] = w * delta_s[...] + skip_ref[...] * bs_s[...]
    back_delta = bd_s[:rows, :] + w * u_ref[...].astype(F32)
    back_pre = (back_delta * jax.nn.sigmoid(pre_s[...])).astype(BF16)
    pre_ref[...] = back_pre
    turned = [
        jnp.concatenate([ref[k] for k in range(rows // sub)], 1).T for ref in (bb_s, bc_s)
    ]
    mixed_ref[...] = jnp.concatenate(
        [nt(back_pre, step_proj_ref[...]), nt(back_pre, step_up_ref[0])] + turned + [low_out_ref[...]], 1
    ).astype(BF16)


def scan_backward(
    meta, shared, step_proj, step_up, bias, u, z, scanned, bg, kept, rate, decay, skip, low_out, parts, sub,
):
    length, chans = u.shape
    block = length // parts
    states, rank, ranks = rate.shape[0], step_up.shape[1], step_proj.shape[0]
    end = parts
    seq = lambda cols: pl.BlockSpec((block, cols), lambda i, meta: (end - 1 - i, 0))
    cols = ranks + 2 * rank + 2 * states
    out = lambda cols, dtype=BF16: jax.ShapeDtypeStruct((length, cols), dtype)
    args = (shared, step_proj, step_up, bias, u, z, scanned, bg, kept, kept, rate, decay, skip, low_out)
    return pl.pallas_call(
        functools.partial(scan_backward_kernel, sub=sub, ranks=ranks),
        grid_spec=pltpu.PrefetchScalarGridSpec(
            num_scalar_prefetch=1,
            grid=(parts,),
            in_specs=[
                pl.BlockSpec(
                    (1,) + shared.shape[1:], lambda i, meta: (place_of_block(end - 1 - i, meta[1], parts), 0, 0)
                ),
                once(step_proj), chosen(step_up), once(bias), seq(chans), seq(chans), seq(chans), seq(chans),
                pl.BlockSpec((block * states, chans), lambda i, meta: (end - 1 - i, 0)),
                pl.BlockSpec((states, chans), lambda i, meta: (jnp.maximum((end - 1 - i) * block - 1, 0), 0)),
                once(rate), once(decay), once(skip), seq(rank),
            ],
            out_specs=[seq(chans), seq(chans), seq(chans), seq(cols)],
            scratch_shapes=[
                pltpu.VMEM((states, chans), F32),
                pltpu.VMEM((block, chans), F32),
                pltpu.VMEM((block + sub, chans), F32),
                pltpu.VMEM((block, chans), F32),
                pltpu.VMEM((block, chans), F32),
                pltpu.VMEM((block + sub, sub * states), BF16),
                pltpu.VMEM((block + sub, chans), F32),
                pltpu.VMEM((block + sub, chans), F32),
                pltpu.VMEM((block // sub + 1, states, sub), F32),
                pltpu.VMEM((block // sub, states, sub), F32),
                pltpu.VMEM((block // sub, states, sub), F32),
                pltpu.VMEM((sub * states, chans), BF16),
                pltpu.VMEM((sub * states, chans), BF16),
                pltpu.VMEM((sub * states, chans), BF16),
                pltpu.VMEM((sub * states, chans), BF16),
            ],
        ),
        out_shape=[out(chans), out(chans, F32), out(chans), out(cols)],
        compiler_params=pltpu.CompilerParams(vmem_limit_bytes=LIMIT),
        name="scan_backward",
    )(meta, *args)


def finish_kernel(
    meta, *refs, ranks, states, parts, groups,
):
    pieces, refs = refs[: parts + 1], refs[parts + 1 :]
    columns_x, columns_z, refs = refs[:groups], refs[groups], refs[groups + 1 :]
    (back_ref, shared_ref, conv_grad_ref, back_z_ref, back_pre_ref, x_ref, x_before_ref, u_ref, low_in_ref,
     gated_ref, back_low_ref, cols_ref, up_x_ref, up_z_ref, proj_ref, down_ref,
     state_up_ref, in_down_ref, weight_ref, bias_ref,
     parts_ref, wide_ref, down_grad_ref, local_ref,
     after, sums_s, down_s, local_s, rows_s, whole_x, whole_z, piece_sems, x_sems, z_sems) = refs
    copies = (
        ring_copies(rows_s, pieces, meta[1], piece_sems)
        + row_copies(whole_x, columns_x, meta[2], x_sems)
        + row_copies(whole_z, columns_z, None, z_sems)
    )
    step = pl.program_id(0)
    steps = pl.num_programs(0)
    rows, chans = u_ref.shape
    rank = state_up_ref.shape[1]
    taps = weight_ref.shape[0]
    mixes = ranks + 2 * states

    @pl.when(step == 0)
    def _():
        for copy in copies:
            copy.start()
        after[...] = jnp.zeros_like(after)
        sums_s[...] = jnp.zeros_like(sums_s)
        down_s[...] = jnp.zeros_like(down_s)
        local_s[...] = jnp.zeros_like(local_s)

    per = rows // back_ref.shape[1]
    places = [place_of_block((steps - 1 - step) * per + j, meta[1], parts) for j in range(per)]
    back = jnp.concatenate([back_ref[place] for place in places], 0)
    shared = jnp.concatenate([shared_ref[place] for place in places], 0)
    u = u_ref[...]
    mixed = back[:, :mixes]
    back_low_state = nt(mixed, state_up_ref[0]).astype(BF16)
    grad = conv_grad_ref[...] + nn(mixed, proj_ref[...]) + nn(back_low_state, down_ref[0])
    keep = jnp.where(step == steps - 1, 0.0, 1.0)
    conv_pre = conv_before(x_ref[...].astype(F32), x_before_ref[...].astype(F32) * keep, weight_ref, bias_ref)
    grad = grad * silu_grad(conv_pre)
    padded = jnp.concatenate([grad, after[...]], 0)
    back_x = weight_ref[taps - 1 : taps, :] * grad
    for tap in range(taps - 1):
        at = taps - 1 - tap
        back_x = back_x + weight_ref[tap : tap + 1, :] * padded[at : at + rows]
    after[...] = grad[:8]
    back_x, back_z = back_x.astype(BF16), back_z_ref[...]

    @pl.when(step == 0)
    def _():
        for copy in copies:
            copy.wait()

    normed = rows_s[pl.ds(pl.multiple_of((steps - 1 - step) * rows, rows), rows), :]
    back_low_in = (nt(back_x, up_x_ref[0]) + nt(back_z, up_z_ref[0])).astype(BF16)
    parts_ref[...] = (
        nt(back_x, flat(whole_x)) + nt(back_z, flat(whole_z)) + nn(back_low_in, in_down_ref[0])
    ).astype(BF16)
    down_s[...] += tn(back_low_in, normed)
    low_in = low_in_ref[...]
    sums_s[:, :chans] += tn(low_in, back_x)
    sums_s[:, chans : 2 * chans] += tn(low_in, back_z)
    sums_s[:, 2 * chans : 3 * chans] += tn(back_low_ref[...], gated_ref[...])
    sums_s[:, 3 * chans :] += tn(back[:, mixes + rank :], cols_ref[...])
    local_s[:, :chans] += tn(back_low_state, u)
    local_s[:, chans : 2 * chans] += tn(shared[:, ranks : ranks + rank], back_pre_ref[...])
    local_s[:, 2 * chans : 2 * chans + ranks] += tn(back[:, mixes : mixes + rank], shared[:, :ranks])
    at = 2 * chans + ranks
    local_s[:, at : at + mixes] += tn(shared[:, ranks + rank + 2 * states :], mixed)

    @pl.when(step == steps - 1)
    def _():
        wide_ref[...] = sums_s[...].astype(BF16)
        down_grad_ref[...] = down_s[...].astype(BF16)
        lane = lax.broadcasted_iota(jnp.int32, (rank, 128), 1)
        local_ref[:, :-128] = local_s[...].astype(BF16)
        local_ref[:, -128:] = (lane == meta[0]).astype(BF16)


def finish(
    meta, pieces, columns_x, columns_z, back, shared, conv_grad, back_z, back_pre, x, u, low_in, gated, back_low, cols, up,
    proj, down, state_up, in_down, weight, bias, parts, groups, states,
):
    length, chans = u.shape
    block, rank, span = AT_ONCE * length // parts, low_in.shape[1], cols.shape[1]
    mixes = proj.shape[0]
    ranks = mixes - 2 * states
    width = pieces[0].shape[1]
    whole_shape = (parts, groups) + columns_x[0].shape[1:]
    end = length // block - 1
    seq = lambda size: pl.BlockSpec((block, size), lambda i, meta: (end - i, 0))
    wide = 3 * chans + span
    local = 2 * chans + ranks + 2 * 128
    fixed = lambda size: pl.BlockSpec((rank, size), lambda i, meta: (0, 0))
    return pl.pallas_call(
        functools.partial(finish_kernel, ranks=ranks, states=states, parts=parts, groups=groups),
        grid_spec=pltpu.PrefetchScalarGridSpec(
            num_scalar_prefetch=1,
            grid=(length // block,),
            in_specs=[pl.BlockSpec(memory_space=pl.ANY)] * (len(pieces) + groups + 1)
            + [
                once(back), once(shared), seq(chans), seq(chans), seq(chans), seq(chans),
                pl.BlockSpec((16, chans), lambda i, meta: (jnp.maximum((end - i) * (block // 16) - 1, 0), 0)),
                seq(chans), seq(rank), seq(chans), seq(rank), seq(span),
                chosen(up, 0, chans), chosen(up, parts, chans), once(proj), chosen(down), chosen(state_up),
                chosen(in_down), once(weight), once(bias),
            ],
            out_specs=[seq(width), fixed(wide), fixed(width), fixed(local + 128)],
            scratch_shapes=[
                pltpu.VMEM((8, chans), F32), pltpu.VMEM((rank, wide), F32), pltpu.VMEM((rank, width), F32),
                pltpu.VMEM((rank, local), F32), pltpu.VMEM((length, width), BF16),
                pltpu.VMEM(whole_shape, BF16), pltpu.VMEM(whole_shape, BF16),
                pltpu.SemaphoreType.DMA((len(pieces),)), pltpu.SemaphoreType.DMA((groups,)),
                pltpu.SemaphoreType.DMA((groups,)),
            ],
        ),
        out_shape=[
            jax.ShapeDtypeStruct((length, width), BF16),
            jax.ShapeDtypeStruct((rank, wide), BF16),
            jax.ShapeDtypeStruct((rank, width), BF16),
            jax.ShapeDtypeStruct((rank, local + 128), BF16),
        ],
        compiler_params=pltpu.CompilerParams(vmem_limit_bytes=LIMIT),
        name="finish",
    )(
        meta, *pieces, *columns_x, columns_z, back, shared, conv_grad, back_z, back_pre, x, x, u, low_in, gated, back_low,
        cols, up, up, proj, down, state_up, in_down, weight, bias,
    )


def placed(values, idents, e):
    total = None
    for value, ident in zip(values, idents):
        term = jnp.where(ident == e, value, 0.0)
        total = term if total is None else total + term
    return total


def place_kernel(meta, *refs, first, size, every):
    values_refs, out_ref = refs[:-1], refs[-1]
    groups, parts = len(values_refs), values_refs[0].shape[0]
    count = parts // every
    per = out_ref.shape[2] // size
    idents = [meta[3 + groups + g] for g in range(groups)]
    step = pl.program_id(0)
    column = pl.multiple_of((first + lax.div(step * per, count)) * size, size)
    for j in range(per):
        at = place_of_block(lax.rem(step * per + j, count) * every, meta[1], parts)
        values = [ref[at, :, pl.ds(column, size)].astype(F32) for ref in values_refs]
        for e in range(out_ref.shape[0]):
            out_ref[e, :, j * size : (j + 1) * size] = placed(values, idents, e)


def place(meta, values, adapters, first, size, parts, every=1, runs=1):
    rank = values[0].shape[1]
    count = parts // every
    per = count // 2
    return pl.pallas_call(
        functools.partial(place_kernel, first=first, size=size, every=every),
        grid_spec=pltpu.PrefetchScalarGridSpec(
            num_scalar_prefetch=1,
            grid=(runs * count // per,),
            in_specs=[once(value) for value in values],
            out_specs=pl.BlockSpec((adapters, rank, size * per), lambda i, meta: (0, 0, i)),
        ),
        out_shape=jax.ShapeDtypeStruct((adapters, rank, size * count * runs), F32),
        compiler_params=pltpu.CompilerParams(vmem_limit_bytes=16 << 20),
        name="place",
    )(meta, *values)


def place_local_kernel(meta, values_ref, *out_refs):
    groups = values_ref.shape[0]
    idents = [meta[3 + g] for g in range(groups)]
    at = 0
    for ref in out_refs:
        size = ref.shape[2]
        values = [values_ref[g, :, at : at + size].astype(F32) for g in range(groups)]
        for e in range(ref.shape[0]):
            ref[e] = placed(values, idents, e)
        at += size


def place_local(meta, values, adapters, sizes):
    rank = values.shape[1]
    return pl.pallas_call(
        place_local_kernel,
        grid_spec=pltpu.PrefetchScalarGridSpec(
            num_scalar_prefetch=1,
            grid=(1,),
            in_specs=[once(values)],
            out_specs=[pl.BlockSpec((adapters, rank, size), lambda i, meta: (0, 0, 0)) for size in sizes],
        ),
        out_shape=[jax.ShapeDtypeStruct((adapters, rank, size), F32) for size in sizes],
        name="place_local",
    )(meta, values)


EPS = 1e-05


def ring_send(value, size, hop, axis):
    order = list(range(0, size, 2)) + list(range(1, size, 2))[::-1]
    pairs = [(order[i], order[(i + hop) % size]) for i in range(size)]
    return lax.ppermute(value, axis, pairs)


class RingGather:
    def __init__(self, own, size, axis):
        self.size, self.axis, self.rows, self.done = size, axis, own.shape[0], 0
        self.pieces = [own]
        self.ends = (own, own)

    def advance(self, hops):
        far, half = self.size // 2, self.rows // 2
        for _ in range(min(hops, far - self.done)):
            self.done += 1
            ahead, back = self.ends
            if self.done == far:
                ahead, back = ahead[:half], back[half:]
            self.ends = (ring_send(ahead, self.size, 1, self.axis), ring_send(back, self.size, -1, self.axis))
            self.pieces += list(self.ends)

    def all_pieces(self):
        self.advance(self.size)
        return self.pieces


class RingScatter:
    def __init__(self, partial, size, axis):
        self.partial, self.size, self.axis, self.done = partial, size, axis, 0
        self.rows = partial.shape[0] // size
        self.position = ring_position(lax.axis_index(axis), size)
        self.ends = None

    def block(self, offset, start=0, rows=None):
        at = ring_place(self.position + offset, self.size) * self.rows + start
        return lax.dynamic_slice_in_dim(self.partial, at, rows or self.rows, 0)

    def advance(self, hops):
        far, half = self.size // 2, self.rows // 2
        for _ in range(min(hops, far - self.done)):
            left = far - self.done
            if left == far:
                mine, other = self.block(far, 0, half), self.block(far, half, half)
            else:
                mine, other = self.block(left).astype(F32), self.block(-left).astype(F32)
                ahead, back = (end.astype(F32) for end in self.ends)
                if left == far - 1:
                    blank = jnp.zeros_like(ahead)
                    ahead, back = jnp.concatenate([ahead, blank], 0), jnp.concatenate([blank, back], 0)
                mine, other = (mine + ahead).astype(BF16), (other + back).astype(BF16)
            self.ends = (
                ring_send(mine, self.size, 1, self.axis),
                ring_send(other, self.size, -1, self.axis),
            )
            self.done += 1

    def total(self):
        self.advance(self.size)
        return self.block(0).astype(F32) + self.ends[0].astype(F32) + self.ends[1].astype(F32)


def together(*values):
    return lax.optimization_barrier(values)


def swap(value, size, bit, axis):
    return lax.ppermute(value, axis, [(i, i ^ bit) for i in range(size)])


def bits_of(size):
    bit = size // 2
    while bit:
        yield bit
        bit //= 2


def swap_gather(own, size, axis):
    held = [own]
    for bit in bits_of(size):
        held += [swap(block, size, bit, axis) for block in held]
    return held


def small_gather(own, size, axis):
    held = own[None]
    for bit in bits_of(size):
        held = jnp.concatenate([held, swap(held, size, bit, axis)], 0)
    return held


def exchange(values, size, axis):
    got = lax.all_to_all(values, axis, split_axis=0, concat_axis=0, tiled=True)
    return got.reshape((size, -1) + values.shape[1:])


def body(
    hidden, lengths, adapter_ids, norm_gain, in_proj_x, in_proj_z, conv_weight, conv_bias, state_proj,
    step_proj, step_bias, decay_log, skip_gain, out_proj, in_down, in_up, state_down, state_up, step_down,
    step_up, out_down, out_up, cotangent,
):
    parts, groups = lax.axis_size("seq"), lax.axis_size("fsdp")
    part, group = lax.axis_index("seq"), lax.axis_index("fsdp")
    tokens, width = hidden.shape[1:]
    chans = conv_weight.shape[1]
    ranks = step_proj.shape[0]
    states = decay_log.shape[0]
    rank = in_down.shape[2]
    adapters = in_down.shape[0]
    ident = adapter_ids[0]
    sub = 16
    meta = jnp.stack([ident, part, group]).astype(jnp.int32)
    in_down, state_down, step_down, out_down = (
        table.transpose(0, 2, 1) for table in (in_down, state_down, step_down, out_down)
    )
    state_proj = state_proj.T

    hidden_f = hidden[0].astype(F32)
    gain_f = norm_gain.astype(F32)
    inverse = lax.rsqrt(jnp.mean(hidden_f * hidden_f, axis=-1, keepdims=True) + EPS)
    normed = (hidden_f * inverse * gain_f).astype(BF16)
    positions = part * tokens + lax.broadcasted_iota(jnp.int32, (tokens, 1), 0)
    valid = (positions < lengths[0]).astype(F32)
    cot_f = cotangent[0].astype(F32)
    back_out = (valid * cot_f).astype(BF16)
    conv_weight, conv_bias = conv_weight.astype(F32), conv_bias.astype(F32)[None]
    bias, skip = step_bias.astype(F32)[None], skip_gain.astype(F32)[None]
    decay = -jnp.exp(decay_log.astype(F32))
    rate, decay = decay * LOG2E, decay.astype(BF16)
    rows = in_proj_x.shape[0]

    def own_columns_of(weight):
        return lax.all_to_all(weight, "seq", split_axis=1, concat_axis=0, tiled=True).reshape(parts, rows, chans)

    hops = max(parts // 8, 1)
    whole_out = lax.all_gather(out_proj, "fsdp", axis=0, tiled=True)
    pieces = RingGather(normed, parts, "seq").all_pieces()
    columns = swap_gather(own_columns_of(in_proj_x), groups, "fsdp")

    pieces, columns, back_out, in_proj_z = together(pieces, columns, back_out, in_proj_z)
    cot_ring = RingGather(back_out, parts, "seq")
    cot_ring.advance(hops)
    mine_z = own_columns_of(in_proj_z)
    low_in, x, conv_out, sums = project(
        meta, pieces, columns, in_down, in_up, conv_weight, conv_bias, state_proj, state_down, parts, groups
    )
    sums, cot_ring.ends, mine_z = together(sums, cot_ring.ends, mine_z)
    cot_ring.advance(hops)
    columns_z = lax.all_gather(mine_z, "fsdp")
    shared = share(meta, exchange(sums, parts, "seq"), state_up, step_down, ranks, states)
    shared, cot_ring.ends = together(shared, cot_ring.ends)
    shared = small_gather(shared, parts, "seq")
    z = gate(meta, pieces, columns_z, low_in, in_up, parts, groups)
    shared, z, cot_ring.ends = together(shared, z, cot_ring.ends)
    cot_ring.advance(hops)
    gated, scanned, kept = scan_forward(meta, shared, conv_out, z, step_proj, step_up, bias, rate, skip, parts, sub)
    gated, cot_ring.ends = together(gated, cot_ring.ends)
    cot_ring.advance(parts)
    out_down_sel = lax.dynamic_slice(out_down, (ident, 0, part * chans), (1, rank, chans))[0]
    out_parts, low_out = nn(gated, whole_out).astype(BF16), nt(gated, out_down_sel)
    out_parts, low_out, cot_ring.pieces = together(out_parts, low_out, cot_ring.pieces)
    out_ring = RingScatter(out_parts, parts, "seq")
    out_ring.advance(hops)
    back_low, cols, back_gated = back_gate(meta, cot_ring.pieces, whole_out, out_down, out_up, parts)
    back_gated, out_ring.ends = together(back_gated, out_ring.ends)
    out_ring.advance(hops)
    back_pre, conv_grad, back_z, mixed = scan_backward(
        meta, shared, step_proj, step_up, bias, conv_out, z, scanned, back_gated, kept, rate, decay, skip, low_out, parts,
        sub,
    )
    mixed, out_ring.ends = together(mixed, out_ring.ends)
    out_ring.advance(hops)
    back_own = share_back(meta, exchange(mixed, parts, "seq"), step_down, ranks, states)
    back_own, out_ring.ends = together(back_own, out_ring.ends)
    back = small_gather(back_own, parts, "seq")
    back, out_ring.ends = together(back, out_ring.ends)
    out_ring.advance(parts)
    in_parts, wide, down_grad, local = finish(
        meta, pieces, columns, columns_z, back, shared, conv_grad, back_z, back_pre, x, conv_out, low_in, gated, back_low,
        cols, in_up, state_proj, state_down, state_up, in_down, conv_weight, conv_bias, parts, groups, states,
    )
    in_parts, wide, down_grad, local, out_ring.ends = together(in_parts, wide, down_grad, local, out_ring.ends)
    in_ring = RingScatter(in_parts, parts, "seq")
    span = cols.shape[1]
    share_of = max(span * parts // width, 1)
    held = jnp.concatenate([wide, down_grad], 1)[None]
    for bit in bits_of(parts):
        in_ring.advance(hops)
        held = jnp.concatenate([held, swap(held, parts, bit, "seq")], 0)
        held, in_ring.ends = together(held, in_ring.ends)
    in_ring.advance(parts)
    down_grad = held[:, :, wide.shape[1] :].astype(F32).sum(0).astype(BF16)
    held = held[:, :, : wide.shape[1]]
    wide = [held]
    for bit in bits_of(groups):
        wide += [swap(block, groups, bit, "fsdp") for block in wide]
    local = lax.all_gather(jnp.concatenate([down_grad, local], 1), "fsdp")
    out_up_sel = lax.dynamic_index_in_dim(out_up, ident, 0, keepdims=False)
    block_out = (hidden_f + valid * (out_ring.total() + nn(back_own[:, -rank:], out_up_sel))).astype(BF16)
    gained = in_ring.total() * gain_f
    input_grad = (
        cot_f
        + inverse * gained
        - hidden_f * inverse * inverse * inverse * jnp.mean(hidden_f * gained, axis=-1, keepdims=True)
    )

    lane = lax.broadcasted_iota(jnp.int32, (groups, adapters), 1)
    idents = jnp.sum(local[:, 0, -128 : -128 + adapters].astype(F32) * lane.astype(F32), axis=1).astype(jnp.int32)
    apart = jnp.asarray(swap_order(groups), jnp.int32)
    meta = jnp.concatenate([meta, idents, idents[jnp.bitwise_xor(group, apart)]])
    in_up_grad = place(meta, wide, adapters, 0, chans, parts, runs=2)
    out_down_grad = place(meta, wide, adapters, 2, chans, parts)
    first = 3 * chans // span
    out_up_grad = place(meta, wide, adapters, first, span, parts, every=share_of)
    in_down_grad, state_down_grad, step_up_grad, step_down_grad, state_up_grad = place_local(
        meta, local, adapters, (width, chans, chans, ranks, ranks + 2 * states)
    )
    return (
        block_out[None], input_grad[None], in_down_grad.transpose(0, 2, 1), in_up_grad,
        state_down_grad.transpose(0, 2, 1), state_up_grad, step_down_grad.transpose(0, 2, 1), step_up_grad,
        out_down_grad.transpose(0, 2, 1), out_up_grad,
    )


def solution(mesh):
    seq, rows = P("fsdp", "seq", None), P(("seq", "fsdp"), None)
    in_specs = (
        seq, P("fsdp"), P("fsdp"), P(), rows, rows, P(None, "seq"), P("seq"), P("seq", None), P(None, "seq"),
        P("seq"), P(None, "seq"), P("seq"), rows, P(), P(), P(None, "seq", None), P(), P(), P(None, None, "seq"),
        P(), P(), seq,
    )
    out_specs = (seq, seq, P(), P(), P(None, "seq", None), P(), P(), P(None, None, "seq"), P(), P())
    return jax.shard_map(body, mesh=mesh, in_specs=in_specs, out_specs=out_specs, check_vma=False)
```

time: 468 us -> 386 us (0.82); the launches traced: 460 us -> 384 us
  matrix products: 68.7 us -> 7.82 us
  Pallas kernels: 61.6 us -> 119 us
  local copies, waits for them, and re-layouts: 70.8 us -> 14.4 us
  starting transfers between devices: 37.7 us -> 79.8 us
  waiting for transfers between devices: 145 us -> 111 us
  blocking collectives: 21.7 us -> 7.02 us
  between operations: 21.8 us -> 15.9 us
    pallas_call x2 -> x12, Pallas kernels: 61.6 us -> 119 us  [the longest x1 34.2 us: scan_backward(): pl.pallas_call(functools.partial(scan_backward_kernel, sub=sub, ranks=ran...]
    ppermute x16 -> x32, waiting for transfers between devices: 71.6 us -> 44.9 us  [ring_send(): return lax.ppermute(value, axis, pairs)]
    dot_general x12 -> x1, matrix products: 24.5 us -> 1.14 us  [nt(): lax.dot_general(left, right, (((1,), (1,)), ((), ())), preferred_element_...]
    ppermute x16 -> x32, starting transfers between devices: 15.7 us -> 38.5 us  [ring_send(): return lax.ppermute(value, axis, pairs)]
    dot_general x11 -> x2, matrix products: 29.3 us -> 6.67 us  [nn(): return jnp.dot(left, right, preferred_element_type=F32)]
    all_to_all x1 -> x0, blocking collectives: 21.7 us -> none  [columns_later(): lax.all_to_all(weight, 'seq', split_axis=1, concat_axis=0, tiled=True)]
    ppermute x9 -> x15, starting transfers between devices: 5.25 us -> 21 us  [swap(): return lax.ppermute(value, axis, [(i, i ^ bit) for i in range(size)])]
    dot_general x9 -> x0, matrix products: 14.9 us -> none  [tn(): lax.dot_general(left, right, (((0,), (0,)), ((), ())), preferred_element_...]
  transfers between devices with their start and end apart: 34 -> 53, of which waited for: 19 -> 28; matrix products, arithmetic and copies ran while one was open for 28% -> 9% of each run, Pallas kernels for 13% -> 29%
where the time goes in v2:
time: 386 us; the launch traced here: 384 us
  Pallas kernels  119 us (31%)
  waiting for transfers between devices  111 us (29%)
  starting transfers between devices  79.8 us (21%)
  other arithmetic  29.1 us (8%)
  between operations  15.9 us (4%)
  local copies, waits for them, and re-layouts  14.4 us (4%)
  matrix products  7.82 us (2%)
  blocking collectives  7.02 us (2%)
    ppermute x32, waiting for transfers between devices, ring_send(): return lax.ppermute(value, axis, pairs)  44.9 us
    ppermute x32, starting transfers between devices, ring_send(): return lax.ppermute(value, axis, pairs)  38.5 us
    ppermute x15, waiting for transfers between devices, swap(): return lax.ppermute(value, axis, [(i, i ^ bit) for i in range(size)])  36.7 us
    pallas_call x1, Pallas kernels, scan_backward(): pl.pallas_call(functools.partial(scan_backward_kernel, sub=sub, ranks=ran...  34.2 us
    ppermute x15, starting transfers between devices, swap(): return lax.ppermute(value, axis, [(i, i ^ bit) for i in range(size)])  21 us
    pallas_call x1, Pallas kernels, finish(): pl.pallas_call(functools.partial(finish_kernel, ranks=ranks, states=state...  18.8 us
    all_to_all x2, waiting for transfers between devices, exchange(): got = lax.all_to_all(values, axis, split_axis=0, concat_axis=0, tiled=True)  16.9 us
    pallas_call x1, Pallas kernels, scan_forward(): pl.pallas_call(functools.partial(scan_forward_kernel, sub=sub, ranks=rank...  16.6 us
  transfers between devices with their start and end apart: 53, of which 28 were waited for; matrix products, arithmetic and copies ran while one was open for 9% of the time, Pallas kernels for 29%

profile of v2, /device:TPU:0, one launch (start us, length us, event | category | flops | bytes accessed | tf_op | source)
XLA Modules:
  0.0 384.0 jit_solution(9735029840136104419)
XLA Ops:
  10.4 3.1 collective-permute-start
  13.5 1.9 copy.64
  15.3 6.3 %all-to-all-start = ((bf16[64,8,512]{2,0,1:T(8,128)(2,1)}), bf16[64,8,512]{2,0,1:T(8,128)(2,1)}, u32[]{:S(2)}, u32[]{:S(2)}) async-start(bf16[64,8,512]{2,0,1:T(8,128)(2,1)} %bitcast.62), calls=%async_computation | async-start | bytes 1048576 | tf_op jit(solution)/shard_map/all_to_all | solution.py:883
  21.6 4.4 %collective-permute-done.refs_1_ = bf16[128,2048]{1,0:T(8,128)(2,1)S(1)} collective-permute-done((bf16[128,2048]{1,0:T(8,128)(2,1)S(1)}, bf16[128,2048]{1,0:T(8,128)(2,1)S(1)}, u32[]{:S(2)}, u32[]{:S(2)}) %collective-permute-start) | collective-permute-done | bytes 524320 | tf_op jit(solution)/shard_map/ppermute | solution.py:754
  26.0 3.3 collective-permute-start.2
  29.3 11.4 %all-to-all-done = bf16[64,8,512]{2,0,1:T(8,128)(2,1)} async-done(((bf16[64,8,512]{2,0,1:T(8,128)(2,1)}), bf16[64,8,512]{2,0,1:T(8,128)(2,1)}, u32[]{:S(2)}, u32[]{:S(2)}) %all-to-all-start) | async-done | bytes 524320 | tf_op jit(solution)/shard_map/all_to_all | solution.py:883
  42.2 2.1 collective-permute-done.2.refs_3_
  44.3 4.4 %collective-permute-start.4 = (bf16[128,2048]{1,0:T(8,128)(2,1)S(1)}, bf16[128,2048]{1,0:T(8,128)(2,1)S(1)}, u32[]{:S(2)}, u32[]{:S(2)}) collective-permute-start(bf16[128,2048]{1,0:T(8,128)(2,1)S(1)} %collective-permute-done.2.refs_3_), channel_id=1, source_target_pairs={{0,8},{8,16},{16,24},{24,28},{28,20},{20,12},{12,4},{4,0},{1,9},{9... | collective-permute-start | bytes 1572872 | tf_op jit(solution)/shard_map/ppermute | solution.py:754
  50.8 8.2 %collective-permute-done.4.refs_5_ = bf16[128,2048]{1,0:T(8,128)(2,1)S(1)} collective-permute-done((bf16[128,2048]{1,0:T(8,128)(2,1)S(1)}, bf16[128,2048]{1,0:T(8,128)(2,1)S(1)}, u32[]{:S(2)}, u32[]{:S(2)}) %collective-permute-start.4) | collective-permute-done | bytes 524320 | tf_op jit(solution)/shard_map/ppermute | solution.py:754
  59.0 2.6 collective-permute-start.6
  62.4 2.0 fusion.7.refs_0_
  64.5 2.7 collective-permute-done.6.refs_7_
  68.8 1.9 copy.63
  70.7 4.1 %all-to-all-start.1 = ((bf16[64,8,512]{2,0,1:T(8,128)(2,1)}), bf16[64,8,512]{2,0,1:T(8,128)(2,1)}, u32[]{:S(2)}, u32[]{:S(2)}) async-start(bf16[64,8,512]{2,0,1:T(8,128)(2,1)} %bitcast.72), calls=%async_computation.1 | async-start | bytes 1048576 | tf_op jit(solution)/shard_map/all_to_all | solution.py:883
  74.9 1.9 collective-permute-start.11
  79.5 14.1 %project.1 = (bf16[1024,16]{1,0:T(8,128)(2,1)}, bf16[1024,512]{1,0:T(8,128)(2,1)}, bf16[1024,512]{1,0:T(8,128)(2,1)}, bf16[1024,176]{1,0:T(8,128)(2,1)}) custom-call(s32[3]{0:T(128)} %pad_add_fusion.meta, bf16[128,2048]{1,0:T(8,128)(2,1)} %copy-done.2, bf16[128,2048]{1,0:T(8,128)(2,1)} %copy-done.6, bf16[128,2048]{1,0:T(8,128)(2,1)} %copy-done.7, ...), custom_call_target="tpu_custom_call" | custom-call | tf_op jit(solution)/shard_map/project/pallas_call | solution.py:244
  95.4 2.0 copy.54
  97.4 6.4 %all-to-all-start.2 = ((bf16[8,128,176]{1,2,0:T(8,128)(2,1)}), bf16[8,128,176]{1,2,0:T(8,128)(2,1)S(1)}, u32[]{:S(2)}, u32[]{:S(2)}) async-start(bf16[8,128,176]{1,2,0:T(8,128)(2,1)} %copy.54), calls=%async_computation.2 | async-start | bytes 720896 | tf_op jit(solution)/shard_map/all_to_all | solution.py:843
  103.7 2.0 collective-permute-start.13
  105.8 9.6 %all-to-all-done.2 = bf16[8,128,176]{1,2,0:T(8,128)(2,1)S(1)} async-done(((bf16[8,128,176]{1,2,0:T(8,128)(2,1)}), bf16[8,128,176]{1,2,0:T(8,128)(2,1)S(1)}, u32[]{:S(2)}, u32[]{:S(2)}) %all-to-all-start.2) | async-done | bytes 360480 | tf_op jit(solution)/shard_map/all_to_all | solution.py:843
  116.4 2.7 share.1
  119.9 2.4 collective-permute-done.14.refs_4_
  122.4 2.7 collective-permute-start.15
  125.0 3.0 collective-permute-done.15
  129.0 2.6 collective-permute-start.16
  131.6 2.9 collective-permute-done.16
  137.0 4.9 %collective-permute-done.17 = bf16[4,128,192]{2,1,0:T(8,128)(2,1)S(1)} collective-permute-done((bf16[4,128,192]{2,1,0:T(8,128)(2,1)S(1)}, bf16[4,128,192]{2,1,0:T(8,128)(2,1)S(1)}, u32[]{:S(2)}, u32[]{:S(2)}) %collective-permute-start.17) | collective-permute-done | bytes 196640 | tf_op jit(solution)/shard_map/ppermute | solution.py:818
  141.9 1.7 pad_maximum_fusion.1.shared_ref.refs_0_.refs_15_
  143.7 8.2 %gate.1.z_ref.refs_5_ = bf16[1024,512]{1,0:T(8,128)(2,1)} custom-call(s32[3]{0:T(128)} %pad_add_fusion.meta, bf16[128,2048]{1,0:T(8,128)(2,1)} %copy-done.2, bf16[128,2048]{1,0:T(8,128)(2,1)} %copy-done.6, bf16[128,2048]{1,0:T(8,128)(2,1)} %copy-done.7, bf16[128,2048]{1,0:T(8,128)(2,1)} %copy-done.8, bf16[128,2048]{1,0:T(8,128)(2,1)} %collective-permute-done.3.refs_4_, ...), custom_call_target="tpu_custom_call" | custom-call | tf_op jit(solution)/shard_map/gate/pallas_call | solution.py:178
  151.8 2.1 collective-permute-start.18
  155.7 16.6 %scan_forward.1 = (bf16[1024,512]{1,0:T(8,128)(2,1)}, f32[1024,512]{1,0:T(8,128)}, bf16[16384,512]{1,0:T(8,128)(2,1)}) custom-call(s32[3]{0:T(128)} %pad_add_fusion.meta, bf16[8,128,192]{2,1,0:T(8,128)(2,1)} %pad_maximum_fusion.1.shared_ref.refs_0_.refs_15_, bf16[1024,512]{1,0:T(8,128)(2,1)} %get-tuple-element.125.u_ref.refs_4_.refs_21_, ...), custom_call_target="tpu_custom_call" | custom-call | tf_op jit(solution)/shard_map/scan_forward/pallas_call | solution.py:379
  172.3 2.1 collective-permute-start.20
  174.5 4.3 %convolution_convert_fusion = bf16[1024,2048]{1,0:T(8,128)(2,1)S(1)} fusion(bf16[1024,512]{1,0:T(8,128)(2,1)} %get-tuple-element.130.refs_23_, bf16[512,2048]{1,0:T(8,128)(2,1)} %all-gather.5.cloned.1.call-done.refs_9_), kind=kOutput, calls=%fused_computation.1 | convolution fusion | flops 2149580800 | bytes 7340032 | tf_op jit(solution)/shard_map/dot_general | solution.py:28
  180.1 1.8 collective-permute-done.21.refs_8_
  184.0 11.3 %back_gate.1 = (bf16[1024,16]{1,0:T(8,128)(2,1)}, bf16[1024,256]{1,0:T(8,128)(2,1)}, bf16[1024,512]{1,0:T(8,128)(2,1)}) custom-call(s32[3]{0:T(128)} %pad_add_fusion.meta, bf16[128,2048]{1,0:T(8,128)(2,1)} %fusion.7.refs_0_, bf16[128,2048]{1,0:T(8,128)(2,1)} %collective-permute-done.11.refs_1_, bf16[128,2048]{1,0:T(8,128)(2,1)} %collective-permute-done.12.refs_2_, ...), custom_call_target="tpu_custom_call" | custom-call | tf_op jit(solution)/shard_map/back_gate/pallas_call | solution.py:221
  199.8 34.2 %scan_backward.1 = (bf16[1024,512]{1,0:T(8,128)(2,1)}, f32[1024,512]{1,0:T(8,128)}, bf16[1024,512]{1,0:T(8,128)(2,1)}, bf16[1024,192]{1,0:T(8,128)(2,1)}) custom-call(s32[3]{0:T(128)} %pad_add_fusion.meta, bf16[8,128,192]{2,1,0:T(8,128)(2,1)} %pad_maximum_fusion.1.shared_ref.refs_0_.refs_15_, bf16[128,512]{1,0:T(8,128)(2,1)} %refs_1_.1, ...), custom_call_target="tpu_custom_call" | custom-call | tf_op jit(solution)/shard_map/scan_backward/pallas_call | solution.py:509
  234.1 2.0 copy.57
  236.0 3.5 all-to-all-start.3
  241.2 2.1 collective-permute-start.26
  243.3 7.3 %all-to-all-done.3 = bf16[8,128,192]{1,2,0:T(8,128)(2,1)S(1)} async-done(((bf16[8,128,192]{1,2,0:T(8,128)(2,1)}), bf16[8,128,192]{1,2,0:T(8,128)(2,1)S(1)}, u32[]{:S(2)}, u32[]{:S(2)}) %all-to-all-start.3) | async-done | bytes 393248 | tf_op jit(solution)/shard_map/all_to_all | solution.py:843
  251.6 2.5 share_back.1
  255.0 3.1 collective-permute-start.28
  258.2 2.5 collective-permute-done.28
  261.5 3.3 collective-permute-start.29
  264.8 2.9 collective-permute-done.29
  270.1 7.8 %collective-permute-done.30 = bf16[4,128,192]{2,1,0:T(8,128)(2,1)S(1)} collective-permute-done((bf16[4,128,192]{2,1,0:T(8,128)(2,1)S(1)}, bf16[4,128,192]{2,1,0:T(8,128)(2,1)S(1)}, u32[]{:S(2)}, u32[]{:S(2)}) %collective-permute-start.30) | collective-permute-done | bytes 196640 | tf_op jit(solution)/shard_map/ppermute | solution.py:818
  281.2 2.0 collective-permute-start.32
  283.3 18.8 %finish.1 = (bf16[1024,2048]{1,0:T(8,128)(2,1)}, bf16[16,1792]{1,0:T(8,128)(2,1)}, bf16[16,2048]{1,0:T(8,128)(2,1)}, bf16[16,1536]{1,0:T(8,128)(2,1)}) custom-call(s32[3]{0:T(128)} %pad_add_fusion.meta, bf16[128,2048]{1,0:T(8,128)(2,1)} %copy-done.2, bf16[128,2048]{1,0:T(8,128)(2,1)} %copy-done.6, bf16[128,2048]{1,0:T(8,128)(2,1)} %copy-done.7, ...), custom_call_target="tpu_custom_call" | custom-call | tf_op jit(solution)/shard_map/finish/pallas_call | solution.py:644
  306.7 4.8 %collective-permute-done.33 = bf16[1,16,3840]{2,1,0:T(8,128)(2,1)S(1)} collective-permute-done((bf16[1,16,3840]{2,1,0:T(8,128)(2,1)S(1)}, bf16[1,16,3840]{2,1,0:T(8,128)(2,1)S(1)}, u32[]{:S(2)}, u32[]{:S(2)}) %collective-permute-start.33) | collective-permute-done | bytes 122912 | tf_op jit(solution)/shard_map/ppermute | solution.py:818
  312.6 2.3 collective-permute-done.35
  314.9 2.6 collective-permute-start.36
  318.9 2.0 collective-permute-start.38
  320.9 2.8 collective-permute-done.36
  323.8 9.3 %collective-permute-done.37 = bf16[128,2048]{1,0:T(8,128)(2,1)S(1)} collective-permute-done((bf16[128,2048]{1,0:T(8,128)(2,1)S(1)}, bf16[128,2048]{1,0:T(8,128)(2,1)S(1)}, u32[]{:S(2)}, u32[]{:S(2)}) %collective-permute-start.37) | collective-permute-done | bytes 524320 | tf_op jit(solution)/shard_map/ppermute | solution.py:754
  335.9 2.4 fusion.11
  338.2 3.7 collective-permute-done.39
  342.0 5.5 %collective-permute-done.40 = bf16[128,2048]{1,0:T(8,128)(2,1)S(1)} collective-permute-done((bf16[128,2048]{1,0:T(8,128)(2,1)S(1)}, bf16[128,2048]{1,0:T(8,128)(2,1)S(1)}, u32[]{:S(2)}, u32[]{:S(2)}) %collective-permute-start.40) | collective-permute-done | bytes 524320 | tf_op jit(solution)/shard_map/ppermute | solution.py:754
  350.7 1.8 collective-permute-start.42
  352.5 7.0 %all-gather.1 = bf16[64,3584]{1,0:T(8,128)(2,1)S(1)} all-gather(bf16[16,3584]{1,0:T(8,128)(2,1)S(1)} %pad_maximum_fusion.9), channel_id=3, replica_groups=mesh['seq'=8,'fsdp'=4] {'fsdp'}, dimensions={0}, use_global_device_ids=true | all-gather | bytes 573440 | tf_op jit(solution)/shard_map/all_gather | solution.py:947
  361.7 3.4 place_local.1
  366.9 2.6 fusion.6
  369.5 3.6 place.3
  373.1 2.3 place.4
  375.4 1.8 place.5
  (173 shorter events, 54.6 us)
Async XLA Ops:
  7.2 70.5 %copy-start.24 = (bf16[4,512]{1,0:T(4,128)(2,1)S(1)}, bf16[4,512]{1,0:T(4,128)(2,1)}, u32[]{:S(2)}) copy-start(bf16[4,512]{1,0:T(4,128)(2,1)} %param.30) | copy-start | bytes 12292
  7.2 71.1 %copy-start.25 = (bf16[512]{0:T(512)(128)(2,1)S(1)}, bf16[512]{0:T(512)(128)(2,1)}, u32[]{:S(2)}) copy-start(bf16[512]{0:T(512)(128)(2,1)} %param.31) | copy-start | bytes 3076
  10.4 69.1 %copy-start.2 = (bf16[128,2048]{1,0:T(8,128)(2,1)}, bf16[128,2048]{1,0:T(8,128)(2,1)S(1)}, u32[]{:S(2)}) copy-start(bf16[128,2048]{1,0:T(8,128)(2,1)S(1)} %fusion.2.refs_0_) | copy-start | bytes 1572868
  10.4 15.6 %collective-permute-start = (bf16[128,2048]{1,0:T(8,128)(2,1)S(1)}, bf16[128,2048]{1,0:T(8,128)(2,1)S(1)}, u32[]{:S(2)}, u32[]{:S(2)}) collective-permute-start(bf16[128,2048]{1,0:T(8,128)(2,1)S(1)} %fusion.2.refs_0_), channel_id=1, source_target_pairs={{0,8},{8,16},{16,24},{24,28},{28,20},{20,12},{12,4},{4,0},{1,9},{9... | collective-permute-start | bytes 1572872 | tf_op jit(solution)/shard_map/ppermute | solution.py:754
  13.5 15.8 %collective-permute-start.1 = (bf16[128,2048]{1,0:T(8,128)(2,1)S(1)}, bf16[128,2048]{1,0:T(8,128)(2,1)S(1)}, u32[]{:S(2)}, u32[]{:S(2)}) collective-permute-start(bf16[128,2048]{1,0:T(8,128)(2,1)S(1)} %fusion.2.refs_0_), channel_id=1, source_target_pairs={{0,4},{8,0},{16,8},{24,16},{28,24},{20,28},{12,20},{4,12},{1,5},{9... | collective-permute-start | bytes 1572872 | tf_op jit(solution)/shard_map/ppermute | solution.py:754
  15.3 25.3 %all-to-all-start = ((bf16[64,8,512]{2,0,1:T(8,128)(2,1)}), bf16[64,8,512]{2,0,1:T(8,128)(2,1)}, u32[]{:S(2)}, u32[]{:S(2)}) async-start(bf16[64,8,512]{2,0,1:T(8,128)(2,1)} %bitcast.62), calls=%async_computation | async-start | bytes 1048576 | tf_op jit(solution)/shard_map/all_to_all | solution.py:883
  26.0 53.5 %copy-start.6 = (bf16[128,2048]{1,0:T(8,128)(2,1)}, bf16[128,2048]{1,0:T(8,128)(2,1)S(1)}, u32[]{:S(2)}) copy-start(bf16[128,2048]{1,0:T(8,128)(2,1)S(1)} %collective-permute-done.refs_1_) | copy-start | bytes 1572868
  26.0 18.3 %collective-permute-start.2 = (bf16[128,2048]{1,0:T(8,128)(2,1)S(1)}, bf16[128,2048]{1,0:T(8,128)(2,1)S(1)}, u32[]{:S(2)}, u32[]{:S(2)}) collective-permute-start(bf16[128,2048]{1,0:T(8,128)(2,1)S(1)} %collective-permute-done.refs_1_), channel_id=1, source_target_pairs={{0,8},{8,16},{16,24},{24,28},{28,20},{20,12},{12,4},{4,0},{1,9},{9... | collective-permute-start | bytes 1572872 | tf_op jit(solution)/shard_map/ppermute | solution.py:754
  29.3 50.2 %copy-start.7 = (bf16[128,2048]{1,0:T(8,128)(2,1)}, bf16[128,2048]{1,0:T(8,128)(2,1)S(1)}, u32[]{:S(2)}) copy-start(bf16[128,2048]{1,0:T(8,128)(2,1)S(1)} %collective-permute-done.1.refs_2_) | copy-start | bytes 1572868
  29.3 19.4 %collective-permute-start.3 = (bf16[128,2048]{1,0:T(8,128)(2,1)S(1)}, bf16[128,2048]{1,0:T(8,128)(2,1)}, u32[]{:S(2)}, u32[]{:S(2)}) collective-permute-start(bf16[128,2048]{1,0:T(8,128)(2,1)S(1)} %collective-permute-done.1.refs_2_), channel_id=1, source_target_pairs={{0,4},{8,0},{16,8},{24,16},{28,24},{20,28},{12,20},{4,12},{1,5},{9... | collective-permute-start | bytes 1572872 | tf_op jit(solution)/shard_map/ppermute | solution.py:754
  40.7 10.1 %collective-permute-start.8 = (bf16[8,64,512]{2,1,0:T(8,128)(2,1)}, bf16[8,64,512]{2,1,0:T(8,128)(2,1)}, u32[]{:S(2)}, u32[]{:S(2)}) collective-permute-start(bf16[8,64,512]{2,1,0:T(8,128)(2,1)} %bitcast.5.refs_9_), channel_id=1, source_target_pairs={{0,2},{1,3},{2,0},{3,1},{4,6},{5,7},{6,4},{7,5},{8,10},{9,11},{10,... | collective-permute-start | bytes 1572872 | tf_op jit(solution)/shard_map/ppermute | solution.py:818
  44.3 35.2 %copy-start.8 = (bf16[128,2048]{1,0:T(8,128)(2,1)}, bf16[128,2048]{1,0:T(8,128)(2,1)S(1)}, u32[]{:S(2)}) copy-start(bf16[128,2048]{1,0:T(8,128)(2,1)S(1)} %collective-permute-done.2.refs_3_) | copy-start | bytes 1572868
  44.3 14.7 %collective-permute-start.4 = (bf16[128,2048]{1,0:T(8,128)(2,1)S(1)}, bf16[128,2048]{1,0:T(8,128)(2,1)S(1)}, u32[]{:S(2)}, u32[]{:S(2)}) collective-permute-start(bf16[128,2048]{1,0:T(8,128)(2,1)S(1)} %collective-permute-done.2.refs_3_), channel_id=1, source_target_pairs={{0,8},{8,16},{16,24},{24,28},{28,20},{20,12},{12,4},{4,0},{1,9},{9... | collective-permute-start | bytes 1572872 | tf_op jit(solution)/shard_map/ppermute | solution.py:754
  48.7 13.6 %collective-permute-start.5 = (bf16[128,2048]{1,0:T(8,128)(2,1)}, bf16[128,2048]{1,0:T(8,128)(2,1)S(1)}, u32[]{:S(2)}, u32[]{:S(2)}) collective-permute-start(bf16[128,2048]{1,0:T(8,128)(2,1)} %collective-permute-done.3.refs_4_), channel_id=1, source_target_pairs={{0,4},{8,0},{16,8},{24,16},{28,24},{20,28},{12,20},{4,12},{1,5},{9... | collective-permute-start | bytes 1572872 | tf_op jit(solution)/shard_map/ppermute | solution.py:754
  49.4 15.1 %collective-permute-start.9 = (bf16[8,64,512]{2,1,0:T(8,128)(2,1)}, bf16[8,64,512]{2,1,0:T(8,128)(2,1)S(1)}, u32[]{:S(2)}, u32[]{:S(2)}) collective-permute-start(bf16[8,64,512]{2,1,0:T(8,128)(2,1)} %bitcast.5.refs_9_), channel_id=1, source_target_pairs={{0,1},{1,0},{2,3},{3,2},{4,5},{5,4},{6,7},{7,6},{8,9},{9,8},{10,11... | collective-permute-start | bytes 1572872 | tf_op jit(solution)/shard_map/ppermute | solution.py:818
  50.8 18.0 %collective-permute-start.10 = (bf16[8,64,512]{2,1,0:T(8,128)(2,1)}, bf16[8,64,512]{2,1,0:T(8,128)(2,1)}, u32[]{:S(2)}, u32[]{:S(2)}) collective-permute-start(bf16[8,64,512]{2,1,0:T(8,128)(2,1)} %collective-permute-done.8.refs_10_), channel_id=1, source_target_pairs={{0,1},{1,0},{2,3},{3,2},{4,5},{5,4},{6,7},{7,6},{8,9},{9,8},{10,11... | collective-permute-start | bytes 1572872 | tf_op jit(solution)/shard_map/ppermute | solution.py:818
  59.0 8.2 %collective-permute-start.6 = (bf16[64,2048]{1,0:T(8,128)(2,1)S(1)}, bf16[64,2048]{1,0:T(8,128)(2,1)S(1)}, u32[]{:S(2)}, u32[]{:S(2)}) collective-permute-start(bf16[64,2048]{1,0:T(8,128)(2,1)S(1)} %slice.34), channel_id=1, source_target_pairs={{0,8},{8,16},{16,24},{24,28},{28,20},{20,12},{12,4},{4,0},{1,9},{9... | collective-permute-start | bytes 786440 | tf_op jit(solution)/shard_map/ppermute | solution.py:754
  62.3 6.5 %collective-permute-start.7 = (bf16[64,2048]{1,0:T(8,128)(2,1)S(1)}, bf16[64,2048]{1,0:T(8,128)(2,1)}, u32[]{:S(2)}, u32[]{:S(2)}) collective-permute-start(bf16[64,2048]{1,0:T(8,128)(2,1)S(1)} %slice.35), channel_id=1, source_target_pairs={{0,4},{8,0},{16,8},{24,16},{28,24},{20,28},{12,20},{4,12},{1,5},{9... | collective-permute-start | bytes 786440 | tf_op jit(solution)/shard_map/ppermute | solution.py:754
  70.7 23.9 %all-to-all-start.1 = ((bf16[64,8,512]{2,0,1:T(8,128)(2,1)}), bf16[64,8,512]{2,0,1:T(8,128)(2,1)}, u32[]{:S(2)}, u32[]{:S(2)}) async-start(bf16[64,8,512]{2,0,1:T(8,128)(2,1)} %bitcast.72), calls=%async_computation.1 | async-start | bytes 1048576 | tf_op jit(solution)/shard_map/all_to_all | solution.py:883
  74.9 68.8 %all-gather.7.cloned.1.call-start = ((), (), s32[]{:S(2)}) async-start(), calls=%async_computation.5 | async-start | bytes 2621440 | tf_op jit(solution)/shard_map/all_gather | solution.py:899
  74.9 18.8 %collective-permute-start.11 = (bf16[128,2048]{1,0:T(8,128)(2,1)}, bf16[128,2048]{1,0:T(8,128)(2,1)}, u32[]{:S(2)}, u32[]{:S(2)}) collective-permute-start(bf16[128,2048]{1,0:T(8,128)(2,1)} %fusion.7.refs_0_), channel_id=1, source_target_pairs={{0,8},{8,16},{16,24},{24,28},{28,20},{20,12},{12,4},{4,0},{1,9},{9... | collective-permute-start | bytes 1572872 | tf_op jit(solution)/shard_map/ppermute | solution.py:754
  76.8 17.8 %collective-permute-start.12 = (bf16[128,2048]{1,0:T(8,128)(2,1)}, bf16[128,2048]{1,0:T(8,128)(2,1)}, u32[]{:S(2)}, u32[]{:S(2)}) collective-permute-start(bf16[128,2048]{1,0:T(8,128)(2,1)} %fusion.7.refs_0_), channel_id=1, source_target_pairs={{0,4},{8,0},{16,8},{24,16},{28,24},{20,28},{12,20},{4,12},{1,5},{9... | collective-permute-start | bytes 1572872 | tf_op jit(solution)/shard_map/ppermute | solution.py:754
  94.6 79.9 %all-gather.5.cloned.1.call-start = ((), (), s32[]{:S(2)}) async-start(), calls=%async_computation.4 | async-start | bytes 2621440 | tf_op jit(solution)/shard_map/all_gather | solution.py:886
  97.4 18.0 %all-to-all-start.2 = ((bf16[8,128,176]{1,2,0:T(8,128)(2,1)}), bf16[8,128,176]{1,2,0:T(8,128)(2,1)S(1)}, u32[]{:S(2)}, u32[]{:S(2)}) async-start(bf16[8,128,176]{1,2,0:T(8,128)(2,1)} %copy.54), calls=%async_computation.2 | async-start | bytes 720896 | tf_op jit(solution)/shard_map/all_to_all | solution.py:843
  103.7 16.2 %collective-permute-start.13 = (bf16[128,2048]{1,0:T(8,128)(2,1)}, bf16[128,2048]{1,0:T(8,128)(2,1)S(1)}, u32[]{:S(2)}, u32[]{:S(2)}) collective-permute-start(bf16[128,2048]{1,0:T(8,128)(2,1)} %collective-permute-done.11.refs_1_), channel_id=1, source_target_pairs={{0,8},{8,16},{16,24},{24,28},{28,20},{20,12},{12,4},{4,0},{1,9},{9... | collective-permute-start | bytes 1572872 | tf_op jit(solution)/shard_map/ppermute | solution.py:754
  105.8 16.6 %collective-permute-start.14 = (bf16[128,2048]{1,0:T(8,128)(2,1)}, bf16[128,2048]{1,0:T(8,128)(2,1)S(1)}, u32[]{:S(2)}, u32[]{:S(2)}) collective-permute-start(bf16[128,2048]{1,0:T(8,128)(2,1)} %collective-permute-done.12.refs_2_), channel_id=1, source_target_pairs={{0,4},{8,0},{16,8},{24,16},{28,24},{20,28},{12,20},{4,12},{1,5},{9... | collective-permute-start | bytes 1572872 | tf_op jit(solution)/shard_map/ppermute | solution.py:754
  119.9 31.9 %copy-start.18 = (bf16[128,2048]{1,0:T(8,128)(2,1)}, bf16[128,2048]{1,0:T(8,128)(2,1)S(1)}, u32[]{:S(2)}) copy-start(bf16[128,2048]{1,0:T(8,128)(2,1)S(1)} %collective-permute-done.13.refs_3_) | copy-start | bytes 1572868
  122.4 31.5 %copy-start.19 = (bf16[128,2048]{1,0:T(8,128)(2,1)}, bf16[128,2048]{1,0:T(8,128)(2,1)S(1)}, u32[]{:S(2)}) copy-start(bf16[128,2048]{1,0:T(8,128)(2,1)S(1)} %collective-permute-done.14.refs_4_) | copy-start | bytes 1572868
  122.4 5.7 %collective-permute-start.15 = (bf16[1,128,192]{2,1,0:T(8,128)(2,1)}, bf16[1,128,192]{2,1,0:T(8,128)(2,1)S(1)}, u32[]{:S(2)}, u32[]{:S(2)}) collective-permute-start(bf16[1,128,192]{2,1,0:T(8,128)(2,1)} %bitcast.80), channel_id=1, source_target_pairs={{0,16},{4,20},{8,24},{12,28},{16,0},{20,4},{24,8},{28,12},{1,17},{... | collective-permute-start | bytes 147464 | tf_op jit(solution)/shard_map/ppermute | solution.py:818
  129.0 5.6 %collective-permute-start.16 = (bf16[2,128,192]{2,1,0:T(8,128)(2,1)S(1)}, bf16[2,128,192]{2,1,0:T(8,128)(2,1)S(1)}, u32[]{:S(2)}, u32[]{:S(2)}) collective-permute-start(bf16[2,128,192]{2,1,0:T(8,128)(2,1)S(1)} %pad_maximum_fusion.7), channel_id=1, source_target_pairs={{0,8},{4,12},{8,0},{12,4},{16,24},{20,28},{24,16},{28,20},{1,9},{5... | collective-permute-start | bytes 294920 | tf_op jit(solution)/shard_map/ppermute | solution.py:818
  135.5 6.4 %collective-permute-start.17 = (bf16[4,128,192]{2,1,0:T(8,128)(2,1)S(1)}, bf16[4,128,192]{2,1,0:T(8,128)(2,1)S(1)}, u32[]{:S(2)}, u32[]{:S(2)}) collective-permute-start(bf16[4,128,192]{2,1,0:T(8,128)(2,1)S(1)} %pad_maximum_fusion.4), channel_id=1, source_target_pairs={{0,4},{4,0},{8,12},{12,8},{16,20},{20,16},{24,28},{28,24},{1,5},{5... | collective-permute-start | bytes 589832 | tf_op jit(solution)/shard_map/ppermute | solution.py:818
  151.8 20.5 %collective-permute-start.18 = (bf16[128,2048]{1,0:T(8,128)(2,1)S(1)}, bf16[128,2048]{1,0:T(8,128)(2,1)S(1)}, u32[]{:S(2)}, u32[]{:S(2)}) collective-permute-start(bf16[128,2048]{1,0:T(8,128)(2,1)S(1)} %collective-permute-done.13.refs_3_), channel_id=1, source_target_pairs={{0,8},{8,16},{16,24},{24,28},{28,20},{20,12},{12,4},{4,0},{1,9},{9... | collective-permute-start | bytes 1572872 | tf_op jit(solution)/shard_map/ppermute | solution.py:754
  153.9 18.4 %collective-permute-start.19 = (bf16[128,2048]{1,0:T(8,128)(2,1)S(1)}, bf16[128,2048]{1,0:T(8,128)(2,1)S(1)}, u32[]{:S(2)}, u32[]{:S(2)}) collective-permute-start(bf16[128,2048]{1,0:T(8,128)(2,1)S(1)} %collective-permute-done.14.refs_4_), channel_id=1, source_target_pairs={{0,4},{8,0},{16,8},{24,16},{28,24},{20,28},{12,20},{4,12},{1,5},{9... | collective-permute-start | bytes 1572872 | tf_op jit(solution)/shard_map/ppermute | solution.py:754
  172.3 7.7 %collective-permute-start.20 = (bf16[64,2048]{1,0:T(8,128)(2,1)S(1)}, bf16[64,2048]{1,0:T(8,128)(2,1)S(1)}, u32[]{:S(2)}, u32[]{:S(2)}) collective-permute-start(bf16[64,2048]{1,0:T(8,128)(2,1)S(1)} %slice.26), channel_id=1, source_target_pairs={{0,8},{8,16},{16,24},{24,28},{28,20},{20,12},{12,4},{4,0},{1,9},{9... | collective-permute-start | bytes 786440 | tf_op jit(solution)/shard_map/ppermute | solution.py:754
  174.4 7.4 %collective-permute-start.21 = (bf16[64,2048]{1,0:T(8,128)(2,1)S(1)}, bf16[64,2048]{1,0:T(8,128)(2,1)S(1)}, u32[]{:S(2)}, u32[]{:S(2)}) collective-permute-start(bf16[64,2048]{1,0:T(8,128)(2,1)S(1)} %slice.27), channel_id=1, source_target_pairs={{0,4},{8,0},{16,8},{24,16},{28,24},{20,28},{12,20},{4,12},{1,5},{9... | collective-permute-start | bytes 786440 | tf_op jit(solution)/shard_map/ppermute | solution.py:754
  181.9 13.4 %collective-permute-start.22 = (bf16[64,2048]{1,0:T(8,128)(2,1)S(1)}, bf16[64,2048]{1,0:T(8,128)(2,1)S(1)}, u32[]{:S(2)}, u32[]{:S(2)}) collective-permute-start(bf16[64,2048]{1,0:T(8,128)(2,1)S(1)} %get-tuple-element.205), channel_id=1, source_target_pairs={{0,8},{8,16},{16,24},{24,28},{28,20},{20,12},{12,4},{4,0},{1,9},{9... | collective-permute-start | bytes 786440 | tf_op jit(solution)/shard_map/ppermute | solution.py:754
  182.9 12.4 %collective-permute-start.23 = (bf16[64,2048]{1,0:T(8,128)(2,1)S(1)}, bf16[64,2048]{1,0:T(8,128)(2,1)S(1)}, u32[]{:S(2)}, u32[]{:S(2)}) collective-permute-start(bf16[64,2048]{1,0:T(8,128)(2,1)S(1)} %get-tuple-element.204), channel_id=1, source_target_pairs={{0,4},{8,0},{16,8},{24,16},{28,24},{20,28},{12,20},{4,12},{1,5},{9... | collective-permute-start | bytes 786440 | tf_op jit(solution)/shard_map/ppermute | solution.py:754
  196.7 37.3 %collective-permute-start.24 = (bf16[128,2048]{1,0:T(8,128)(2,1)S(1)}, bf16[128,2048]{1,0:T(8,128)(2,1)S(1)}, u32[]{:S(2)}, u32[]{:S(2)}) collective-permute-start(bf16[128,2048]{1,0:T(8,128)(2,1)S(1)} %get-tuple-element.203), channel_id=1, source_target_pairs={{0,8},{8,16},{16,24},{24,28},{28,20},{20,12},{12,4},{4,0},{1,9},{9... | collective-permute-start | bytes 1572872 | tf_op jit(solution)/shard_map/ppermute | solution.py:754
  197.7 36.4 %collective-permute-start.25 = (bf16[128,2048]{1,0:T(8,128)(2,1)S(1)}, bf16[128,2048]{1,0:T(8,128)(2,1)S(1)}, u32[]{:S(2)}, u32[]{:S(2)}) collective-permute-start(bf16[128,2048]{1,0:T(8,128)(2,1)S(1)} %get-tuple-element.202), channel_id=1, source_target_pairs={{0,4},{8,0},{16,8},{24,16},{28,24},{20,28},{12,20},{4,12},{1,5},{9... | collective-permute-start | bytes 1572872 | tf_op jit(solution)/shard_map/ppermute | solution.py:754
  236.0 14.6 %all-to-all-start.3 = ((bf16[8,128,192]{1,2,0:T(8,128)(2,1)}), bf16[8,128,192]{1,2,0:T(8,128)(2,1)S(1)}, u32[]{:S(2)}, u32[]{:S(2)}) async-start(bf16[8,128,192]{1,2,0:T(8,128)(2,1)} %copy.57), calls=%async_computation.3 | async-start | bytes 786432 | tf_op jit(solution)/shard_map/all_to_all | solution.py:843
  239.6 43.7 %copy-start.28 = (s32[4]{0:T(128)S(1)}, s32[4]{0:T(128)}, u32[]{:S(2)}) copy-start(s32[4]{0:T(128)} %constant.92.clone) | copy-start | bytes 52
  241.2 13.0 %collective-permute-start.26 = (bf16[128,2048]{1,0:T(8,128)(2,1)S(1)}, bf16[128,2048]{1,0:T(8,128)(2,1)S(1)}, u32[]{:S(2)}, u32[]{:S(2)}) collective-permute-start(bf16[128,2048]{1,0:T(8,128)(2,1)S(1)} %get-tuple-element.201), channel_id=1, source_target_pairs={{0,8},{8,16},{16,24},{24,28},{28,20},{20,12},{12,4},{4,0},{1,9},{9... | collective-permute-start | bytes 1572872 | tf_op jit(solution)/shard_map/ppermute | solution.py:754
  243.3 11.8 %collective-permute-start.27 = (bf16[128,2048]{1,0:T(8,128)(2,1)S(1)}, bf16[128,2048]{1,0:T(8,128)(2,1)S(1)}, u32[]{:S(2)}, u32[]{:S(2)}) collective-permute-start(bf16[128,2048]{1,0:T(8,128)(2,1)S(1)} %get-tuple-element.200), channel_id=1, source_target_pairs={{0,4},{8,0},{16,8},{24,16},{28,24},{20,28},{12,20},{4,12},{1,5},{9... | collective-permute-start | bytes 1572872 | tf_op jit(solution)/shard_map/ppermute | solution.py:754
  255.0 5.6 %collective-permute-start.28 = (bf16[1,128,192]{2,1,0:T(8,128)(2,1)}, bf16[1,128,192]{2,1,0:T(8,128)(2,1)S(1)}, u32[]{:S(2)}, u32[]{:S(2)}) collective-permute-start(bf16[1,128,192]{2,1,0:T(8,128)(2,1)} %bitcast.75), channel_id=1, source_target_pairs={{0,16},{4,20},{8,24},{12,28},{16,0},{20,4},{24,8},{28,12},{1,17},{... | collective-permute-start | bytes 147464 | tf_op jit(solution)/shard_map/ppermute | solution.py:818
  261.5 6.3 %collective-permute-start.29 = (bf16[2,128,192]{2,1,0:T(8,128)(2,1)S(1)}, bf16[2,128,192]{2,1,0:T(8,128)(2,1)S(1)}, u32[]{:S(2)}, u32[]{:S(2)}) collective-permute-start(bf16[2,128,192]{2,1,0:T(8,128)(2,1)S(1)} %pad_maximum_fusion.8), channel_id=1, source_target_pairs={{0,8},{4,12},{8,0},{12,4},{16,24},{20,28},{24,16},{28,20},{1,9},{5... | collective-permute-start | bytes 294920 | tf_op jit(solution)/shard_map/ppermute | solution.py:818
  268.7 9.2 %collective-permute-start.30 = (bf16[4,128,192]{2,1,0:T(8,128)(2,1)S(1)}, bf16[4,128,192]{2,1,0:T(8,128)(2,1)S(1)}, u32[]{:S(2)}, u32[]{:S(2)}) collective-permute-start(bf16[4,128,192]{2,1,0:T(8,128)(2,1)S(1)} %pad_maximum_fusion.5), channel_id=1, source_target_pairs={{0,4},{4,0},{8,12},{12,8},{16,20},{20,16},{24,28},{28,24},{1,5},{5... | collective-permute-start | bytes 589832 | tf_op jit(solution)/shard_map/ppermute | solution.py:818
  281.2 20.9 %collective-permute-start.31 = (bf16[128,2048]{1,0:T(8,128)(2,1)S(1)}, bf16[128,2048]{1,0:T(8,128)(2,1)S(1)}, u32[]{:S(2)}, u32[]{:S(2)}) collective-permute-start(bf16[128,2048]{1,0:T(8,128)(2,1)S(1)} %get-tuple-element.199), channel_id=1, source_target_pairs={{0,8},{8,16},{16,24},{24,28},{28,20},{20,12},{12,4},{4,0},{1,9},{9... | collective-permute-start | bytes 1572872 | tf_op jit(solution)/shard_map/ppermute | solution.py:754
  281.2 20.8 %collective-permute-start.32 = (bf16[128,2048]{1,0:T(8,128)(2,1)S(1)}, bf16[128,2048]{1,0:T(8,128)(2,1)S(1)}, u32[]{:S(2)}, u32[]{:S(2)}) collective-permute-start(bf16[128,2048]{1,0:T(8,128)(2,1)S(1)} %get-tuple-element.198), channel_id=1, source_target_pairs={{0,4},{8,0},{16,8},{24,16},{28,24},{20,28},{12,20},{4,12},{1,5},{9... | collective-permute-start | bytes 1572872 | tf_op jit(solution)/shard_map/ppermute | solution.py:754
  303.1 32.8 %copy-start.1 = (bf16[1,128,2048]{2,1,0:T(8,128)(2,1)S(1)}, bf16[1,128,2048]{2,1,0:T(8,128)(2,1)}, u32[]{:S(2)}) copy-start(bf16[1,128,2048]{2,1,0:T(8,128)(2,1)} %param.24) | copy-start | bytes 1572868
  303.1 32.8 %copy-start.15 = (bf16[128,192]{1,0:T(8,128)(2,1)S(1)}, bf16[128,192]{1,0:T(8,128)(2,1)}, u32[]{:S(2)}) copy-start(bf16[128,192]{1,0:T(8,128)(2,1)} %share_back.1) | copy-start | bytes 147460
  303.1 8.3 %collective-permute-start.33 = (bf16[1,16,3840]{2,1,0:T(8,128)(2,1)S(1)}, bf16[1,16,3840]{2,1,0:T(8,128)(2,1)S(1)}, u32[]{:S(2)}, u32[]{:S(2)}) collective-permute-start(bf16[1,16,3840]{2,1,0:T(8,128)(2,1)S(1)} %maximum_bitcast_fusion), channel_id=1, source_target_pairs={{0,16},{4,20},{8,24},{12,28},{16,0},{20,4},{24,8},{28,12},{1,17},{... | collective-permute-start | bytes 368648 | tf_op jit(solution)/shard_map/ppermute | solution.py:818
  304.6 8.0 %collective-permute-start.34 = (bf16[64,2048]{1,0:T(8,128)(2,1)S(1)}, bf16[64,2048]{1,0:T(8,128)(2,1)S(1)}, u32[]{:S(2)}, u32[]{:S(2)}) collective-permute-start(bf16[64,2048]{1,0:T(8,128)(2,1)S(1)} %get-tuple-element.197), channel_id=1, source_target_pairs={{0,8},{8,16},{16,24},{24,28},{28,20},{20,12},{12,4},{4,0},{1,9},{9... | collective-permute-start | bytes 786440 | tf_op jit(solution)/shard_map/ppermute | solution.py:754
  305.2 9.7 %collective-permute-start.35 = (bf16[64,2048]{1,0:T(8,128)(2,1)S(1)}, bf16[64,2048]{1,0:T(8,128)(2,1)S(1)}, u32[]{:S(2)}, u32[]{:S(2)}) collective-permute-start(bf16[64,2048]{1,0:T(8,128)(2,1)S(1)} %get-tuple-element.196), channel_id=1, source_target_pairs={{0,4},{8,0},{16,8},{24,16},{28,24},{20,28},{12,20},{4,12},{1,5},{9... | collective-permute-start | bytes 786440 | tf_op jit(solution)/shard_map/ppermute | solution.py:754
  314.9 8.8 %collective-permute-start.36 = (bf16[2,16,3840]{2,1,0:T(8,128)(2,1)S(1)}, bf16[2,16,3840]{2,1,0:T(8,128)(2,1)S(1)}, u32[]{:S(2)}, u32[]{:S(2)}) collective-permute-start(bf16[2,16,3840]{2,1,0:T(8,128)(2,1)S(1)} %pad_maximum_fusion.6), channel_id=1, source_target_pairs={{0,8},{4,12},{8,0},{12,4},{16,24},{20,28},{24,16},{28,20},{1,9},{5... | collective-permute-start | bytes 737288 | tf_op jit(solution)/shard_map/ppermute | solution.py:818
  318.8 14.2 %collective-permute-start.37 = (bf16[128,2048]{1,0:T(8,128)(2,1)S(1)}, bf16[128,2048]{1,0:T(8,128)(2,1)S(1)}, u32[]{:S(2)}, u32[]{:S(2)}) collective-permute-start(bf16[128,2048]{1,0:T(8,128)(2,1)S(1)} %get-tuple-element.195), channel_id=1, source_target_pairs={{0,8},{8,16},{16,24},{24,28},{28,20},{20,12},{12,4},{4,0},{1,9},{9... | collective-permute-start | bytes 1572872 | tf_op jit(solution)/shard_map/ppermute | solution.py:754
  318.9 14.2 %collective-permute-start.38 = (bf16[128,2048]{1,0:T(8,128)(2,1)S(1)}, bf16[128,2048]{1,0:T(8,128)(2,1)S(1)}, u32[]{:S(2)}, u32[]{:S(2)}) collective-permute-start(bf16[128,2048]{1,0:T(8,128)(2,1)S(1)} %get-tuple-element.194), channel_id=1, source_target_pairs={{0,4},{8,0},{16,8},{24,16},{28,24},{20,28},{12,20},{4,12},{1,5},{9... | collective-permute-start | bytes 1572872 | tf_op jit(solution)/shard_map/ppermute | solution.py:754
  333.1 8.8 %collective-permute-start.39 = (bf16[4,16,3840]{2,1,0:T(8,128)(2,1)S(1)}, bf16[4,16,3840]{2,1,0:T(8,128)(2,1)S(1)}, u32[]{:S(2)}, u32[]{:S(2)}) collective-permute-start(bf16[4,16,3840]{2,1,0:T(8,128)(2,1)S(1)} %pad_maximum_fusion.3), channel_id=1, source_target_pairs={{0,4},{4,0},{8,12},{12,8},{16,20},{20,16},{24,28},{28,24},{1,5},{5... | collective-permute-start | bytes 1474568 | tf_op jit(solution)/shard_map/ppermute | solution.py:818
  333.8 13.8 %collective-permute-start.40 = (bf16[128,2048]{1,0:T(8,128)(2,1)S(1)}, bf16[128,2048]{1,0:T(8,128)(2,1)S(1)}, u32[]{:S(2)}, u32[]{:S(2)}) collective-permute-start(bf16[128,2048]{1,0:T(8,128)(2,1)S(1)} %get-tuple-element.193), channel_id=1, source_target_pairs={{0,8},{8,16},{16,24},{24,28},{28,20},{20,12},{12,4},{4,0},{1,9},{9... | collective-permute-start | bytes 1572872 | tf_op jit(solution)/shard_map/ppermute | solution.py:754
  335.2 12.3 %collective-permute-start.41 = (bf16[128,2048]{1,0:T(8,128)(2,1)S(1)}, bf16[128,2048]{1,0:T(8,128)(2,1)S(1)}, u32[]{:S(2)}, u32[]{:S(2)}) collective-permute-start(bf16[128,2048]{1,0:T(8,128)(2,1)S(1)} %get-tuple-element.192), channel_id=1, source_target_pairs={{0,4},{8,0},{16,8},{24,16},{28,24},{20,28},{12,20},{4,12},{1,5},{9... | collective-permute-start | bytes 1572872 | tf_op jit(solution)/shard_map/ppermute | solution.py:754
  347.7 17.4 %collective-permute-start.44 = (bf16[8,16,1792]{2,1,0:T(8,128)(2,1)S(1)}, bf16[8,16,1792]{2,1,0:T(8,128)(2,1)S(1)}, u32[]{:S(2)}, u32[]{:S(2)}) collective-permute-start(bf16[8,16,1792]{2,1,0:T(8,128)(2,1)S(1)} %slice.31.refs_0_), channel_id=1, source_target_pairs={{0,2},{1,3},{2,0},{3,1},{4,6},{5,7},{6,4},{7,5},{8,10},{9,11},{10,... | collective-permute-start | bytes 1376264 | tf_op jit(solution)/shard_map/ppermute | solution.py:818
  349.0 20.5 %collective-permute-start.45 = (bf16[8,16,1792]{2,1,0:T(8,128)(2,1)S(1)}, bf16[8,16,1792]{2,1,0:T(8,128)(2,1)S(1)}, u32[]{:S(2)}, u32[]{:S(2)}) collective-permute-start(bf16[8,16,1792]{2,1,0:T(8,128)(2,1)S(1)} %slice.31.refs_0_), channel_id=1, source_target_pairs={{0,1},{1,0},{2,3},{3,2},{4,5},{5,4},{6,7},{7,6},{8,9},{9,8},{10,11... | collective-permute-start | bytes 1376264 | tf_op jit(solution)/shard_map/ppermute | solution.py:818
  350.5 15.0 %collective-permute-start.43 = (bf16[128,2048]{1,0:T(8,128)(2,1)}, bf16[128,2048]{1,0:T(8,128)(2,1)S(1)}, u32[]{:S(2)}, u32[]{:S(2)}) collective-permute-start(bf16[128,2048]{1,0:T(8,128)(2,1)} %get-tuple-element.191), channel_id=1, source_target_pairs={{0,4},{8,0},{16,8},{24,16},{28,24},{20,28},{12,20},{4,12},{1,5},{9... | collective-permute-start | bytes 1572872 | tf_op jit(solution)/shard_map/ppermute | solution.py:754
  350.7 14.7 %collective-permute-start.42 = (bf16[128,2048]{1,0:T(8,128)(2,1)}, bf16[128,2048]{1,0:T(8,128)(2,1)S(1)}, u32[]{:S(2)}, u32[]{:S(2)}) collective-permute-start(bf16[128,2048]{1,0:T(8,128)(2,1)} %get-tuple-element.190), channel_id=1, source_target_pairs={{0,8},{8,16},{16,24},{24,28},{28,20},{20,12},{12,4},{4,0},{1,9},{9... | collective-permute-start | bytes 1572872 | tf_op jit(solution)/shard_map/ppermute | solution.py:754
  365.1 4.4 %collective-permute-start.46 = (bf16[8,16,1792]{2,1,0:T(8,128)(2,1)S(1)}, bf16[8,16,1792]{2,1,0:T(8,128)(2,1)S(1)}, u32[]{:S(2)}, u32[]{:S(2)}) collective-permute-start(bf16[8,16,1792]{2,1,0:T(8,128)(2,1)S(1)} %collective-permute-done.44.refs_1_), channel_id=1, source_target_pairs={{0,1},{1,0},{2,3},{3,2},{4,5},{5,4},{6,7},{7,6},{8,9},{9,8},{10,11... | collective-permute-start | bytes 1376264 | tf_op jit(solution)/shard_map/ppermute | solution.py:818
  (18 other events, 194.3 us)
Sparse Core Ops, SparseCore 0:
  94.7 24.3 all-gather.6
  120.7 22.5 all-gather.4

commit v3 on v2

--- a/solution.py
+++ b/solution.py
@@ -137,9 +137,10 @@
     conv_out = jax.nn.silu(conv_before(x_f, before[...], weight_ref, bias_ref)).astype(BF16)
     before[...] = x_f[-8:]
     conv_ref[...] = conv_out
-    cut = proj_ref.shape[0]
-    sums_ref[:, :cut] = nt(conv_out, proj_ref[...]).astype(BF16)
-    sums_ref[:, cut:] = nt(conv_out, down_ref[0]).astype(BF16)
+    sums = jnp.concatenate([nt(proj_ref[...], conv_out), nt(down_ref[0], conv_out)], 0).astype(BF16)
+    tokens = sums_ref.shape[2]
+    for j in range(sums_ref.shape[0]):
+        sums_ref[j] = sums[:, j * tokens : (j + 1) * tokens]
 
 
 def once(array):
@@ -238,23 +239,27 @@
     tokens, width = pieces[0].shape
     length, chans, rank = tokens * parts, columns[0].shape[-1], in_down.shape[1]
     cols = proj.shape[0] + rank
-    seq = lambda size: pl.BlockSpec((AT_ONCE * tokens, size), lambda i, meta: (i, 0))
+    once_rows = AT_ONCE // 2
+    seq = lambda size: pl.BlockSpec((once_rows * tokens, size), lambda i, meta: (i, 0))
     rows = columns[0].shape[1]
     whole_shape = (parts, groups, rows, chans)
     return pl.pallas_call(
         functools.partial(project_kernel, parts=parts, groups=groups),
         grid_spec=pltpu.PrefetchScalarGridSpec(
             num_scalar_prefetch=1,
-            grid=(parts // AT_ONCE,),
+            grid=(parts // once_rows,),
             in_specs=[pl.BlockSpec(memory_space=pl.ANY)] * (len(pieces) + groups)
             + [chosen(in_down), chosen(up, 0, chans), once(weight), once(bias), once(proj), chosen(down)],
-            out_specs=[seq(rank), seq(chans), seq(chans), seq(cols)],
+            out_specs=[
+                seq(rank), seq(chans), seq(chans), pl.BlockSpec((once_rows, cols, tokens), lambda i, meta: (i, 0, 0))
+            ],
             scratch_shapes=[
                 pltpu.VMEM((8, chans), F32), pltpu.VMEM((length, width), BF16), pltpu.VMEM(whole_shape, BF16),
                 pltpu.SemaphoreType.DMA((len(pieces),)), pltpu.SemaphoreType.DMA((groups,)),
             ],
         ),
-        out_shape=[jax.ShapeDtypeStruct((length, size), BF16) for size in (rank, chans, chans, cols)],
+        out_shape=[jax.ShapeDtypeStruct((length, size), BF16) for size in (rank, chans, chans)]
+        + [jax.ShapeDtypeStruct((parts, cols, tokens), BF16)],
         compiler_params=pltpu.CompilerParams(vmem_limit_bytes=LIMIT),
         name="project",
     )(meta, *pieces, *columns, in_down, up, weight, bias, proj, down)
@@ -264,6 +269,7 @@
     sums = got_ref[0].astype(F32)
     for i in range(1, got_ref.shape[0]):
         sums = sums + got_ref[i].astype(F32)
+    sums = sums.T
     cut = ranks + 2 * states
     low_state = sums[:, cut:].astype(BF16)
     mixed = sums[:, :cut] + nn(low_state, state_up_ref[0])
@@ -273,7 +279,7 @@
 
 
 def share(meta, got, state_up, step_down, ranks, states):
-    tokens, rank = got.shape[1], step_down.shape[1]
+    tokens, rank = got.shape[2], step_down.shape[1]
     cols = ranks + 2 * rank + 2 * states
     return pl.pallas_call(
         functools.partial(share_kernel, ranks=ranks, states=states),
@@ -292,6 +298,7 @@
     sums = got_ref[0].astype(F32)
     for i in range(1, got_ref.shape[0]):
         sums = sums + got_ref[i].astype(F32)
+    sums = sums.T
     rank = step_down_ref.shape[1]
     mid, end = ranks + rank, ranks + rank + 2 * states
     back_mid = sums[:, ranks:mid]
@@ -301,7 +308,7 @@
 
 
 def share_back(meta, got, step_down, ranks, states):
-    tokens, cols = got.shape[1:]
+    cols, tokens = got.shape[1:]
     return pl.pallas_call(
         functools.partial(share_back_kernel, ranks=ranks, states=states),
         grid_spec=pltpu.PrefetchScalarGridSpec(
@@ -321,211 +328,171 @@
         ref[k] = turned[:, k * sub : (k + 1) * sub]
 
 
-def scan_forward_kernel(
-    meta, shared_ref, u_ref, z_ref, step_proj_ref, step_up_ref, bias_ref, rate_ref, skip_ref,
-    gated_ref, scanned_ref, states_ref,
-    carry, delta_s, du_s, cm_s, y_s, bt_s, held_a, held_b, *, sub, ranks,
+def scan_kernel(
+    meta, shared_ref, u_ref, z_ref, bg_ref, step_proj_ref, step_up_ref, bias_ref, rate_ref, decay_ref, skip_ref, down_ref,
+    gated_ref, pre_ref, conv_ref, bz_ref, mixed_ref,
+    carry, states_s, pre_s, delta_s, du_s, scanned_s, bs_s, wide_s, w_s, bd_s, bb_s, bc_s, turned_s, held_a, held_b,
+    q_a, q_b, *, sub, ranks,
 ):
-    rows = u_ref.shape[0]
-    states = rate_ref.shape[0]
-    rank = step_up_ref.shape[1]
-
-    @pl.when(pl.program_id(0) == 0)
-    def _():
-        carry[...] = jnp.zeros_like(carry)
-        held_b[...] = jnp.zeros_like(held_b)
-        cm_s[:sub, :] = jnp.zeros((sub, sub * states), BF16)
-
-    shared = shared_ref[0]
-    step_mid = shared[:, ranks : ranks + rank]
-    pre = nn(shared[:, :ranks], step_proj_ref[...]) + nn(step_mid, step_up_ref[0]) + bias_ref[...]
-    delta = softplus(pre)
-    delta_s[...] = delta
-    du_s[...] = delta * u_ref[...].astype(F32)
+    rows, chans = u_ref.shape
+    parts, tokens = shared_ref.shape[:2]
+    per = rows // tokens
+    states, rank = rate_ref.shape[0], step_up_ref.shape[1]
+    step = pl.program_id(0)
+    blocks = pl.num_programs(0) // 2
+    block = jnp.where(step < blocks, step, 2 * blocks - 1 - step)
+    origin = pl.multiple_of(block * rows, rows)
+    here = pl.ds(origin, rows)
+    shared = jnp.concatenate(
+        [shared_ref[place_of_block(block * per + j, meta[1], parts)] for j in range(per)], 0
+    )
     b_rows = shared[:, ranks + rank : ranks + rank + states]
     c_rows = shared[:, ranks + rank + states : ranks + rank + 2 * states]
-    columns_of_groups(b_rows, bt_s, sub)
-    cm = nn(c_rows, spread_matrix(states, sub)) * own_step_mask(rows, states, sub)
-    cm_s[sub:, :] = cm.astype(BF16)
     rate = rate_ref[...]
-
-    def pair(k, s):
-        for turn, (mine, other) in enumerate(((held_a, held_b), (held_b, held_a))):
-            base = pl.multiple_of(k * (2 * sub) + turn * sub, sub)
-            y_s[pl.ds(base, sub), :] = nn(cm_s[pl.ds(base, sub), :], other[...])
-            bt = bt_s[k * 2 + turn]
-            for t in range(sub):
-                dl = delta_s[pl.ds(base + t, 1), :]
-                du = du_s[pl.ds(base + t, 1), :]
-                s = jnp.exp2(dl * rate) * s + du * bt[:, t : t + 1]
-                low = s.astype(BF16)
-                mine[t * states : (t + 1) * states, :] = low
-                states_ref[pl.ds(pl.multiple_of((base + t) * states, states), states), :] = low
-        return s
-
-    carry[...] = lax.fori_loop(0, rows // (2 * sub), pair, carry[...])
-    y_s[rows:, :] = nn(cm_s[rows:, :], held_b[...])
-    scanned = y_s[sub:, :] + skip_ref[...] * u_ref[...].astype(F32)
-    scanned_ref[...] = scanned
-    gated_ref[...] = (scanned * jax.nn.silu(z_ref[...].astype(F32))).astype(BF16)
-
-
-def scan_forward(meta, shared, u, z, step_proj, step_up, bias, rate, skip, parts, sub):
+    pairs = rows // (2 * sub)
+
+    @pl.when(step < blocks)
+    def _():
+        @pl.when(step == 0)
+        def _():
+            carry[...] = jnp.zeros_like(carry)
+            held_b[...] = jnp.zeros_like(held_b)
+            states_s[:states, :] = jnp.zeros((states, chans), BF16)
+            wide_s[:sub, :] = jnp.zeros((sub, sub * states), BF16)
+
+        pre = nn(shared[:, :ranks], step_proj_ref[...]) + nn(shared[:, ranks : ranks + rank], step_up_ref[0]) + bias_ref[...]
+        delta = softplus(pre)
+        pre_s[here, :] = pre
+        delta_s[here, :] = delta
+        du_s[here, :] = delta * u_ref[...].astype(F32)
+        columns_of_groups(b_rows, turned_s, sub)
+        spread = nn(c_rows, spread_matrix(states, sub)) * own_step_mask(rows, states, sub)
+        wide_s[sub:, :] = spread.astype(BF16)
+
+        def pair(k, s):
+            for turn, (mine, other) in enumerate(((held_a, held_b), (held_b, held_a))):
+                base = pl.multiple_of(k * (2 * sub) + turn * sub, sub)
+                w_s[pl.ds(base, sub), :] = nn(wide_s[pl.ds(base, sub), :], other[...])
+                bt = turned_s[k * 2 + turn]
+                for t in range(sub):
+                    dl = delta_s[pl.ds(origin + base + t, 1), :]
+                    du = du_s[pl.ds(origin + base + t, 1), :]
+                    s = jnp.exp2(dl * rate) * s + du * bt[:, t : t + 1]
+                    low = s.astype(BF16)
+                    mine[t * states : (t + 1) * states, :] = low
+                    states_s[pl.ds(pl.multiple_of((origin + base + t + 1) * states, states), states), :] = low
+            return s
+
+        carry[...] = lax.fori_loop(0, pairs, pair, carry[...])
+        w_s[rows:, :] = nn(wide_s[rows:, :], held_b[...])
+        scanned = w_s[sub:, :] + skip_ref[...] * u_ref[...].astype(F32)
+        scanned_s[here, :] = scanned
+        gated_ref[...] = (scanned * jax.nn.silu(z_ref[...].astype(F32))).astype(BF16)
+
+    @pl.when(step >= blocks)
+    def _():
+        @pl.when(step == blocks)
+        def _():
+            carry[...] = jnp.zeros_like(carry)
+            for ref in (held_a, q_a):
+                ref[...] = jnp.zeros_like(ref)
+            wide_s[rows:, :] = jnp.zeros((sub, sub * states), BF16)
+            du_s[pl.ds(blocks * rows, sub), :] = jnp.zeros((sub, chans), F32)
+
+        z = z_ref[...].astype(F32)
+        bg = bg_ref[...].astype(F32)
+        sigma = jax.nn.sigmoid(z)
+        bs_s[...] = bg * (z * sigma)
+        bz_ref[...] = (bg * scanned_s[here, :] * (sigma * (1.0 + z * (1.0 - sigma)))).astype(BF16)
+        columns_of_groups(c_rows, turned_s, sub)
+        spread = nn(b_rows, spread_matrix(states, sub)) * own_step_mask(rows, states, sub)
+        wide_s[:rows, :] = spread.astype(BF16)
+        ones = own_step_mask(sub, states, sub).astype(BF16)
+        col = lax.broadcasted_iota(jnp.int32, (states, sub), 1)
+        decay = decay_ref[...]
+
+        def diagonal(wide):
+            out = wide[:states]
+            for t in range(1, sub):
+                out = jnp.where(col == t, wide[t * states : (t + 1) * states], out)
+            return out
+
+        def sums(at, k, g_ref, q_ref):
+            w_s[pl.ds(at, sub), :] = nn(wide_s[pl.ds(at, sub), :], g_ref[...])
+            bd_s[pl.ds(at, sub), :] = nn(ones, q_ref[...])
+            bb_s[k] = diagonal(nt(g_ref[...], du_s[pl.ds(pl.multiple_of(origin + at, sub), sub), :].astype(BF16)))
+
+        def pair(i, h):
+            for turn, (g_mine, q_mine, g_other, q_other) in enumerate(
+                ((held_b, q_b, held_a, q_a), (held_a, q_a, held_b, q_b))
+            ):
+                k = (pairs - 1 - i) * 2 + 1 - turn
+                base = pl.multiple_of(k * sub, sub)
+                sums(pl.multiple_of(base + sub, sub), k + 1, g_other, q_other)
+                kept = states_s[pl.ds(pl.multiple_of((origin + base + 1) * states, states), sub * states), :]
+                bc_s[k] = diagonal(nt(kept, bs_s[pl.ds(base, sub), :].astype(BF16)))
+                ct = turned_s[k]
+                for t in range(sub - 1, -1, -1):
+                    dl = delta_s[pl.ds(origin + base + t, 1), :]
+                    bs = bs_s[pl.ds(base + t, 1), :]
+                    g = bs * ct[:, t : t + 1] + h
+                    h = g * jnp.exp2(dl * rate)
+                    before = states_s[pl.ds(pl.multiple_of((origin + base + t) * states, states), states), :]
+                    g_mine[t * states : (t + 1) * states, :] = g.astype(BF16)
+                    q_mine[t * states : (t + 1) * states, :] = h.astype(BF16) * (decay * before)
+            return h
+
+        carry[...] = lax.fori_loop(0, pairs, pair, carry[...])
+        sums(0, 0, held_a, q_a)
+        w = w_s[:rows, :]
+        conv_ref[...] = w * delta_s[here, :] + skip_ref[...] * bs_s[...]
+        back_delta = bd_s[:rows, :] + w * u_ref[...].astype(F32)
+        back_pre = (back_delta * jax.nn.sigmoid(pre_s[here, :])).astype(BF16)
+        pre_ref[...] = back_pre
+        gated_low = nt(down_ref[0], gated_block(scanned_s[here, :], z))
+        mixed = [nt(step_proj_ref[...], back_pre), nt(step_up_ref[0], back_pre)]
+        mixed += [jnp.concatenate([ref[k] for k in range(rows // sub)], 1) for ref in (bb_s, bc_s)]
+        mixed = jnp.concatenate(mixed + [gated_low], 0).astype(BF16)
+        for j in range(per):
+            mixed_ref[j] = mixed[:, j * tokens : (j + 1) * tokens]
+
+
+def gated_block(scanned, z):
+    return (scanned * jax.nn.silu(z)).astype(BF16)
+
+
+def scan(meta, shared, u, z, bg, step_proj, step_up, bias, rate, decay, skip, out_down, parts, sub):
     length, chans = u.shape
-    block = length // parts
-    states, ranks = rate.shape[0], step_proj.shape[0]
-    seq = lambda cols: pl.BlockSpec((block, cols), lambda i, meta: (i, 0))
-    out = lambda cols, dtype=BF16, rows=length: jax.ShapeDtypeStruct((rows, cols), dtype)
+    tokens = length // parts
+    block = 2 * tokens
+    blocks = length // block
+    states, rank, ranks = rate.shape[0], step_up.shape[1], step_proj.shape[0]
+    cols = ranks + 2 * rank + 2 * states
+    mirrored = lambda i: jnp.where(i < blocks, i, 2 * blocks - 1 - i)
+    back = lambda i: jnp.where(i < blocks, blocks - 1, 2 * blocks - 1 - i)
+    both = pl.BlockSpec((block, chans), lambda i, meta: (mirrored(i), 0))
+    first = pl.BlockSpec((block, chans), lambda i, meta: (jnp.minimum(i, blocks - 1), 0))
+    second = pl.BlockSpec((block, chans), lambda i, meta: (back(i), 0))
     return pl.pallas_call(
-        functools.partial(scan_forward_kernel, sub=sub, ranks=ranks),
+        functools.partial(scan_kernel, sub=sub, ranks=ranks),
         grid_spec=pltpu.PrefetchScalarGridSpec(
             num_scalar_prefetch=1,
-            grid=(parts,),
+            grid=(2 * blocks,),
             in_specs=[
-                pl.BlockSpec((1,) + shared.shape[1:], lambda i, meta: (place_of_block(i, meta[1], parts), 0, 0)),
-                seq(chans), seq(chans), once(step_proj), chosen(step_up), once(bias), once(rate), once(skip),
+                once(shared), both, both, second, once(step_proj), chosen(step_up), once(bias), once(rate), once(decay),
+                once(skip), chosen(out_down, 0, chans),
             ],
-            out_specs=[seq(chans), seq(chans), pl.BlockSpec((block * states, chans), lambda i, meta: (i, 0))],
+            out_specs=[
+                first, second, second, second,
+                pl.BlockSpec((2, cols, tokens), lambda i, meta: (back(i), 0, 0)),
+            ],
             scratch_shapes=[
                 pltpu.VMEM((states, chans), F32),
-                pltpu.VMEM((block, chans), F32),
-                pltpu.VMEM((block, chans), F32),
-                pltpu.VMEM((block + sub, sub * states), BF16),
-                pltpu.VMEM((block + sub, chans), F32),
-                pltpu.VMEM((block // sub, states, sub), F32),
-                pltpu.VMEM((sub * states, chans), BF16),
-                pltpu.VMEM((sub * states, chans), BF16),
-            ],
-        ),
-        out_shape=[out(chans), out(chans, F32), out(chans, rows=length * states)],
-        compiler_params=pltpu.CompilerParams(vmem_limit_bytes=LIMIT),
-        name="scan_forward",
-    )(meta, shared, u, z, step_proj, step_up, bias, rate, skip)
-
-
-def scan_backward_kernel(meta, *refs, sub, ranks):
-    (shared_ref, step_proj_ref, step_up_ref, bias_ref, u_ref, z_ref, scanned_ref, bg_ref, states_ref, before_ref,
-     rate_ref, decay_ref, skip_ref, low_out_ref) = refs[:14]
-    pre_ref, conv_ref, bz_ref, mixed_ref = refs[14:18]
-    carry, delta_s, du_s, bs_s, pre_s, bm_s, w_s, bd_s, bb_s, bc_s, ct_s, g_a, g_b, q_a, q_b = refs[18:]
-    rows, chans = u_ref.shape
-    states, rank = rate_ref.shape[0], step_up_ref.shape[1]
-    step = pl.program_id(0)
-    first = step == pl.num_programs(0) - 1
-
-    @pl.when(step == 0)
-    def _():
-        carry[...] = jnp.zeros_like(carry)
-        for ref in (g_a, q_a):
-            ref[...] = jnp.zeros_like(ref)
-        bm_s[rows:, :] = jnp.zeros((sub, sub * states), BF16)
-        du_s[rows:, :] = jnp.zeros((sub, chans), F32)
-
-    shared = shared_ref[0]
-    step_mid = shared[:, ranks : ranks + rank]
-    pre = nn(shared[:, :ranks], step_proj_ref[...]) + nn(step_mid, step_up_ref[0]) + bias_ref[...]
-    delta = softplus(pre)
-    z = z_ref[...].astype(F32)
-    bg = bg_ref[...].astype(F32)
-    sigma = jax.nn.sigmoid(z)
-    bs_s[...] = bg * (z * sigma)
-    bz_ref[...] = (bg * scanned_ref[...] * (sigma * (1.0 + z * (1.0 - sigma)))).astype(BF16)
-    pre_s[...] = pre
-    delta_s[...] = delta
-    du_s[:rows, :] = delta * u_ref[...].astype(F32)
-    b_rows = shared[:, ranks + rank : ranks + rank + states]
-    c_rows = shared[:, ranks + rank + states : ranks + rank + 2 * states]
-    columns_of_groups(c_rows, ct_s, sub)
-    bm = nn(b_rows, spread_matrix(states, sub)) * own_step_mask(rows, states, sub)
-    bm_s[:rows, :] = bm.astype(BF16)
-    ones = own_step_mask(sub, states, sub).astype(BF16)
-    col = lax.broadcasted_iota(jnp.int32, (states, sub), 1)
-    rate = rate_ref[...]
-    decay = decay_ref[...]
-    pairs = rows // (2 * sub)
-
-    def diagonal(wide):
-        out = wide[:states]
-        for t in range(1, sub):
-            out = jnp.where(col == t, wide[t * states : (t + 1) * states], out)
-        return out
-
-    def finish(at, k, g_ref, q_ref):
-        w_s[at, :] = nn(bm_s[at, :], g_ref[...])
-        bd_s[at, :] = nn(ones, q_ref[...])
-        bb_s[k] = diagonal(nt(g_ref[...], du_s[at, :].astype(BF16)))
-
-    def pair(i, h):
-        for turn, (g_mine, q_mine, g_other, q_other) in enumerate(((g_b, q_b, g_a, q_a), (g_a, q_a, g_b, q_b))):
-            k = (pairs - 1 - i) * 2 + 1 - turn
-            base = pl.multiple_of(k * sub, sub)
-            finish(pl.ds(pl.multiple_of(base + sub, sub), sub), k + 1, g_other, q_other)
-            wide = pl.ds(pl.multiple_of(base * states, sub * states), sub * states)
-            bc_s[k] = diagonal(nt(states_ref[wide, :], bs_s[pl.ds(base, sub), :].astype(BF16)))
-            ct = ct_s[k]
-            for t in range(sub - 1, -1, -1):
-                dl = delta_s[pl.ds(base + t, 1), :]
-                bs = bs_s[pl.ds(base + t, 1), :]
-                g = bs * ct[:, t : t + 1] + h
-                h = g * jnp.exp2(dl * rate)
-                if t:
-                    sp = states_ref[pl.ds(pl.multiple_of((base + t - 1) * states, states), states), :]
-                else:
-                    at = pl.multiple_of(jnp.maximum(base - 1, 0) * states, states)
-                    inside = jnp.where(k > 0, 1.0, 0.0)
-                    outside = jnp.where(first, 0.0, 1.0 - inside)
-                    sp = states_ref[pl.ds(at, states), :] * inside.astype(BF16)
-                    sp = sp + before_ref[...] * outside.astype(BF16)
-                g_mine[t * states : (t + 1) * states, :] = g.astype(BF16)
-                q_mine[t * states : (t + 1) * states, :] = h.astype(BF16) * (decay * sp)
-        return h
-
-    carry[...] = lax.fori_loop(0, pairs, pair, carry[...])
-    finish(pl.ds(0, sub), 0, g_a, q_a)
-    w = w_s[:rows, :]
-    conv_ref[...] = w * delta_s[...] + skip_ref[...] * bs_s[...]
-    back_delta = bd_s[:rows, :] + w * u_ref[...].astype(F32)
-    back_pre = (back_delta * jax.nn.sigmoid(pre_s[...])).astype(BF16)
-    pre_ref[...] = back_pre
-    turned = [
-        jnp.concatenate([ref[k] for k in range(rows // sub)], 1).T for ref in (bb_s, bc_s)
-    ]
-    mixed_ref[...] = jnp.concatenate(
-        [nt(back_pre, step_proj_ref[...]), nt(back_pre, step_up_ref[0])] + turned + [low_out_ref[...]], 1
-    ).astype(BF16)
-
-
-def scan_backward(
-    meta, shared, step_proj, step_up, bias, u, z, scanned, bg, kept, rate, decay, skip, low_out, parts, sub,
-):
-    length, chans = u.shape
-    block = length // parts
-    states, rank, ranks = rate.shape[0], step_up.shape[1], step_proj.shape[0]
-    end = parts
-    seq = lambda cols: pl.BlockSpec((block, cols), lambda i, meta: (end - 1 - i, 0))
-    cols = ranks + 2 * rank + 2 * states
-    out = lambda cols, dtype=BF16: jax.ShapeDtypeStruct((length, cols), dtype)
-    args = (shared, step_proj, step_up, bias, u, z, scanned, bg, kept, kept, rate, decay, skip, low_out)
-    return pl.pallas_call(
-        functools.partial(scan_backward_kernel, sub=sub, ranks=ranks),
-        grid_spec=pltpu.PrefetchScalarGridSpec(
-            num_scalar_prefetch=1,
-            grid=(parts,),
-            in_specs=[
-                pl.BlockSpec(
-                    (1,) + shared.shape[1:], lambda i, meta: (place_of_block(end - 1 - i, meta[1], parts), 0, 0)
-                ),
-                once(step_proj), chosen(step_up), once(bias), seq(chans), seq(chans), seq(chans), seq(chans),
-                pl.BlockSpec((block * states, chans), lambda i, meta: (end - 1 - i, 0)),
-                pl.BlockSpec((states, chans), lambda i, meta: (jnp.maximum((end - 1 - i) * block - 1, 0), 0)),
-                once(rate), once(decay), once(skip), seq(rank),
-            ],
-            out_specs=[seq(chans), seq(chans), seq(chans), seq(cols)],
-            scratch_shapes=[
-                pltpu.VMEM((states, chans), F32),
-                pltpu.VMEM((block, chans), F32),
-                pltpu.VMEM((block + sub, chans), F32),
-                pltpu.VMEM((block, chans), F32),
+                pltpu.VMEM(((length + 1) * states, chans), BF16),
+                pltpu.VMEM((length, chans), F32),
+                pltpu.VMEM((length, chans), F32),
+                pltpu.VMEM((length + sub, chans), F32),
+                pltpu.VMEM((length, chans), F32),
                 pltpu.VMEM((block, chans), F32),
                 pltpu.VMEM((block + sub, sub * states), BF16),
                 pltpu.VMEM((block + sub, chans), F32),
@@ -539,10 +506,16 @@
                 pltpu.VMEM((sub * states, chans), BF16),
             ],
         ),
-        out_shape=[out(chans), out(chans, F32), out(chans), out(cols)],
+        out_shape=[
+            jax.ShapeDtypeStruct((length, chans), BF16),
+            jax.ShapeDtypeStruct((length, chans), BF16),
+            jax.ShapeDtypeStruct((length, chans), F32),
+            jax.ShapeDtypeStruct((length, chans), BF16),
+            jax.ShapeDtypeStruct((parts, cols, tokens), BF16),
+        ],
         compiler_params=pltpu.CompilerParams(vmem_limit_bytes=LIMIT),
-        name="scan_backward",
-    )(meta, *args)
+        name="scan",
+    )(meta, shared, u, z, bg, step_proj, step_up, bias, rate, decay, skip, out_down)
 
 
 def finish_kernel(
@@ -553,7 +526,7 @@
     (back_ref, shared_ref, conv_grad_ref, back_z_ref, back_pre_ref, x_ref, x_before_ref, u_ref, low_in_ref,
      gated_ref, back_low_ref, cols_ref, up_x_ref, up_z_ref, proj_ref, down_ref,
      state_up_ref, in_down_ref, weight_ref, bias_ref,
-     parts_ref, wide_ref, down_grad_ref, local_ref,
+     parts_ref, wide_ref, local_ref,
      after, sums_s, down_s, local_s, rows_s, whole_x, whole_z, piece_sems, x_sems, z_sems) = refs
     copies = (
         ring_copies(rows_s, pieces, meta[1], piece_sems)
@@ -619,11 +592,13 @@
 
     @pl.when(step == steps - 1)
     def _():
-        wide_ref[...] = sums_s[...].astype(BF16)
-        down_grad_ref[...] = down_s[...].astype(BF16)
+        for values, ref, first in (
+            (sums_s, wide_ref, 0), (down_s, wide_ref, sums_s.shape[1] // 128), (local_s, local_ref, 0)
+        ):
+            for j in range(values.shape[1] // 128):
+                ref[first + j] = values[:, j * 128 : (j + 1) * 128].astype(BF16)
         lane = lax.broadcasted_iota(jnp.int32, (rank, 128), 1)
-        local_ref[:, :-128] = local_s[...].astype(BF16)
-        local_ref[:, -128:] = (lane == meta[0]).astype(BF16)
+        local_ref[local_ref.shape[0] - 1] = (lane == meta[0]).astype(BF16)
 
 
 def finish(
@@ -640,7 +615,8 @@
     seq = lambda size: pl.BlockSpec((block, size), lambda i, meta: (end - i, 0))
     wide = 3 * chans + span
     local = 2 * chans + ranks + 2 * 128
-    fixed = lambda size: pl.BlockSpec((rank, size), lambda i, meta: (0, 0))
+    chunks = ((wide + width) // 128, local // 128 + 1)
+    fixed = lambda count: pl.BlockSpec((count, rank, 128), lambda i, meta: (0, 0, 0))
     return pl.pallas_call(
         functools.partial(finish_kernel, ranks=ranks, states=states, parts=parts, groups=groups),
         grid_spec=pltpu.PrefetchScalarGridSpec(
@@ -654,7 +630,7 @@
                 chosen(up, 0, chans), chosen(up, parts, chans), once(proj), chosen(down), chosen(state_up),
                 chosen(in_down), once(weight), once(bias),
             ],
-            out_specs=[seq(width), fixed(wide), fixed(width), fixed(local + 128)],
+            out_specs=[seq(width)] + [fixed(count) for count in chunks],
             scratch_shapes=[
                 pltpu.VMEM((8, chans), F32), pltpu.VMEM((rank, wide), F32), pltpu.VMEM((rank, width), F32),
                 pltpu.VMEM((rank, local), F32), pltpu.VMEM((length, width), BF16),
@@ -665,10 +641,8 @@
         ),
         out_shape=[
             jax.ShapeDtypeStruct((length, width), BF16),
-            jax.ShapeDtypeStruct((rank, wide), BF16),
-            jax.ShapeDtypeStruct((rank, width), BF16),
-            jax.ShapeDtypeStruct((rank, local + 128), BF16),
-        ],
+        ]
+        + [jax.ShapeDtypeStruct((count, rank, 128), BF16) for count in chunks],
         compiler_params=pltpu.CompilerParams(vmem_limit_bytes=LIMIT),
         name="finish",
     )(
@@ -677,72 +651,65 @@
     )
 
 
-def placed(values, idents, e):
-    total = None
-    for value, ident in zip(values, idents):
-        term = jnp.where(ident == e, value, 0.0)
-        total = term if total is None else total + term
-    return total
-
-
-def place_kernel(meta, *refs, first, size, every):
-    values_refs, out_ref = refs[:-1], refs[-1]
-    groups, parts = len(values_refs), values_refs[0].shape[0]
-    count = parts // every
-    per = out_ref.shape[2] // size
-    idents = [meta[3 + groups + g] for g in range(groups)]
-    step = pl.program_id(0)
-    column = pl.multiple_of((first + lax.div(step * per, count)) * size, size)
-    for j in range(per):
-        at = place_of_block(lax.rem(step * per + j, count) * every, meta[1], parts)
-        values = [ref[at, :, pl.ds(column, size)].astype(F32) for ref in values_refs]
-        for e in range(out_ref.shape[0]):
-            out_ref[e, :, j * size : (j + 1) * size] = placed(values, idents, e)
-
-
-def place(meta, values, adapters, first, size, parts, every=1, runs=1):
-    rank = values[0].shape[1]
-    count = parts // every
-    per = count // 2
+def place_kernel(meta, *refs, groups, parts, chans, span, every, wide):
+    values, outs = refs[:groups], refs[groups:]
+    in_up_ref, out_down_ref, out_up_ref, in_down_ref, state_down_ref, step_up_ref, step_down_ref, state_up_ref = outs
+    adapter = pl.program_id(0)
+    uses = [meta[3 + g] == adapter for g in range(groups)]
+
+    def put(ref, column, at, size=128):
+        total = None
+        for use, value in zip(uses, values):
+            term = jnp.where(use, value[at].astype(F32), 0.0)
+            total = term if total is None else total + term
+        ref[0, :, column : column + size] = total[:, :size]
+
+    inner = parts * chans
+    for p in range(parts):
+        at = place_of_block(p, meta[1], parts) * wide
+        for j in range(chans // 128):
+            put(in_up_ref, p * chans + j * 128, at + j)
+            put(in_up_ref, inner + p * chans + j * 128, at + chans // 128 + j)
+            put(out_down_ref, p * chans + j * 128, at + 2 * (chans // 128) + j)
+        if p % every == 0:
+            for j in range(span // 128):
+                put(out_up_ref, p // every * span + j * 128, at + 3 * (chans // 128) + j)
+    at = parts * wide
+    for ref in (in_down_ref, state_down_ref, step_up_ref, step_down_ref, state_up_ref):
+        for j in range(pl.cdiv(ref.shape[2], 128)):
+            put(ref, j * 128, at, min(128, ref.shape[2] - j * 128))
+            at += 1
+
+
+def place(meta, values, adapters, parts, chans, span, width, wide, ranks, mixes):
+    groups, rank = len(values), values[0].shape[1]
+    every = max(span * parts // width, 1)
+    sizes = (2 * parts * chans, parts * chans, width, width, chans, chans, ranks, mixes)
     return pl.pallas_call(
-        functools.partial(place_kernel, first=first, size=size, every=every),
+        functools.partial(place_kernel, groups=groups, parts=parts, chans=chans, span=span, every=every, wide=wide),
         grid_spec=pltpu.PrefetchScalarGridSpec(
             num_scalar_prefetch=1,
-            grid=(runs * count // per,),
+            grid=(adapters,),
             in_specs=[once(value) for value in values],
-            out_specs=pl.BlockSpec((adapters, rank, size * per), lambda i, meta: (0, 0, i)),
+            out_specs=[pl.BlockSpec((1, rank, size), lambda i, meta: (i, 0, 0)) for size in sizes],
         ),
-        out_shape=jax.ShapeDtypeStruct((adapters, rank, size * count * runs), F32),
+        out_shape=[jax.ShapeDtypeStruct((adapters, rank, size), F32) for size in sizes],
         compiler_params=pltpu.CompilerParams(vmem_limit_bytes=16 << 20),
         name="place",
     )(meta, *values)
 
 
-def place_local_kernel(meta, values_ref, *out_refs):
-    groups = values_ref.shape[0]
-    idents = [meta[3 + g] for g in range(groups)]
-    at = 0
-    for ref in out_refs:
-        size = ref.shape[2]
-        values = [values_ref[g, :, at : at + size].astype(F32) for g in range(groups)]
-        for e in range(ref.shape[0]):
-            ref[e] = placed(values, idents, e)
-        at += size
-
-
-def place_local(meta, values, adapters, sizes):
-    rank = values.shape[1]
+def split_kernel(values_ref, out_ref):
+    chans = out_ref.shape[2]
+    for i in range(out_ref.shape[0]):
+        out_ref[i] = values_ref[:, i * chans : (i + 1) * chans]
+
+
+def split_columns(values, parts):
+    rows, cols = values.shape
     return pl.pallas_call(
-        place_local_kernel,
-        grid_spec=pltpu.PrefetchScalarGridSpec(
-            num_scalar_prefetch=1,
-            grid=(1,),
-            in_specs=[once(values)],
-            out_specs=[pl.BlockSpec((adapters, rank, size), lambda i, meta: (0, 0, 0)) for size in sizes],
-        ),
-        out_shape=[jax.ShapeDtypeStruct((adapters, rank, size), F32) for size in sizes],
-        name="place_local",
-    )(meta, values)
+        split_kernel, out_shape=jax.ShapeDtypeStruct((parts, rows, cols // parts), values.dtype), name="split_columns"
+    )(values)
 
 
 EPS = 1e-05
@@ -839,9 +806,8 @@
     return held
 
 
-def exchange(values, size, axis):
-    got = lax.all_to_all(values, axis, split_axis=0, concat_axis=0, tiled=True)
-    return got.reshape((size, -1) + values.shape[1:])
+def exchange(values, axis):
+    return lax.all_to_all(values, axis, split_axis=0, concat_axis=0, tiled=True)
 
 
 def body(
@@ -880,12 +846,18 @@
     rows = in_proj_x.shape[0]
 
     def own_columns_of(weight):
-        return lax.all_to_all(weight, "seq", split_axis=1, concat_axis=0, tiled=True).reshape(parts, rows, chans)
+        return lax.all_to_all(weight, "seq", split_axis=0, concat_axis=0, tiled=True)
 
     hops = max(parts // 8, 1)
     whole_out = lax.all_gather(out_proj, "fsdp", axis=0, tiled=True)
-    pieces = RingGather(normed, parts, "seq").all_pieces()
-    columns = swap_gather(own_columns_of(in_proj_x), groups, "fsdp")
+    ring = RingGather(normed, parts, "seq")
+    ring.advance(hops)
+    mine_x = own_columns_of(split_columns(in_proj_x, parts))
+    small = (conv_weight, conv_bias, bias, skip, rate, decay, meta, split_columns(in_proj_z, parts))
+    ring.ends, small = together(ring.ends, small)
+    conv_weight, conv_bias, bias, skip, rate, decay, meta, in_proj_z = small
+    pieces = ring.all_pieces()
+    columns = swap_gather(mine_x, groups, "fsdp")
 
     pieces, columns, back_out, in_proj_z = together(pieces, columns, back_out, in_proj_z)
     cot_ring = RingGather(back_out, parts, "seq")
@@ -897,56 +869,58 @@
     sums, cot_ring.ends, mine_z = together(sums, cot_ring.ends, mine_z)
     cot_ring.advance(hops)
     columns_z = lax.all_gather(mine_z, "fsdp")
-    shared = share(meta, exchange(sums, parts, "seq"), state_up, step_down, ranks, states)
-    shared, cot_ring.ends = together(shared, cot_ring.ends)
-    shared = small_gather(shared, parts, "seq")
-    z = gate(meta, pieces, columns_z, low_in, in_up, parts, groups)
-    shared, z, cot_ring.ends = together(shared, z, cot_ring.ends)
+    sums = exchange(sums, "seq")
+    sums, cot_ring.ends = together(sums, cot_ring.ends)
     cot_ring.advance(hops)
-    gated, scanned, kept = scan_forward(meta, shared, conv_out, z, step_proj, step_up, bias, rate, skip, parts, sub)
-    gated, cot_ring.ends = together(gated, cot_ring.ends)
-    cot_ring.advance(parts)
-    out_down_sel = lax.dynamic_slice(out_down, (ident, 0, part * chans), (1, rank, chans))[0]
-    out_parts, low_out = nn(gated, whole_out).astype(BF16), nt(gated, out_down_sel)
-    out_parts, low_out, cot_ring.pieces = together(out_parts, low_out, cot_ring.pieces)
-    out_ring = RingScatter(out_parts, parts, "seq")
+    shared = share(meta, sums, state_up, step_down, ranks, states)[None]
+    z = back = None
+    for i, bit in enumerate(bits_of(parts)):
+        shared = jnp.concatenate([shared, swap(shared, parts, bit, "seq")], 0)
+        if i == 0:
+            shared, cot_ring.ends, columns_z = together(shared, cot_ring.ends, columns_z)
+            cot_ring.advance(parts)
+            z = gate(meta, pieces, columns_z, low_in, in_up, parts, groups)
+        elif i == 1:
+            shared, cot_ring.pieces, z = together(shared, cot_ring.pieces, z)
+            back = back_gate(meta, cot_ring.pieces, whole_out, out_down, out_up, parts)
+    back_low, cols, back_gated = back
+    gated, back_pre, conv_grad, back_z, mixed = scan(
+        meta, shared, conv_out, z, back_gated, step_proj, step_up, bias, rate, decay, skip, out_down, parts, sub
+    )
+    out_ring = RingScatter(nn(gated, whole_out).astype(BF16), parts, "seq")
     out_ring.advance(hops)
-    back_low, cols, back_gated = back_gate(meta, cot_ring.pieces, whole_out, out_down, out_up, parts)
-    back_gated, out_ring.ends = together(back_gated, out_ring.ends)
-    out_ring.advance(hops)
-    back_pre, conv_grad, back_z, mixed = scan_backward(
-        meta, shared, step_proj, step_up, bias, conv_out, z, scanned, back_gated, kept, rate, decay, skip, low_out, parts,
-        sub,
-    )
-    mixed, out_ring.ends = together(mixed, out_ring.ends)
-    out_ring.advance(hops)
-    back_own = share_back(meta, exchange(mixed, parts, "seq"), step_down, ranks, states)
-    back_own, out_ring.ends = together(back_own, out_ring.ends)
-    back = small_gather(back_own, parts, "seq")
-    back, out_ring.ends = together(back, out_ring.ends)
-    out_ring.advance(parts)
-    in_parts, wide, down_grad, local = finish(
+    back_own = share_back(meta, exchange(mixed, "seq"), step_down, ranks, states)
+    back = back_own[None]
+    for i, bit in enumerate(bits_of(parts)):
+        back = jnp.concatenate([back, swap(back, parts, bit, "seq")], 0)
+        if i % 2 == 0:
+            back, out_ring.ends = together(back, out_ring.ends)
+            out_ring.advance(hops)
+    in_parts, wide, local = finish(
         meta, pieces, columns, columns_z, back, shared, conv_grad, back_z, back_pre, x, conv_out, low_in, gated, back_low,
         cols, in_up, state_proj, state_down, state_up, in_down, conv_weight, conv_bias, parts, groups, states,
     )
-    in_parts, wide, down_grad, local, out_ring.ends = together(in_parts, wide, down_grad, local, out_ring.ends)
+    in_parts, wide, local, out_ring.ends = together(in_parts, wide, local, out_ring.ends)
+    out_ring.advance(parts)
     in_ring = RingScatter(in_parts, parts, "seq")
-    span = cols.shape[1]
-    share_of = max(span * parts // width, 1)
-    held = jnp.concatenate([wide, down_grad], 1)[None]
+    held = wide[None]
     for bit in bits_of(parts):
         in_ring.advance(hops)
         held = jnp.concatenate([held, swap(held, parts, bit, "seq")], 0)
         held, in_ring.ends = together(held, in_ring.ends)
     in_ring.advance(parts)
-    down_grad = held[:, :, wide.shape[1] :].astype(F32).sum(0).astype(BF16)
-    held = held[:, :, : wide.shape[1]]
-    wide = [held]
-    for bit in bits_of(groups):
-        wide += [swap(block, groups, bit, "fsdp") for block in wide]
-    local = lax.all_gather(jnp.concatenate([down_grad, local], 1), "fsdp")
+    span = cols.shape[1]
+    own = (3 * chans + span) // 128
+    down_grad = held[:, own:].astype(F32).sum(0).astype(BF16)
+    chunks = [jnp.concatenate([held[:, :own].reshape(parts * own, rank, 128), down_grad, local], 0)]
+    first, *others = bits_of(groups)
+    chunks += [swap(chunks[0], groups, first, "fsdp")]
+    branch = out_ring.total()
+    chunks, in_ring.ends, branch = together(chunks, in_ring.ends, branch)
+    for bit in others:
+        chunks += [swap(block, groups, bit, "fsdp") for block in chunks]
     out_up_sel = lax.dynamic_index_in_dim(out_up, ident, 0, keepdims=False)
-    block_out = (hidden_f + valid * (out_ring.total() + nn(back_own[:, -rank:], out_up_sel))).astype(BF16)
+    block_out = (hidden_f + valid * (branch + nn(back_own[:, -rank:], out_up_sel))).astype(BF16)
     gained = in_ring.total() * gain_f
     input_grad = (
         cot_f
@@ -955,15 +929,11 @@
     )
 
     lane = lax.broadcasted_iota(jnp.int32, (groups, adapters), 1)
-    idents = jnp.sum(local[:, 0, -128 : -128 + adapters].astype(F32) * lane.astype(F32), axis=1).astype(jnp.int32)
-    apart = jnp.asarray(swap_order(groups), jnp.int32)
-    meta = jnp.concatenate([meta, idents, idents[jnp.bitwise_xor(group, apart)]])
-    in_up_grad = place(meta, wide, adapters, 0, chans, parts, runs=2)
-    out_down_grad = place(meta, wide, adapters, 2, chans, parts)
-    first = 3 * chans // span
-    out_up_grad = place(meta, wide, adapters, first, span, parts, every=share_of)
-    in_down_grad, state_down_grad, step_up_grad, step_down_grad, state_up_grad = place_local(
-        meta, local, adapters, (width, chans, chans, ranks, ranks + 2 * states)
+    picks = jnp.stack([block[-1, 0, :adapters] for block in chunks]).astype(F32)
+    idents = jnp.sum(picks * lane.astype(F32), axis=1).astype(jnp.int32)
+    (in_up_grad, out_down_grad, out_up_grad, in_down_grad, state_down_grad, step_up_grad, step_down_grad,
+     state_up_grad) = place(
+        jnp.concatenate([meta, idents]), chunks, adapters, parts, chans, span, width, own, ranks, ranks + 2 * states
     )
     return (
         block_out[None], input_grad[None], in_down_grad.transpose(0, 2, 1), in_up_grad,

time: 386 us -> 357 us (0.925)
  waiting for transfers between devices: 111 us -> 125 us
  Pallas kernels: 119 us -> 107 us
  starting transfers between devices: 79.8 us -> 70 us
  local copies, waits for them, and re-layouts: 14.4 us -> 4.92 us
  blocking collectives: 7.02 us -> 0 us
    ppermute x15, waiting for transfers between devices: 36.7 us -> 61.3 us  [swap(): return lax.ppermute(value, axis, [(i, i ^ bit) for i in range(size)])]
    all_to_all x4, waiting for transfers between devices: 28.3 us -> 11.8 us  [the longest x2 8.07 us: own_columns_of(): lax.all_to_all(weight, 'seq', split_axis=0, concat_axis=0, tiled=True)]
    ppermute x15, starting transfers between devices: 21 us -> 8.54 us  [swap(): return lax.ppermute(value, axis, [(i, i ^ bit) for i in range(size)])]
    pallas_call x6 -> x4, Pallas kernels: 61.8 us -> 51.5 us  [the longest x1 41.6 us: scan(): pl.pallas_call(functools.partial(scan_kernel, sub=sub, ranks=ranks), grid...]
    all_to_all x6 -> x0, local copies, waits for them, and re-layouts: 9.76 us -> none  [the longest x4 5.99 us: exchange(): got = lax.all_to_all(values, axis, split_axis=0, concat_axis=0, tiled=True)]
    all_gather x1 -> x0, blocking collectives: 7.02 us -> none  [body(): local = lax.all_gather(jnp.concatenate([down_grad, local], 1), 'fsdp')]
    ppermute x32, waiting for transfers between devices: 44.9 us -> 51.2 us  [ring_send(): return lax.ppermute(value, axis, pairs)]
    concatenate x7, other arithmetic: 7.02 us -> 2.86 us  [the longest x3 1.8 us: body(): back = jnp.concatenate([back, swap(back, parts, bit, 'seq')], 0)]
  transfers between devices with their start and end apart: 53 -> 53, of which waited for: 28 -> 24; matrix products, arithmetic and copies ran while one was open for 9% -> 7% of each run, Pallas kernels for 29% -> 17%
where the time goes in v3:
time: 357 us; the launch traced here: 356 us
  waiting for transfers between devices  125 us (35%)
  Pallas kernels  107 us (30%)
  starting transfers between devices  70 us (20%)
  other arithmetic  28.2 us (8%)
  between operations  16.1 us (5%)
  local copies, waits for them, and re-layouts  4.92 us (1%)
  matrix products  4.73 us (1%)
    ppermute x15, waiting for transfers between devices, swap(): return lax.ppermute(value, axis, [(i, i ^ bit) for i in range(size)])  61.3 us
    ppermute x32, waiting for transfers between devices, ring_send(): return lax.ppermute(value, axis, pairs)  51.2 us
    pallas_call x1, Pallas kernels, scan(): pl.pallas_call(functools.partial(scan_kernel, sub=sub, ranks=ranks), grid...  41.6 us
    ppermute x32, starting transfers between devices, ring_send(): return lax.ppermute(value, axis, pairs)  40.1 us
    pallas_call x1, Pallas kernels, finish(): pl.pallas_call(functools.partial(finish_kernel, ranks=ranks, states=state...  18.7 us
    pallas_call x1, Pallas kernels, project(): pl.pallas_call(functools.partial(project_kernel, parts=parts, groups=grou...  11.9 us
    pallas_call x1, Pallas kernels, back_gate(): pl.pallas_call(functools.partial(back_gate_kernel, parts=parts), grid_spe...  11.3 us
    all_to_all x2, starting transfers between devices, exchange(): return lax.all_to_all(values, axis, split_axis=0, concat_axis=0, tiled=True)  10.9 us
  transfers between devices with their start and end apart: 53, of which 24 were waited for; matrix products, arithmetic and copies ran while one was open for 7% of the time, Pallas kernels for 17%

profile of v3, /device:TPU:0, one launch (start us, length us, event | category | flops | bytes accessed | tf_op | source)
XLA Modules:
  0.0 355.6 jit_solution(2530126055065167910)
XLA Ops:
  10.4 3.1 collective-permute-start
  13.4 1.9 split_columns.3
  15.3 6.3 %all-to-all-start = ((bf16[8,64,512]{2,1,0:T(8,128)(2,1)}), bf16[8,64,512]{2,1,0:T(8,128)(2,1)}, u32[]{:S(2)}, u32[]{:S(2)}) async-start(bf16[8,64,512]{2,1,0:T(8,128)(2,1)} %split_columns.3), calls=%async_computation | async-start | bytes 1048576 | tf_op jit(solution)/shard_map/all_to_all | solution.py:849
  21.6 1.3 convert_element_type.182.refs_15_.refs_32_
  24.1 1.3 broadcast_in_dim.49
  27.3 1.9 split_columns.2
  30.4 2.1 collective-permute-start.2
  32.6 8.1 %all-to-all-done.refs_9_ = bf16[8,64,512]{2,1,0:T(8,128)(2,1)} async-done(((bf16[8,64,512]{2,1,0:T(8,128)(2,1)}), bf16[8,64,512]{2,1,0:T(8,128)(2,1)}, u32[]{:S(2)}, u32[]{:S(2)}) %all-to-all-start) | async-done | bytes 524320 | tf_op jit(solution)/shard_map/all_to_all | solution.py:849
  40.6 1.5 collective-permute-start.8
  42.2 2.6 collective-permute-done.2.refs_3_
  44.8 3.9 %collective-permute-start.4 = (bf16[128,2048]{1,0:T(8,128)(2,1)S(1)}, bf16[128,2048]{1,0:T(8,128)(2,1)S(1)}, u32[]{:S(2)}, u32[]{:S(2)}) collective-permute-start(bf16[128,2048]{1,0:T(8,128)(2,1)S(1)} %collective-permute-done.2.refs_3_), channel_id=1, source_target_pairs={{0,8},{8,16},{16,24},{24,28},{28,20},{20,12},{12,4},{4,0},{1,9},{9... | collective-permute-start | bytes 1572872 | tf_op jit(solution)/shard_map/ppermute | solution.py:721
  49.4 1.4 collective-permute-done.8.refs_10_
  50.8 8.6 %collective-permute-done.4.refs_5_ = bf16[128,2048]{1,0:T(8,128)(2,1)S(1)} collective-permute-done((bf16[128,2048]{1,0:T(8,128)(2,1)S(1)}, bf16[128,2048]{1,0:T(8,128)(2,1)S(1)}, u32[]{:S(2)}, u32[]{:S(2)}) %collective-permute-start.4) | collective-permute-done | bytes 524320 | tf_op jit(solution)/shard_map/ppermute | solution.py:721
  59.4 2.2 collective-permute-start.6
  62.4 2.0 fusion.7.refs_0_
  64.4 2.8 collective-permute-done.6.refs_7_
  67.2 1.6 collective-permute-done.7.refs_8_
  68.8 4.1 %all-to-all-start.1 = ((bf16[8,64,512]{2,1,0:T(8,128)(2,1)}), bf16[8,64,512]{2,1,0:T(8,128)(2,1)}, u32[]{:S(2)}, u32[]{:S(2)}) async-start(bf16[8,64,512]{2,1,0:T(8,128)(2,1)} %split_columns.2), calls=%async_computation.1 | async-start | bytes 1048576 | tf_op jit(solution)/shard_map/all_to_all | solution.py:849
  73.0 1.9 collective-permute-start.11
  75.1 11.9 %project.1 = (bf16[1024,16]{1,0:T(8,128)(2,1)}, bf16[1024,512]{1,0:T(8,128)(2,1)}, bf16[1024,512]{1,0:T(8,128)(2,1)}, bf16[8,176,128]{2,1,0:T(8,128)(2,1)}) custom-call(s32[3]{0:T(128)} %pad_add_fusion.meta, bf16[128,2048]{1,0:T(8,128)(2,1)} %copy-done, bf16[128,2048]{1,0:T(8,128)(2,1)} %copy-done.5, bf16[128,2048]{1,0:T(8,128)(2,1)} %copy-done.6, ...), custom_call_target="tpu_custom_call" | custom-call | tf_op jit(solution)/shard_map/project/pallas_call | solution.py:246
  87.1 3.4 collective-permute-done.11.refs_1_
  90.5 2.2 collective-permute-done.12.refs_2_
  93.5 6.4 %all-to-all-start.2 = ((bf16[8,176,128]{2,1,0:T(8,128)(2,1)}), bf16[8,176,128]{2,1,0:T(8,128)(2,1)S(1)}, u32[]{:S(2)}, u32[]{:S(2)}) async-start(bf16[8,176,128]{2,1,0:T(8,128)(2,1)} %get-tuple-element.127), calls=%async_computation.2 | async-start | bytes 720896 | tf_op jit(solution)/shard_map/all_to_all | solution.py:810
  99.9 2.0 collective-permute-start.13
  101.9 14.2 %collective-permute-done.13.refs_3_ = bf16[128,2048]{1,0:T(8,128)(2,1)S(1)} collective-permute-done((bf16[128,2048]{1,0:T(8,128)(2,1)}, bf16[128,2048]{1,0:T(8,128)(2,1)S(1)}, u32[]{:S(2)}, u32[]{:S(2)}) %collective-permute-start.13) | collective-permute-done | bytes 524320 | tf_op jit(solution)/shard_map/ppermute | solution.py:721
  116.1 2.4 collective-permute-done.14.refs_4_
  118.5 3.0 collective-permute-start.16
  121.5 2.7 share.1
  124.2 1.7 collective-permute-start.15
  125.9 10.7 %collective-permute-done.15 = bf16[1,128,192]{2,1,0:T(8,128)(2,1)S(1)} collective-permute-done((bf16[1,128,192]{2,1,0:T(8,128)(2,1)}, bf16[1,128,192]{2,1,0:T(8,128)(2,1)S(1)}, u32[]{:S(2)}, u32[]{:S(2)}) %collective-permute-start.15) | collective-permute-done | bytes 49184 | tf_op jit(solution)/shard_map/ppermute | solution.py:785
  137.7 2.1 collective-permute-start.20
  139.8 8.0 %gate.1.z_ref = bf16[1024,512]{1,0:T(8,128)(2,1)} custom-call(s32[3]{0:T(128)} %pad_add_fusion.meta, bf16[128,2048]{1,0:T(8,128)(2,1)} %copy-done, bf16[128,2048]{1,0:T(8,128)(2,1)} %copy-done.5, bf16[128,2048]{1,0:T(8,128)(2,1)} %copy-done.6, bf16[128,2048]{1,0:T(8,128)(2,1)} %copy-done.7, bf16[128,2048]{1,0:T(8,128)(2,1)} %collective-permute-done.3.refs_4_, ...), custom_call_target="tpu_custom_call" | custom-call | tf_op jit(solution)/shard_map/gate/pallas_call | solution.py:179
  148.8 11.3 %back_gate.1 = (bf16[1024,16]{1,0:T(8,128)(2,1)}, bf16[1024,256]{1,0:T(8,128)(2,1)}, bf16[1024,512]{1,0:T(8,128)(2,1)}) custom-call(s32[3]{0:T(128)} %pad_add_fusion.meta, bf16[128,2048]{1,0:T(8,128)(2,1)} %fusion.7.refs_0_, bf16[128,2048]{1,0:T(8,128)(2,1)} %collective-permute-done.11.refs_1_, bf16[128,2048]{1,0:T(8,128)(2,1)} %collective-permute-done.12.refs_2_, ...), custom_call_target="tpu_custom_call" | custom-call | tf_op jit(solution)/shard_map/back_gate/pallas_call | solution.py:222
  161.0 41.6 %scan.1 = (bf16[1024,512]{1,0:T(8,128)(2,1)}, bf16[1024,512]{1,0:T(8,128)(2,1)}, f32[1024,512]{1,0:T(8,128)}, bf16[1024,512]{1,0:T(8,128)(2,1)}, bf16[8,192,128]{2,1,0:T(8,128)(2,1)}) custom-call(s32[3]{0:T(128)} %pad_add_fusion.meta, bf16[8,128,192]{2,1,0:T(8,128)(2,1)} %copy-done.9, bf16[1024,512]{1,0:T(8,128)(2,1)} %get-tuple-element.140.u_ref.refs_21_, ...), custom_call_target="tpu_custom_call" | custom-call | tf_op jit(solution)/shard_map/scan/pallas_call | solution.py:476
  202.6 4.5 %all-to-all-start.3 = ((bf16[8,192,128]{2,1,0:T(8,128)(2,1)}), bf16[8,192,128]{2,1,0:T(8,128)(2,1)S(1)}, u32[]{:S(2)}, u32[]{:S(2)}) async-start(bf16[8,192,128]{2,1,0:T(8,128)(2,1)} %get-tuple-element.156), calls=%async_computation.3 | async-start | bytes 786432 | tf_op jit(solution)/shard_map/all_to_all | solution.py:810
  207.1 3.6 %convolution_convert_fusion = bf16[1024,2048]{1,0:T(8,128)(2,1)S(1)} fusion(bf16[1024,512]{1,0:T(8,128)(2,1)} %get-tuple-element.157.refs_23_, bf16[512,2048]{1,0:T(8,128)(2,1)S(1)} %copy-done.13), kind=kOutput, calls=%fused_computation | convolution fusion | flops 2149580800 | bytes 7340032 | tf_op jit(solution)/shard_map/dot_general | solution.py:28
  210.6 2.0 copy-done.8
  212.7 2.1 collective-permute-start.23
  214.8 3.7 %all-to-all-done.3.got_ref = bf16[8,192,128]{2,1,0:T(8,128)(2,1)S(1)} async-done(((bf16[8,192,128]{2,1,0:T(8,128)(2,1)}), bf16[8,192,128]{2,1,0:T(8,128)(2,1)S(1)}, u32[]{:S(2)}, u32[]{:S(2)}) %all-to-all-start.3) | async-done | bytes 393248 | tf_op jit(solution)/shard_map/all_to_all | solution.py:810
  219.3 2.6 share_back.1
  221.9 5.6 %collective-permute-done.22 = bf16[1,128,192]{2,1,0:T(8,128)(2,1)S(1)} collective-permute-done((bf16[1,128,192]{2,1,0:T(8,128)(2,1)}, bf16[1,128,192]{2,1,0:T(8,128)(2,1)S(1)}, u32[]{:S(2)}, u32[]{:S(2)}) %collective-permute-start.22) | collective-permute-done | bytes 49184 | tf_op jit(solution)/shard_map/ppermute | solution.py:785
  228.4 1.4 add_convert_fusion.10
  229.8 2.1 collective-permute-start.27
  232.7 1.6 collective-permute-done.25
  235.3 10.4 %collective-permute-done.26 = bf16[4,128,192]{2,1,0:T(8,128)(2,1)S(1)} collective-permute-done((bf16[4,128,192]{2,1,0:T(8,128)(2,1)S(1)}, bf16[4,128,192]{2,1,0:T(8,128)(2,1)S(1)}, u32[]{:S(2)}, u32[]{:S(2)}) %collective-permute-start.26) | collective-permute-done | bytes 196640 | tf_op jit(solution)/shard_map/ppermute | solution.py:785
  246.6 1.6 add_convert_fusion.8
  248.3 2.3 collective-permute-start.30
  250.6 18.7 %finish.1 = (bf16[1024,2048]{1,0:T(8,128)(2,1)}, bf16[30,16,128]{2,1,0:T(8,128)(2,1)}, bf16[12,16,128]{2,1,0:T(8,128)(2,1)}) custom-call(s32[3]{0:T(128)} %pad_add_fusion.meta, bf16[128,2048]{1,0:T(8,128)(2,1)} %copy-done, bf16[128,2048]{1,0:T(8,128)(2,1)} %copy-done.5, bf16[128,2048]{1,0:T(8,128)(2,1)} %copy-done.6, bf16[128,2048]{1,0:T(8,128)(2,1)} %copy-done.7, ...), custom_call_target="tpu_custom_call" | custom-call | tf_op jit(solution)/shard_map/finish/pallas_call | solution.py:620
  270.4 2.0 collective-permute-start.33
  272.5 10.5 %collective-permute-done.31 = bf16[1,30,16,128]{3,2,1,0:T(8,128)(2,1)S(1)} collective-permute-done((bf16[1,30,16,128]{3,2,1,0:T(8,128)(2,1)}, bf16[1,30,16,128]{3,2,1,0:T(8,128)(2,1)S(1)}, u32[]{:S(2)}, u32[]{:S(2)}) %collective-permute-start.31) | collective-permute-done | bytes 122912 | tf_op jit(solution)/shard_map/ppermute | solution.py:785
  283.9 1.4 add_convert_fusion.6
  288.4 15.8 %collective-permute-done.34 = bf16[2,30,16,128]{3,2,1,0:T(8,128)(2,1)} collective-permute-done((bf16[2,30,16,128]{3,2,1,0:T(8,128)(2,1)S(1)}, bf16[2,30,16,128]{3,2,1,0:T(8,128)(2,1)}, u32[]{:S(2)}, u32[]{:S(2)}) %collective-permute-start.34) | collective-permute-done | bytes 245792 | tf_op jit(solution)/shard_map/ppermute | solution.py:785
  305.3 1.6 add_convert_fusion.4
  306.9 1.8 collective-permute-start.38
  309.0 1.6 add_convert_fusion.1
  310.6 2.0 collective-permute-start.44
  312.6 1.7 collective-permute-start.43
  314.3 5.1 %collective-permute-done.37 = bf16[4,30,16,128]{3,2,1,0:T(8,128)(2,1)S(1)} collective-permute-done((bf16[4,30,16,128]{3,2,1,0:T(8,128)(2,1)S(1)}, bf16[4,30,16,128]{3,2,1,0:T(8,128)(2,1)S(1)}, u32[]{:S(2)}, u32[]{:S(2)}) %collective-permute-start.37) | collective-permute-done | bytes 491552 | tf_op jit(solution)/shard_map/ppermute | solution.py:785
  319.5 8.0 %collective-permute-done.38 = bf16[128,2048]{1,0:T(8,128)(2,1)S(1)} collective-permute-done((bf16[128,2048]{1,0:T(8,128)(2,1)S(1)}, bf16[128,2048]{1,0:T(8,128)(2,1)S(1)}, u32[]{:S(2)}, u32[]{:S(2)}) %collective-permute-start.38) | collective-permute-done | bytes 524320 | tf_op jit(solution)/shard_map/ppermute | solution.py:721
  327.8 1.6 collective-permute-start.40
  329.8 2.0 collective-permute-start.42
  334.4 4.6 %collective-permute-done.41 = bf16[128,2048]{1,0:T(8,128)(2,1)S(1)} collective-permute-done((bf16[128,2048]{1,0:T(8,128)(2,1)S(1)}, bf16[128,2048]{1,0:T(8,128)(2,1)S(1)}, u32[]{:S(2)}, u32[]{:S(2)}) %collective-permute-start.41) | collective-permute-done | bytes 524320 | tf_op jit(solution)/shard_map/ppermute | solution.py:721
  340.1 2.0 fusion.6
  342.6 6.2 %place.1 = (f32[8,16,8192]{2,1,0:T(8,128)}, f32[8,16,4096]{2,1,0:T(8,128)}, f32[8,16,2048]{2,1,0:T(8,128)}, f32[8,16,2048]{2,1,0:T(8,128)}, f32[8,16,512]{2,1,0:...) custom-call(s32[7]{0:T(128)S(1)} %pad_add_fusion.1.meta, ...), custom_call_target="tpu_custom_call" | custom-call | tf_op jit(solution)/shard_map/place/pallas_call | solution.py:688
  (156 shorter events, 27.9 us)
Async XLA Ops:
  7.2 22.6 %copy-start.25 = (bf16[16,512]{1,0:T(8,128)(2,1)S(1)}, bf16[16,512]{1,0:T(8,128)(2,1)}, u32[]{:S(2)}) copy-start(bf16[16,512]{1,0:T(8,128)(2,1)} %param.34) | copy-start | bytes 49156
  10.4 64.7 %copy-start = (bf16[128,2048]{1,0:T(8,128)(2,1)}, bf16[128,2048]{1,0:T(8,128)(2,1)S(1)}, u32[]{:S(2)}) copy-start(bf16[128,2048]{1,0:T(8,128)(2,1)S(1)} %fusion.2.refs_0_) | copy-start | bytes 1572868
  10.4 20.1 %collective-permute-start = (bf16[128,2048]{1,0:T(8,128)(2,1)S(1)}, bf16[128,2048]{1,0:T(8,128)(2,1)S(1)}, u32[]{:S(2)}, u32[]{:S(2)}) collective-permute-start(bf16[128,2048]{1,0:T(8,128)(2,1)S(1)} %fusion.2.refs_0_), channel_id=1, source_target_pairs={{0,8},{8,16},{16,24},{24,28},{28,20},{20,12},{12,4},{4,0},{1,9},{9... | collective-permute-start | bytes 1572872 | tf_op jit(solution)/shard_map/ppermute | solution.py:721
  13.4 17.0 %collective-permute-start.1 = (bf16[128,2048]{1,0:T(8,128)(2,1)S(1)}, bf16[128,2048]{1,0:T(8,128)(2,1)S(1)}, u32[]{:S(2)}, u32[]{:S(2)}) collective-permute-start(bf16[128,2048]{1,0:T(8,128)(2,1)S(1)} %fusion.2.refs_0_), channel_id=1, source_target_pairs={{0,4},{8,0},{16,8},{24,16},{28,24},{20,28},{12,20},{4,12},{1,5},{9... | collective-permute-start | bytes 1572872 | tf_op jit(solution)/shard_map/ppermute | solution.py:721
  15.3 25.3 %all-to-all-start = ((bf16[8,64,512]{2,1,0:T(8,128)(2,1)}), bf16[8,64,512]{2,1,0:T(8,128)(2,1)}, u32[]{:S(2)}, u32[]{:S(2)}) async-start(bf16[8,64,512]{2,1,0:T(8,128)(2,1)} %split_columns.3), calls=%async_computation | async-start | bytes 1048576 | tf_op jit(solution)/shard_map/all_to_all | solution.py:849
  30.4 44.7 %copy-start.5 = (bf16[128,2048]{1,0:T(8,128)(2,1)}, bf16[128,2048]{1,0:T(8,128)(2,1)S(1)}, u32[]{:S(2)}) copy-start(bf16[128,2048]{1,0:T(8,128)(2,1)S(1)} %collective-permute-done.refs_1_) | copy-start | bytes 1572868
  30.4 44.7 %copy-start.6 = (bf16[128,2048]{1,0:T(8,128)(2,1)}, bf16[128,2048]{1,0:T(8,128)(2,1)S(1)}, u32[]{:S(2)}) copy-start(bf16[128,2048]{1,0:T(8,128)(2,1)S(1)} %collective-permute-done.1.refs_2_) | copy-start | bytes 1572868
  30.4 14.3 %collective-permute-start.2 = (bf16[128,2048]{1,0:T(8,128)(2,1)S(1)}, bf16[128,2048]{1,0:T(8,128)(2,1)S(1)}, u32[]{:S(2)}, u32[]{:S(2)}) collective-permute-start(bf16[128,2048]{1,0:T(8,128)(2,1)S(1)} %collective-permute-done.refs_1_), channel_id=1, source_target_pairs={{0,8},{8,16},{16,24},{24,28},{28,20},{20,12},{12,4},{4,0},{1,9},{9... | collective-permute-start | bytes 1572872 | tf_op jit(solution)/shard_map/ppermute | solution.py:721
  32.5 16.2 %collective-permute-start.3 = (bf16[128,2048]{1,0:T(8,128)(2,1)S(1)}, bf16[128,2048]{1,0:T(8,128)(2,1)}, u32[]{:S(2)}, u32[]{:S(2)}) collective-permute-start(bf16[128,2048]{1,0:T(8,128)(2,1)S(1)} %collective-permute-done.1.refs_2_), channel_id=1, source_target_pairs={{0,4},{8,0},{16,8},{24,16},{28,24},{20,28},{12,20},{4,12},{1,5},{9... | collective-permute-start | bytes 1572872 | tf_op jit(solution)/shard_map/ppermute | solution.py:721
  40.6 10.1 %collective-permute-start.8 = (bf16[8,64,512]{2,1,0:T(8,128)(2,1)}, bf16[8,64,512]{2,1,0:T(8,128)(2,1)}, u32[]{:S(2)}, u32[]{:S(2)}) collective-permute-start(bf16[8,64,512]{2,1,0:T(8,128)(2,1)} %all-to-all-done.refs_9_), channel_id=1, source_target_pairs={{0,2},{1,3},{2,0},{3,1},{4,6},{5,7},{6,4},{7,5},{8,10},{9,11},{10,... | collective-permute-start | bytes 1572872 | tf_op jit(solution)/shard_map/ppermute | solution.py:785
  44.7 30.3 %copy-start.7 = (bf16[128,2048]{1,0:T(8,128)(2,1)}, bf16[128,2048]{1,0:T(8,128)(2,1)S(1)}, u32[]{:S(2)}) copy-start(bf16[128,2048]{1,0:T(8,128)(2,1)S(1)} %collective-permute-done.2.refs_3_) | copy-start | bytes 1572868
  44.8 14.6 %collective-permute-start.4 = (bf16[128,2048]{1,0:T(8,128)(2,1)S(1)}, bf16[128,2048]{1,0:T(8,128)(2,1)S(1)}, u32[]{:S(2)}, u32[]{:S(2)}) collective-permute-start(bf16[128,2048]{1,0:T(8,128)(2,1)S(1)} %collective-permute-done.2.refs_3_), channel_id=1, source_target_pairs={{0,8},{8,16},{16,24},{24,28},{28,20},{20,12},{12,4},{4,0},{1,9},{9... | collective-permute-start | bytes 1572872 | tf_op jit(solution)/shard_map/ppermute | solution.py:721
  48.7 13.6 %collective-permute-start.5 = (bf16[128,2048]{1,0:T(8,128)(2,1)}, bf16[128,2048]{1,0:T(8,128)(2,1)S(1)}, u32[]{:S(2)}, u32[]{:S(2)}) collective-permute-start(bf16[128,2048]{1,0:T(8,128)(2,1)} %collective-permute-done.3.refs_4_), channel_id=1, source_target_pairs={{0,4},{8,0},{16,8},{24,16},{28,24},{20,28},{12,20},{4,12},{1,5},{9... | collective-permute-start | bytes 1572872 | tf_op jit(solution)/shard_map/ppermute | solution.py:721
  49.3 15.1 %collective-permute-start.9 = (bf16[8,64,512]{2,1,0:T(8,128)(2,1)}, bf16[8,64,512]{2,1,0:T(8,128)(2,1)S(1)}, u32[]{:S(2)}, u32[]{:S(2)}) collective-permute-start(bf16[8,64,512]{2,1,0:T(8,128)(2,1)} %all-to-all-done.refs_9_), channel_id=1, source_target_pairs={{0,1},{1,0},{2,3},{3,2},{4,5},{5,4},{6,7},{7,6},{8,9},{9,8},{10,11... | collective-permute-start | bytes 1572872 | tf_op jit(solution)/shard_map/ppermute | solution.py:785
  50.8 18.0 %collective-permute-start.10 = (bf16[8,64,512]{2,1,0:T(8,128)(2,1)}, bf16[8,64,512]{2,1,0:T(8,128)(2,1)}, u32[]{:S(2)}, u32[]{:S(2)}) collective-permute-start(bf16[8,64,512]{2,1,0:T(8,128)(2,1)} %collective-permute-done.8.refs_10_), channel_id=1, source_target_pairs={{0,1},{1,0},{2,3},{3,2},{4,5},{5,4},{6,7},{7,6},{8,9},{9,8},{10,11... | collective-permute-start | bytes 1572872 | tf_op jit(solution)/shard_map/ppermute | solution.py:785
  59.4 7.8 %collective-permute-start.6 = (bf16[64,2048]{1,0:T(8,128)(2,1)S(1)}, bf16[64,2048]{1,0:T(8,128)(2,1)S(1)}, u32[]{:S(2)}, u32[]{:S(2)}) collective-permute-start(bf16[64,2048]{1,0:T(8,128)(2,1)S(1)} %slice.44), channel_id=1, source_target_pairs={{0,8},{8,16},{16,24},{24,28},{28,20},{20,12},{12,4},{4,0},{1,9},{9... | collective-permute-start | bytes 786440 | tf_op jit(solution)/shard_map/ppermute | solution.py:721
  62.3 6.5 %collective-permute-start.7 = (bf16[64,2048]{1,0:T(8,128)(2,1)S(1)}, bf16[64,2048]{1,0:T(8,128)(2,1)}, u32[]{:S(2)}, u32[]{:S(2)}) collective-permute-start(bf16[64,2048]{1,0:T(8,128)(2,1)S(1)} %slice.45), channel_id=1, source_target_pairs={{0,4},{8,0},{16,8},{24,16},{28,24},{20,28},{12,20},{4,12},{1,5},{9... | collective-permute-start | bytes 786440 | tf_op jit(solution)/shard_map/ppermute | solution.py:721
  68.8 23.9 %all-to-all-start.1 = ((bf16[8,64,512]{2,1,0:T(8,128)(2,1)}), bf16[8,64,512]{2,1,0:T(8,128)(2,1)}, u32[]{:S(2)}, u32[]{:S(2)}) async-start(bf16[8,64,512]{2,1,0:T(8,128)(2,1)} %split_columns.2), calls=%async_computation.1 | async-start | bytes 1048576 | tf_op jit(solution)/shard_map/all_to_all | solution.py:849
  73.0 64.6 %all-gather.6.cloned.1.call-start = ((), (), s32[]{:S(2)}) async-start(), calls=%async_computation.5 | async-start | bytes 2621440 | tf_op jit(solution)/shard_map/all_gather | solution.py:871
  73.0 17.5 %collective-permute-start.11 = (bf16[128,2048]{1,0:T(8,128)(2,1)}, bf16[128,2048]{1,0:T(8,128)(2,1)}, u32[]{:S(2)}, u32[]{:S(2)}) collective-permute-start(bf16[128,2048]{1,0:T(8,128)(2,1)} %fusion.7.refs_0_), channel_id=1, source_target_pairs={{0,8},{8,16},{16,24},{24,28},{28,20},{20,12},{12,4},{4,0},{1,9},{9... | collective-permute-start | bytes 1572872 | tf_op jit(solution)/shard_map/ppermute | solution.py:721
  74.9 17.8 %collective-permute-start.12 = (bf16[128,2048]{1,0:T(8,128)(2,1)}, bf16[128,2048]{1,0:T(8,128)(2,1)}, u32[]{:S(2)}, u32[]{:S(2)}) collective-permute-start(bf16[128,2048]{1,0:T(8,128)(2,1)} %fusion.7.refs_0_), channel_id=1, source_target_pairs={{0,4},{8,0},{16,8},{24,16},{28,24},{20,28},{12,20},{4,12},{1,5},{9... | collective-permute-start | bytes 1572872 | tf_op jit(solution)/shard_map/ppermute | solution.py:721
  92.7 56.1 %all-gather.4.cloned.1.call-start = ((), (), s32[]{:S(2)}) async-start(), calls=%async_computation.4 | async-start | bytes 2621440 | tf_op jit(solution)/shard_map/all_gather | solution.py:852
  93.5 25.0 %all-to-all-start.2 = ((bf16[8,176,128]{2,1,0:T(8,128)(2,1)}), bf16[8,176,128]{2,1,0:T(8,128)(2,1)S(1)}, u32[]{:S(2)}, u32[]{:S(2)}) async-start(bf16[8,176,128]{2,1,0:T(8,128)(2,1)} %get-tuple-element.127), calls=%async_computation.2 | async-start | bytes 720896 | tf_op jit(solution)/shard_map/all_to_all | solution.py:810
  99.9 16.2 %collective-permute-start.13 = (bf16[128,2048]{1,0:T(8,128)(2,1)}, bf16[128,2048]{1,0:T(8,128)(2,1)S(1)}, u32[]{:S(2)}, u32[]{:S(2)}) collective-permute-start(bf16[128,2048]{1,0:T(8,128)(2,1)} %collective-permute-done.11.refs_1_), channel_id=1, source_target_pairs={{0,8},{8,16},{16,24},{24,28},{28,20},{20,12},{12,4},{4,0},{1,9},{9... | collective-permute-start | bytes 1572872 | tf_op jit(solution)/shard_map/ppermute | solution.py:721
  101.9 16.6 %collective-permute-start.14 = (bf16[128,2048]{1,0:T(8,128)(2,1)}, bf16[128,2048]{1,0:T(8,128)(2,1)S(1)}, u32[]{:S(2)}, u32[]{:S(2)}) collective-permute-start(bf16[128,2048]{1,0:T(8,128)(2,1)} %collective-permute-done.12.refs_2_), channel_id=1, source_target_pairs={{0,4},{8,0},{16,8},{24,16},{28,24},{20,28},{12,20},{4,12},{1,5},{9... | collective-permute-start | bytes 1572872 | tf_op jit(solution)/shard_map/ppermute | solution.py:721
  116.1 32.7 %copy-start.18 = (bf16[128,2048]{1,0:T(8,128)(2,1)}, bf16[128,2048]{1,0:T(8,128)(2,1)S(1)}, u32[]{:S(2)}) copy-start(bf16[128,2048]{1,0:T(8,128)(2,1)S(1)} %collective-permute-done.13.refs_3_) | copy-start | bytes 1572868
  118.5 30.3 %copy-start.19 = (bf16[128,2048]{1,0:T(8,128)(2,1)}, bf16[128,2048]{1,0:T(8,128)(2,1)S(1)}, u32[]{:S(2)}) copy-start(bf16[128,2048]{1,0:T(8,128)(2,1)S(1)} %collective-permute-done.14.refs_4_) | copy-start | bytes 1572868
  118.5 19.0 %collective-permute-start.16 = (bf16[128,2048]{1,0:T(8,128)(2,1)S(1)}, bf16[128,2048]{1,0:T(8,128)(2,1)S(1)}, u32[]{:S(2)}, u32[]{:S(2)}) collective-permute-start(bf16[128,2048]{1,0:T(8,128)(2,1)S(1)} %collective-permute-done.13.refs_3_), channel_id=1, source_target_pairs={{0,8},{8,16},{16,24},{24,28},{28,20},{20,12},{12,4},{4,0},{1,9},{9... | collective-permute-start | bytes 1572872 | tf_op jit(solution)/shard_map/ppermute | solution.py:721
  121.5 16.0 %collective-permute-start.17 = (bf16[128,2048]{1,0:T(8,128)(2,1)S(1)}, bf16[128,2048]{1,0:T(8,128)(2,1)S(1)}, u32[]{:S(2)}, u32[]{:S(2)}) collective-permute-start(bf16[128,2048]{1,0:T(8,128)(2,1)S(1)} %collective-permute-done.14.refs_4_), channel_id=1, source_target_pairs={{0,4},{8,0},{16,8},{24,16},{28,24},{20,28},{12,20},{4,12},{1,5},{9... | collective-permute-start | bytes 1572872 | tf_op jit(solution)/shard_map/ppermute | solution.py:721
  124.2 12.4 %collective-permute-start.15 = (bf16[1,128,192]{2,1,0:T(8,128)(2,1)}, bf16[1,128,192]{2,1,0:T(8,128)(2,1)S(1)}, u32[]{:S(2)}, u32[]{:S(2)}) collective-permute-start(bf16[1,128,192]{2,1,0:T(8,128)(2,1)} %bitcast.66), channel_id=1, source_target_pairs={{0,16},{4,20},{8,24},{12,28},{16,0},{20,4},{24,8},{28,12},{1,17},{... | collective-permute-start | bytes 147464 | tf_op jit(solution)/shard_map/ppermute | solution.py:785
  137.6 10.3 %collective-permute-start.19 = (bf16[64,2048]{1,0:T(8,128)(2,1)S(1)}, bf16[64,2048]{1,0:T(8,128)(2,1)S(1)}, u32[]{:S(2)}, u32[]{:S(2)}) collective-permute-start(bf16[64,2048]{1,0:T(8,128)(2,1)S(1)} %slice.35), channel_id=1, source_target_pairs={{0,8},{8,16},{16,24},{24,28},{28,20},{20,12},{12,4},{4,0},{1,9},{9... | collective-permute-start | bytes 786440 | tf_op jit(solution)/shard_map/ppermute | solution.py:721
  137.7 10.2 %collective-permute-start.20 = (bf16[64,2048]{1,0:T(8,128)(2,1)S(1)}, bf16[64,2048]{1,0:T(8,128)(2,1)S(1)}, u32[]{:S(2)}, u32[]{:S(2)}) collective-permute-start(bf16[64,2048]{1,0:T(8,128)(2,1)S(1)} %slice.36), channel_id=1, source_target_pairs={{0,4},{8,0},{16,8},{24,16},{28,24},{20,28},{12,20},{4,12},{1,5},{9... | collective-permute-start | bytes 786440 | tf_op jit(solution)/shard_map/ppermute | solution.py:721
  139.7 8.1 %collective-permute-start.18 = (bf16[2,128,192]{2,1,0:T(8,128)(2,1)S(1)}, bf16[2,128,192]{2,1,0:T(8,128)(2,1)S(1)}, u32[]{:S(2)}, u32[]{:S(2)}) collective-permute-start(bf16[2,128,192]{2,1,0:T(8,128)(2,1)S(1)} %pad_maximum_fusion.7), channel_id=1, source_target_pairs={{0,8},{4,12},{8,0},{12,4},{16,24},{20,28},{24,16},{28,20},{1,9},{5... | collective-permute-start | bytes 294920 | tf_op jit(solution)/shard_map/ppermute | solution.py:785
  147.9 12.2 %collective-permute-start.21 = (bf16[4,128,192]{2,1,0:T(8,128)(2,1)S(1)}, bf16[4,128,192]{2,1,0:T(8,128)(2,1)S(1)}, u32[]{:S(2)}, u32[]{:S(2)}) collective-permute-start(bf16[4,128,192]{2,1,0:T(8,128)(2,1)S(1)} %pad_maximum_fusion.4), channel_id=1, source_target_pairs={{0,4},{4,0},{8,12},{12,8},{16,20},{20,16},{24,28},{28,24},{1,5},{5... | collective-permute-start | bytes 589832 | tf_op jit(solution)/shard_map/ppermute | solution.py:785
  160.1 46.9 %copy-start.13 = (bf16[512,2048]{1,0:T(8,128)(2,1)S(1)}, bf16[512,2048]{1,0:T(8,128)(2,1)}, u32[]{:S(2)}) copy-start(bf16[512,2048]{1,0:T(8,128)(2,1)} %all-gather.4.cloned.1.call-done.refs_9_) | copy-start | bytes 6291460
  202.6 16.0 %all-to-all-start.3 = ((bf16[8,192,128]{2,1,0:T(8,128)(2,1)}), bf16[8,192,128]{2,1,0:T(8,128)(2,1)S(1)}, u32[]{:S(2)}, u32[]{:S(2)}) async-start(bf16[8,192,128]{2,1,0:T(8,128)(2,1)} %get-tuple-element.156), calls=%async_computation.3 | async-start | bytes 786432 | tf_op jit(solution)/shard_map/all_to_all | solution.py:810
  212.7 15.6 %collective-permute-start.23 = (bf16[64,2048]{1,0:T(8,128)(2,1)S(1)}, bf16[64,2048]{1,0:T(8,128)(2,1)S(1)}, u32[]{:S(2)}, u32[]{:S(2)}) collective-permute-start(bf16[64,2048]{1,0:T(8,128)(2,1)S(1)} %get-tuple-element.215), channel_id=1, source_target_pairs={{0,8},{8,16},{16,24},{24,28},{28,20},{20,12},{12,4},{4,0},{1,9},{9... | collective-permute-start | bytes 786440 | tf_op jit(solution)/shard_map/ppermute | solution.py:721
  214.8 13.6 %collective-permute-start.24 = (bf16[64,2048]{1,0:T(8,128)(2,1)S(1)}, bf16[64,2048]{1,0:T(8,128)(2,1)S(1)}, u32[]{:S(2)}, u32[]{:S(2)}) collective-permute-start(bf16[64,2048]{1,0:T(8,128)(2,1)S(1)} %get-tuple-element.214), channel_id=1, source_target_pairs={{0,4},{8,0},{16,8},{24,16},{28,24},{20,28},{12,20},{4,12},{1,5},{9... | collective-permute-start | bytes 786440 | tf_op jit(solution)/shard_map/ppermute | solution.py:721
  221.9 5.6 %collective-permute-start.22 = (bf16[1,128,192]{2,1,0:T(8,128)(2,1)}, bf16[1,128,192]{2,1,0:T(8,128)(2,1)S(1)}, u32[]{:S(2)}, u32[]{:S(2)}) collective-permute-start(bf16[1,128,192]{2,1,0:T(8,128)(2,1)} %bitcast.64), channel_id=1, source_target_pairs={{0,16},{4,20},{8,24},{12,28},{16,0},{20,4},{24,8},{28,12},{1,17},{... | collective-permute-start | bytes 147464 | tf_op jit(solution)/shard_map/ppermute | solution.py:785
  228.3 5.9 %collective-permute-start.25 = (bf16[2,128,192]{2,1,0:T(8,128)(2,1)S(1)}, bf16[2,128,192]{2,1,0:T(8,128)(2,1)S(1)}, u32[]{:S(2)}, u32[]{:S(2)}) collective-permute-start(bf16[2,128,192]{2,1,0:T(8,128)(2,1)S(1)} %pad_maximum_fusion.8), channel_id=1, source_target_pairs={{0,8},{4,12},{8,0},{12,4},{16,24},{20,28},{24,16},{28,20},{1,9},{5... | collective-permute-start | bytes 294920 | tf_op jit(solution)/shard_map/ppermute | solution.py:785
  229.8 16.8 %collective-permute-start.27 = (bf16[128,2048]{1,0:T(8,128)(2,1)S(1)}, bf16[128,2048]{1,0:T(8,128)(2,1)S(1)}, u32[]{:S(2)}, u32[]{:S(2)}) collective-permute-start(bf16[128,2048]{1,0:T(8,128)(2,1)S(1)} %get-tuple-element.213), channel_id=1, source_target_pairs={{0,8},{8,16},{16,24},{24,28},{28,20},{20,12},{12,4},{4,0},{1,9},{9... | collective-permute-start | bytes 1572872 | tf_op jit(solution)/shard_map/ppermute | solution.py:721
  231.9 14.8 %collective-permute-start.28 = (bf16[128,2048]{1,0:T(8,128)(2,1)S(1)}, bf16[128,2048]{1,0:T(8,128)(2,1)S(1)}, u32[]{:S(2)}, u32[]{:S(2)}) collective-permute-start(bf16[128,2048]{1,0:T(8,128)(2,1)S(1)} %get-tuple-element.212), channel_id=1, source_target_pairs={{0,4},{8,0},{16,8},{24,16},{28,24},{20,28},{12,20},{4,12},{1,5},{9... | collective-permute-start | bytes 1572872 | tf_op jit(solution)/shard_map/ppermute | solution.py:721
  234.3 11.4 %collective-permute-start.26 = (bf16[4,128,192]{2,1,0:T(8,128)(2,1)S(1)}, bf16[4,128,192]{2,1,0:T(8,128)(2,1)S(1)}, u32[]{:S(2)}, u32[]{:S(2)}) collective-permute-start(bf16[4,128,192]{2,1,0:T(8,128)(2,1)S(1)} %pad_maximum_fusion.5), channel_id=1, source_target_pairs={{0,4},{4,0},{8,12},{12,8},{16,20},{20,16},{24,28},{28,24},{1,5},{5... | collective-permute-start | bytes 589832 | tf_op jit(solution)/shard_map/ppermute | solution.py:785
  248.2 21.0 %collective-permute-start.29 = (bf16[128,2048]{1,0:T(8,128)(2,1)S(1)}, bf16[128,2048]{1,0:T(8,128)(2,1)S(1)}, u32[]{:S(2)}, u32[]{:S(2)}) collective-permute-start(bf16[128,2048]{1,0:T(8,128)(2,1)S(1)} %get-tuple-element.211), channel_id=1, source_target_pairs={{0,8},{8,16},{16,24},{24,28},{28,20},{20,12},{12,4},{4,0},{1,9},{9... | collective-permute-start | bytes 1572872 | tf_op jit(solution)/shard_map/ppermute | solution.py:721
  248.3 21.0 %collective-permute-start.30 = (bf16[128,2048]{1,0:T(8,128)(2,1)S(1)}, bf16[128,2048]{1,0:T(8,128)(2,1)S(1)}, u32[]{:S(2)}, u32[]{:S(2)}) collective-permute-start(bf16[128,2048]{1,0:T(8,128)(2,1)S(1)} %get-tuple-element.210), channel_id=1, source_target_pairs={{0,4},{8,0},{16,8},{24,16},{28,24},{20,28},{12,20},{4,12},{1,5},{9... | collective-permute-start | bytes 1572872 | tf_op jit(solution)/shard_map/ppermute | solution.py:721
  270.4 13.5 %collective-permute-start.32 = (bf16[64,2048]{1,0:T(8,128)(2,1)S(1)}, bf16[64,2048]{1,0:T(8,128)(2,1)S(1)}, u32[]{:S(2)}, u32[]{:S(2)}) collective-permute-start(bf16[64,2048]{1,0:T(8,128)(2,1)S(1)} %get-tuple-element.209), channel_id=1, source_target_pairs={{0,8},{8,16},{16,24},{24,28},{28,20},{20,12},{12,4},{4,0},{1,9},{9... | collective-permute-start | bytes 786440 | tf_op jit(solution)/shard_map/ppermute | solution.py:721
  270.4 13.4 %collective-permute-start.33 = (bf16[64,2048]{1,0:T(8,128)(2,1)S(1)}, bf16[64,2048]{1,0:T(8,128)(2,1)S(1)}, u32[]{:S(2)}, u32[]{:S(2)}) collective-permute-start(bf16[64,2048]{1,0:T(8,128)(2,1)S(1)} %get-tuple-element.208), channel_id=1, source_target_pairs={{0,4},{8,0},{16,8},{24,16},{28,24},{20,28},{12,20},{4,12},{1,5},{9... | collective-permute-start | bytes 786440 | tf_op jit(solution)/shard_map/ppermute | solution.py:721
  272.5 10.5 %collective-permute-start.31 = (bf16[1,30,16,128]{3,2,1,0:T(8,128)(2,1)}, bf16[1,30,16,128]{3,2,1,0:T(8,128)(2,1)S(1)}, u32[]{:S(2)}, u32[]{:S(2)}) collective-permute-start(bf16[1,30,16,128]{3,2,1,0:T(8,128)(2,1)} %bitcast.70), channel_id=1, source_target_pairs={{0,16},{4,20},{8,24},{12,28},{16,0},{20,4},{24,8},{28,12},{1,17},{... | collective-permute-start | bytes 368648 | tf_op jit(solution)/shard_map/ppermute | solution.py:785
  285.3 19.9 %collective-permute-start.35 = (bf16[128,2048]{1,0:T(8,128)(2,1)S(1)}, bf16[128,2048]{1,0:T(8,128)(2,1)S(1)}, u32[]{:S(2)}, u32[]{:S(2)}) collective-permute-start(bf16[128,2048]{1,0:T(8,128)(2,1)S(1)} %get-tuple-element.207), channel_id=1, source_target_pairs={{0,8},{8,16},{16,24},{24,28},{28,20},{20,12},{12,4},{4,0},{1,9},{9... | collective-permute-start | bytes 1572872 | tf_op jit(solution)/shard_map/ppermute | solution.py:721
  286.4 18.8 %collective-permute-start.36 = (bf16[128,2048]{1,0:T(8,128)(2,1)S(1)}, bf16[128,2048]{1,0:T(8,128)(2,1)S(1)}, u32[]{:S(2)}, u32[]{:S(2)}) collective-permute-start(bf16[128,2048]{1,0:T(8,128)(2,1)S(1)} %get-tuple-element.206), channel_id=1, source_target_pairs={{0,4},{8,0},{16,8},{24,16},{28,24},{20,28},{12,20},{4,12},{1,5},{9... | collective-permute-start | bytes 1572872 | tf_op jit(solution)/shard_map/ppermute | solution.py:721
  287.4 16.8 %collective-permute-start.34 = (bf16[2,30,16,128]{3,2,1,0:T(8,128)(2,1)S(1)}, bf16[2,30,16,128]{3,2,1,0:T(8,128)(2,1)}, u32[]{:S(2)}, u32[]{:S(2)}) collective-permute-start(bf16[2,30,16,128]{3,2,1,0:T(8,128)(2,1)S(1)} %pad_maximum_fusion.6), channel_id=1, source_target_pairs={{0,8},{4,12},{8,0},{12,4},{16,24},{20,28},{24,16},{28,20},{1,9},{5... | collective-permute-start | bytes 737288 | tf_op jit(solution)/shard_map/ppermute | solution.py:785
  305.2 22.5 %copy-start.23 = (bf16[12,16,128]{2,1,0:T(8,128)(2,1)S(1)}, bf16[12,16,128]{2,1,0:T(8,128)(2,1)}, u32[]{:S(2)}) copy-start(bf16[12,16,128]{2,1,0:T(8,128)(2,1)} %get-tuple-element.182) | copy-start | bytes 147460
  305.2 14.2 %collective-permute-start.37 = (bf16[4,30,16,128]{3,2,1,0:T(8,128)(2,1)S(1)}, bf16[4,30,16,128]{3,2,1,0:T(8,128)(2,1)S(1)}, u32[]{:S(2)}, u32[]{:S(2)}) collective-permute-start(bf16[4,30,16,128]{3,2,1,0:T(8,128)(2,1)S(1)} %pad_maximum_fusion.3), channel_id=1, source_target_pairs={{0,4},{4,0},{8,12},{12,8},{16,20},{20,16},{24,28},{28,24},{1,5},{5... | collective-permute-start | bytes 1474568 | tf_op jit(solution)/shard_map/ppermute | solution.py:785
  306.9 22.5 %copy-start.4 = (bf16[1024,2048]{1,0:T(8,128)(2,1)S(1)}, bf16[1024,2048]{1,0:T(8,128)(2,1)}, u32[]{:S(2)}) copy-start(bf16[1024,2048]{1,0:T(8,128)(2,1)} %get-tuple-element.174) | copy-start | bytes 12582916
  306.9 20.6 %collective-permute-start.38 = (bf16[128,2048]{1,0:T(8,128)(2,1)S(1)}, bf16[128,2048]{1,0:T(8,128)(2,1)S(1)}, u32[]{:S(2)}, u32[]{:S(2)}) collective-permute-start(bf16[128,2048]{1,0:T(8,128)(2,1)S(1)} %get-tuple-element.205), channel_id=1, source_target_pairs={{0,8},{8,16},{16,24},{24,28},{28,20},{20,12},{12,4},{4,0},{1,9},{9... | collective-permute-start | bytes 1572872 | tf_op jit(solution)/shard_map/ppermute | solution.py:721
  308.7 18.9 %collective-permute-start.39 = (bf16[128,2048]{1,0:T(8,128)(2,1)S(1)}, bf16[128,2048]{1,0:T(8,128)(2,1)S(1)}, u32[]{:S(2)}, u32[]{:S(2)}) collective-permute-start(bf16[128,2048]{1,0:T(8,128)(2,1)S(1)} %get-tuple-element.204), channel_id=1, source_target_pairs={{0,4},{8,0},{16,8},{24,16},{28,24},{20,28},{12,20},{4,12},{1,5},{9... | collective-permute-start | bytes 1572872 | tf_op jit(solution)/shard_map/ppermute | solution.py:721
  310.6 21.2 %copy-start.20 = (bf16[128,192]{1,0:T(8,128)(2,1)S(1)}, bf16[128,192]{1,0:T(8,128)(2,1)}, u32[]{:S(2)}) copy-start(bf16[128,192]{1,0:T(8,128)(2,1)} %share_back.1) | copy-start | bytes 147460
  310.6 22.4 %collective-permute-start.44 = (bf16[128,2048]{1,0:T(8,128)(2,1)S(1)}, bf16[128,2048]{1,0:T(8,128)(2,1)S(1)}, u32[]{:S(2)}, u32[]{:S(2)}) collective-permute-start(bf16[128,2048]{1,0:T(8,128)(2,1)S(1)} %get-tuple-element.201), channel_id=1, source_target_pairs={{0,4},{8,0},{16,8},{24,16},{28,24},{20,28},{12,20},{4,12},{1,5},{9... | collective-permute-start | bytes 1572872 | tf_op jit(solution)/shard_map/ppermute | solution.py:721
  312.6 20.5 %collective-permute-start.43 = (bf16[128,2048]{1,0:T(8,128)(2,1)S(1)}, bf16[128,2048]{1,0:T(8,128)(2,1)S(1)}, u32[]{:S(2)}, u32[]{:S(2)}) collective-permute-start(bf16[128,2048]{1,0:T(8,128)(2,1)S(1)} %get-tuple-element.200), channel_id=1, source_target_pairs={{0,8},{8,16},{16,24},{24,28},{28,20},{20,12},{12,4},{4,0},{1,9},{9... | collective-permute-start | bytes 1572872 | tf_op jit(solution)/shard_map/ppermute | solution.py:721
  327.8 11.3 %collective-permute-start.40 = (bf16[140,16,128]{2,1,0:T(8,128)(2,1)S(1)}, bf16[140,16,128]{2,1,0:T(8,128)(2,1)S(1)}, u32[]{:S(2)}, u32[]{:S(2)}) collective-permute-start(bf16[140,16,128]{2,1,0:T(8,128)(2,1)S(1)} %pad_maximum_fusion.1.refs_0_), channel_id=1, source_target_pairs={{0,2},{1,3},{2,0},{3,1},{4,6},{5,7},{6,4},{7,5},{8,10},{9,11},{10,... | collective-permute-start | bytes 1720328 | tf_op jit(solution)/shard_map/ppermute | solution.py:785
  329.8 9.2 %collective-permute-start.41 = (bf16[128,2048]{1,0:T(8,128)(2,1)S(1)}, bf16[128,2048]{1,0:T(8,128)(2,1)S(1)}, u32[]{:S(2)}, u32[]{:S(2)}) collective-permute-start(bf16[128,2048]{1,0:T(8,128)(2,1)S(1)} %get-tuple-element.203), channel_id=1, source_target_pairs={{0,8},{8,16},{16,24},{24,28},{28,20},{20,12},{12,4},{4,0},{1,9},{9... | collective-permute-start | bytes 1572872 | tf_op jit(solution)/shard_map/ppermute | solution.py:721
  329.8 9.2 %collective-permute-start.42 = (bf16[128,2048]{1,0:T(8,128)(2,1)S(1)}, bf16[128,2048]{1,0:T(8,128)(2,1)S(1)}, u32[]{:S(2)}, u32[]{:S(2)}) collective-permute-start(bf16[128,2048]{1,0:T(8,128)(2,1)S(1)} %get-tuple-element.202), channel_id=1, source_target_pairs={{0,4},{8,0},{16,8},{24,16},{28,24},{20,28},{12,20},{4,12},{1,5},{9... | collective-permute-start | bytes 1572872 | tf_op jit(solution)/shard_map/ppermute | solution.py:721
  339.5 2.6 collective-permute-start.46
  339.6 2.8 collective-permute-start.45
  (15 other events, 100.0 us)
Sparse Core Ops, SparseCore 0:
  92.8 24.3 all-gather.5
  118.8 22.5 all-gather.3

commit v4 on v3

--- a/solution.py
+++ b/solution.py
@@ -866,7 +866,7 @@
     low_in, x, conv_out, sums = project(
         meta, pieces, columns, in_down, in_up, conv_weight, conv_bias, state_proj, state_down, parts, groups
     )
-    sums, cot_ring.ends, mine_z = together(sums, cot_ring.ends, mine_z)
+    sums, mine_z = together(sums, mine_z)
     cot_ring.advance(hops)
     columns_z = lax.all_gather(mine_z, "fsdp")
     sums = exchange(sums, "seq")
@@ -903,16 +903,18 @@
     in_parts, wide, local, out_ring.ends = together(in_parts, wide, local, out_ring.ends)
     out_ring.advance(parts)
     in_ring = RingScatter(in_parts, parts, "seq")
-    held = wide[None]
+    span = cols.shape[1]
+    own = (3 * chans + span) // 128
+    held, down_grad = wide[:own], wide[own:]
     for bit in bits_of(parts):
         in_ring.advance(hops)
-        held = jnp.concatenate([held, swap(held, parts, bit, "seq")], 0)
-        held, in_ring.ends = together(held, in_ring.ends)
+        got = swap(jnp.concatenate([held, down_grad], 0), parts, bit, "seq")
+        count = held.shape[0]
+        held = jnp.concatenate([held, got[:count]], 0)
+        down_grad = (down_grad.astype(F32) + got[count:].astype(F32)).astype(BF16)
+        held, down_grad, in_ring.ends = together(held, down_grad, in_ring.ends)
     in_ring.advance(parts)
-    span = cols.shape[1]
-    own = (3 * chans + span) // 128
-    down_grad = held[:, own:].astype(F32).sum(0).astype(BF16)
-    chunks = [jnp.concatenate([held[:, :own].reshape(parts * own, rank, 128), down_grad, local], 0)]
+    chunks = [jnp.concatenate([held, down_grad, local], 0)]
     first, *others = bits_of(groups)
     chunks += [swap(chunks[0], groups, first, "fsdp")]
     branch = out_ring.total()

time: 357 us -> 343 us (0.961)
  waiting for transfers between devices: 125 us -> 107 us
    ppermute x15, waiting for transfers between devices: 61.3 us -> 38.3 us  [swap(): return lax.ppermute(value, axis, [(i, i ^ bit) for i in range(size)])]
    ppermute x32, waiting for transfers between devices: 51.2 us -> 57.8 us  [ring_send(): return lax.ppermute(value, axis, pairs)]
  transfers between devices with their start and end apart: 53 -> 53, of which waited for: 24 -> 27; matrix products, arithmetic and copies ran while one was open for 7% -> 8% of each run, Pallas kernels for 17% -> 17%
where the time goes in v4:
time: 343 us; the launch traced here: 342 us
  Pallas kernels  107 us (31%)
  waiting for transfers between devices  107 us (31%)
  starting transfers between devices  71.6 us (21%)
  other arithmetic  27.7 us (8%)
  between operations  16 us (5%)
  local copies, waits for them, and re-layouts  7.7 us (2%)
  matrix products  4.73 us (1%)
    ppermute x32, waiting for transfers between devices, ring_send(): return lax.ppermute(value, axis, pairs)  57.8 us
    pallas_call x1, Pallas kernels, scan(): pl.pallas_call(functools.partial(scan_kernel, sub=sub, ranks=ranks), grid...  41.6 us
    ppermute x32, starting transfers between devices, ring_send(): return lax.ppermute(value, axis, pairs)  39.3 us
    ppermute x15, waiting for transfers between devices, swap(): return lax.ppermute(value, axis, [(i, i ^ bit) for i in range(size)])  38.3 us
    pallas_call x1, Pallas kernels, finish(): pl.pallas_call(functools.partial(finish_kernel, ranks=ranks, states=state...  18.7 us
    pallas_call x1, Pallas kernels, project(): pl.pallas_call(functools.partial(project_kernel, parts=parts, groups=grou...  11.9 us
    ppermute x15, starting transfers between devices, swap(): return lax.ppermute(value, axis, [(i, i ^ bit) for i in range(size)])  11.9 us
    pallas_call x1, Pallas kernels, back_gate(): pl.pallas_call(functools.partial(back_gate_kernel, parts=parts), grid_spe...  11.3 us
  transfers between devices with their start and end apart: 53, of which 27 were waited for; matrix products, arithmetic and copies ran while one was open for 8% of the time, Pallas kernels for 17%

profile of v4, /device:TPU:0, one launch (start us, length us, event | category | flops | bytes accessed | tf_op | source)
XLA Modules:
  0.0 341.9 jit_solution(6139602063748239888)
XLA Ops:
  10.4 3.1 collective-permute-start
  13.4 1.9 split_columns.3
  15.3 6.3 %all-to-all-start = ((bf16[8,64,512]{2,1,0:T(8,128)(2,1)}), bf16[8,64,512]{2,1,0:T(8,128)(2,1)}, u32[]{:S(2)}, u32[]{:S(2)}) async-start(bf16[8,64,512]{2,1,0:T(8,128)(2,1)} %split_columns.3), calls=%async_computation | async-start | bytes 1048576 | tf_op jit(solution)/shard_map/all_to_all | solution.py:849
  21.6 1.3 convert_element_type.207.refs_15_.refs_32_
  24.1 1.3 broadcast_in_dim.45
  25.4 1.3 broadcast_in_dim.46
  27.3 1.9 split_columns.2
  30.4 2.1 collective-permute-start.2
  32.6 8.1 %all-to-all-done.refs_9_ = bf16[8,64,512]{2,1,0:T(8,128)(2,1)} async-done(((bf16[8,64,512]{2,1,0:T(8,128)(2,1)}), bf16[8,64,512]{2,1,0:T(8,128)(2,1)}, u32[]{:S(2)}, u32[]{:S(2)}) %all-to-all-start) | async-done | bytes 524320 | tf_op jit(solution)/shard_map/all_to_all | solution.py:849
  40.6 1.5 collective-permute-start.8
  42.2 2.6 collective-permute-done.2.refs_3_
  44.8 3.9 %collective-permute-start.4 = (bf16[128,2048]{1,0:T(8,128)(2,1)S(1)}, bf16[128,2048]{1,0:T(8,128)(2,1)S(1)}, u32[]{:S(2)}, u32[]{:S(2)}) collective-permute-start(bf16[128,2048]{1,0:T(8,128)(2,1)S(1)} %collective-permute-done.2.refs_3_), channel_id=1, source_target_pairs={{0,8},{8,16},{16,24},{24,28},{28,20},{20,12},{12,4},{4,0},{1,9},{9... | collective-permute-start | bytes 1572872 | tf_op jit(solution)/shard_map/ppermute | solution.py:721
  49.4 1.4 collective-permute-done.8.refs_10_
  50.8 8.6 %collective-permute-done.4.refs_5_ = bf16[128,2048]{1,0:T(8,128)(2,1)S(1)} collective-permute-done((bf16[128,2048]{1,0:T(8,128)(2,1)S(1)}, bf16[128,2048]{1,0:T(8,128)(2,1)S(1)}, u32[]{:S(2)}, u32[]{:S(2)}) %collective-permute-start.4) | collective-permute-done | bytes 524320 | tf_op jit(solution)/shard_map/ppermute | solution.py:721
  59.4 2.2 collective-permute-start.6
  62.4 2.0 fusion.7.refs_0_
  64.4 2.8 collective-permute-done.6.refs_7_
  67.2 1.6 collective-permute-done.7.refs_8_
  68.8 4.1 %all-to-all-start.1 = ((bf16[8,64,512]{2,1,0:T(8,128)(2,1)}), bf16[8,64,512]{2,1,0:T(8,128)(2,1)}, u32[]{:S(2)}, u32[]{:S(2)}) async-start(bf16[8,64,512]{2,1,0:T(8,128)(2,1)} %split_columns.2), calls=%async_computation.1 | async-start | bytes 1048576 | tf_op jit(solution)/shard_map/all_to_all | solution.py:849
  73.1 11.9 %project.1 = (bf16[1024,16]{1,0:T(8,128)(2,1)}, bf16[1024,512]{1,0:T(8,128)(2,1)}, bf16[1024,512]{1,0:T(8,128)(2,1)}, bf16[8,176,128]{2,1,0:T(8,128)(2,1)}) custom-call(s32[3]{0:T(128)} %pad_add_fusion.meta, bf16[128,2048]{1,0:T(8,128)(2,1)} %copy-done, bf16[128,2048]{1,0:T(8,128)(2,1)} %copy-done.5, bf16[128,2048]{1,0:T(8,128)(2,1)} %copy-done.6, ...), custom_call_target="tpu_custom_call" | custom-call | tf_op jit(solution)/shard_map/project/pallas_call | solution.py:246
  85.8 1.9 collective-permute-start.11
  87.9 5.8 %all-to-all-start.2 = ((bf16[8,176,128]{2,1,0:T(8,128)(2,1)}), bf16[8,176,128]{2,1,0:T(8,128)(2,1)S(1)}, u32[]{:S(2)}, u32[]{:S(2)}) async-start(bf16[8,176,128]{2,1,0:T(8,128)(2,1)} %get-tuple-element.127), calls=%async_computation.2 | async-start | bytes 720896 | tf_op jit(solution)/shard_map/all_to_all | solution.py:810
  93.7 7.6 %collective-permute-done.11.refs_1_ = bf16[128,2048]{1,0:T(8,128)(2,1)S(1)} collective-permute-done((bf16[128,2048]{1,0:T(8,128)(2,1)}, bf16[128,2048]{1,0:T(8,128)(2,1)S(1)}, u32[]{:S(2)}, u32[]{:S(2)}) %collective-permute-start.11) | collective-permute-done | bytes 524320 | tf_op jit(solution)/shard_map/ppermute | solution.py:721
  101.4 2.9 collective-permute-start.12
  104.4 8.8 %collective-permute-done.12.refs_3_ = bf16[128,2048]{1,0:T(8,128)(2,1)S(1)} collective-permute-done((bf16[128,2048]{1,0:T(8,128)(2,1)S(1)}, bf16[128,2048]{1,0:T(8,128)(2,1)S(1)}, u32[]{:S(2)}, u32[]{:S(2)}) %collective-permute-start.12) | collective-permute-done | bytes 524320 | tf_op jit(solution)/shard_map/ppermute | solution.py:721
  113.2 2.2 collective-permute-done.14.refs_4_
  116.2 3.7 %collective-permute-start.16 = (bf16[128,2048]{1,0:T(8,128)(2,1)S(1)}, bf16[128,2048]{1,0:T(8,128)(2,1)S(1)}, u32[]{:S(2)}, u32[]{:S(2)}) collective-permute-start(bf16[128,2048]{1,0:T(8,128)(2,1)S(1)} %collective-permute-done.12.refs_3_), channel_id=1, source_target_pairs={{0,8},{8,16},{16,24},{24,28},{28,20},{20,12},{12,4},{4,0},{1,9},{9... | collective-permute-start | bytes 1572872 | tf_op jit(solution)/shard_map/ppermute | solution.py:721
  119.9 2.7 share.1
  122.6 2.0 collective-permute-start.15
  124.6 9.5 %collective-permute-done.15 = bf16[1,128,192]{2,1,0:T(8,128)(2,1)S(1)} collective-permute-done((bf16[1,128,192]{2,1,0:T(8,128)(2,1)}, bf16[1,128,192]{2,1,0:T(8,128)(2,1)S(1)}, u32[]{:S(2)}, u32[]{:S(2)}) %collective-permute-start.15) | collective-permute-done | bytes 49184 | tf_op jit(solution)/shard_map/ppermute | solution.py:785
  135.2 2.1 collective-permute-start.20
  137.3 8.0 %gate.1.z_ref = bf16[1024,512]{1,0:T(8,128)(2,1)} custom-call(s32[3]{0:T(128)} %pad_add_fusion.meta, bf16[128,2048]{1,0:T(8,128)(2,1)} %copy-done, bf16[128,2048]{1,0:T(8,128)(2,1)} %copy-done.5, bf16[128,2048]{1,0:T(8,128)(2,1)} %copy-done.6, bf16[128,2048]{1,0:T(8,128)(2,1)} %copy-done.7, bf16[128,2048]{1,0:T(8,128)(2,1)} %collective-permute-done.3.refs_4_, ...), custom_call_target="tpu_custom_call" | custom-call | tf_op jit(solution)/shard_map/gate/pallas_call | solution.py:179
  146.1 11.3 %back_gate.1 = (bf16[1024,16]{1,0:T(8,128)(2,1)}, bf16[1024,256]{1,0:T(8,128)(2,1)}, bf16[1024,512]{1,0:T(8,128)(2,1)}) custom-call(s32[3]{0:T(128)} %pad_add_fusion.meta, bf16[128,2048]{1,0:T(8,128)(2,1)} %fusion.7.refs_0_, bf16[128,2048]{1,0:T(8,128)(2,1)} %copy-done.18, bf16[128,2048]{1,0:T(8,128)(2,1)} %copy-done.19, bf16[128,2048]{1,0:T(8,128)(2,1)} %copy-done.20, ...), custom_call_target="tpu_custom_call" | custom-call | tf_op jit(solution)/shard_map/back_gate/pallas_call | solution.py:222
  159.4 41.6 %scan.1 = (bf16[1024,512]{1,0:T(8,128)(2,1)}, bf16[1024,512]{1,0:T(8,128)(2,1)}, f32[1024,512]{1,0:T(8,128)}, bf16[1024,512]{1,0:T(8,128)(2,1)}, bf16[8,192,128]{2,1,0:T(8,128)(2,1)}) custom-call(s32[3]{0:T(128)} %pad_add_fusion.meta, bf16[8,128,192]{2,1,0:T(8,128)(2,1)} %copy-done.9, bf16[1024,512]{1,0:T(8,128)(2,1)} %get-tuple-element.139.u_ref.refs_21_, ...), custom_call_target="tpu_custom_call" | custom-call | tf_op jit(solution)/shard_map/scan/pallas_call | solution.py:476
  200.9 4.1 %all-to-all-start.3 = ((bf16[8,192,128]{2,1,0:T(8,128)(2,1)}), bf16[8,192,128]{2,1,0:T(8,128)(2,1)S(1)}, u32[]{:S(2)}, u32[]{:S(2)}) async-start(bf16[8,192,128]{2,1,0:T(8,128)(2,1)} %get-tuple-element.155), calls=%async_computation.3 | async-start | bytes 786432 | tf_op jit(solution)/shard_map/all_to_all | solution.py:810
  205.1 3.6 %convolution_convert_fusion = bf16[1024,2048]{1,0:T(8,128)(2,1)S(1)} fusion(bf16[1024,512]{1,0:T(8,128)(2,1)} %get-tuple-element.156.refs_23_, bf16[512,2048]{1,0:T(8,128)(2,1)S(1)} %copy-done.13), kind=kOutput, calls=%fused_computation | convolution fusion | flops 2149580800 | bytes 7340032 | tf_op jit(solution)/shard_map/dot_general | solution.py:28
  208.7 2.0 copy-done.8
  210.7 2.1 collective-permute-start.23
  212.8 2.5 all-to-all-done.3.got_ref
  216.1 2.6 share_back.1
  219.6 5.9 %collective-permute-done.22 = bf16[1,128,192]{2,1,0:T(8,128)(2,1)S(1)} collective-permute-done((bf16[1,128,192]{2,1,0:T(8,128)(2,1)}, bf16[1,128,192]{2,1,0:T(8,128)(2,1)S(1)}, u32[]{:S(2)}, u32[]{:S(2)}) %collective-permute-start.22) | collective-permute-done | bytes 49184 | tf_op jit(solution)/shard_map/ppermute | solution.py:785
  226.7 1.4 add_convert_fusion.10
  228.0 1.9 collective-permute-start.27
  230.1 1.3 collective-permute-done.25
  232.7 13.0 %collective-permute-done.26 = bf16[4,128,192]{2,1,0:T(8,128)(2,1)S(1)} collective-permute-done((bf16[4,128,192]{2,1,0:T(8,128)(2,1)S(1)}, bf16[4,128,192]{2,1,0:T(8,128)(2,1)S(1)}, u32[]{:S(2)}, u32[]{:S(2)}) %collective-permute-start.26) | collective-permute-done | bytes 196640 | tf_op jit(solution)/shard_map/ppermute | solution.py:785
  246.6 1.6 add_convert_fusion.8
  248.2 2.1 collective-permute-start.30
  250.3 18.7 %finish.1 = (bf16[1024,2048]{1,0:T(8,128)(2,1)}, bf16[30,16,128]{2,1,0:T(8,128)(2,1)}, bf16[12,16,128]{2,1,0:T(8,128)(2,1)}) custom-call(s32[3]{0:T(128)} %pad_add_fusion.meta, bf16[128,2048]{1,0:T(8,128)(2,1)} %copy-done, bf16[128,2048]{1,0:T(8,128)(2,1)} %copy-done.5, bf16[128,2048]{1,0:T(8,128)(2,1)} %copy-done.6, bf16[128,2048]{1,0:T(8,128)(2,1)} %copy-done.7, ...), custom_call_target="tpu_custom_call" | custom-call | tf_op jit(solution)/shard_map/finish/pallas_call | solution.py:620
  272.1 2.1 collective-permute-start.32
  274.2 3.1 collective-permute-done.31
  281.6 1.4 add_convert_fusion.6
  283.1 1.7 collective-permute-start.35
  285.2 3.8 %collective-permute-done.34 = bf16[44,16,128]{2,1,0:T(8,128)(2,1)S(1)} collective-permute-done((bf16[44,16,128]{2,1,0:T(8,128)(2,1)}, bf16[44,16,128]{2,1,0:T(8,128)(2,1)S(1)}, u32[]{:S(2)}, u32[]{:S(2)}) %collective-permute-start.34) | collective-permute-done | bytes 180256 | tf_op jit(solution)/shard_map/ppermute | solution.py:785
  289.0 9.1 %collective-permute-done.35 = bf16[128,2048]{1,0:T(8,128)(2,1)S(1)} collective-permute-done((bf16[128,2048]{1,0:T(8,128)(2,1)S(1)}, bf16[128,2048]{1,0:T(8,128)(2,1)S(1)}, u32[]{:S(2)}, u32[]{:S(2)}) %collective-permute-start.35) | collective-permute-done | bytes 524320 | tf_op jit(solution)/shard_map/ppermute | solution.py:721
  298.1 2.1 collective-permute-done.36
  300.2 1.5 collective-permute-start.37
  301.7 1.6 add_convert_fusion.4
  303.6 1.8 collective-permute-start.39
  305.4 1.6 add_convert_fusion.1
  309.2 3.8 %collective-permute-done.38 = bf16[128,2048]{1,0:T(8,128)(2,1)S(1)} collective-permute-done((bf16[128,2048]{1,0:T(8,128)(2,1)S(1)}, bf16[128,2048]{1,0:T(8,128)(2,1)S(1)}, u32[]{:S(2)}, u32[]{:S(2)}) %collective-permute-start.38) | collective-permute-done | bytes 524320 | tf_op jit(solution)/shard_map/ppermute | solution.py:721
  313.0 1.6 collective-permute-start.40
  319.8 4.4 %collective-permute-done.41 = bf16[128,2048]{1,0:T(8,128)(2,1)S(1)} collective-permute-done((bf16[128,2048]{1,0:T(8,128)(2,1)S(1)}, bf16[128,2048]{1,0:T(8,128)(2,1)S(1)}, u32[]{:S(2)}, u32[]{:S(2)}) %collective-permute-start.41) | collective-permute-done | bytes 524320 | tf_op jit(solution)/shard_map/ppermute | solution.py:721
  326.4 2.0 fusion.6
  328.9 6.2 %place.1 = (f32[8,16,8192]{2,1,0:T(8,128)}, f32[8,16,4096]{2,1,0:T(8,128)}, f32[8,16,2048]{2,1,0:T(8,128)}, f32[8,16,2048]{2,1,0:T(8,128)}, f32[8,16,512]{2,1,0:...) custom-call(s32[7]{0:T(128)S(1)} %pad_add_fusion.1.meta, ...), custom_call_target="tpu_custom_call" | custom-call | tf_op jit(solution)/shard_map/place/pallas_call | solution.py:688
  (167 shorter events, 35.9 us)
Async XLA Ops:
  7.2 22.6 %copy-start.26 = (bf16[16,512]{1,0:T(8,128)(2,1)S(1)}, bf16[16,512]{1,0:T(8,128)(2,1)}, u32[]{:S(2)}) copy-start(bf16[16,512]{1,0:T(8,128)(2,1)} %param.34) | copy-start | bytes 49156
  10.4 62.7 %copy-start = (bf16[128,2048]{1,0:T(8,128)(2,1)}, bf16[128,2048]{1,0:T(8,128)(2,1)S(1)}, u32[]{:S(2)}) copy-start(bf16[128,2048]{1,0:T(8,128)(2,1)S(1)} %fusion.2.refs_0_) | copy-start | bytes 1572868
  10.4 20.1 %collective-permute-start = (bf16[128,2048]{1,0:T(8,128)(2,1)S(1)}, bf16[128,2048]{1,0:T(8,128)(2,1)S(1)}, u32[]{:S(2)}, u32[]{:S(2)}) collective-permute-start(bf16[128,2048]{1,0:T(8,128)(2,1)S(1)} %fusion.2.refs_0_), channel_id=1, source_target_pairs={{0,8},{8,16},{16,24},{24,28},{28,20},{20,12},{12,4},{4,0},{1,9},{9... | collective-permute-start | bytes 1572872 | tf_op jit(solution)/shard_map/ppermute | solution.py:721
  13.4 17.0 %collective-permute-start.1 = (bf16[128,2048]{1,0:T(8,128)(2,1)S(1)}, bf16[128,2048]{1,0:T(8,128)(2,1)S(1)}, u32[]{:S(2)}, u32[]{:S(2)}) collective-permute-start(bf16[128,2048]{1,0:T(8,128)(2,1)S(1)} %fusion.2.refs_0_), channel_id=1, source_target_pairs={{0,4},{8,0},{16,8},{24,16},{28,24},{20,28},{12,20},{4,12},{1,5},{9... | collective-permute-start | bytes 1572872 | tf_op jit(solution)/shard_map/ppermute | solution.py:721
  15.3 25.3 %all-to-all-start = ((bf16[8,64,512]{2,1,0:T(8,128)(2,1)}), bf16[8,64,512]{2,1,0:T(8,128)(2,1)}, u32[]{:S(2)}, u32[]{:S(2)}) async-start(bf16[8,64,512]{2,1,0:T(8,128)(2,1)} %split_columns.3), calls=%async_computation | async-start | bytes 1048576 | tf_op jit(solution)/shard_map/all_to_all | solution.py:849
  30.4 42.6 %copy-start.5 = (bf16[128,2048]{1,0:T(8,128)(2,1)}, bf16[128,2048]{1,0:T(8,128)(2,1)S(1)}, u32[]{:S(2)}) copy-start(bf16[128,2048]{1,0:T(8,128)(2,1)S(1)} %collective-permute-done.refs_1_) | copy-start | bytes 1572868
  30.4 42.6 %copy-start.6 = (bf16[128,2048]{1,0:T(8,128)(2,1)}, bf16[128,2048]{1,0:T(8,128)(2,1)S(1)}, u32[]{:S(2)}) copy-start(bf16[128,2048]{1,0:T(8,128)(2,1)S(1)} %collective-permute-done.1.refs_2_) | copy-start | bytes 1572868
  30.4 14.3 %collective-permute-start.2 = (bf16[128,2048]{1,0:T(8,128)(2,1)S(1)}, bf16[128,2048]{1,0:T(8,128)(2,1)S(1)}, u32[]{:S(2)}, u32[]{:S(2)}) collective-permute-start(bf16[128,2048]{1,0:T(8,128)(2,1)S(1)} %collective-permute-done.refs_1_), channel_id=1, source_target_pairs={{0,8},{8,16},{16,24},{24,28},{28,20},{20,12},{12,4},{4,0},{1,9},{9... | collective-permute-start | bytes 1572872 | tf_op jit(solution)/shard_map/ppermute | solution.py:721
  32.5 16.2 %collective-permute-start.3 = (bf16[128,2048]{1,0:T(8,128)(2,1)S(1)}, bf16[128,2048]{1,0:T(8,128)(2,1)}, u32[]{:S(2)}, u32[]{:S(2)}) collective-permute-start(bf16[128,2048]{1,0:T(8,128)(2,1)S(1)} %collective-permute-done.1.refs_2_), channel_id=1, source_target_pairs={{0,4},{8,0},{16,8},{24,16},{28,24},{20,28},{12,20},{4,12},{1,5},{9... | collective-permute-start | bytes 1572872 | tf_op jit(solution)/shard_map/ppermute | solution.py:721
  40.6 10.1 %collective-permute-start.8 = (bf16[8,64,512]{2,1,0:T(8,128)(2,1)}, bf16[8,64,512]{2,1,0:T(8,128)(2,1)}, u32[]{:S(2)}, u32[]{:S(2)}) collective-permute-start(bf16[8,64,512]{2,1,0:T(8,128)(2,1)} %all-to-all-done.refs_9_), channel_id=1, source_target_pairs={{0,2},{1,3},{2,0},{3,1},{4,6},{5,7},{6,4},{7,5},{8,10},{9,11},{10,... | collective-permute-start | bytes 1572872 | tf_op jit(solution)/shard_map/ppermute | solution.py:785
  44.8 28.3 %copy-start.7 = (bf16[128,2048]{1,0:T(8,128)(2,1)}, bf16[128,2048]{1,0:T(8,128)(2,1)S(1)}, u32[]{:S(2)}) copy-start(bf16[128,2048]{1,0:T(8,128)(2,1)S(1)} %collective-permute-done.2.refs_3_) | copy-start | bytes 1572868
  44.8 14.6 %collective-permute-start.4 = (bf16[128,2048]{1,0:T(8,128)(2,1)S(1)}, bf16[128,2048]{1,0:T(8,128)(2,1)S(1)}, u32[]{:S(2)}, u32[]{:S(2)}) collective-permute-start(bf16[128,2048]{1,0:T(8,128)(2,1)S(1)} %collective-permute-done.2.refs_3_), channel_id=1, source_target_pairs={{0,8},{8,16},{16,24},{24,28},{28,20},{20,12},{12,4},{4,0},{1,9},{9... | collective-permute-start | bytes 1572872 | tf_op jit(solution)/shard_map/ppermute | solution.py:721
  48.7 13.6 %collective-permute-start.5 = (bf16[128,2048]{1,0:T(8,128)(2,1)}, bf16[128,2048]{1,0:T(8,128)(2,1)S(1)}, u32[]{:S(2)}, u32[]{:S(2)}) collective-permute-start(bf16[128,2048]{1,0:T(8,128)(2,1)} %collective-permute-done.3.refs_4_), channel_id=1, source_target_pairs={{0,4},{8,0},{16,8},{24,16},{28,24},{20,28},{12,20},{4,12},{1,5},{9... | collective-permute-start | bytes 1572872 | tf_op jit(solution)/shard_map/ppermute | solution.py:721
  49.3 15.1 %collective-permute-start.9 = (bf16[8,64,512]{2,1,0:T(8,128)(2,1)}, bf16[8,64,512]{2,1,0:T(8,128)(2,1)S(1)}, u32[]{:S(2)}, u32[]{:S(2)}) collective-permute-start(bf16[8,64,512]{2,1,0:T(8,128)(2,1)} %all-to-all-done.refs_9_), channel_id=1, source_target_pairs={{0,1},{1,0},{2,3},{3,2},{4,5},{5,4},{6,7},{7,6},{8,9},{9,8},{10,11... | collective-permute-start | bytes 1572872 | tf_op jit(solution)/shard_map/ppermute | solution.py:785
  50.8 18.0 %collective-permute-start.10 = (bf16[8,64,512]{2,1,0:T(8,128)(2,1)}, bf16[8,64,512]{2,1,0:T(8,128)(2,1)}, u32[]{:S(2)}, u32[]{:S(2)}) collective-permute-start(bf16[8,64,512]{2,1,0:T(8,128)(2,1)} %collective-permute-done.8.refs_10_), channel_id=1, source_target_pairs={{0,1},{1,0},{2,3},{3,2},{4,5},{5,4},{6,7},{7,6},{8,9},{9,8},{10,11... | collective-permute-start | bytes 1572872 | tf_op jit(solution)/shard_map/ppermute | solution.py:785
  59.4 7.8 %collective-permute-start.6 = (bf16[64,2048]{1,0:T(8,128)(2,1)S(1)}, bf16[64,2048]{1,0:T(8,128)(2,1)S(1)}, u32[]{:S(2)}, u32[]{:S(2)}) collective-permute-start(bf16[64,2048]{1,0:T(8,128)(2,1)S(1)} %slice.69), channel_id=1, source_target_pairs={{0,8},{8,16},{16,24},{24,28},{28,20},{20,12},{12,4},{4,0},{1,9},{9... | collective-permute-start | bytes 786440 | tf_op jit(solution)/shard_map/ppermute | solution.py:721
  62.3 6.5 %collective-permute-start.7 = (bf16[64,2048]{1,0:T(8,128)(2,1)S(1)}, bf16[64,2048]{1,0:T(8,128)(2,1)}, u32[]{:S(2)}, u32[]{:S(2)}) collective-permute-start(bf16[64,2048]{1,0:T(8,128)(2,1)S(1)} %slice.70), channel_id=1, source_target_pairs={{0,4},{8,0},{16,8},{24,16},{28,24},{20,28},{12,20},{4,12},{1,5},{9... | collective-permute-start | bytes 786440 | tf_op jit(solution)/shard_map/ppermute | solution.py:721
  68.8 16.3 %all-to-all-start.1 = ((bf16[8,64,512]{2,1,0:T(8,128)(2,1)}), bf16[8,64,512]{2,1,0:T(8,128)(2,1)}, u32[]{:S(2)}, u32[]{:S(2)}) async-start(bf16[8,64,512]{2,1,0:T(8,128)(2,1)} %split_columns.2), calls=%async_computation.1 | async-start | bytes 1048576 | tf_op jit(solution)/shard_map/all_to_all | solution.py:849
  73.0 62.1 %all-gather.6.cloned.1.call-start = ((), (), s32[]{:S(2)}) async-start(), calls=%async_computation.5 | async-start | bytes 2621440 | tf_op jit(solution)/shard_map/all_gather | solution.py:871
  85.1 61.0 %all-gather.4.cloned.1.call-start = ((), (), s32[]{:S(2)}) async-start(), calls=%async_computation.4 | async-start | bytes 2621440 | tf_op jit(solution)/shard_map/all_gather | solution.py:852
  85.8 15.5 %collective-permute-start.11 = (bf16[128,2048]{1,0:T(8,128)(2,1)}, bf16[128,2048]{1,0:T(8,128)(2,1)S(1)}, u32[]{:S(2)}, u32[]{:S(2)}) collective-permute-start(bf16[128,2048]{1,0:T(8,128)(2,1)} %fusion.7.refs_0_), channel_id=1, source_target_pairs={{0,8},{8,16},{16,24},{24,28},{28,20},{20,12},{12,4},{4,0},{1,9},{9... | collective-permute-start | bytes 1572872 | tf_op jit(solution)/shard_map/ppermute | solution.py:721
  87.7 16.6 %collective-permute-start.13 = (bf16[128,2048]{1,0:T(8,128)(2,1)}, bf16[128,2048]{1,0:T(8,128)(2,1)S(1)}, u32[]{:S(2)}, u32[]{:S(2)}) collective-permute-start(bf16[128,2048]{1,0:T(8,128)(2,1)} %fusion.7.refs_0_), channel_id=1, source_target_pairs={{0,4},{8,0},{16,8},{24,16},{28,24},{20,28},{12,20},{4,12},{1,5},{9... | collective-permute-start | bytes 1572872 | tf_op jit(solution)/shard_map/ppermute | solution.py:721
  87.9 28.3 %all-to-all-start.2 = ((bf16[8,176,128]{2,1,0:T(8,128)(2,1)}), bf16[8,176,128]{2,1,0:T(8,128)(2,1)S(1)}, u32[]{:S(2)}, u32[]{:S(2)}) async-start(bf16[8,176,128]{2,1,0:T(8,128)(2,1)} %get-tuple-element.127), calls=%async_computation.2 | async-start | bytes 720896 | tf_op jit(solution)/shard_map/all_to_all | solution.py:810
  101.4 44.8 %copy-start.18 = (bf16[128,2048]{1,0:T(8,128)(2,1)}, bf16[128,2048]{1,0:T(8,128)(2,1)S(1)}, u32[]{:S(2)}) copy-start(bf16[128,2048]{1,0:T(8,128)(2,1)S(1)} %collective-permute-done.11.refs_1_) | copy-start | bytes 1572868
  101.4 11.9 %collective-permute-start.12 = (bf16[128,2048]{1,0:T(8,128)(2,1)S(1)}, bf16[128,2048]{1,0:T(8,128)(2,1)S(1)}, u32[]{:S(2)}, u32[]{:S(2)}) collective-permute-start(bf16[128,2048]{1,0:T(8,128)(2,1)S(1)} %collective-permute-done.11.refs_1_), channel_id=1, source_target_pairs={{0,8},{8,16},{16,24},{24,28},{28,20},{20,12},{12,4},{4,0},{1,9},{9... | collective-permute-start | bytes 1572872 | tf_op jit(solution)/shard_map/ppermute | solution.py:721
  104.3 41.8 %copy-start.19 = (bf16[128,2048]{1,0:T(8,128)(2,1)}, bf16[128,2048]{1,0:T(8,128)(2,1)S(1)}, u32[]{:S(2)}) copy-start(bf16[128,2048]{1,0:T(8,128)(2,1)S(1)} %collective-permute-done.13.refs_2_) | copy-start | bytes 1572868
  104.3 11.1 %collective-permute-start.14 = (bf16[128,2048]{1,0:T(8,128)(2,1)S(1)}, bf16[128,2048]{1,0:T(8,128)(2,1)S(1)}, u32[]{:S(2)}, u32[]{:S(2)}) collective-permute-start(bf16[128,2048]{1,0:T(8,128)(2,1)S(1)} %collective-permute-done.13.refs_2_), channel_id=1, source_target_pairs={{0,4},{8,0},{16,8},{24,16},{28,24},{20,28},{12,20},{4,12},{1,5},{9... | collective-permute-start | bytes 1572872 | tf_op jit(solution)/shard_map/ppermute | solution.py:721
  113.2 32.9 %copy-start.20 = (bf16[128,2048]{1,0:T(8,128)(2,1)}, bf16[128,2048]{1,0:T(8,128)(2,1)S(1)}, u32[]{:S(2)}) copy-start(bf16[128,2048]{1,0:T(8,128)(2,1)S(1)} %collective-permute-done.12.refs_3_) | copy-start | bytes 1572868
  116.2 18.8 %collective-permute-start.16 = (bf16[128,2048]{1,0:T(8,128)(2,1)S(1)}, bf16[128,2048]{1,0:T(8,128)(2,1)S(1)}, u32[]{:S(2)}, u32[]{:S(2)}) collective-permute-start(bf16[128,2048]{1,0:T(8,128)(2,1)S(1)} %collective-permute-done.12.refs_3_), channel_id=1, source_target_pairs={{0,8},{8,16},{16,24},{24,28},{28,20},{20,12},{12,4},{4,0},{1,9},{9... | collective-permute-start | bytes 1572872 | tf_op jit(solution)/shard_map/ppermute | solution.py:721
  119.9 15.1 %collective-permute-start.17 = (bf16[128,2048]{1,0:T(8,128)(2,1)}, bf16[128,2048]{1,0:T(8,128)(2,1)S(1)}, u32[]{:S(2)}, u32[]{:S(2)}) collective-permute-start(bf16[128,2048]{1,0:T(8,128)(2,1)} %copy-done.21), channel_id=1, source_target_pairs={{0,4},{8,0},{16,8},{24,16},{28,24},{20,28},{12,20},{4,12},{1,5},{9... | collective-permute-start | bytes 1572872 | tf_op jit(solution)/shard_map/ppermute | solution.py:721
  122.6 11.5 %collective-permute-start.15 = (bf16[1,128,192]{2,1,0:T(8,128)(2,1)}, bf16[1,128,192]{2,1,0:T(8,128)(2,1)S(1)}, u32[]{:S(2)}, u32[]{:S(2)}) collective-permute-start(bf16[1,128,192]{2,1,0:T(8,128)(2,1)} %bitcast.63), channel_id=1, source_target_pairs={{0,16},{4,20},{8,24},{12,28},{16,0},{20,4},{24,8},{28,12},{1,17},{... | collective-permute-start | bytes 147464 | tf_op jit(solution)/shard_map/ppermute | solution.py:785
  135.1 10.3 %collective-permute-start.19 = (bf16[64,2048]{1,0:T(8,128)(2,1)S(1)}, bf16[64,2048]{1,0:T(8,128)(2,1)S(1)}, u32[]{:S(2)}, u32[]{:S(2)}) collective-permute-start(bf16[64,2048]{1,0:T(8,128)(2,1)S(1)} %slice.54), channel_id=1, source_target_pairs={{0,8},{8,16},{16,24},{24,28},{28,20},{20,12},{12,4},{4,0},{1,9},{9... | collective-permute-start | bytes 786440 | tf_op jit(solution)/shard_map/ppermute | solution.py:721
  135.2 10.2 %collective-permute-start.20 = (bf16[64,2048]{1,0:T(8,128)(2,1)S(1)}, bf16[64,2048]{1,0:T(8,128)(2,1)}, u32[]{:S(2)}, u32[]{:S(2)}) collective-permute-start(bf16[64,2048]{1,0:T(8,128)(2,1)S(1)} %slice.55), channel_id=1, source_target_pairs={{0,4},{8,0},{16,8},{24,16},{28,24},{20,28},{12,20},{4,12},{1,5},{9... | collective-permute-start | bytes 786440 | tf_op jit(solution)/shard_map/ppermute | solution.py:721
  137.3 8.1 %collective-permute-start.18 = (bf16[2,128,192]{2,1,0:T(8,128)(2,1)S(1)}, bf16[2,128,192]{2,1,0:T(8,128)(2,1)S(1)}, u32[]{:S(2)}, u32[]{:S(2)}) collective-permute-start(bf16[2,128,192]{2,1,0:T(8,128)(2,1)S(1)} %pad_maximum_fusion.7), channel_id=1, source_target_pairs={{0,8},{4,12},{8,0},{12,4},{16,24},{20,28},{24,16},{28,20},{1,9},{5... | collective-permute-start | bytes 294920 | tf_op jit(solution)/shard_map/ppermute | solution.py:785
  145.4 12.1 %collective-permute-start.21 = (bf16[4,128,192]{2,1,0:T(8,128)(2,1)S(1)}, bf16[4,128,192]{2,1,0:T(8,128)(2,1)}, u32[]{:S(2)}, u32[]{:S(2)}) collective-permute-start(bf16[4,128,192]{2,1,0:T(8,128)(2,1)S(1)} %pad_maximum_fusion.3), channel_id=1, source_target_pairs={{0,4},{4,0},{8,12},{12,8},{16,20},{20,16},{24,28},{28,24},{1,5},{5... | collective-permute-start | bytes 589832 | tf_op jit(solution)/shard_map/ppermute | solution.py:785
  157.4 47.7 %copy-start.13 = (bf16[512,2048]{1,0:T(8,128)(2,1)S(1)}, bf16[512,2048]{1,0:T(8,128)(2,1)}, u32[]{:S(2)}) copy-start(bf16[512,2048]{1,0:T(8,128)(2,1)} %all-gather.4.cloned.1.call-done.refs_9_) | copy-start | bytes 6291460
  200.9 14.4 %all-to-all-start.3 = ((bf16[8,192,128]{2,1,0:T(8,128)(2,1)}), bf16[8,192,128]{2,1,0:T(8,128)(2,1)S(1)}, u32[]{:S(2)}, u32[]{:S(2)}) async-start(bf16[8,192,128]{2,1,0:T(8,128)(2,1)} %get-tuple-element.155), calls=%async_computation.3 | async-start | bytes 786432 | tf_op jit(solution)/shard_map/all_to_all | solution.py:810
  210.7 15.7 %collective-permute-start.23 = (bf16[64,2048]{1,0:T(8,128)(2,1)S(1)}, bf16[64,2048]{1,0:T(8,128)(2,1)S(1)}, u32[]{:S(2)}, u32[]{:S(2)}) collective-permute-start(bf16[64,2048]{1,0:T(8,128)(2,1)S(1)} %get-tuple-element.217), channel_id=1, source_target_pairs={{0,8},{8,16},{16,24},{24,28},{28,20},{20,12},{12,4},{4,0},{1,9},{9... | collective-permute-start | bytes 786440 | tf_op jit(solution)/shard_map/ppermute | solution.py:721
  212.8 13.6 %collective-permute-start.24 = (bf16[64,2048]{1,0:T(8,128)(2,1)S(1)}, bf16[64,2048]{1,0:T(8,128)(2,1)S(1)}, u32[]{:S(2)}, u32[]{:S(2)}) collective-permute-start(bf16[64,2048]{1,0:T(8,128)(2,1)S(1)} %get-tuple-element.216), channel_id=1, source_target_pairs={{0,4},{8,0},{16,8},{24,16},{28,24},{20,28},{12,20},{4,12},{1,5},{9... | collective-permute-start | bytes 786440 | tf_op jit(solution)/shard_map/ppermute | solution.py:721
  218.7 6.8 %collective-permute-start.22 = (bf16[1,128,192]{2,1,0:T(8,128)(2,1)}, bf16[1,128,192]{2,1,0:T(8,128)(2,1)S(1)}, u32[]{:S(2)}, u32[]{:S(2)}) collective-permute-start(bf16[1,128,192]{2,1,0:T(8,128)(2,1)} %bitcast.61), channel_id=1, source_target_pairs={{0,16},{4,20},{8,24},{12,28},{16,0},{20,4},{24,8},{28,12},{1,17},{... | collective-permute-start | bytes 147464 | tf_op jit(solution)/shard_map/ppermute | solution.py:785
  226.4 5.0 %collective-permute-start.25 = (bf16[2,128,192]{2,1,0:T(8,128)(2,1)S(1)}, bf16[2,128,192]{2,1,0:T(8,128)(2,1)S(1)}, u32[]{:S(2)}, u32[]{:S(2)}) collective-permute-start(bf16[2,128,192]{2,1,0:T(8,128)(2,1)S(1)} %pad_maximum_fusion.8), channel_id=1, source_target_pairs={{0,8},{4,12},{8,0},{12,4},{16,24},{20,28},{24,16},{28,20},{1,9},{5... | collective-permute-start | bytes 294920 | tf_op jit(solution)/shard_map/ppermute | solution.py:785
  228.0 18.6 %collective-permute-start.27 = (bf16[128,2048]{1,0:T(8,128)(2,1)S(1)}, bf16[128,2048]{1,0:T(8,128)(2,1)S(1)}, u32[]{:S(2)}, u32[]{:S(2)}) collective-permute-start(bf16[128,2048]{1,0:T(8,128)(2,1)S(1)} %get-tuple-element.215), channel_id=1, source_target_pairs={{0,8},{8,16},{16,24},{24,28},{28,20},{20,12},{12,4},{4,0},{1,9},{9... | collective-permute-start | bytes 1572872 | tf_op jit(solution)/shard_map/ppermute | solution.py:721
  229.9 16.7 %collective-permute-start.28 = (bf16[128,2048]{1,0:T(8,128)(2,1)S(1)}, bf16[128,2048]{1,0:T(8,128)(2,1)S(1)}, u32[]{:S(2)}, u32[]{:S(2)}) collective-permute-start(bf16[128,2048]{1,0:T(8,128)(2,1)S(1)} %get-tuple-element.214), channel_id=1, source_target_pairs={{0,4},{8,0},{16,8},{24,16},{28,24},{20,28},{12,20},{4,12},{1,5},{9... | collective-permute-start | bytes 1572872 | tf_op jit(solution)/shard_map/ppermute | solution.py:721
  231.5 14.2 %collective-permute-start.26 = (bf16[4,128,192]{2,1,0:T(8,128)(2,1)S(1)}, bf16[4,128,192]{2,1,0:T(8,128)(2,1)S(1)}, u32[]{:S(2)}, u32[]{:S(2)}) collective-permute-start(bf16[4,128,192]{2,1,0:T(8,128)(2,1)S(1)} %pad_maximum_fusion.4), channel_id=1, source_target_pairs={{0,4},{4,0},{8,12},{12,8},{16,20},{20,16},{24,28},{28,24},{1,5},{5... | collective-permute-start | bytes 589832 | tf_op jit(solution)/shard_map/ppermute | solution.py:785
  248.2 20.8 %collective-permute-start.29 = (bf16[128,2048]{1,0:T(8,128)(2,1)S(1)}, bf16[128,2048]{1,0:T(8,128)(2,1)S(1)}, u32[]{:S(2)}, u32[]{:S(2)}) collective-permute-start(bf16[128,2048]{1,0:T(8,128)(2,1)S(1)} %get-tuple-element.213), channel_id=1, source_target_pairs={{0,8},{8,16},{16,24},{24,28},{28,20},{20,12},{12,4},{4,0},{1,9},{9... | collective-permute-start | bytes 1572872 | tf_op jit(solution)/shard_map/ppermute | solution.py:721
  248.2 20.8 %collective-permute-start.30 = (bf16[128,2048]{1,0:T(8,128)(2,1)S(1)}, bf16[128,2048]{1,0:T(8,128)(2,1)S(1)}, u32[]{:S(2)}, u32[]{:S(2)}) collective-permute-start(bf16[128,2048]{1,0:T(8,128)(2,1)S(1)} %get-tuple-element.212), channel_id=1, source_target_pairs={{0,4},{8,0},{16,8},{24,16},{28,24},{20,28},{12,20},{4,12},{1,5},{9... | collective-permute-start | bytes 1572872 | tf_op jit(solution)/shard_map/ppermute | solution.py:721
  269.0 8.2 %collective-permute-start.31 = (bf16[30,16,128]{2,1,0:T(8,128)(2,1)}, bf16[30,16,128]{2,1,0:T(8,128)(2,1)S(1)}, u32[]{:S(2)}, u32[]{:S(2)}) collective-permute-start(bf16[30,16,128]{2,1,0:T(8,128)(2,1)} %get-tuple-element.172), channel_id=1, source_target_pairs={{0,16},{4,20},{8,24},{12,28},{16,0},{20,4},{24,8},{28,12},{1,17},{... | collective-permute-start | bytes 368648 | tf_op jit(solution)/shard_map/ppermute | solution.py:785
  272.1 7.3 %collective-permute-start.32 = (bf16[64,2048]{1,0:T(8,128)(2,1)S(1)}, bf16[64,2048]{1,0:T(8,128)(2,1)S(1)}, u32[]{:S(2)}, u32[]{:S(2)}) collective-permute-start(bf16[64,2048]{1,0:T(8,128)(2,1)S(1)} %get-tuple-element.211), channel_id=1, source_target_pairs={{0,8},{8,16},{16,24},{24,28},{28,20},{20,12},{12,4},{4,0},{1,9},{9... | collective-permute-start | bytes 786440 | tf_op jit(solution)/shard_map/ppermute | solution.py:721
  274.2 6.4 %collective-permute-start.33 = (bf16[64,2048]{1,0:T(8,128)(2,1)S(1)}, bf16[64,2048]{1,0:T(8,128)(2,1)S(1)}, u32[]{:S(2)}, u32[]{:S(2)}) collective-permute-start(bf16[64,2048]{1,0:T(8,128)(2,1)S(1)} %get-tuple-element.210), channel_id=1, source_target_pairs={{0,4},{8,0},{16,8},{24,16},{28,24},{20,28},{12,20},{4,12},{1,5},{9... | collective-permute-start | bytes 786440 | tf_op jit(solution)/shard_map/ppermute | solution.py:721
  281.2 7.7 %collective-permute-start.34 = (bf16[44,16,128]{2,1,0:T(8,128)(2,1)}, bf16[44,16,128]{2,1,0:T(8,128)(2,1)S(1)}, u32[]{:S(2)}, u32[]{:S(2)}) collective-permute-start(bf16[44,16,128]{2,1,0:T(8,128)(2,1)} %pad_maximum_fusion.6), channel_id=1, source_target_pairs={{0,8},{4,12},{8,0},{12,4},{16,24},{20,28},{24,16},{28,20},{1,9},{5... | collective-permute-start | bytes 540680 | tf_op jit(solution)/shard_map/ppermute | solution.py:785
  283.1 15.0 %collective-permute-start.35 = (bf16[128,2048]{1,0:T(8,128)(2,1)S(1)}, bf16[128,2048]{1,0:T(8,128)(2,1)S(1)}, u32[]{:S(2)}, u32[]{:S(2)}) collective-permute-start(bf16[128,2048]{1,0:T(8,128)(2,1)S(1)} %get-tuple-element.209), channel_id=1, source_target_pairs={{0,8},{8,16},{16,24},{24,28},{28,20},{20,12},{12,4},{4,0},{1,9},{9... | collective-permute-start | bytes 1572872 | tf_op jit(solution)/shard_map/ppermute | solution.py:721
  284.8 15.4 %collective-permute-start.36 = (bf16[128,2048]{1,0:T(8,128)(2,1)S(1)}, bf16[128,2048]{1,0:T(8,128)(2,1)S(1)}, u32[]{:S(2)}, u32[]{:S(2)}) collective-permute-start(bf16[128,2048]{1,0:T(8,128)(2,1)S(1)} %get-tuple-element.208), channel_id=1, source_target_pairs={{0,4},{8,0},{16,8},{24,16},{28,24},{20,28},{12,20},{4,12},{1,5},{9... | collective-permute-start | bytes 1572872 | tf_op jit(solution)/shard_map/ppermute | solution.py:721
  300.2 14.4 %copy-start.4 = (bf16[1024,2048]{1,0:T(8,128)(2,1)S(1)}, bf16[1024,2048]{1,0:T(8,128)(2,1)}, u32[]{:S(2)}) copy-start(bf16[1024,2048]{1,0:T(8,128)(2,1)} %get-tuple-element.173) | copy-start | bytes 12582916
  300.2 8.8 %collective-permute-start.37 = (bf16[72,16,128]{2,1,0:T(8,128)(2,1)S(1)}, bf16[72,16,128]{2,1,0:T(8,128)(2,1)S(1)}, u32[]{:S(2)}, u32[]{:S(2)}) collective-permute-start(bf16[72,16,128]{2,1,0:T(8,128)(2,1)S(1)} %pad_maximum_fusion.2), channel_id=1, source_target_pairs={{0,4},{4,0},{8,12},{12,8},{16,20},{20,16},{24,28},{28,24},{1,5},{5... | collective-permute-start | bytes 884744 | tf_op jit(solution)/shard_map/ppermute | solution.py:785
  303.3 9.6 %collective-permute-start.38 = (bf16[128,2048]{1,0:T(8,128)(2,1)S(1)}, bf16[128,2048]{1,0:T(8,128)(2,1)S(1)}, u32[]{:S(2)}, u32[]{:S(2)}) collective-permute-start(bf16[128,2048]{1,0:T(8,128)(2,1)S(1)} %get-tuple-element.207), channel_id=1, source_target_pairs={{0,8},{8,16},{16,24},{24,28},{28,20},{20,12},{12,4},{4,0},{1,9},{9... | collective-permute-start | bytes 1572872 | tf_op jit(solution)/shard_map/ppermute | solution.py:721
  303.6 9.3 %collective-permute-start.39 = (bf16[128,2048]{1,0:T(8,128)(2,1)S(1)}, bf16[128,2048]{1,0:T(8,128)(2,1)S(1)}, u32[]{:S(2)}, u32[]{:S(2)}) collective-permute-start(bf16[128,2048]{1,0:T(8,128)(2,1)S(1)} %get-tuple-element.206), channel_id=1, source_target_pairs={{0,4},{8,0},{16,8},{24,16},{28,24},{20,28},{12,20},{4,12},{1,5},{9... | collective-permute-start | bytes 1572872 | tf_op jit(solution)/shard_map/ppermute | solution.py:721
  307.0 11.4 %collective-permute-start.44 = (bf16[128,2048]{1,0:T(8,128)(2,1)S(1)}, bf16[128,2048]{1,0:T(8,128)(2,1)S(1)}, u32[]{:S(2)}, u32[]{:S(2)}) collective-permute-start(bf16[128,2048]{1,0:T(8,128)(2,1)S(1)} %get-tuple-element.203), channel_id=1, source_target_pairs={{0,4},{8,0},{16,8},{24,16},{28,24},{20,28},{12,20},{4,12},{1,5},{9... | collective-permute-start | bytes 1572872 | tf_op jit(solution)/shard_map/ppermute | solution.py:721
  308.0 10.6 %collective-permute-start.43 = (bf16[128,2048]{1,0:T(8,128)(2,1)S(1)}, bf16[128,2048]{1,0:T(8,128)(2,1)S(1)}, u32[]{:S(2)}, u32[]{:S(2)}) collective-permute-start(bf16[128,2048]{1,0:T(8,128)(2,1)S(1)} %get-tuple-element.202), channel_id=1, source_target_pairs={{0,8},{8,16},{16,24},{24,28},{28,20},{20,12},{12,4},{4,0},{1,9},{9... | collective-permute-start | bytes 1572872 | tf_op jit(solution)/shard_map/ppermute | solution.py:721
  309.1 16.2 %copy-start.1 = (bf16[1,128,2048]{2,1,0:T(8,128)(2,1)S(1)}, bf16[1,128,2048]{2,1,0:T(8,128)(2,1)}, u32[]{:S(2)}) copy-start(bf16[1,128,2048]{2,1,0:T(8,128)(2,1)} %param.23) | copy-start | bytes 1572868
  313.0 12.3 %collective-permute-start.40 = (bf16[140,16,128]{2,1,0:T(8,128)(2,1)S(1)}, bf16[140,16,128]{2,1,0:T(8,128)(2,1)S(1)}, u32[]{:S(2)}, u32[]{:S(2)}) collective-permute-start(bf16[140,16,128]{2,1,0:T(8,128)(2,1)S(1)} %constant_dynamic-update-slice_fusion.2.refs_0_), channel_id=1, source_target_pairs={{0,2},{1,3},{2,0},{3,1},{4,6},{5,7},{6,4},{7,5},{8,10},{9,11},{10,... | collective-permute-start | bytes 1720328 | tf_op jit(solution)/shard_map/ppermute | solution.py:785
  315.0 9.2 %collective-permute-start.41 = (bf16[128,2048]{1,0:T(8,128)(2,1)S(1)}, bf16[128,2048]{1,0:T(8,128)(2,1)S(1)}, u32[]{:S(2)}, u32[]{:S(2)}) collective-permute-start(bf16[128,2048]{1,0:T(8,128)(2,1)S(1)} %get-tuple-element.205), channel_id=1, source_target_pairs={{0,8},{8,16},{16,24},{24,28},{28,20},{20,12},{12,4},{4,0},{1,9},{9... | collective-permute-start | bytes 1572872 | tf_op jit(solution)/shard_map/ppermute | solution.py:721
  316.1 9.2 %collective-permute-start.42 = (bf16[128,2048]{1,0:T(8,128)(2,1)S(1)}, bf16[128,2048]{1,0:T(8,128)(2,1)S(1)}, u32[]{:S(2)}, u32[]{:S(2)}) collective-permute-start(bf16[128,2048]{1,0:T(8,128)(2,1)S(1)} %get-tuple-element.204), channel_id=1, source_target_pairs={{0,4},{8,0},{16,8},{24,16},{28,24},{20,28},{12,20},{4,12},{1,5},{9... | collective-permute-start | bytes 1572872 | tf_op jit(solution)/shard_map/ppermute | solution.py:721
  325.8 2.6 collective-permute-start.46
  325.9 2.8 collective-permute-start.45
  (16 other events, 111.1 us)
Sparse Core Ops, SparseCore 0:
  85.2 23.8 all-gather.5
  110.7 22.5 all-gather.3

commit v5 on v4

--- a/solution.py
+++ b/solution.py
@@ -654,15 +654,17 @@
 def place_kernel(meta, *refs, groups, parts, chans, span, every, wide):
     values, outs = refs[:groups], refs[groups:]
     in_up_ref, out_down_ref, out_up_ref, in_down_ref, state_down_ref, step_up_ref, step_down_ref, state_up_ref = outs
-    adapter = pl.program_id(0)
-    uses = [meta[3 + g] == adapter for g in range(groups)]
+    per = in_up_ref.shape[0]
+    first = pl.program_id(0) * per
 
     def put(ref, column, at, size=128):
-        total = None
-        for use, value in zip(uses, values):
-            term = jnp.where(use, value[at].astype(F32), 0.0)
-            total = term if total is None else total + term
-        ref[0, :, column : column + size] = total[:, :size]
+        terms = [value[at].astype(F32) for value in values]
+        for i in range(per):
+            total = None
+            for g, term in enumerate(terms):
+                term = jnp.where(meta[3 + g] == first + i, term, 0.0)
+                total = term if total is None else total + term
+            ref[i, :, column : column + size] = total[:, :size]
 
     inner = parts * chans
     for p in range(parts):
@@ -689,12 +691,12 @@
         functools.partial(place_kernel, groups=groups, parts=parts, chans=chans, span=span, every=every, wide=wide),
         grid_spec=pltpu.PrefetchScalarGridSpec(
             num_scalar_prefetch=1,
-            grid=(adapters,),
+            grid=(adapters // 2,),
             in_specs=[once(value) for value in values],
-            out_specs=[pl.BlockSpec((1, rank, size), lambda i, meta: (i, 0, 0)) for size in sizes],
+            out_specs=[pl.BlockSpec((2, rank, size), lambda i, meta: (i, 0, 0)) for size in sizes],
         ),
         out_shape=[jax.ShapeDtypeStruct((adapters, rank, size), F32) for size in sizes],
-        compiler_params=pltpu.CompilerParams(vmem_limit_bytes=16 << 20),
+        compiler_params=pltpu.CompilerParams(vmem_limit_bytes=32 << 20),
         name="place",
     )(meta, *values)
 
@@ -873,16 +875,14 @@
     sums, cot_ring.ends = together(sums, cot_ring.ends)
     cot_ring.advance(hops)
     shared = share(meta, sums, state_up, step_down, ranks, states)[None]
-    z = back = None
+    shared, columns_z = together(shared, columns_z)
+    z = gate(meta, pieces, columns_z, low_in, in_up, parts, groups)
     for i, bit in enumerate(bits_of(parts)):
         shared = jnp.concatenate([shared, swap(shared, parts, bit, "seq")], 0)
         if i == 0:
-            shared, cot_ring.ends, columns_z = together(shared, cot_ring.ends, columns_z)
+            shared, cot_ring.ends, z = together(shared, cot_ring.ends, z)
             cot_ring.advance(parts)
-            z = gate(meta, pieces, columns_z, low_in, in_up, parts, groups)
-        elif i == 1:
-            shared, cot_ring.pieces, z = together(shared, cot_ring.pieces, z)
-            back = back_gate(meta, cot_ring.pieces, whole_out, out_down, out_up, parts)
+    back = back_gate(meta, cot_ring.pieces, whole_out, out_down, out_up, parts)
     back_low, cols, back_gated = back
     gated, back_pre, conv_grad, back_z, mixed = scan(
         meta, shared, conv_out, z, back_gated, step_proj, step_up, bias, rate, decay, skip, out_down, parts, sub

time: 343 us -> 340 us (level)
    ppermute x15, waiting for transfers between devices: 38.3 us -> 30.1 us  [swap(): return lax.ppermute(value, axis, [(i, i ^ bit) for i in range(size)])]
    ppermute x32, waiting for transfers between devices: 57.8 us -> 61.4 us  [ring_send(): return lax.ppermute(value, axis, pairs)]
  transfers between devices with their start and end apart: 53 -> 53, of which waited for: 27 -> 29; matrix products, arithmetic and copies ran while one was open for 8% -> 9% of each run, Pallas kernels for 17% -> 17%
where the time goes in v5:
time: 340 us; the launch traced here: 338 us
  Pallas kernels  106 us (31%)
  waiting for transfers between devices  104 us (31%)
  starting transfers between devices  70.5 us (21%)
  other arithmetic  27.8 us (8%)
  between operations  16 us (5%)
  local copies, waits for them, and re-layouts  9.25 us (3%)
  matrix products  4.73 us (1%)
    ppermute x32, waiting for transfers between devices, ring_send(): return lax.ppermute(value, axis, pairs)  61.4 us
    pallas_call x1, Pallas kernels, scan(): pl.pallas_call(functools.partial(scan_kernel, sub=sub, ranks=ranks), grid...  41.6 us
    ppermute x32, starting transfers between devices, ring_send(): return lax.ppermute(value, axis, pairs)  39.4 us
    ppermute x15, waiting for transfers between devices, swap(): return lax.ppermute(value, axis, [(i, i ^ bit) for i in range(size)])  30.1 us
    pallas_call x1, Pallas kernels, finish(): pl.pallas_call(functools.partial(finish_kernel, ranks=ranks, states=state...  18.7 us
    pallas_call x1, Pallas kernels, project(): pl.pallas_call(functools.partial(project_kernel, parts=parts, groups=grou...  11.9 us
    pallas_call x1, Pallas kernels, back_gate(): pl.pallas_call(functools.partial(back_gate_kernel, parts=parts), grid_spe...  11.3 us
    ppermute x15, starting transfers between devices, swap(): return lax.ppermute(value, axis, [(i, i ^ bit) for i in range(size)])  11.2 us
  transfers between devices with their start and end apart: 53, of which 29 were waited for; matrix products, arithmetic and copies ran while one was open for 9% of the time, Pallas kernels for 17%

profile of v5, /device:TPU:0, one launch (start us, length us, event | category | flops | bytes accessed | tf_op | source)
XLA Modules:
  0.0 338.4 jit_solution(469086838449577361)
XLA Ops:
  10.4 3.1 collective-permute-start
  13.4 1.9 split_columns.3
  15.3 6.3 %all-to-all-start = ((bf16[8,64,512]{2,1,0:T(8,128)(2,1)}), bf16[8,64,512]{2,1,0:T(8,128)(2,1)}, u32[]{:S(2)}, u32[]{:S(2)}) async-start(bf16[8,64,512]{2,1,0:T(8,128)(2,1)} %split_columns.3), calls=%async_computation | async-start | bytes 1048576 | tf_op jit(solution)/shard_map/all_to_all | solution.py:851
  21.6 1.3 convert_element_type.207.refs_15_.refs_32_
  27.3 1.9 split_columns.2
  30.4 2.1 collective-permute-start.2
  32.6 8.1 %all-to-all-done.refs_9_ = bf16[8,64,512]{2,1,0:T(8,128)(2,1)} async-done(((bf16[8,64,512]{2,1,0:T(8,128)(2,1)}), bf16[8,64,512]{2,1,0:T(8,128)(2,1)}, u32[]{:S(2)}, u32[]{:S(2)}) %all-to-all-start) | async-done | bytes 524320 | tf_op jit(solution)/shard_map/all_to_all | solution.py:851
  40.6 1.5 collective-permute-start.8
  42.2 2.6 collective-permute-done.2.refs_3_
  44.8 3.9 %collective-permute-start.4 = (bf16[128,2048]{1,0:T(8,128)(2,1)S(1)}, bf16[128,2048]{1,0:T(8,128)(2,1)S(1)}, u32[]{:S(2)}, u32[]{:S(2)}) collective-permute-start(bf16[128,2048]{1,0:T(8,128)(2,1)S(1)} %collective-permute-done.2.refs_3_), channel_id=1, source_target_pairs={{0,8},{8,16},{16,24},{24,28},{28,20},{20,12},{12,4},{4,0},{1,9},{9... | collective-permute-start | bytes 1572872 | tf_op jit(solution)/shard_map/ppermute | solution.py:723
  49.4 1.4 collective-permute-done.8.refs_10_
  50.8 8.6 %collective-permute-done.4.refs_5_ = bf16[128,2048]{1,0:T(8,128)(2,1)S(1)} collective-permute-done((bf16[128,2048]{1,0:T(8,128)(2,1)S(1)}, bf16[128,2048]{1,0:T(8,128)(2,1)S(1)}, u32[]{:S(2)}, u32[]{:S(2)}) %collective-permute-start.4) | collective-permute-done | bytes 524320 | tf_op jit(solution)/shard_map/ppermute | solution.py:723
  59.4 2.2 collective-permute-start.6
  62.4 2.0 fusion.7.refs_0_
  64.4 2.8 collective-permute-done.6.refs_7_
  67.2 1.6 collective-permute-done.7.refs_8_
  68.8 4.1 %all-to-all-start.1 = ((bf16[8,64,512]{2,1,0:T(8,128)(2,1)}), bf16[8,64,512]{2,1,0:T(8,128)(2,1)}, u32[]{:S(2)}, u32[]{:S(2)}) async-start(bf16[8,64,512]{2,1,0:T(8,128)(2,1)} %split_columns.2), calls=%async_computation.1 | async-start | bytes 1048576 | tf_op jit(solution)/shard_map/all_to_all | solution.py:851
  73.1 11.9 %project.1 = (bf16[1024,16]{1,0:T(8,128)(2,1)}, bf16[1024,512]{1,0:T(8,128)(2,1)}, bf16[1024,512]{1,0:T(8,128)(2,1)}, bf16[8,176,128]{2,1,0:T(8,128)(2,1)}) custom-call(s32[3]{0:T(128)} %pad_add_fusion.meta, bf16[128,2048]{1,0:T(8,128)(2,1)} %copy-done, bf16[128,2048]{1,0:T(8,128)(2,1)} %copy-done.5, bf16[128,2048]{1,0:T(8,128)(2,1)} %copy-done.6, ...), custom_call_target="tpu_custom_call" | custom-call | tf_op jit(solution)/shard_map/project/pallas_call | solution.py:246
  85.8 1.9 collective-permute-start.11
  87.9 5.8 %all-to-all-start.2 = ((bf16[8,176,128]{2,1,0:T(8,128)(2,1)}), bf16[8,176,128]{2,1,0:T(8,128)(2,1)S(1)}, u32[]{:S(2)}, u32[]{:S(2)}) async-start(bf16[8,176,128]{2,1,0:T(8,128)(2,1)} %get-tuple-element.118), calls=%async_computation.2 | async-start | bytes 720896 | tf_op jit(solution)/shard_map/all_to_all | solution.py:812
  93.7 7.6 %collective-permute-done.11.refs_1_ = bf16[128,2048]{1,0:T(8,128)(2,1)S(1)} collective-permute-done((bf16[128,2048]{1,0:T(8,128)(2,1)}, bf16[128,2048]{1,0:T(8,128)(2,1)S(1)}, u32[]{:S(2)}, u32[]{:S(2)}) %collective-permute-start.11) | collective-permute-done | bytes 524320 | tf_op jit(solution)/shard_map/ppermute | solution.py:723
  101.4 2.9 collective-permute-start.12
  104.4 8.8 %collective-permute-done.12.refs_3_ = bf16[128,2048]{1,0:T(8,128)(2,1)S(1)} collective-permute-done((bf16[128,2048]{1,0:T(8,128)(2,1)S(1)}, bf16[128,2048]{1,0:T(8,128)(2,1)S(1)}, u32[]{:S(2)}, u32[]{:S(2)}) %collective-permute-start.12) | collective-permute-done | bytes 524320 | tf_op jit(solution)/shard_map/ppermute | solution.py:723
  113.2 2.2 collective-permute-done.14.refs_4_
  116.2 3.7 %collective-permute-start.16 = (bf16[128,2048]{1,0:T(8,128)(2,1)S(1)}, bf16[128,2048]{1,0:T(8,128)(2,1)S(1)}, u32[]{:S(2)}, u32[]{:S(2)}) collective-permute-start(bf16[128,2048]{1,0:T(8,128)(2,1)S(1)} %collective-permute-done.12.refs_3_), channel_id=1, source_target_pairs={{0,8},{8,16},{16,24},{24,28},{28,20},{20,12},{12,4},{4,0},{1,9},{9... | collective-permute-start | bytes 1572872 | tf_op jit(solution)/shard_map/ppermute | solution.py:723
  119.9 2.7 share.1
  122.6 2.0 collective-permute-start.15
  124.6 8.2 %gate.1.z_ref = bf16[1024,512]{1,0:T(8,128)(2,1)} custom-call(s32[3]{0:T(128)} %pad_add_fusion.meta, bf16[128,2048]{1,0:T(8,128)(2,1)} %copy-done, bf16[128,2048]{1,0:T(8,128)(2,1)} %copy-done.5, bf16[128,2048]{1,0:T(8,128)(2,1)} %copy-done.6, bf16[128,2048]{1,0:T(8,128)(2,1)} %copy-done.7, bf16[128,2048]{1,0:T(8,128)(2,1)} %collective-permute-done.3.refs_4_, ...), custom_call_target="tpu_custom_call" | custom-call | tf_op jit(solution)/shard_map/gate/pallas_call | solution.py:179
  133.9 1.8 collective-permute-start.20
  136.7 1.3 collective-permute-done.18
  138.7 1.5 collective-permute-start.19
  141.1 2.1 collective-permute-done.21.refs_8_
  143.2 11.3 %back_gate.1 = (bf16[1024,16]{1,0:T(8,128)(2,1)}, bf16[1024,256]{1,0:T(8,128)(2,1)}, bf16[1024,512]{1,0:T(8,128)(2,1)}) custom-call(s32[3]{0:T(128)} %pad_add_fusion.meta, bf16[128,2048]{1,0:T(8,128)(2,1)} %fusion.7.refs_0_, bf16[128,2048]{1,0:T(8,128)(2,1)} %copy-done.18, bf16[128,2048]{1,0:T(8,128)(2,1)} %copy-done.19, bf16[128,2048]{1,0:T(8,128)(2,1)} %copy-done.20, ...), custom_call_target="tpu_custom_call" | custom-call | tf_op jit(solution)/shard_map/back_gate/pallas_call | solution.py:222
  156.4 41.6 %scan.1 = (bf16[1024,512]{1,0:T(8,128)(2,1)}, bf16[1024,512]{1,0:T(8,128)(2,1)}, f32[1024,512]{1,0:T(8,128)}, bf16[1024,512]{1,0:T(8,128)(2,1)}, bf16[8,192,128]{2,1,0:T(8,128)(2,1)}) custom-call(s32[3]{0:T(128)} %pad_add_fusion.meta, bf16[8,128,192]{2,1,0:T(8,128)(2,1)} %copy-done.9, bf16[1024,512]{1,0:T(8,128)(2,1)} %get-tuple-element.128.u_ref.refs_21_, ...), custom_call_target="tpu_custom_call" | custom-call | tf_op jit(solution)/shard_map/scan/pallas_call | solution.py:476
  197.9 3.7 %all-to-all-start.3 = ((bf16[8,192,128]{2,1,0:T(8,128)(2,1)}), bf16[8,192,128]{2,1,0:T(8,128)(2,1)S(1)}, u32[]{:S(2)}, u32[]{:S(2)}) async-start(bf16[8,192,128]{2,1,0:T(8,128)(2,1)} %get-tuple-element.137), calls=%async_computation.3 | async-start | bytes 786432 | tf_op jit(solution)/shard_map/all_to_all | solution.py:812
  201.6 3.6 %convolution_convert_fusion = bf16[1024,2048]{1,0:T(8,128)(2,1)S(1)} fusion(bf16[1024,512]{1,0:T(8,128)(2,1)} %get-tuple-element.138.refs_23_, bf16[512,2048]{1,0:T(8,128)(2,1)S(1)} %copy-done.13), kind=kOutput, calls=%fused_computation | convolution fusion | flops 2149580800 | bytes 7340032 | tf_op jit(solution)/shard_map/dot_general | solution.py:28
  205.2 2.0 copy-done.8
  207.3 2.1 collective-permute-start.23
  209.4 4.0 %all-to-all-done.3.got_ref = bf16[8,192,128]{2,1,0:T(8,128)(2,1)S(1)} async-done(((bf16[8,192,128]{2,1,0:T(8,128)(2,1)}), bf16[8,192,128]{2,1,0:T(8,128)(2,1)S(1)}, u32[]{:S(2)}, u32[]{:S(2)}) %all-to-all-start.3) | async-done | bytes 393248 | tf_op jit(solution)/shard_map/all_to_all | solution.py:812
  214.1 2.6 share_back.1
  217.1 6.1 %collective-permute-done.22 = bf16[1,128,192]{2,1,0:T(8,128)(2,1)S(1)} collective-permute-done((bf16[1,128,192]{2,1,0:T(8,128)(2,1)}, bf16[1,128,192]{2,1,0:T(8,128)(2,1)S(1)}, u32[]{:S(2)}, u32[]{:S(2)}) %collective-permute-start.22) | collective-permute-done | bytes 49184 | tf_op jit(solution)/shard_map/ppermute | solution.py:787
  224.2 1.4 add_convert_fusion.10
  225.5 2.1 collective-permute-start.27
  227.6 1.5 collective-permute-done.25
  229.9 13.1 %collective-permute-done.26 = bf16[4,128,192]{2,1,0:T(8,128)(2,1)S(1)} collective-permute-done((bf16[4,128,192]{2,1,0:T(8,128)(2,1)S(1)}, bf16[4,128,192]{2,1,0:T(8,128)(2,1)S(1)}, u32[]{:S(2)}, u32[]{:S(2)}) %collective-permute-start.26) | collective-permute-done | bytes 196640 | tf_op jit(solution)/shard_map/ppermute | solution.py:787
  243.9 1.6 add_convert_fusion.8
  245.5 2.3 collective-permute-start.30
  247.8 18.7 %finish.1 = (bf16[1024,2048]{1,0:T(8,128)(2,1)}, bf16[30,16,128]{2,1,0:T(8,128)(2,1)}, bf16[12,16,128]{2,1,0:T(8,128)(2,1)}) custom-call(s32[3]{0:T(128)} %pad_add_fusion.meta, bf16[128,2048]{1,0:T(8,128)(2,1)} %copy-done, bf16[128,2048]{1,0:T(8,128)(2,1)} %copy-done.5, bf16[128,2048]{1,0:T(8,128)(2,1)} %copy-done.6, bf16[128,2048]{1,0:T(8,128)(2,1)} %copy-done.7, ...), custom_call_target="tpu_custom_call" | custom-call | tf_op jit(solution)/shard_map/finish/pallas_call | solution.py:620
  269.1 2.1 collective-permute-start.32
  271.2 3.1 collective-permute-done.31
  279.1 1.4 add_convert_fusion.6
  282.7 3.3 collective-permute-done.34
  286.0 9.6 %collective-permute-done.35 = bf16[128,2048]{1,0:T(8,128)(2,1)S(1)} collective-permute-done((bf16[128,2048]{1,0:T(8,128)(2,1)S(1)}, bf16[128,2048]{1,0:T(8,128)(2,1)S(1)}, u32[]{:S(2)}, u32[]{:S(2)}) %collective-permute-start.35) | collective-permute-done | bytes 524320 | tf_op jit(solution)/shard_map/ppermute | solution.py:723
  295.6 1.6 collective-permute-done.36
  298.4 1.7 add_convert_fusion.4
  300.8 1.4 collective-permute-start.39
  302.2 1.6 add_convert_fusion.1
  306.0 4.0 %collective-permute-done.38 = bf16[128,2048]{1,0:T(8,128)(2,1)S(1)} collective-permute-done((bf16[128,2048]{1,0:T(8,128)(2,1)S(1)}, bf16[128,2048]{1,0:T(8,128)(2,1)S(1)}, u32[]{:S(2)}, u32[]{:S(2)}) %collective-permute-start.38) | collective-permute-done | bytes 524320 | tf_op jit(solution)/shard_map/ppermute | solution.py:723
  310.1 1.6 collective-permute-start.40
  312.1 1.5 collective-permute-start.41
  316.9 4.4 %collective-permute-done.41 = bf16[128,2048]{1,0:T(8,128)(2,1)S(1)} collective-permute-done((bf16[128,2048]{1,0:T(8,128)(2,1)S(1)}, bf16[128,2048]{1,0:T(8,128)(2,1)S(1)}, u32[]{:S(2)}, u32[]{:S(2)}) %collective-permute-start.41) | collective-permute-done | bytes 524320 | tf_op jit(solution)/shard_map/ppermute | solution.py:723
  321.3 1.4 collective-permute-done.42
  323.8 2.0 fusion.6
  326.3 5.2 %place.1 = (f32[8,16,8192]{2,1,0:T(8,128)}, f32[8,16,4096]{2,1,0:T(8,128)}, f32[8,16,2048]{2,1,0:T(8,128)}, f32[8,16,2048]{2,1,0:T(8,128)}, f32[8,16,512]{2,1,0:...) custom-call(s32[7]{0:T(128)S(1)} %pad_add_fusion.1.meta, ...), custom_call_target="tpu_custom_call" | custom-call | tf_op jit(solution)/shard_map/place/pallas_call | solution.py:690
  (168 shorter events, 39.6 us)
Async XLA Ops:
  7.2 22.6 %copy-start.26 = (bf16[16,512]{1,0:T(8,128)(2,1)S(1)}, bf16[16,512]{1,0:T(8,128)(2,1)}, u32[]{:S(2)}) copy-start(bf16[16,512]{1,0:T(8,128)(2,1)} %param.34) | copy-start | bytes 49156
  10.4 62.7 %copy-start = (bf16[128,2048]{1,0:T(8,128)(2,1)}, bf16[128,2048]{1,0:T(8,128)(2,1)S(1)}, u32[]{:S(2)}) copy-start(bf16[128,2048]{1,0:T(8,128)(2,1)S(1)} %fusion.2.refs_0_) | copy-start | bytes 1572868
  10.4 20.1 %collective-permute-start = (bf16[128,2048]{1,0:T(8,128)(2,1)S(1)}, bf16[128,2048]{1,0:T(8,128)(2,1)S(1)}, u32[]{:S(2)}, u32[]{:S(2)}) collective-permute-start(bf16[128,2048]{1,0:T(8,128)(2,1)S(1)} %fusion.2.refs_0_), channel_id=1, source_target_pairs={{0,8},{8,16},{16,24},{24,28},{28,20},{20,12},{12,4},{4,0},{1,9},{9... | collective-permute-start | bytes 1572872 | tf_op jit(solution)/shard_map/ppermute | solution.py:723
  13.4 17.0 %collective-permute-start.1 = (bf16[128,2048]{1,0:T(8,128)(2,1)S(1)}, bf16[128,2048]{1,0:T(8,128)(2,1)S(1)}, u32[]{:S(2)}, u32[]{:S(2)}) collective-permute-start(bf16[128,2048]{1,0:T(8,128)(2,1)S(1)} %fusion.2.refs_0_), channel_id=1, source_target_pairs={{0,4},{8,0},{16,8},{24,16},{28,24},{20,28},{12,20},{4,12},{1,5},{9... | collective-permute-start | bytes 1572872 | tf_op jit(solution)/shard_map/ppermute | solution.py:723
  15.3 25.3 %all-to-all-start = ((bf16[8,64,512]{2,1,0:T(8,128)(2,1)}), bf16[8,64,512]{2,1,0:T(8,128)(2,1)}, u32[]{:S(2)}, u32[]{:S(2)}) async-start(bf16[8,64,512]{2,1,0:T(8,128)(2,1)} %split_columns.3), calls=%async_computation | async-start | bytes 1048576 | tf_op jit(solution)/shard_map/all_to_all | solution.py:851
  30.4 42.6 %copy-start.5 = (bf16[128,2048]{1,0:T(8,128)(2,1)}, bf16[128,2048]{1,0:T(8,128)(2,1)S(1)}, u32[]{:S(2)}) copy-start(bf16[128,2048]{1,0:T(8,128)(2,1)S(1)} %collective-permute-done.refs_1_) | copy-start | bytes 1572868
  30.4 42.6 %copy-start.6 = (bf16[128,2048]{1,0:T(8,128)(2,1)}, bf16[128,2048]{1,0:T(8,128)(2,1)S(1)}, u32[]{:S(2)}) copy-start(bf16[128,2048]{1,0:T(8,128)(2,1)S(1)} %collective-permute-done.1.refs_2_) | copy-start | bytes 1572868
  30.4 14.3 %collective-permute-start.2 = (bf16[128,2048]{1,0:T(8,128)(2,1)S(1)}, bf16[128,2048]{1,0:T(8,128)(2,1)S(1)}, u32[]{:S(2)}, u32[]{:S(2)}) collective-permute-start(bf16[128,2048]{1,0:T(8,128)(2,1)S(1)} %collective-permute-done.refs_1_), channel_id=1, source_target_pairs={{0,8},{8,16},{16,24},{24,28},{28,20},{20,12},{12,4},{4,0},{1,9},{9... | collective-permute-start | bytes 1572872 | tf_op jit(solution)/shard_map/ppermute | solution.py:723
  32.5 16.2 %collective-permute-start.3 = (bf16[128,2048]{1,0:T(8,128)(2,1)S(1)}, bf16[128,2048]{1,0:T(8,128)(2,1)}, u32[]{:S(2)}, u32[]{:S(2)}) collective-permute-start(bf16[128,2048]{1,0:T(8,128)(2,1)S(1)} %collective-permute-done.1.refs_2_), channel_id=1, source_target_pairs={{0,4},{8,0},{16,8},{24,16},{28,24},{20,28},{12,20},{4,12},{1,5},{9... | collective-permute-start | bytes 1572872 | tf_op jit(solution)/shard_map/ppermute | solution.py:723
  40.6 10.1 %collective-permute-start.8 = (bf16[8,64,512]{2,1,0:T(8,128)(2,1)}, bf16[8,64,512]{2,1,0:T(8,128)(2,1)}, u32[]{:S(2)}, u32[]{:S(2)}) collective-permute-start(bf16[8,64,512]{2,1,0:T(8,128)(2,1)} %all-to-all-done.refs_9_), channel_id=1, source_target_pairs={{0,2},{1,3},{2,0},{3,1},{4,6},{5,7},{6,4},{7,5},{8,10},{9,11},{10,... | collective-permute-start | bytes 1572872 | tf_op jit(solution)/shard_map/ppermute | solution.py:787
  44.8 28.3 %copy-start.7 = (bf16[128,2048]{1,0:T(8,128)(2,1)}, bf16[128,2048]{1,0:T(8,128)(2,1)S(1)}, u32[]{:S(2)}) copy-start(bf16[128,2048]{1,0:T(8,128)(2,1)S(1)} %collective-permute-done.2.refs_3_) | copy-start | bytes 1572868
  44.8 14.6 %collective-permute-start.4 = (bf16[128,2048]{1,0:T(8,128)(2,1)S(1)}, bf16[128,2048]{1,0:T(8,128)(2,1)S(1)}, u32[]{:S(2)}, u32[]{:S(2)}) collective-permute-start(bf16[128,2048]{1,0:T(8,128)(2,1)S(1)} %collective-permute-done.2.refs_3_), channel_id=1, source_target_pairs={{0,8},{8,16},{16,24},{24,28},{28,20},{20,12},{12,4},{4,0},{1,9},{9... | collective-permute-start | bytes 1572872 | tf_op jit(solution)/shard_map/ppermute | solution.py:723
  48.7 13.6 %collective-permute-start.5 = (bf16[128,2048]{1,0:T(8,128)(2,1)}, bf16[128,2048]{1,0:T(8,128)(2,1)S(1)}, u32[]{:S(2)}, u32[]{:S(2)}) collective-permute-start(bf16[128,2048]{1,0:T(8,128)(2,1)} %collective-permute-done.3.refs_4_), channel_id=1, source_target_pairs={{0,4},{8,0},{16,8},{24,16},{28,24},{20,28},{12,20},{4,12},{1,5},{9... | collective-permute-start | bytes 1572872 | tf_op jit(solution)/shard_map/ppermute | solution.py:723
  49.3 15.1 %collective-permute-start.9 = (bf16[8,64,512]{2,1,0:T(8,128)(2,1)}, bf16[8,64,512]{2,1,0:T(8,128)(2,1)S(1)}, u32[]{:S(2)}, u32[]{:S(2)}) collective-permute-start(bf16[8,64,512]{2,1,0:T(8,128)(2,1)} %all-to-all-done.refs_9_), channel_id=1, source_target_pairs={{0,1},{1,0},{2,3},{3,2},{4,5},{5,4},{6,7},{7,6},{8,9},{9,8},{10,11... | collective-permute-start | bytes 1572872 | tf_op jit(solution)/shard_map/ppermute | solution.py:787
  50.8 18.0 %collective-permute-start.10 = (bf16[8,64,512]{2,1,0:T(8,128)(2,1)}, bf16[8,64,512]{2,1,0:T(8,128)(2,1)}, u32[]{:S(2)}, u32[]{:S(2)}) collective-permute-start(bf16[8,64,512]{2,1,0:T(8,128)(2,1)} %collective-permute-done.8.refs_10_), channel_id=1, source_target_pairs={{0,1},{1,0},{2,3},{3,2},{4,5},{5,4},{6,7},{7,6},{8,9},{9,8},{10,11... | collective-permute-start | bytes 1572872 | tf_op jit(solution)/shard_map/ppermute | solution.py:787
  59.4 7.8 %collective-permute-start.6 = (bf16[64,2048]{1,0:T(8,128)(2,1)S(1)}, bf16[64,2048]{1,0:T(8,128)(2,1)S(1)}, u32[]{:S(2)}, u32[]{:S(2)}) collective-permute-start(bf16[64,2048]{1,0:T(8,128)(2,1)S(1)} %slice.69), channel_id=1, source_target_pairs={{0,8},{8,16},{16,24},{24,28},{28,20},{20,12},{12,4},{4,0},{1,9},{9... | collective-permute-start | bytes 786440 | tf_op jit(solution)/shard_map/ppermute | solution.py:723
  62.3 6.5 %collective-permute-start.7 = (bf16[64,2048]{1,0:T(8,128)(2,1)S(1)}, bf16[64,2048]{1,0:T(8,128)(2,1)}, u32[]{:S(2)}, u32[]{:S(2)}) collective-permute-start(bf16[64,2048]{1,0:T(8,128)(2,1)S(1)} %slice.70), channel_id=1, source_target_pairs={{0,4},{8,0},{16,8},{24,16},{28,24},{20,28},{12,20},{4,12},{1,5},{9... | collective-permute-start | bytes 786440 | tf_op jit(solution)/shard_map/ppermute | solution.py:723
  68.8 16.3 %all-to-all-start.1 = ((bf16[8,64,512]{2,1,0:T(8,128)(2,1)}), bf16[8,64,512]{2,1,0:T(8,128)(2,1)}, u32[]{:S(2)}, u32[]{:S(2)}) async-start(bf16[8,64,512]{2,1,0:T(8,128)(2,1)} %split_columns.2), calls=%async_computation.1 | async-start | bytes 1048576 | tf_op jit(solution)/shard_map/all_to_all | solution.py:851
  73.0 49.7 %all-gather.6.cloned.1.call-start = ((), (), s32[]{:S(2)}) async-start(), calls=%async_computation.5 | async-start | bytes 2621440 | tf_op jit(solution)/shard_map/all_gather | solution.py:873
  85.1 55.1 %all-gather.4.cloned.1.call-start = ((), (), s32[]{:S(2)}) async-start(), calls=%async_computation.4 | async-start | bytes 2621440 | tf_op jit(solution)/shard_map/all_gather | solution.py:854
  85.8 15.5 %collective-permute-start.11 = (bf16[128,2048]{1,0:T(8,128)(2,1)}, bf16[128,2048]{1,0:T(8,128)(2,1)S(1)}, u32[]{:S(2)}, u32[]{:S(2)}) collective-permute-start(bf16[128,2048]{1,0:T(8,128)(2,1)} %fusion.7.refs_0_), channel_id=1, source_target_pairs={{0,8},{8,16},{16,24},{24,28},{28,20},{20,12},{12,4},{4,0},{1,9},{9... | collective-permute-start | bytes 1572872 | tf_op jit(solution)/shard_map/ppermute | solution.py:723
  87.7 16.6 %collective-permute-start.13 = (bf16[128,2048]{1,0:T(8,128)(2,1)}, bf16[128,2048]{1,0:T(8,128)(2,1)S(1)}, u32[]{:S(2)}, u32[]{:S(2)}) collective-permute-start(bf16[128,2048]{1,0:T(8,128)(2,1)} %fusion.7.refs_0_), channel_id=1, source_target_pairs={{0,4},{8,0},{16,8},{24,16},{28,24},{20,28},{12,20},{4,12},{1,5},{9... | collective-permute-start | bytes 1572872 | tf_op jit(solution)/shard_map/ppermute | solution.py:723
  87.9 28.3 %all-to-all-start.2 = ((bf16[8,176,128]{2,1,0:T(8,128)(2,1)}), bf16[8,176,128]{2,1,0:T(8,128)(2,1)S(1)}, u32[]{:S(2)}, u32[]{:S(2)}) async-start(bf16[8,176,128]{2,1,0:T(8,128)(2,1)} %get-tuple-element.118), calls=%async_computation.2 | async-start | bytes 720896 | tf_op jit(solution)/shard_map/all_to_all | solution.py:812
  101.4 41.8 %copy-start.18 = (bf16[128,2048]{1,0:T(8,128)(2,1)}, bf16[128,2048]{1,0:T(8,128)(2,1)S(1)}, u32[]{:S(2)}) copy-start(bf16[128,2048]{1,0:T(8,128)(2,1)S(1)} %collective-permute-done.11.refs_1_) | copy-start | bytes 1572868
  101.4 11.9 %collective-permute-start.12 = (bf16[128,2048]{1,0:T(8,128)(2,1)S(1)}, bf16[128,2048]{1,0:T(8,128)(2,1)S(1)}, u32[]{:S(2)}, u32[]{:S(2)}) collective-permute-start(bf16[128,2048]{1,0:T(8,128)(2,1)S(1)} %collective-permute-done.11.refs_1_), channel_id=1, source_target_pairs={{0,8},{8,16},{16,24},{24,28},{28,20},{20,12},{12,4},{4,0},{1,9},{9... | collective-permute-start | bytes 1572872 | tf_op jit(solution)/shard_map/ppermute | solution.py:723
  104.3 38.8 %copy-start.19 = (bf16[128,2048]{1,0:T(8,128)(2,1)}, bf16[128,2048]{1,0:T(8,128)(2,1)S(1)}, u32[]{:S(2)}) copy-start(bf16[128,2048]{1,0:T(8,128)(2,1)S(1)} %collective-permute-done.13.refs_2_) | copy-start | bytes 1572868
  104.3 11.1 %collective-permute-start.14 = (bf16[128,2048]{1,0:T(8,128)(2,1)S(1)}, bf16[128,2048]{1,0:T(8,128)(2,1)S(1)}, u32[]{:S(2)}, u32[]{:S(2)}) collective-permute-start(bf16[128,2048]{1,0:T(8,128)(2,1)S(1)} %collective-permute-done.13.refs_2_), channel_id=1, source_target_pairs={{0,4},{8,0},{16,8},{24,16},{28,24},{20,28},{12,20},{4,12},{1,5},{9... | collective-permute-start | bytes 1572872 | tf_op jit(solution)/shard_map/ppermute | solution.py:723
  113.2 29.9 %copy-start.20 = (bf16[128,2048]{1,0:T(8,128)(2,1)}, bf16[128,2048]{1,0:T(8,128)(2,1)S(1)}, u32[]{:S(2)}) copy-start(bf16[128,2048]{1,0:T(8,128)(2,1)S(1)} %collective-permute-done.12.refs_3_) | copy-start | bytes 1572868
  116.2 16.6 %collective-permute-start.16 = (bf16[128,2048]{1,0:T(8,128)(2,1)S(1)}, bf16[128,2048]{1,0:T(8,128)(2,1)S(1)}, u32[]{:S(2)}, u32[]{:S(2)}) collective-permute-start(bf16[128,2048]{1,0:T(8,128)(2,1)S(1)} %collective-permute-done.12.refs_3_), channel_id=1, source_target_pairs={{0,8},{8,16},{16,24},{24,28},{28,20},{20,12},{12,4},{4,0},{1,9},{9... | collective-permute-start | bytes 1572872 | tf_op jit(solution)/shard_map/ppermute | solution.py:723
  119.9 13.0 %collective-permute-start.17 = (bf16[128,2048]{1,0:T(8,128)(2,1)}, bf16[128,2048]{1,0:T(8,128)(2,1)S(1)}, u32[]{:S(2)}, u32[]{:S(2)}) collective-permute-start(bf16[128,2048]{1,0:T(8,128)(2,1)} %copy-done.21), channel_id=1, source_target_pairs={{0,4},{8,0},{16,8},{24,16},{28,24},{20,28},{12,20},{4,12},{1,5},{9... | collective-permute-start | bytes 1572872 | tf_op jit(solution)/shard_map/ppermute | solution.py:723
  122.6 10.2 %collective-permute-start.15 = (bf16[1,128,192]{2,1,0:T(8,128)(2,1)}, bf16[1,128,192]{2,1,0:T(8,128)(2,1)S(1)}, u32[]{:S(2)}, u32[]{:S(2)}) collective-permute-start(bf16[1,128,192]{2,1,0:T(8,128)(2,1)} %bitcast.63), channel_id=1, source_target_pairs={{0,16},{4,20},{8,24},{12,28},{16,0},{20,4},{24,8},{28,12},{1,17},{... | collective-permute-start | bytes 147464 | tf_op jit(solution)/shard_map/ppermute | solution.py:787
  132.9 5.0 %collective-permute-start.18 = (bf16[2,128,192]{2,1,0:T(8,128)(2,1)S(1)}, bf16[2,128,192]{2,1,0:T(8,128)(2,1)S(1)}, u32[]{:S(2)}, u32[]{:S(2)}) collective-permute-start(bf16[2,128,192]{2,1,0:T(8,128)(2,1)S(1)} %pad_maximum_fusion.7), channel_id=1, source_target_pairs={{0,8},{4,12},{8,0},{12,4},{16,24},{20,28},{24,16},{28,20},{1,9},{5... | collective-permute-start | bytes 294920 | tf_op jit(solution)/shard_map/ppermute | solution.py:787
  133.9 7.2 %collective-permute-start.20 = (bf16[64,2048]{1,0:T(8,128)(2,1)}, bf16[64,2048]{1,0:T(8,128)(2,1)}, u32[]{:S(2)}, u32[]{:S(2)}) collective-permute-start(bf16[64,2048]{1,0:T(8,128)(2,1)} %slice.54), channel_id=1, source_target_pairs={{0,8},{8,16},{16,24},{24,28},{28,20},{20,12},{12,4},{4,0},{1,9},{9... | collective-permute-start | bytes 786440 | tf_op jit(solution)/shard_map/ppermute | solution.py:723
  136.4 6.7 %collective-permute-start.21 = (bf16[64,2048]{1,0:T(8,128)(2,1)}, bf16[64,2048]{1,0:T(8,128)(2,1)}, u32[]{:S(2)}, u32[]{:S(2)}) collective-permute-start(bf16[64,2048]{1,0:T(8,128)(2,1)} %slice.55), channel_id=1, source_target_pairs={{0,4},{8,0},{16,8},{24,16},{28,24},{20,28},{12,20},{4,12},{1,5},{9... | collective-permute-start | bytes 786440 | tf_op jit(solution)/shard_map/ppermute | solution.py:723
  138.7 15.8 %collective-permute-start.19 = (bf16[4,128,192]{2,1,0:T(8,128)(2,1)}, bf16[4,128,192]{2,1,0:T(8,128)(2,1)}, u32[]{:S(2)}, u32[]{:S(2)}) collective-permute-start(bf16[4,128,192]{2,1,0:T(8,128)(2,1)} %pad_maximum_fusion.3), channel_id=1, source_target_pairs={{0,4},{4,0},{8,12},{12,8},{16,20},{20,16},{24,28},{28,24},{1,5},{5... | collective-permute-start | bytes 589832 | tf_op jit(solution)/shard_map/ppermute | solution.py:787
  154.4 47.2 %copy-start.13 = (bf16[512,2048]{1,0:T(8,128)(2,1)S(1)}, bf16[512,2048]{1,0:T(8,128)(2,1)}, u32[]{:S(2)}) copy-start(bf16[512,2048]{1,0:T(8,128)(2,1)} %all-gather.4.cloned.1.call-done.refs_9_) | copy-start | bytes 6291460
  197.9 15.4 %all-to-all-start.3 = ((bf16[8,192,128]{2,1,0:T(8,128)(2,1)}), bf16[8,192,128]{2,1,0:T(8,128)(2,1)S(1)}, u32[]{:S(2)}, u32[]{:S(2)}) async-start(bf16[8,192,128]{2,1,0:T(8,128)(2,1)} %get-tuple-element.137), calls=%async_computation.3 | async-start | bytes 786432 | tf_op jit(solution)/shard_map/all_to_all | solution.py:812
  207.3 16.8 %collective-permute-start.23 = (bf16[64,2048]{1,0:T(8,128)(2,1)S(1)}, bf16[64,2048]{1,0:T(8,128)(2,1)S(1)}, u32[]{:S(2)}, u32[]{:S(2)}) collective-permute-start(bf16[64,2048]{1,0:T(8,128)(2,1)S(1)} %get-tuple-element.199), channel_id=1, source_target_pairs={{0,8},{8,16},{16,24},{24,28},{28,20},{20,12},{12,4},{4,0},{1,9},{9... | collective-permute-start | bytes 786440 | tf_op jit(solution)/shard_map/ppermute | solution.py:723
  209.3 14.8 %collective-permute-start.24 = (bf16[64,2048]{1,0:T(8,128)(2,1)S(1)}, bf16[64,2048]{1,0:T(8,128)(2,1)S(1)}, u32[]{:S(2)}, u32[]{:S(2)}) collective-permute-start(bf16[64,2048]{1,0:T(8,128)(2,1)S(1)} %get-tuple-element.198), channel_id=1, source_target_pairs={{0,4},{8,0},{16,8},{24,16},{28,24},{20,28},{12,20},{4,12},{1,5},{9... | collective-permute-start | bytes 786440 | tf_op jit(solution)/shard_map/ppermute | solution.py:723
  216.7 6.5 %collective-permute-start.22 = (bf16[1,128,192]{2,1,0:T(8,128)(2,1)}, bf16[1,128,192]{2,1,0:T(8,128)(2,1)S(1)}, u32[]{:S(2)}, u32[]{:S(2)}) collective-permute-start(bf16[1,128,192]{2,1,0:T(8,128)(2,1)} %bitcast.61), channel_id=1, source_target_pairs={{0,16},{4,20},{8,24},{12,28},{16,0},{20,4},{24,8},{28,12},{1,17},{... | collective-permute-start | bytes 147464 | tf_op jit(solution)/shard_map/ppermute | solution.py:787
  224.1 5.0 %collective-permute-start.25 = (bf16[2,128,192]{2,1,0:T(8,128)(2,1)S(1)}, bf16[2,128,192]{2,1,0:T(8,128)(2,1)S(1)}, u32[]{:S(2)}, u32[]{:S(2)}) collective-permute-start(bf16[2,128,192]{2,1,0:T(8,128)(2,1)S(1)} %pad_maximum_fusion.8), channel_id=1, source_target_pairs={{0,8},{4,12},{8,0},{12,4},{16,24},{20,28},{24,16},{28,20},{1,9},{5... | collective-permute-start | bytes 294920 | tf_op jit(solution)/shard_map/ppermute | solution.py:787
  225.5 18.3 %collective-permute-start.27 = (bf16[128,2048]{1,0:T(8,128)(2,1)S(1)}, bf16[128,2048]{1,0:T(8,128)(2,1)S(1)}, u32[]{:S(2)}, u32[]{:S(2)}) collective-permute-start(bf16[128,2048]{1,0:T(8,128)(2,1)S(1)} %get-tuple-element.197), channel_id=1, source_target_pairs={{0,8},{8,16},{16,24},{24,28},{28,20},{20,12},{12,4},{4,0},{1,9},{9... | collective-permute-start | bytes 1572872 | tf_op jit(solution)/shard_map/ppermute | solution.py:723
  227.6 16.3 %collective-permute-start.28 = (bf16[128,2048]{1,0:T(8,128)(2,1)S(1)}, bf16[128,2048]{1,0:T(8,128)(2,1)S(1)}, u32[]{:S(2)}, u32[]{:S(2)}) collective-permute-start(bf16[128,2048]{1,0:T(8,128)(2,1)S(1)} %get-tuple-element.196), channel_id=1, source_target_pairs={{0,4},{8,0},{16,8},{24,16},{28,24},{20,28},{12,20},{4,12},{1,5},{9... | collective-permute-start | bytes 1572872 | tf_op jit(solution)/shard_map/ppermute | solution.py:723
  229.2 13.8 %collective-permute-start.26 = (bf16[4,128,192]{2,1,0:T(8,128)(2,1)S(1)}, bf16[4,128,192]{2,1,0:T(8,128)(2,1)S(1)}, u32[]{:S(2)}, u32[]{:S(2)}) collective-permute-start(bf16[4,128,192]{2,1,0:T(8,128)(2,1)S(1)} %pad_maximum_fusion.4), channel_id=1, source_target_pairs={{0,4},{4,0},{8,12},{12,8},{16,20},{20,16},{24,28},{28,24},{1,5},{5... | collective-permute-start | bytes 589832 | tf_op jit(solution)/shard_map/ppermute | solution.py:787
  245.5 21.1 %collective-permute-start.29 = (bf16[128,2048]{1,0:T(8,128)(2,1)S(1)}, bf16[128,2048]{1,0:T(8,128)(2,1)S(1)}, u32[]{:S(2)}, u32[]{:S(2)}) collective-permute-start(bf16[128,2048]{1,0:T(8,128)(2,1)S(1)} %get-tuple-element.195), channel_id=1, source_target_pairs={{0,8},{8,16},{16,24},{24,28},{28,20},{20,12},{12,4},{4,0},{1,9},{9... | collective-permute-start | bytes 1572872 | tf_op jit(solution)/shard_map/ppermute | solution.py:723
  245.5 21.0 %collective-permute-start.30 = (bf16[128,2048]{1,0:T(8,128)(2,1)S(1)}, bf16[128,2048]{1,0:T(8,128)(2,1)S(1)}, u32[]{:S(2)}, u32[]{:S(2)}) collective-permute-start(bf16[128,2048]{1,0:T(8,128)(2,1)S(1)} %get-tuple-element.194), channel_id=1, source_target_pairs={{0,4},{8,0},{16,8},{24,16},{28,24},{20,28},{12,20},{4,12},{1,5},{9... | collective-permute-start | bytes 1572872 | tf_op jit(solution)/shard_map/ppermute | solution.py:723
  266.5 7.8 %collective-permute-start.31 = (bf16[30,16,128]{2,1,0:T(8,128)(2,1)}, bf16[30,16,128]{2,1,0:T(8,128)(2,1)S(1)}, u32[]{:S(2)}, u32[]{:S(2)}) collective-permute-start(bf16[30,16,128]{2,1,0:T(8,128)(2,1)} %get-tuple-element.154), channel_id=1, source_target_pairs={{0,16},{4,20},{8,24},{12,28},{16,0},{20,4},{24,8},{28,12},{1,17},{... | collective-permute-start | bytes 368648 | tf_op jit(solution)/shard_map/ppermute | solution.py:787
  269.1 7.2 %collective-permute-start.32 = (bf16[64,2048]{1,0:T(8,128)(2,1)S(1)}, bf16[64,2048]{1,0:T(8,128)(2,1)S(1)}, u32[]{:S(2)}, u32[]{:S(2)}) collective-permute-start(bf16[64,2048]{1,0:T(8,128)(2,1)S(1)} %get-tuple-element.193), channel_id=1, source_target_pairs={{0,8},{8,16},{16,24},{24,28},{28,20},{20,12},{12,4},{4,0},{1,9},{9... | collective-permute-start | bytes 786440 | tf_op jit(solution)/shard_map/ppermute | solution.py:723
  271.2 6.4 %collective-permute-start.33 = (bf16[64,2048]{1,0:T(8,128)(2,1)S(1)}, bf16[64,2048]{1,0:T(8,128)(2,1)S(1)}, u32[]{:S(2)}, u32[]{:S(2)}) collective-permute-start(bf16[64,2048]{1,0:T(8,128)(2,1)S(1)} %get-tuple-element.192), channel_id=1, source_target_pairs={{0,4},{8,0},{16,8},{24,16},{28,24},{20,28},{12,20},{4,12},{1,5},{9... | collective-permute-start | bytes 786440 | tf_op jit(solution)/shard_map/ppermute | solution.py:723
  278.3 7.7 %collective-permute-start.34 = (bf16[44,16,128]{2,1,0:T(8,128)(2,1)}, bf16[44,16,128]{2,1,0:T(8,128)(2,1)S(1)}, u32[]{:S(2)}, u32[]{:S(2)}) collective-permute-start(bf16[44,16,128]{2,1,0:T(8,128)(2,1)} %pad_maximum_fusion.6), channel_id=1, source_target_pairs={{0,8},{4,12},{8,0},{12,4},{16,24},{20,28},{24,16},{28,20},{1,9},{5... | collective-permute-start | bytes 540680 | tf_op jit(solution)/shard_map/ppermute | solution.py:787
  280.6 15.0 %collective-permute-start.35 = (bf16[128,2048]{1,0:T(8,128)(2,1)S(1)}, bf16[128,2048]{1,0:T(8,128)(2,1)S(1)}, u32[]{:S(2)}, u32[]{:S(2)}) collective-permute-start(bf16[128,2048]{1,0:T(8,128)(2,1)S(1)} %get-tuple-element.191), channel_id=1, source_target_pairs={{0,8},{8,16},{16,24},{24,28},{28,20},{20,12},{12,4},{4,0},{1,9},{9... | collective-permute-start | bytes 1572872 | tf_op jit(solution)/shard_map/ppermute | solution.py:723
  281.8 15.4 %collective-permute-start.36 = (bf16[128,2048]{1,0:T(8,128)(2,1)S(1)}, bf16[128,2048]{1,0:T(8,128)(2,1)S(1)}, u32[]{:S(2)}, u32[]{:S(2)}) collective-permute-start(bf16[128,2048]{1,0:T(8,128)(2,1)S(1)} %get-tuple-element.190), channel_id=1, source_target_pairs={{0,4},{8,0},{16,8},{24,16},{28,24},{20,28},{12,20},{4,12},{1,5},{9... | collective-permute-start | bytes 1572872 | tf_op jit(solution)/shard_map/ppermute | solution.py:723
  297.2 14.5 %copy-start.4 = (bf16[1024,2048]{1,0:T(8,128)(2,1)S(1)}, bf16[1024,2048]{1,0:T(8,128)(2,1)}, u32[]{:S(2)}) copy-start(bf16[1024,2048]{1,0:T(8,128)(2,1)} %get-tuple-element.155) | copy-start | bytes 12582916
  297.2 8.6 %collective-permute-start.37 = (bf16[72,16,128]{2,1,0:T(8,128)(2,1)S(1)}, bf16[72,16,128]{2,1,0:T(8,128)(2,1)S(1)}, u32[]{:S(2)}, u32[]{:S(2)}) collective-permute-start(bf16[72,16,128]{2,1,0:T(8,128)(2,1)S(1)} %pad_maximum_fusion.2), channel_id=1, source_target_pairs={{0,4},{4,0},{8,12},{12,8},{16,20},{20,16},{24,28},{28,24},{1,5},{5... | collective-permute-start | bytes 884744 | tf_op jit(solution)/shard_map/ppermute | solution.py:787
  300.1 9.8 %collective-permute-start.38 = (bf16[128,2048]{1,0:T(8,128)(2,1)S(1)}, bf16[128,2048]{1,0:T(8,128)(2,1)S(1)}, u32[]{:S(2)}, u32[]{:S(2)}) collective-permute-start(bf16[128,2048]{1,0:T(8,128)(2,1)S(1)} %get-tuple-element.189), channel_id=1, source_target_pairs={{0,8},{8,16},{16,24},{24,28},{28,20},{20,12},{12,4},{4,0},{1,9},{9... | collective-permute-start | bytes 1572872 | tf_op jit(solution)/shard_map/ppermute | solution.py:723
  300.8 9.2 %collective-permute-start.39 = (bf16[128,2048]{1,0:T(8,128)(2,1)S(1)}, bf16[128,2048]{1,0:T(8,128)(2,1)S(1)}, u32[]{:S(2)}, u32[]{:S(2)}) collective-permute-start(bf16[128,2048]{1,0:T(8,128)(2,1)S(1)} %get-tuple-element.188), channel_id=1, source_target_pairs={{0,4},{8,0},{16,8},{24,16},{28,24},{20,28},{12,20},{4,12},{1,5},{9... | collective-permute-start | bytes 1572872 | tf_op jit(solution)/shard_map/ppermute | solution.py:723
  303.8 11.9 %collective-permute-start.44 = (bf16[128,2048]{1,0:T(8,128)(2,1)S(1)}, bf16[128,2048]{1,0:T(8,128)(2,1)S(1)}, u32[]{:S(2)}, u32[]{:S(2)}) collective-permute-start(bf16[128,2048]{1,0:T(8,128)(2,1)S(1)} %get-tuple-element.185), channel_id=1, source_target_pairs={{0,4},{8,0},{16,8},{24,16},{28,24},{20,28},{12,20},{4,12},{1,5},{9... | collective-permute-start | bytes 1572872 | tf_op jit(solution)/shard_map/ppermute | solution.py:723
  304.9 10.7 %collective-permute-start.43 = (bf16[128,2048]{1,0:T(8,128)(2,1)S(1)}, bf16[128,2048]{1,0:T(8,128)(2,1)S(1)}, u32[]{:S(2)}, u32[]{:S(2)}) collective-permute-start(bf16[128,2048]{1,0:T(8,128)(2,1)S(1)} %get-tuple-element.184), channel_id=1, source_target_pairs={{0,8},{8,16},{16,24},{24,28},{28,20},{20,12},{12,4},{4,0},{1,9},{9... | collective-permute-start | bytes 1572872 | tf_op jit(solution)/shard_map/ppermute | solution.py:723
  305.9 16.8 %copy-start.1 = (bf16[1,128,2048]{2,1,0:T(8,128)(2,1)S(1)}, bf16[1,128,2048]{2,1,0:T(8,128)(2,1)}, u32[]{:S(2)}) copy-start(bf16[1,128,2048]{2,1,0:T(8,128)(2,1)} %param.23) | copy-start | bytes 1572868
  310.1 12.7 %collective-permute-start.40 = (bf16[140,16,128]{2,1,0:T(8,128)(2,1)S(1)}, bf16[140,16,128]{2,1,0:T(8,128)(2,1)S(1)}, u32[]{:S(2)}, u32[]{:S(2)}) collective-permute-start(bf16[140,16,128]{2,1,0:T(8,128)(2,1)S(1)} %constant_dynamic-update-slice_fusion.3.refs_0_), channel_id=1, source_target_pairs={{0,2},{1,3},{2,0},{3,1},{4,6},{5,7},{6,4},{7,5},{8,10},{9,11},{10,... | collective-permute-start | bytes 1720328 | tf_op jit(solution)/shard_map/ppermute | solution.py:787
  312.1 9.2 %collective-permute-start.41 = (bf16[128,2048]{1,0:T(8,128)(2,1)S(1)}, bf16[128,2048]{1,0:T(8,128)(2,1)S(1)}, u32[]{:S(2)}, u32[]{:S(2)}) collective-permute-start(bf16[128,2048]{1,0:T(8,128)(2,1)S(1)} %get-tuple-element.187), channel_id=1, source_target_pairs={{0,8},{8,16},{16,24},{24,28},{28,20},{20,12},{12,4},{4,0},{1,9},{9... | collective-permute-start | bytes 1572872 | tf_op jit(solution)/shard_map/ppermute | solution.py:723
  313.6 9.2 %collective-permute-start.42 = (bf16[128,2048]{1,0:T(8,128)(2,1)S(1)}, bf16[128,2048]{1,0:T(8,128)(2,1)S(1)}, u32[]{:S(2)}, u32[]{:S(2)}) collective-permute-start(bf16[128,2048]{1,0:T(8,128)(2,1)S(1)} %get-tuple-element.186), channel_id=1, source_target_pairs={{0,4},{8,0},{16,8},{24,16},{28,24},{20,28},{12,20},{4,12},{1,5},{9... | collective-permute-start | bytes 1572872 | tf_op jit(solution)/shard_map/ppermute | solution.py:723
  323.2 2.6 collective-permute-start.46
  323.3 2.8 collective-permute-start.45
  (16 other events, 119.2 us)
Sparse Core Ops, SparseCore 0:
  85.2 23.8 all-gather.5
  110.7 22.5 all-gather.3

commit v6 on v5

--- a/solution.py
+++ b/solution.py
@@ -113,6 +113,22 @@
         at = before.shape[0] - (taps - 1 - tap)
         out = out + weight_ref[tap : tap + 1, :] * padded[at : at + x.shape[0]]
     return out
+
+
+def normalise_kernel(rows_ref, gain_ref, out_ref, inverse_ref):
+    rows = rows_ref[0].astype(F32)
+    inverse = lax.rsqrt(jnp.mean(rows * rows, axis=-1, keepdims=True) + EPS)
+    out_ref[...] = (rows * inverse * gain_ref[...].astype(F32)).astype(BF16)
+    inverse_ref[...] = jnp.broadcast_to(inverse, inverse_ref.shape)
+
+
+def normalise(rows, gain):
+    _, tokens, width = rows.shape
+    return pl.pallas_call(
+        normalise_kernel,
+        out_shape=[jax.ShapeDtypeStruct((tokens, width), BF16), jax.ShapeDtypeStruct((tokens, 128), F32)],
+        name="normalise",
+    )(rows, gain)
 
 
 def project_kernel(meta, *refs, parts, groups):
@@ -691,9 +707,9 @@
         functools.partial(place_kernel, groups=groups, parts=parts, chans=chans, span=span, every=every, wide=wide),
         grid_spec=pltpu.PrefetchScalarGridSpec(
             num_scalar_prefetch=1,
-            grid=(adapters // 2,),
+            grid=(adapters // 4,),
             in_specs=[once(value) for value in values],
-            out_specs=[pl.BlockSpec((2, rank, size), lambda i, meta: (i, 0, 0)) for size in sizes],
+            out_specs=[pl.BlockSpec((4, rank, size), lambda i, meta: (i, 0, 0)) for size in sizes],
         ),
         out_shape=[jax.ShapeDtypeStruct((adapters, rank, size), F32) for size in sizes],
         compiler_params=pltpu.CompilerParams(vmem_limit_bytes=32 << 20),
@@ -835,8 +851,8 @@
 
     hidden_f = hidden[0].astype(F32)
     gain_f = norm_gain.astype(F32)
-    inverse = lax.rsqrt(jnp.mean(hidden_f * hidden_f, axis=-1, keepdims=True) + EPS)
-    normed = (hidden_f * inverse * gain_f).astype(BF16)
+    normed, inverse = normalise(hidden, norm_gain[None])
+    inverse = inverse[:, :1]
     positions = part * tokens + lax.broadcasted_iota(jnp.int32, (tokens, 1), 0)
     valid = (positions < lengths[0]).astype(F32)
     cot_f = cotangent[0].astype(F32)

time: 340 us -> 339 us (level)
  other arithmetic: 27.8 us -> 23.2 us
  transfers between devices with their start and end apart: 53 -> 53, of which waited for: 29 -> 27; matrix products, arithmetic and copies ran while one was open for 9% -> 9% of each run, Pallas kernels for 17% -> 17%
where the time goes in v6:
time: 339 us; the launch traced here: 338 us
  Pallas kernels  108 us (32%)
  waiting for transfers between devices  104 us (31%)
  starting transfers between devices  71.3 us (21%)
  other arithmetic  23.2 us (7%)
  between operations  16 us (5%)
  local copies, waits for them, and re-layouts  11 us (3%)
  matrix products  4.74 us (1%)
    ppermute x32, waiting for transfers between devices, ring_send(): return lax.ppermute(value, axis, pairs)  62.2 us
    pallas_call x1, Pallas kernels, scan(): pl.pallas_call(functools.partial(scan_kernel, sub=sub, ranks=ranks), grid...  41.6 us
    ppermute x32, starting transfers between devices, ring_send(): return lax.ppermute(value, axis, pairs)  39.5 us
    ppermute x15, waiting for transfers between devices, swap(): return lax.ppermute(value, axis, [(i, i ^ bit) for i in range(size)])  29.1 us
    pallas_call x1, Pallas kernels, finish(): pl.pallas_call(functools.partial(finish_kernel, ranks=ranks, states=state...  18.7 us
    pallas_call x1, Pallas kernels, project(): pl.pallas_call(functools.partial(project_kernel, parts=parts, groups=grou...  11.9 us
    ppermute x15, starting transfers between devices, swap(): return lax.ppermute(value, axis, [(i, i ^ bit) for i in range(size)])  11.8 us
    pallas_call x1, Pallas kernels, back_gate(): pl.pallas_call(functools.partial(back_gate_kernel, parts=parts), grid_spe...  11.3 us
  transfers between devices with their start and end apart: 53, of which 27 were waited for; matrix products, arithmetic and copies ran while one was open for 9% of the time, Pallas kernels for 17%

profile of v6, /device:TPU:0, one launch (start us, length us, event | category | flops | bytes accessed | tf_op | source)
XLA Modules:
  0.0 338.0 jit_solution(1473288571829162610)
XLA Ops:
  8.5 2.1 normalise.1
  10.5 3.0 collective-permute-start
  13.5 1.9 split_columns.3
  15.4 6.3 %all-to-all-start = ((bf16[8,64,512]{2,1,0:T(8,128)(2,1)}), bf16[8,64,512]{2,1,0:T(8,128)(2,1)}, u32[]{:S(2)}, u32[]{:S(2)}) async-start(bf16[8,64,512]{2,1,0:T(8,128)(2,1)} %split_columns.3), calls=%async_computation | async-start | bytes 1048576 | tf_op jit(solution)/shard_map/all_to_all | solution.py:867
  27.4 1.9 split_columns.2
  31.2 2.1 collective-permute-start.2
  33.4 7.6 %all-to-all-done.refs_9_ = bf16[8,64,512]{2,1,0:T(8,128)(2,1)} async-done(((bf16[8,64,512]{2,1,0:T(8,128)(2,1)}), bf16[8,64,512]{2,1,0:T(8,128)(2,1)}, u32[]{:S(2)}, u32[]{:S(2)}) %all-to-all-start) | async-done | bytes 524320 | tf_op jit(solution)/shard_map/all_to_all | solution.py:867
  41.0 1.5 collective-permute-start.8
  42.5 3.0 collective-permute-done.2.refs_3_
  45.5 3.5 %collective-permute-start.4 = (bf16[128,2048]{1,0:T(8,128)(2,1)S(1)}, bf16[128,2048]{1,0:T(8,128)(2,1)S(1)}, u32[]{:S(2)}, u32[]{:S(2)}) collective-permute-start(bf16[128,2048]{1,0:T(8,128)(2,1)S(1)} %collective-permute-done.2.refs_3_), channel_id=1, source_target_pairs={{0,8},{8,16},{16,24},{24,28},{28,20},{20,12},{12,4},{4,0},{1,9},{9... | collective-permute-start | bytes 1572872 | tf_op jit(solution)/shard_map/ppermute | solution.py:739
  51.1 8.4 %collective-permute-done.4.refs_5_ = bf16[128,2048]{1,0:T(8,128)(2,1)S(1)} collective-permute-done((bf16[128,2048]{1,0:T(8,128)(2,1)S(1)}, bf16[128,2048]{1,0:T(8,128)(2,1)S(1)}, u32[]{:S(2)}, u32[]{:S(2)}) %collective-permute-start.4) | collective-permute-done | bytes 524320 | tf_op jit(solution)/shard_map/ppermute | solution.py:739
  59.5 2.4 collective-permute-start.6
  62.7 2.0 fusion.refs_0_
  64.7 2.8 collective-permute-done.6.refs_7_
  67.5 1.5 collective-permute-done.7.refs_8_
  69.0 4.2 %all-to-all-start.1 = ((bf16[8,64,512]{2,1,0:T(8,128)(2,1)}), bf16[8,64,512]{2,1,0:T(8,128)(2,1)}, u32[]{:S(2)}, u32[]{:S(2)}) async-start(bf16[8,64,512]{2,1,0:T(8,128)(2,1)} %split_columns.2), calls=%async_computation.1 | async-start | bytes 1048576 | tf_op jit(solution)/shard_map/all_to_all | solution.py:867
  73.3 11.9 %project.1 = (bf16[1024,16]{1,0:T(8,128)(2,1)}, bf16[1024,512]{1,0:T(8,128)(2,1)}, bf16[1024,512]{1,0:T(8,128)(2,1)}, bf16[8,176,128]{2,1,0:T(8,128)(2,1)}) custom-call(s32[3]{0:T(128)} %pad_add_fusion.meta, bf16[128,2048]{1,0:T(8,128)(2,1)} %get-tuple-element.104.refs_0_, bf16[128,2048]{1,0:T(8,128)(2,1)} %copy-done.3, bf16[128,2048]{1,0:T(8,128)(2,1)} %copy-done.4, ...), custom_call_target="tpu_custom_call" | custom-call | tf_op jit(solution)/shard_map/project/pallas_call | solution.py:262
  86.0 2.0 collective-permute-start.11
  88.1 5.9 %all-to-all-start.2 = ((bf16[8,176,128]{2,1,0:T(8,128)(2,1)}), bf16[8,176,128]{2,1,0:T(8,128)(2,1)S(1)}, u32[]{:S(2)}, u32[]{:S(2)}) async-start(bf16[8,176,128]{2,1,0:T(8,128)(2,1)} %get-tuple-element.121), calls=%async_computation.2 | async-start | bytes 720896 | tf_op jit(solution)/shard_map/all_to_all | solution.py:828
  94.0 7.6 %collective-permute-done.11.refs_1_ = bf16[128,2048]{1,0:T(8,128)(2,1)S(1)} collective-permute-done((bf16[128,2048]{1,0:T(8,128)(2,1)}, bf16[128,2048]{1,0:T(8,128)(2,1)S(1)}, u32[]{:S(2)}, u32[]{:S(2)}) %collective-permute-start.11) | collective-permute-done | bytes 524320 | tf_op jit(solution)/shard_map/ppermute | solution.py:739
  101.6 2.9 collective-permute-start.12
  104.7 8.8 %collective-permute-done.12.refs_3_ = bf16[128,2048]{1,0:T(8,128)(2,1)S(1)} collective-permute-done((bf16[128,2048]{1,0:T(8,128)(2,1)S(1)}, bf16[128,2048]{1,0:T(8,128)(2,1)S(1)}, u32[]{:S(2)}, u32[]{:S(2)}) %collective-permute-start.12) | collective-permute-done | bytes 524320 | tf_op jit(solution)/shard_map/ppermute | solution.py:739
  113.5 2.2 collective-permute-done.14.refs_4_
  116.5 3.7 %collective-permute-start.16 = (bf16[128,2048]{1,0:T(8,128)(2,1)S(1)}, bf16[128,2048]{1,0:T(8,128)(2,1)S(1)}, u32[]{:S(2)}, u32[]{:S(2)}) collective-permute-start(bf16[128,2048]{1,0:T(8,128)(2,1)S(1)} %collective-permute-done.12.refs_3_), channel_id=1, source_target_pairs={{0,8},{8,16},{16,24},{24,28},{28,20},{20,12},{12,4},{4,0},{1,9},{9... | collective-permute-start | bytes 1572872 | tf_op jit(solution)/shard_map/ppermute | solution.py:739
  120.2 2.7 share.1
  122.9 2.0 collective-permute-start.15
  124.9 8.2 %gate.1.z_ref = bf16[1024,512]{1,0:T(8,128)(2,1)} custom-call(s32[3]{0:T(128)} %pad_add_fusion.meta, bf16[128,2048]{1,0:T(8,128)(2,1)} %get-tuple-element.104.refs_0_, bf16[128,2048]{1,0:T(8,128)(2,1)} %copy-done.3, bf16[128,2048]{1,0:T(8,128)(2,1)} %copy-done.4, bf16[128,2048]{1,0:T(8,128)(2,1)} %copy-done.5, bf16[128,2048]{1,0:T(8,128)(2,1)} %copy-done.6, ...), custom_call_target="tpu_custom_call" | custom-call | tf_op jit(solution)/shard_map/gate/pallas_call | solution.py:195
  134.2 1.8 collective-permute-start.20
  138.9 1.5 collective-permute-start.19
  141.4 2.0 collective-permute-done.21.refs_8_
  143.4 11.3 %back_gate.1 = (bf16[1024,16]{1,0:T(8,128)(2,1)}, bf16[1024,256]{1,0:T(8,128)(2,1)}, bf16[1024,512]{1,0:T(8,128)(2,1)}) custom-call(s32[3]{0:T(128)} %pad_add_fusion.meta, bf16[128,2048]{1,0:T(8,128)(2,1)} %fusion.refs_0_, bf16[128,2048]{1,0:T(8,128)(2,1)} %copy-done.18, bf16[128,2048]{1,0:T(8,128)(2,1)} %copy-done.19, bf16[128,2048]{1,0:T(8,128)(2,1)} %copy-done.20, ...), custom_call_target="tpu_custom_call" | custom-call | tf_op jit(solution)/shard_map/back_gate/pallas_call | solution.py:238
  156.6 41.6 %scan.1 = (bf16[1024,512]{1,0:T(8,128)(2,1)}, bf16[1024,512]{1,0:T(8,128)(2,1)}, f32[1024,512]{1,0:T(8,128)}, bf16[1024,512]{1,0:T(8,128)(2,1)}, bf16[8,192,128]{2,1,0:T(8,128)(2,1)}) custom-call(s32[3]{0:T(128)} %pad_add_fusion.meta, bf16[8,128,192]{2,1,0:T(8,128)(2,1)} %copy-done.9, bf16[1024,512]{1,0:T(8,128)(2,1)} %get-tuple-element.131.u_ref.refs_21_, ...), custom_call_target="tpu_custom_call" | custom-call | tf_op jit(solution)/shard_map/scan/pallas_call | solution.py:492
  198.2 3.7 %all-to-all-start.3 = ((bf16[8,192,128]{2,1,0:T(8,128)(2,1)}), bf16[8,192,128]{2,1,0:T(8,128)(2,1)S(1)}, u32[]{:S(2)}, u32[]{:S(2)}) async-start(bf16[8,192,128]{2,1,0:T(8,128)(2,1)} %get-tuple-element.140), calls=%async_computation.3 | async-start | bytes 786432 | tf_op jit(solution)/shard_map/all_to_all | solution.py:828
  201.9 3.6 %convolution_convert_fusion = bf16[1024,2048]{1,0:T(8,128)(2,1)S(1)} fusion(bf16[1024,512]{1,0:T(8,128)(2,1)} %get-tuple-element.141.refs_23_, bf16[512,2048]{1,0:T(8,128)(2,1)S(1)} %copy-done.13), kind=kOutput, calls=%fused_computation | convolution fusion | flops 2149580800 | bytes 7340032 | tf_op jit(solution)/shard_map/dot_general | solution.py:28
  205.4 2.0 copy-done.8
  207.5 2.1 collective-permute-start.23
  209.6 4.0 %all-to-all-done.3.got_ref = bf16[8,192,128]{2,1,0:T(8,128)(2,1)S(1)} async-done(((bf16[8,192,128]{2,1,0:T(8,128)(2,1)}), bf16[8,192,128]{2,1,0:T(8,128)(2,1)S(1)}, u32[]{:S(2)}, u32[]{:S(2)}) %all-to-all-start.3) | async-done | bytes 393248 | tf_op jit(solution)/shard_map/all_to_all | solution.py:828
  214.4 2.5 share_back.1
  217.3 6.1 %collective-permute-done.22 = bf16[1,128,192]{2,1,0:T(8,128)(2,1)S(1)} collective-permute-done((bf16[1,128,192]{2,1,0:T(8,128)(2,1)}, bf16[1,128,192]{2,1,0:T(8,128)(2,1)S(1)}, u32[]{:S(2)}, u32[]{:S(2)}) %collective-permute-start.22) | collective-permute-done | bytes 49184 | tf_op jit(solution)/shard_map/ppermute | solution.py:803
  224.3 1.4 add_convert_fusion.10
  225.7 2.1 collective-permute-start.27
  227.8 1.5 collective-permute-done.25
  230.0 13.1 %collective-permute-done.26 = bf16[4,128,192]{2,1,0:T(8,128)(2,1)S(1)} collective-permute-done((bf16[4,128,192]{2,1,0:T(8,128)(2,1)S(1)}, bf16[4,128,192]{2,1,0:T(8,128)(2,1)S(1)}, u32[]{:S(2)}, u32[]{:S(2)}) %collective-permute-start.26) | collective-permute-done | bytes 196640 | tf_op jit(solution)/shard_map/ppermute | solution.py:803
  244.0 1.6 add_convert_fusion.8
  245.7 2.3 collective-permute-start.30
  248.0 18.7 %finish.1 = (bf16[1024,2048]{1,0:T(8,128)(2,1)}, bf16[30,16,128]{2,1,0:T(8,128)(2,1)}, bf16[12,16,128]{2,1,0:T(8,128)(2,1)}) custom-call(s32[3]{0:T(128)} %pad_add_fusion.meta, bf16[128,2048]{1,0:T(8,128)(2,1)} %get-tuple-element.104.refs_0_, bf16[128,2048]{1,0:T(8,128)(2,1)} %copy-done.3, bf16[128,2048]{1,0:T(8,128)(2,1)} %copy-done.4, ...), custom_call_target="tpu_custom_call" | custom-call | tf_op jit(solution)/shard_map/finish/pallas_call | solution.py:636
  269.9 1.6 collective-permute-start.32
  271.9 1.9 collective-permute-done.31
  274.8 3.7 %collective-permute-done.32 = bf16[64,2048]{1,0:T(8,128)(2,1)S(1)} collective-permute-done((bf16[64,2048]{1,0:T(8,128)(2,1)S(1)}, bf16[64,2048]{1,0:T(8,128)(2,1)S(1)}, u32[]{:S(2)}, u32[]{:S(2)}) %collective-permute-start.32) | collective-permute-done | bytes 262176 | tf_op jit(solution)/shard_map/ppermute | solution.py:739
  278.7 1.4 add_convert_fusion.6
  280.1 1.9 collective-permute-start.35
  282.5 3.5 %collective-permute-done.34 = bf16[44,16,128]{2,1,0:T(8,128)(2,1)S(1)} collective-permute-done((bf16[44,16,128]{2,1,0:T(8,128)(2,1)S(1)}, bf16[44,16,128]{2,1,0:T(8,128)(2,1)S(1)}, u32[]{:S(2)}, u32[]{:S(2)}) %collective-permute-start.34) | collective-permute-done | bytes 180256 | tf_op jit(solution)/shard_map/ppermute | solution.py:803
  286.1 9.1 %collective-permute-done.35 = bf16[128,2048]{1,0:T(8,128)(2,1)S(1)} collective-permute-done((bf16[128,2048]{1,0:T(8,128)(2,1)S(1)}, bf16[128,2048]{1,0:T(8,128)(2,1)S(1)}, u32[]{:S(2)}, u32[]{:S(2)}) %collective-permute-start.35) | collective-permute-done | bytes 524320 | tf_op jit(solution)/shard_map/ppermute | solution.py:739
  295.2 2.2 collective-permute-done.36
  297.4 2.3 collective-permute-start.37
  300.2 2.0 collective-permute-start.39
  302.2 1.6 add_convert_fusion.1
  303.9 2.0 collective-permute-start.43
  306.0 4.7 %collective-permute-done.38 = bf16[128,2048]{1,0:T(8,128)(2,1)S(1)} collective-permute-done((bf16[128,2048]{1,0:T(8,128)(2,1)S(1)}, bf16[128,2048]{1,0:T(8,128)(2,1)S(1)}, u32[]{:S(2)}, u32[]{:S(2)}) %collective-permute-start.38) | collective-permute-done | bytes 524320 | tf_op jit(solution)/shard_map/ppermute | solution.py:739
  310.8 1.6 collective-permute-start.40
  313.1 1.8 collective-permute-start.42
  317.6 4.4 %collective-permute-done.41 = bf16[128,2048]{1,0:T(8,128)(2,1)S(1)} collective-permute-done((bf16[128,2048]{1,0:T(8,128)(2,1)S(1)}, bf16[128,2048]{1,0:T(8,128)(2,1)S(1)}, u32[]{:S(2)}, u32[]{:S(2)}) %collective-permute-start.41) | collective-permute-done | bytes 524320 | tf_op jit(solution)/shard_map/ppermute | solution.py:739
  323.3 2.0 fusion.2
  325.8 5.4 %place.1 = (f32[8,16,8192]{2,1,0:T(8,128)}, f32[8,16,4096]{2,1,0:T(8,128)}, f32[8,16,2048]{2,1,0:T(8,128)}, f32[8,16,2048]{2,1,0:T(8,128)}, f32[8,16,512]{2,1,0:...) custom-call(s32[7]{0:T(128)S(1)} %pad_add_fusion.1.meta, ...), custom_call_target="tpu_custom_call" | custom-call | tf_op jit(solution)/shard_map/place/pallas_call | solution.py:706
  (170 shorter events, 34.6 us)
Async XLA Ops:
  10.5 20.7 %collective-permute-start = (bf16[128,2048]{1,0:T(8,128)(2,1)}, bf16[128,2048]{1,0:T(8,128)(2,1)S(1)}, u32[]{:S(2)}, u32[]{:S(2)}) collective-permute-start(bf16[128,2048]{1,0:T(8,128)(2,1)} %get-tuple-element.104.refs_0_), channel_id=1, source_target_pairs={{0,8},{8,16},{16,24},{24,28},{28,20},{20,12},{12,4},{4,0},{1,9},{9... | collective-permute-start | bytes 1572872 | tf_op jit(solution)/shard_map/ppermute | solution.py:739
  13.5 17.7 %collective-permute-start.1 = (bf16[128,2048]{1,0:T(8,128)(2,1)}, bf16[128,2048]{1,0:T(8,128)(2,1)S(1)}, u32[]{:S(2)}, u32[]{:S(2)}) collective-permute-start(bf16[128,2048]{1,0:T(8,128)(2,1)} %get-tuple-element.104.refs_0_), channel_id=1, source_target_pairs={{0,4},{8,0},{16,8},{24,16},{28,24},{20,28},{12,20},{4,12},{1,5},{9... | collective-permute-start | bytes 1572872 | tf_op jit(solution)/shard_map/ppermute | solution.py:739
  15.4 25.5 %all-to-all-start = ((bf16[8,64,512]{2,1,0:T(8,128)(2,1)}), bf16[8,64,512]{2,1,0:T(8,128)(2,1)}, u32[]{:S(2)}, u32[]{:S(2)}) async-start(bf16[8,64,512]{2,1,0:T(8,128)(2,1)} %split_columns.3), calls=%async_computation | async-start | bytes 1048576 | tf_op jit(solution)/shard_map/all_to_all | solution.py:867
  31.2 42.0 %copy-start.3 = (bf16[128,2048]{1,0:T(8,128)(2,1)}, bf16[128,2048]{1,0:T(8,128)(2,1)S(1)}, u32[]{:S(2)}) copy-start(bf16[128,2048]{1,0:T(8,128)(2,1)S(1)} %collective-permute-done.refs_1_) | copy-start | bytes 1572868
  31.2 42.0 %copy-start.4 = (bf16[128,2048]{1,0:T(8,128)(2,1)}, bf16[128,2048]{1,0:T(8,128)(2,1)S(1)}, u32[]{:S(2)}) copy-start(bf16[128,2048]{1,0:T(8,128)(2,1)S(1)} %collective-permute-done.1.refs_2_) | copy-start | bytes 1572868
  31.2 14.3 %collective-permute-start.2 = (bf16[128,2048]{1,0:T(8,128)(2,1)S(1)}, bf16[128,2048]{1,0:T(8,128)(2,1)S(1)}, u32[]{:S(2)}, u32[]{:S(2)}) collective-permute-start(bf16[128,2048]{1,0:T(8,128)(2,1)S(1)} %collective-permute-done.refs_1_), channel_id=1, source_target_pairs={{0,8},{8,16},{16,24},{24,28},{28,20},{20,12},{12,4},{4,0},{1,9},{9... | collective-permute-start | bytes 1572872 | tf_op jit(solution)/shard_map/ppermute | solution.py:739
  33.3 15.7 %collective-permute-start.3 = (bf16[128,2048]{1,0:T(8,128)(2,1)S(1)}, bf16[128,2048]{1,0:T(8,128)(2,1)S(1)}, u32[]{:S(2)}, u32[]{:S(2)}) collective-permute-start(bf16[128,2048]{1,0:T(8,128)(2,1)S(1)} %collective-permute-done.1.refs_2_), channel_id=1, source_target_pairs={{0,4},{8,0},{16,8},{24,16},{28,24},{20,28},{12,20},{4,12},{1,5},{9... | collective-permute-start | bytes 1572872 | tf_op jit(solution)/shard_map/ppermute | solution.py:739
  41.0 10.1 %collective-permute-start.8 = (bf16[8,64,512]{2,1,0:T(8,128)(2,1)}, bf16[8,64,512]{2,1,0:T(8,128)(2,1)}, u32[]{:S(2)}, u32[]{:S(2)}) collective-permute-start(bf16[8,64,512]{2,1,0:T(8,128)(2,1)} %all-to-all-done.refs_9_), channel_id=1, source_target_pairs={{0,2},{1,3},{2,0},{3,1},{4,6},{5,7},{6,4},{7,5},{8,10},{9,11},{10,... | collective-permute-start | bytes 1572872 | tf_op jit(solution)/shard_map/ppermute | solution.py:803
  45.5 27.7 %copy-start.5 = (bf16[128,2048]{1,0:T(8,128)(2,1)}, bf16[128,2048]{1,0:T(8,128)(2,1)S(1)}, u32[]{:S(2)}) copy-start(bf16[128,2048]{1,0:T(8,128)(2,1)S(1)} %collective-permute-done.2.refs_3_) | copy-start | bytes 1572868
  45.5 14.0 %collective-permute-start.4 = (bf16[128,2048]{1,0:T(8,128)(2,1)S(1)}, bf16[128,2048]{1,0:T(8,128)(2,1)S(1)}, u32[]{:S(2)}, u32[]{:S(2)}) collective-permute-start(bf16[128,2048]{1,0:T(8,128)(2,1)S(1)} %collective-permute-done.2.refs_3_), channel_id=1, source_target_pairs={{0,8},{8,16},{16,24},{24,28},{28,20},{20,12},{12,4},{4,0},{1,9},{9... | collective-permute-start | bytes 1572872 | tf_op jit(solution)/shard_map/ppermute | solution.py:739
  49.0 24.2 %copy-start.6 = (bf16[128,2048]{1,0:T(8,128)(2,1)}, bf16[128,2048]{1,0:T(8,128)(2,1)S(1)}, u32[]{:S(2)}) copy-start(bf16[128,2048]{1,0:T(8,128)(2,1)S(1)} %collective-permute-done.3.refs_4_) | copy-start | bytes 1572868
  49.0 13.4 %collective-permute-start.5 = (bf16[128,2048]{1,0:T(8,128)(2,1)S(1)}, bf16[128,2048]{1,0:T(8,128)(2,1)S(1)}, u32[]{:S(2)}, u32[]{:S(2)}) collective-permute-start(bf16[128,2048]{1,0:T(8,128)(2,1)S(1)} %collective-permute-done.3.refs_4_), channel_id=1, source_target_pairs={{0,4},{8,0},{16,8},{24,16},{28,24},{20,28},{12,20},{4,12},{1,5},{9... | collective-permute-start | bytes 1572872 | tf_op jit(solution)/shard_map/ppermute | solution.py:739
  49.7 15.1 %collective-permute-start.9 = (bf16[8,64,512]{2,1,0:T(8,128)(2,1)}, bf16[8,64,512]{2,1,0:T(8,128)(2,1)S(1)}, u32[]{:S(2)}, u32[]{:S(2)}) collective-permute-start(bf16[8,64,512]{2,1,0:T(8,128)(2,1)} %all-to-all-done.refs_9_), channel_id=1, source_target_pairs={{0,1},{1,0},{2,3},{3,2},{4,5},{5,4},{6,7},{7,6},{8,9},{9,8},{10,11... | collective-permute-start | bytes 1572872 | tf_op jit(solution)/shard_map/ppermute | solution.py:803
  51.1 17.9 %collective-permute-start.10 = (bf16[8,64,512]{2,1,0:T(8,128)(2,1)}, bf16[8,64,512]{2,1,0:T(8,128)(2,1)}, u32[]{:S(2)}, u32[]{:S(2)}) collective-permute-start(bf16[8,64,512]{2,1,0:T(8,128)(2,1)} %collective-permute-done.8.refs_10_), channel_id=1, source_target_pairs={{0,1},{1,0},{2,3},{3,2},{4,5},{5,4},{6,7},{7,6},{8,9},{9,8},{10,11... | collective-permute-start | bytes 1572872 | tf_op jit(solution)/shard_map/ppermute | solution.py:803
  59.5 8.0 %collective-permute-start.6 = (bf16[64,2048]{1,0:T(8,128)(2,1)S(1)}, bf16[64,2048]{1,0:T(8,128)(2,1)S(1)}, u32[]{:S(2)}, u32[]{:S(2)}) collective-permute-start(bf16[64,2048]{1,0:T(8,128)(2,1)S(1)} %slice.73), channel_id=1, source_target_pairs={{0,8},{8,16},{16,24},{24,28},{28,20},{20,12},{12,4},{4,0},{1,9},{9... | collective-permute-start | bytes 786440 | tf_op jit(solution)/shard_map/ppermute | solution.py:739
  62.4 6.6 %collective-permute-start.7 = (bf16[64,2048]{1,0:T(8,128)(2,1)S(1)}, bf16[64,2048]{1,0:T(8,128)(2,1)}, u32[]{:S(2)}, u32[]{:S(2)}) collective-permute-start(bf16[64,2048]{1,0:T(8,128)(2,1)S(1)} %slice.74), channel_id=1, source_target_pairs={{0,4},{8,0},{16,8},{24,16},{28,24},{20,28},{12,20},{4,12},{1,5},{9... | collective-permute-start | bytes 786440 | tf_op jit(solution)/shard_map/ppermute | solution.py:739
  69.0 16.3 %all-to-all-start.1 = ((bf16[8,64,512]{2,1,0:T(8,128)(2,1)}), bf16[8,64,512]{2,1,0:T(8,128)(2,1)}, u32[]{:S(2)}, u32[]{:S(2)}) async-start(bf16[8,64,512]{2,1,0:T(8,128)(2,1)} %split_columns.2), calls=%async_computation.1 | async-start | bytes 1048576 | tf_op jit(solution)/shard_map/all_to_all | solution.py:867
  73.1 49.7 %all-gather.6.cloned.1.call-start = ((), (), s32[]{:S(2)}) async-start(), calls=%async_computation.5 | async-start | bytes 2621440 | tf_op jit(solution)/shard_map/all_gather | solution.py:889
  85.3 55.2 %all-gather.4.cloned.1.call-start = ((), (), s32[]{:S(2)}) async-start(), calls=%async_computation.4 | async-start | bytes 2621440 | tf_op jit(solution)/shard_map/all_gather | solution.py:870
  86.0 15.5 %collective-permute-start.11 = (bf16[128,2048]{1,0:T(8,128)(2,1)}, bf16[128,2048]{1,0:T(8,128)(2,1)S(1)}, u32[]{:S(2)}, u32[]{:S(2)}) collective-permute-start(bf16[128,2048]{1,0:T(8,128)(2,1)} %fusion.refs_0_), channel_id=1, source_target_pairs={{0,8},{8,16},{16,24},{24,28},{28,20},{20,12},{12,4},{4,0},{1,9},{9... | collective-permute-start | bytes 1572872 | tf_op jit(solution)/shard_map/ppermute | solution.py:739
  88.0 16.5 %collective-permute-start.13 = (bf16[128,2048]{1,0:T(8,128)(2,1)}, bf16[128,2048]{1,0:T(8,128)(2,1)S(1)}, u32[]{:S(2)}, u32[]{:S(2)}) collective-permute-start(bf16[128,2048]{1,0:T(8,128)(2,1)} %fusion.refs_0_), channel_id=1, source_target_pairs={{0,4},{8,0},{16,8},{24,16},{28,24},{20,28},{12,20},{4,12},{1,5},{9... | collective-permute-start | bytes 1572872 | tf_op jit(solution)/shard_map/ppermute | solution.py:739
  88.1 28.4 %all-to-all-start.2 = ((bf16[8,176,128]{2,1,0:T(8,128)(2,1)}), bf16[8,176,128]{2,1,0:T(8,128)(2,1)S(1)}, u32[]{:S(2)}, u32[]{:S(2)}) async-start(bf16[8,176,128]{2,1,0:T(8,128)(2,1)} %get-tuple-element.121), calls=%async_computation.2 | async-start | bytes 720896 | tf_op jit(solution)/shard_map/all_to_all | solution.py:828
  101.6 41.8 %copy-start.18 = (bf16[128,2048]{1,0:T(8,128)(2,1)}, bf16[128,2048]{1,0:T(8,128)(2,1)S(1)}, u32[]{:S(2)}) copy-start(bf16[128,2048]{1,0:T(8,128)(2,1)S(1)} %collective-permute-done.11.refs_1_) | copy-start | bytes 1572868
  101.6 11.9 %collective-permute-start.12 = (bf16[128,2048]{1,0:T(8,128)(2,1)S(1)}, bf16[128,2048]{1,0:T(8,128)(2,1)S(1)}, u32[]{:S(2)}, u32[]{:S(2)}) collective-permute-start(bf16[128,2048]{1,0:T(8,128)(2,1)S(1)} %collective-permute-done.11.refs_1_), channel_id=1, source_target_pairs={{0,8},{8,16},{16,24},{24,28},{28,20},{20,12},{12,4},{4,0},{1,9},{9... | collective-permute-start | bytes 1572872 | tf_op jit(solution)/shard_map/ppermute | solution.py:739
  104.5 38.9 %copy-start.19 = (bf16[128,2048]{1,0:T(8,128)(2,1)}, bf16[128,2048]{1,0:T(8,128)(2,1)S(1)}, u32[]{:S(2)}) copy-start(bf16[128,2048]{1,0:T(8,128)(2,1)S(1)} %collective-permute-done.13.refs_2_) | copy-start | bytes 1572868
  104.5 11.2 %collective-permute-start.14 = (bf16[128,2048]{1,0:T(8,128)(2,1)S(1)}, bf16[128,2048]{1,0:T(8,128)(2,1)S(1)}, u32[]{:S(2)}, u32[]{:S(2)}) collective-permute-start(bf16[128,2048]{1,0:T(8,128)(2,1)S(1)} %collective-permute-done.13.refs_2_), channel_id=1, source_target_pairs={{0,4},{8,0},{16,8},{24,16},{28,24},{20,28},{12,20},{4,12},{1,5},{9... | collective-permute-start | bytes 1572872 | tf_op jit(solution)/shard_map/ppermute | solution.py:739
  113.5 29.9 %copy-start.20 = (bf16[128,2048]{1,0:T(8,128)(2,1)}, bf16[128,2048]{1,0:T(8,128)(2,1)S(1)}, u32[]{:S(2)}) copy-start(bf16[128,2048]{1,0:T(8,128)(2,1)S(1)} %collective-permute-done.12.refs_3_) | copy-start | bytes 1572868
  116.5 16.6 %collective-permute-start.16 = (bf16[128,2048]{1,0:T(8,128)(2,1)S(1)}, bf16[128,2048]{1,0:T(8,128)(2,1)S(1)}, u32[]{:S(2)}, u32[]{:S(2)}) collective-permute-start(bf16[128,2048]{1,0:T(8,128)(2,1)S(1)} %collective-permute-done.12.refs_3_), channel_id=1, source_target_pairs={{0,8},{8,16},{16,24},{24,28},{28,20},{20,12},{12,4},{4,0},{1,9},{9... | collective-permute-start | bytes 1572872 | tf_op jit(solution)/shard_map/ppermute | solution.py:739
  120.2 13.0 %collective-permute-start.17 = (bf16[128,2048]{1,0:T(8,128)(2,1)}, bf16[128,2048]{1,0:T(8,128)(2,1)S(1)}, u32[]{:S(2)}, u32[]{:S(2)}) collective-permute-start(bf16[128,2048]{1,0:T(8,128)(2,1)} %copy-done.21), channel_id=1, source_target_pairs={{0,4},{8,0},{16,8},{24,16},{28,24},{20,28},{12,20},{4,12},{1,5},{9... | collective-permute-start | bytes 1572872 | tf_op jit(solution)/shard_map/ppermute | solution.py:739
  122.9 10.2 %collective-permute-start.15 = (bf16[1,128,192]{2,1,0:T(8,128)(2,1)}, bf16[1,128,192]{2,1,0:T(8,128)(2,1)S(1)}, u32[]{:S(2)}, u32[]{:S(2)}) collective-permute-start(bf16[1,128,192]{2,1,0:T(8,128)(2,1)} %bitcast.61), channel_id=1, source_target_pairs={{0,16},{4,20},{8,24},{12,28},{16,0},{20,4},{24,8},{28,12},{1,17},{... | collective-permute-start | bytes 147464 | tf_op jit(solution)/shard_map/ppermute | solution.py:803
  133.1 5.0 %collective-permute-start.18 = (bf16[2,128,192]{2,1,0:T(8,128)(2,1)S(1)}, bf16[2,128,192]{2,1,0:T(8,128)(2,1)S(1)}, u32[]{:S(2)}, u32[]{:S(2)}) collective-permute-start(bf16[2,128,192]{2,1,0:T(8,128)(2,1)S(1)} %pad_maximum_fusion.7), channel_id=1, source_target_pairs={{0,8},{4,12},{8,0},{12,4},{16,24},{20,28},{24,16},{28,20},{1,9},{5... | collective-permute-start | bytes 294920 | tf_op jit(solution)/shard_map/ppermute | solution.py:803
  134.2 7.2 %collective-permute-start.20 = (bf16[64,2048]{1,0:T(8,128)(2,1)}, bf16[64,2048]{1,0:T(8,128)(2,1)}, u32[]{:S(2)}, u32[]{:S(2)}) collective-permute-start(bf16[64,2048]{1,0:T(8,128)(2,1)} %slice.57), channel_id=1, source_target_pairs={{0,8},{8,16},{16,24},{24,28},{28,20},{20,12},{12,4},{4,0},{1,9},{9... | collective-permute-start | bytes 786440 | tf_op jit(solution)/shard_map/ppermute | solution.py:739
  136.7 6.7 %collective-permute-start.21 = (bf16[64,2048]{1,0:T(8,128)(2,1)}, bf16[64,2048]{1,0:T(8,128)(2,1)}, u32[]{:S(2)}, u32[]{:S(2)}) collective-permute-start(bf16[64,2048]{1,0:T(8,128)(2,1)} %slice.58), channel_id=1, source_target_pairs={{0,4},{8,0},{16,8},{24,16},{28,24},{20,28},{12,20},{4,12},{1,5},{9... | collective-permute-start | bytes 786440 | tf_op jit(solution)/shard_map/ppermute | solution.py:739
  138.9 15.8 %collective-permute-start.19 = (bf16[4,128,192]{2,1,0:T(8,128)(2,1)}, bf16[4,128,192]{2,1,0:T(8,128)(2,1)}, u32[]{:S(2)}, u32[]{:S(2)}) collective-permute-start(bf16[4,128,192]{2,1,0:T(8,128)(2,1)} %pad_maximum_fusion.3), channel_id=1, source_target_pairs={{0,4},{4,0},{8,12},{12,8},{16,20},{20,16},{24,28},{28,24},{1,5},{5... | collective-permute-start | bytes 589832 | tf_op jit(solution)/shard_map/ppermute | solution.py:803
  154.7 47.2 %copy-start.13 = (bf16[512,2048]{1,0:T(8,128)(2,1)S(1)}, bf16[512,2048]{1,0:T(8,128)(2,1)}, u32[]{:S(2)}) copy-start(bf16[512,2048]{1,0:T(8,128)(2,1)} %all-gather.4.cloned.1.call-done.refs_9_) | copy-start | bytes 6291460
  198.2 15.4 %all-to-all-start.3 = ((bf16[8,192,128]{2,1,0:T(8,128)(2,1)}), bf16[8,192,128]{2,1,0:T(8,128)(2,1)S(1)}, u32[]{:S(2)}, u32[]{:S(2)}) async-start(bf16[8,192,128]{2,1,0:T(8,128)(2,1)} %get-tuple-element.140), calls=%async_computation.3 | async-start | bytes 786432 | tf_op jit(solution)/shard_map/all_to_all | solution.py:828
  207.5 40.5 %copy-start.27 = (bf16[2048]{0:T(1024)(128)(2,1)S(1)}, bf16[2048]{0:T(1024)(128)(2,1)}, u32[]{:S(2)}) copy-start(bf16[2048]{0:T(1024)(128)(2,1)} %param.26) | copy-start | bytes 12292
  207.5 16.7 %collective-permute-start.23 = (bf16[64,2048]{1,0:T(8,128)(2,1)S(1)}, bf16[64,2048]{1,0:T(8,128)(2,1)S(1)}, u32[]{:S(2)}, u32[]{:S(2)}) collective-permute-start(bf16[64,2048]{1,0:T(8,128)(2,1)S(1)} %get-tuple-element.203), channel_id=1, source_target_pairs={{0,8},{8,16},{16,24},{24,28},{28,20},{20,12},{12,4},{4,0},{1,9},{9... | collective-permute-start | bytes 786440 | tf_op jit(solution)/shard_map/ppermute | solution.py:739
  209.6 14.7 %collective-permute-start.24 = (bf16[64,2048]{1,0:T(8,128)(2,1)S(1)}, bf16[64,2048]{1,0:T(8,128)(2,1)S(1)}, u32[]{:S(2)}, u32[]{:S(2)}) collective-permute-start(bf16[64,2048]{1,0:T(8,128)(2,1)S(1)} %get-tuple-element.202), channel_id=1, source_target_pairs={{0,4},{8,0},{16,8},{24,16},{28,24},{20,28},{12,20},{4,12},{1,5},{9... | collective-permute-start | bytes 786440 | tf_op jit(solution)/shard_map/ppermute | solution.py:739
  216.9 6.5 %collective-permute-start.22 = (bf16[1,128,192]{2,1,0:T(8,128)(2,1)}, bf16[1,128,192]{2,1,0:T(8,128)(2,1)S(1)}, u32[]{:S(2)}, u32[]{:S(2)}) collective-permute-start(bf16[1,128,192]{2,1,0:T(8,128)(2,1)} %bitcast.59), channel_id=1, source_target_pairs={{0,16},{4,20},{8,24},{12,28},{16,0},{20,4},{24,8},{28,12},{1,17},{... | collective-permute-start | bytes 147464 | tf_op jit(solution)/shard_map/ppermute | solution.py:803
  224.3 5.0 %collective-permute-start.25 = (bf16[2,128,192]{2,1,0:T(8,128)(2,1)S(1)}, bf16[2,128,192]{2,1,0:T(8,128)(2,1)S(1)}, u32[]{:S(2)}, u32[]{:S(2)}) collective-permute-start(bf16[2,128,192]{2,1,0:T(8,128)(2,1)S(1)} %pad_maximum_fusion.8), channel_id=1, source_target_pairs={{0,8},{4,12},{8,0},{12,4},{16,24},{20,28},{24,16},{28,20},{1,9},{5... | collective-permute-start | bytes 294920 | tf_op jit(solution)/shard_map/ppermute | solution.py:803
  225.7 18.3 %collective-permute-start.27 = (bf16[128,2048]{1,0:T(8,128)(2,1)S(1)}, bf16[128,2048]{1,0:T(8,128)(2,1)S(1)}, u32[]{:S(2)}, u32[]{:S(2)}) collective-permute-start(bf16[128,2048]{1,0:T(8,128)(2,1)S(1)} %get-tuple-element.201), channel_id=1, source_target_pairs={{0,8},{8,16},{16,24},{24,28},{28,20},{20,12},{12,4},{4,0},{1,9},{9... | collective-permute-start | bytes 1572872 | tf_op jit(solution)/shard_map/ppermute | solution.py:739
  227.8 16.2 %collective-permute-start.28 = (bf16[128,2048]{1,0:T(8,128)(2,1)S(1)}, bf16[128,2048]{1,0:T(8,128)(2,1)S(1)}, u32[]{:S(2)}, u32[]{:S(2)}) collective-permute-start(bf16[128,2048]{1,0:T(8,128)(2,1)S(1)} %get-tuple-element.200), channel_id=1, source_target_pairs={{0,4},{8,0},{16,8},{24,16},{28,24},{20,28},{12,20},{4,12},{1,5},{9... | collective-permute-start | bytes 1572872 | tf_op jit(solution)/shard_map/ppermute | solution.py:739
  229.3 13.8 %collective-permute-start.26 = (bf16[4,128,192]{2,1,0:T(8,128)(2,1)S(1)}, bf16[4,128,192]{2,1,0:T(8,128)(2,1)S(1)}, u32[]{:S(2)}, u32[]{:S(2)}) collective-permute-start(bf16[4,128,192]{2,1,0:T(8,128)(2,1)S(1)} %pad_maximum_fusion.4), channel_id=1, source_target_pairs={{0,4},{4,0},{8,12},{12,8},{16,20},{20,16},{24,28},{28,24},{1,5},{5... | collective-permute-start | bytes 589832 | tf_op jit(solution)/shard_map/ppermute | solution.py:803
  245.6 21.1 %collective-permute-start.29 = (bf16[128,2048]{1,0:T(8,128)(2,1)S(1)}, bf16[128,2048]{1,0:T(8,128)(2,1)S(1)}, u32[]{:S(2)}, u32[]{:S(2)}) collective-permute-start(bf16[128,2048]{1,0:T(8,128)(2,1)S(1)} %get-tuple-element.199), channel_id=1, source_target_pairs={{0,8},{8,16},{16,24},{24,28},{28,20},{20,12},{12,4},{4,0},{1,9},{9... | collective-permute-start | bytes 1572872 | tf_op jit(solution)/shard_map/ppermute | solution.py:739
  245.7 21.0 %collective-permute-start.30 = (bf16[128,2048]{1,0:T(8,128)(2,1)S(1)}, bf16[128,2048]{1,0:T(8,128)(2,1)S(1)}, u32[]{:S(2)}, u32[]{:S(2)}) collective-permute-start(bf16[128,2048]{1,0:T(8,128)(2,1)S(1)} %get-tuple-element.198), channel_id=1, source_target_pairs={{0,4},{8,0},{16,8},{24,16},{28,24},{20,28},{12,20},{4,12},{1,5},{9... | collective-permute-start | bytes 1572872 | tf_op jit(solution)/shard_map/ppermute | solution.py:739
  266.7 33.0 %copy-start.2 = (bf16[1024,2048]{1,0:T(8,128)(2,1)S(1)}, bf16[1024,2048]{1,0:T(8,128)(2,1)}, u32[]{:S(2)}) copy-start(bf16[1024,2048]{1,0:T(8,128)(2,1)} %get-tuple-element.158) | copy-start | bytes 12582916
  266.7 7.2 %collective-permute-start.31 = (bf16[30,16,128]{2,1,0:T(8,128)(2,1)}, bf16[30,16,128]{2,1,0:T(8,128)(2,1)S(1)}, u32[]{:S(2)}, u32[]{:S(2)}) collective-permute-start(bf16[30,16,128]{2,1,0:T(8,128)(2,1)} %get-tuple-element.157), channel_id=1, source_target_pairs={{0,16},{4,20},{8,24},{12,28},{16,0},{20,4},{24,8},{28,12},{1,17},{... | collective-permute-start | bytes 368648 | tf_op jit(solution)/shard_map/ppermute | solution.py:803
  269.9 8.6 %collective-permute-start.32 = (bf16[64,2048]{1,0:T(8,128)(2,1)S(1)}, bf16[64,2048]{1,0:T(8,128)(2,1)S(1)}, u32[]{:S(2)}, u32[]{:S(2)}) collective-permute-start(bf16[64,2048]{1,0:T(8,128)(2,1)S(1)} %get-tuple-element.197), channel_id=1, source_target_pairs={{0,8},{8,16},{16,24},{24,28},{28,20},{20,12},{12,4},{4,0},{1,9},{9... | collective-permute-start | bytes 786440 | tf_op jit(solution)/shard_map/ppermute | solution.py:739
  271.4 7.0 %collective-permute-start.33 = (bf16[64,2048]{1,0:T(8,128)(2,1)S(1)}, bf16[64,2048]{1,0:T(8,128)(2,1)S(1)}, u32[]{:S(2)}, u32[]{:S(2)}) collective-permute-start(bf16[64,2048]{1,0:T(8,128)(2,1)S(1)} %get-tuple-element.196), channel_id=1, source_target_pairs={{0,4},{8,0},{16,8},{24,16},{28,24},{20,28},{12,20},{4,12},{1,5},{9... | collective-permute-start | bytes 786440 | tf_op jit(solution)/shard_map/ppermute | solution.py:739
  278.4 7.6 %collective-permute-start.34 = (bf16[44,16,128]{2,1,0:T(8,128)(2,1)S(1)}, bf16[44,16,128]{2,1,0:T(8,128)(2,1)S(1)}, u32[]{:S(2)}, u32[]{:S(2)}) collective-permute-start(bf16[44,16,128]{2,1,0:T(8,128)(2,1)S(1)} %pad_maximum_fusion.6), channel_id=1, source_target_pairs={{0,8},{4,12},{8,0},{12,4},{16,24},{20,28},{24,16},{28,20},{1,9},{5... | collective-permute-start | bytes 540680 | tf_op jit(solution)/shard_map/ppermute | solution.py:803
  280.1 15.1 %collective-permute-start.35 = (bf16[128,2048]{1,0:T(8,128)(2,1)S(1)}, bf16[128,2048]{1,0:T(8,128)(2,1)S(1)}, u32[]{:S(2)}, u32[]{:S(2)}) collective-permute-start(bf16[128,2048]{1,0:T(8,128)(2,1)S(1)} %get-tuple-element.195), channel_id=1, source_target_pairs={{0,8},{8,16},{16,24},{24,28},{28,20},{20,12},{12,4},{4,0},{1,9},{9... | collective-permute-start | bytes 1572872 | tf_op jit(solution)/shard_map/ppermute | solution.py:739
  282.0 15.4 %collective-permute-start.36 = (bf16[128,2048]{1,0:T(8,128)(2,1)S(1)}, bf16[128,2048]{1,0:T(8,128)(2,1)S(1)}, u32[]{:S(2)}, u32[]{:S(2)}) collective-permute-start(bf16[128,2048]{1,0:T(8,128)(2,1)S(1)} %get-tuple-element.194), channel_id=1, source_target_pairs={{0,4},{8,0},{16,8},{24,16},{28,24},{20,28},{12,20},{4,12},{1,5},{9... | collective-permute-start | bytes 1572872 | tf_op jit(solution)/shard_map/ppermute | solution.py:739
  297.4 8.4 %collective-permute-start.37 = (bf16[72,16,128]{2,1,0:T(8,128)(2,1)S(1)}, bf16[72,16,128]{2,1,0:T(8,128)(2,1)S(1)}, u32[]{:S(2)}, u32[]{:S(2)}) collective-permute-start(bf16[72,16,128]{2,1,0:T(8,128)(2,1)S(1)} %pad_maximum_fusion.2), channel_id=1, source_target_pairs={{0,4},{4,0},{8,12},{12,8},{16,20},{20,16},{24,28},{28,24},{1,5},{5... | collective-permute-start | bytes 884744 | tf_op jit(solution)/shard_map/ppermute | solution.py:803
  300.1 10.6 %collective-permute-start.38 = (bf16[128,2048]{1,0:T(8,128)(2,1)S(1)}, bf16[128,2048]{1,0:T(8,128)(2,1)S(1)}, u32[]{:S(2)}, u32[]{:S(2)}) collective-permute-start(bf16[128,2048]{1,0:T(8,128)(2,1)S(1)} %get-tuple-element.193), channel_id=1, source_target_pairs={{0,8},{8,16},{16,24},{24,28},{28,20},{20,12},{12,4},{4,0},{1,9},{9... | collective-permute-start | bytes 1572872 | tf_op jit(solution)/shard_map/ppermute | solution.py:739
  300.2 10.5 %collective-permute-start.39 = (bf16[128,2048]{1,0:T(8,128)(2,1)S(1)}, bf16[128,2048]{1,0:T(8,128)(2,1)S(1)}, u32[]{:S(2)}, u32[]{:S(2)}) collective-permute-start(bf16[128,2048]{1,0:T(8,128)(2,1)S(1)} %get-tuple-element.192), channel_id=1, source_target_pairs={{0,4},{8,0},{16,8},{24,16},{28,24},{20,28},{12,20},{4,12},{1,5},{9... | collective-permute-start | bytes 1572872 | tf_op jit(solution)/shard_map/ppermute | solution.py:739
  303.8 12.3 %collective-permute-start.44 = (bf16[128,2048]{1,0:T(8,128)(2,1)S(1)}, bf16[128,2048]{1,0:T(8,128)(2,1)S(1)}, u32[]{:S(2)}, u32[]{:S(2)}) collective-permute-start(bf16[128,2048]{1,0:T(8,128)(2,1)S(1)} %get-tuple-element.189), channel_id=1, source_target_pairs={{0,4},{8,0},{16,8},{24,16},{28,24},{20,28},{12,20},{4,12},{1,5},{9... | collective-permute-start | bytes 1572872 | tf_op jit(solution)/shard_map/ppermute | solution.py:739
  303.9 12.4 %collective-permute-start.43 = (bf16[128,2048]{1,0:T(8,128)(2,1)S(1)}, bf16[128,2048]{1,0:T(8,128)(2,1)S(1)}, u32[]{:S(2)}, u32[]{:S(2)}) collective-permute-start(bf16[128,2048]{1,0:T(8,128)(2,1)S(1)} %get-tuple-element.188), channel_id=1, source_target_pairs={{0,8},{8,16},{16,24},{24,28},{28,20},{20,12},{12,4},{4,0},{1,9},{9... | collective-permute-start | bytes 1572872 | tf_op jit(solution)/shard_map/ppermute | solution.py:739
  306.0 16.3 %copy-start.7 = (bf16[1,128,2048]{2,1,0:T(8,128)(2,1)S(1)}, bf16[1,128,2048]{2,1,0:T(8,128)(2,1)}, u32[]{:S(2)}) copy-start(bf16[1,128,2048]{2,1,0:T(8,128)(2,1)} %rows_ref.1) | copy-start | bytes 1572868
  310.8 11.5 %collective-permute-start.40 = (bf16[140,16,128]{2,1,0:T(8,128)(2,1)S(1)}, bf16[140,16,128]{2,1,0:T(8,128)(2,1)S(1)}, u32[]{:S(2)}, u32[]{:S(2)}) collective-permute-start(bf16[140,16,128]{2,1,0:T(8,128)(2,1)S(1)} %constant_dynamic-update-slice_fusion.3.refs_0_), channel_id=1, source_target_pairs={{0,2},{1,3},{2,0},{3,1},{4,6},{5,7},{6,4},{7,5},{8,10},{9,11},{10,... | collective-permute-start | bytes 1720328 | tf_op jit(solution)/shard_map/ppermute | solution.py:803
  312.8 9.2 %collective-permute-start.41 = (bf16[128,2048]{1,0:T(8,128)(2,1)S(1)}, bf16[128,2048]{1,0:T(8,128)(2,1)S(1)}, u32[]{:S(2)}, u32[]{:S(2)}) collective-permute-start(bf16[128,2048]{1,0:T(8,128)(2,1)S(1)} %get-tuple-element.191), channel_id=1, source_target_pairs={{0,8},{8,16},{16,24},{24,28},{28,20},{20,12},{12,4},{4,0},{1,9},{9... | collective-permute-start | bytes 1572872 | tf_op jit(solution)/shard_map/ppermute | solution.py:739
  313.1 9.2 %collective-permute-start.42 = (bf16[128,2048]{1,0:T(8,128)(2,1)S(1)}, bf16[128,2048]{1,0:T(8,128)(2,1)S(1)}, u32[]{:S(2)}, u32[]{:S(2)}) collective-permute-start(bf16[128,2048]{1,0:T(8,128)(2,1)S(1)} %get-tuple-element.190), channel_id=1, source_target_pairs={{0,4},{8,0},{16,8},{24,16},{28,24},{20,28},{12,20},{4,12},{1,5},{9... | collective-permute-start | bytes 1572872 | tf_op jit(solution)/shard_map/ppermute | solution.py:739
  322.7 2.6 collective-permute-start.46
  322.8 2.8 collective-permute-start.45
  (17 other events, 134.4 us)
Sparse Core Ops, SparseCore 0:
  85.4 23.8 all-gather.5
  110.9 22.5 all-gather.3
